TPU v7x, 32 devices: a whole 2x2x4 slice. The times are simulated.
32 devices in a mesh: grp: 2 (over y), wide: 4 (over z), red: 2 (over x), tok: 2 (over core).
Axes of the slice: x: 2, y: 2, z: 4, core: 2. Of those that a mesh axis runs over, the one named last changes fastest.
Arguments:
- tokens: bfloat16 [1024, 6144], P(('grp', 'tok'), ('red', 'wide')), parts along dimension 0, may hold values from -6 to 6
- ln_gain: bfloat16 [6144], P(('red', 'wide')), may hold values from 0.099609375 to 1.8984375
- q_gain: float32 [4, 128], P('wide'), may hold values from 0.6 to 3
- k_gain: float32 [4, 128], P('wide'), may hold values from 0.6 to 3
- w_qkv: bfloat16 [6144, 4, 384], P(('red', 'tok'), 'wide'), may hold values from -0.078125 to 0.078125
- w_up: bfloat16 [6144, 24576], P(('red', 'tok'), 'wide'), may hold values from -0.078125 to 0.078125
- w_attn: bfloat16 [4, 128, 6144], P('wide', None, ('red', 'tok')), may hold values from -0.25 to 0.25
- w_down: bfloat16 [24576, 6144], P('wide', ('red', 'tok')), may hold values from -0.0546875 to 0.0546875
Outputs:
- block_out: float32 [1024, 6144], P(('grp', 'tok'), ('red', 'wide')), parts along dimension 0
There are 2 independent parts, one for each index of `grp`. A program takes and returns all parts, laid end to end along the dimension named above; an argument that names none is the same for every part. Nothing has to cross between parts.
All inputs are finite; a program needn't handle non-finite values.
Results may differ from a plain program's by a relative error of at most 0.018.
Values may be sent and summed in bfloat16 or wider, within the bound.
No kernel may reach another device: no remote copies, remote signals or barrier semaphores. Data moves between devices by JAX's collectives and lax.ppermute only.
A program may use at most 192 MiB of HBM per device.

v0:
```python
import functools
import math

import jax
import jax.numpy as jnp
from jax import lax
from jax.experimental import pallas as pl
from jax.experimental.pallas import tpu as pltpu
from jax.sharding import PartitionSpec as P

D = 6144
PATCHES = 256
EPS = 1e-06
SHARES = (7, 5, 4)
PIECES = (1, 1)
GAIN_ROWS = 8
BF16, F32 = jnp.bfloat16, jnp.float32
PARAMS = pltpu.CompilerParams(vmem_limit_bytes=44 * 2**20)
SOON = pl.CostEstimate(flops=0, bytes_accessed=0, transcendentals=0)
WHOLE = pl.BlockSpec(memory_space=pl.ANY)


def normalize(values, mean, meansq, gain):
    return (values - mean) * lax.rsqrt(meansq - mean * mean + EPS) * gain.astype(F32)


def head_norm(values, gain):
    mean = jnp.mean(values, axis=-1, keepdims=True)
    meansq = jnp.mean(values * values, axis=-1, keepdims=True)
    return normalize(values, mean, meansq, gain)


def attend(qkv, q_gain, k_gain):
    width = q_gain.shape[1]
    query = head_norm(qkv[:, :width], q_gain[0]).astype(BF16)
    key = head_norm(qkv[:, width : 2 * width], k_gain[0]).astype(BF16)
    value = qkv[:, 2 * width :].astype(BF16)
    query, key, value = (a.reshape(-1, PATCHES, width) for a in (query, key, value))
    scores = jnp.einsum("ipd,iqd->ipq", query, key, preferred_element_type=F32)
    scores = scores * width ** (-0.5)
    weights = jnp.exp(scores - jnp.max(scores, axis=-1, keepdims=True))
    total = jnp.sum(weights, axis=-1, keepdims=True)
    acc = jnp.einsum("ipq,iqd->ipd", weights, value.astype(F32), precision=lax.Precision.HIGHEST)
    return (acc / total).astype(BF16).reshape(-1, width)


def nothing(x):
    corner = x[(0,) * x.ndim].astype(jnp.int32)
    return lax.shift_right_logical(corner & 1, 1).astype(F32)


def slices(size, shares):
    ends = [sum(shares[: i + 1]) * size // sum(shares) for i in range(len(shares))]
    return [slice(a, b) for a, b in zip([0] + ends[:-1], ends)]


def steps_of(piece):
    size = math.gcd(piece.stop - piece.start, piece.start)
    block = next(b for b in (512, 384, 256, 128) if size % b == 0)
    return block, (piece.stop - piece.start) // block, piece.start // block


def call(kernel, earlier, operands, specs, **options):
    def body(*refs):
        n = len(operands)
        kernel(refs[:n], refs[n + len(earlier) :])

    return pl.pallas_call(
        body,
        in_specs=list(specs) + [WHOLE] * len(earlier),
        compiler_params=PARAMS,
        cost_estimate=SOON,
        **options,
    )(*operands, *earlier)


def project_far(other, weight, piece, earlier=()):
    rows, depth = other.shape
    block, steps, skipped = steps_of(piece)

    def kernel(ins, outs):
        part = jnp.dot(ins[0][...], ins[1][...], preferred_element_type=F32)
        outs[0][...] = part.astype(BF16)

    return call(
        kernel,
        earlier,
        (other, weight),
        [
            pl.BlockSpec((rows, depth), lambda j: (0, 0)),
            pl.BlockSpec((depth, block), lambda j: (0, skipped + j)),
        ],
        grid=(steps,),
        out_specs=pl.BlockSpec((rows, block), lambda j: (0, j)),
        out_shape=jax.ShapeDtypeStruct((rows, block * steps), BF16),
    )


def project_near(own, weight, piece, far, cuts, earlier=()):
    rows, depth = own.shape
    block, steps, skipped = steps_of(piece)

    def kernel(ins, outs):
        part = jnp.dot(ins[0][...], ins[1][...], preferred_element_type=F32)
        part = (part + ins[2][...].astype(F32)).astype(BF16)
        for cut, out in zip(cuts, outs):
            out[...] = part[cut]

    heights = [cut.stop - cut.start for cut in cuts]
    return call(
        kernel,
        earlier,
        (own, weight, far),
        [
            pl.BlockSpec((rows, depth), lambda j: (0, 0)),
            pl.BlockSpec((depth, block), lambda j: (0, skipped + j)),
            pl.BlockSpec((rows, block), lambda j: (0, j)),
        ],
        grid=(steps,),
        out_specs=[pl.BlockSpec((height, block), lambda j: (0, j)) for height in heights],
        out_shape=[jax.ShapeDtypeStruct((height, block * steps), BF16) for height in heights],
    )


def gelu_sum(parts, earlier=()):
    rows, units = parts[0].shape
    block, steps, _ = steps_of(slice(0, units))
    spec = pl.BlockSpec((rows, block), lambda j: (0, j))

    def kernel(ins, outs):
        up = ins[0][...].astype(F32)
        for part in ins[1:]:
            up = up + part[...].astype(F32)
        outs[0][...] = (0.5 * up * (1.0 + lax.erf(up * 0.5**0.5))).astype(BF16)

    return call(
        kernel,
        earlier,
        parts,
        [spec] * len(parts),
        grid=(steps,),
        out_specs=spec,
        out_shape=jax.ShapeDtypeStruct((rows, units), BF16),
    )


def project_hidden(own, other, weight, piece, added, attention, last, earlier=()):
    rows = own.shape[0]
    columns = weight.shape[1]
    block, steps, skipped = steps_of(piece)
    whole = pl.BlockSpec((rows, columns), lambda k: (0, 0))
    part = pl.BlockSpec((rows, block), lambda k: (0, k))
    specs = [part, part, pl.BlockSpec((block, columns), lambda k: (skipped + k, 0))]
    specs += [whole] * len(added)
    specs += [pl.BlockSpec(a.shape, lambda k: (0, 0)) for a in attention]

    def kernel(ins, refs):
        outs, totals = refs[:2], refs[2:]
        k = pl.program_id(0)
        both = jnp.concatenate([ins[0][...], ins[1][...]], axis=0)
        product = jnp.dot(both, ins[2][...], preferred_element_type=F32)
        halves = [product[:rows], product[rows:]]

        @pl.when(k == 0)
        def _():
            first = list(halves)
            for at in range(2):
                if added:
                    first[at] = first[at] + ins[3 + at][...]
                if attention:
                    first[at] = first[at] + jnp.dot(
                        ins[-3 + at][...], ins[-1][...], preferred_element_type=F32
                    )
                totals[at][...] = first[at]

        @pl.when(k > 0)
        def _():
            for at in range(2):
                totals[at][...] += halves[at]

        @pl.when(k == steps - 1)
        def _():
            for at in range(2):
                outs[at][...] = totals[at][...].astype(outs[at].dtype)

    return call(
        kernel,
        earlier,
        (own, other, weight, *added, *attention),
        specs,
        grid=(steps,),
        out_specs=[whole] * 2,
        out_shape=[jax.ShapeDtypeStruct((rows, columns), BF16 if last else F32)] * 2,
        scratch_shapes=[pltpu.VMEM((rows, columns), F32)] * 2,
    )


def make_body(mesh):
    n_red, n_wide = mesh.shape["red"], mesh.shape["wide"]
    half_wide = n_wide // 2

    def swap(x):
        return lax.ppermute(x, "tok", [(0, 1), (1, 0)])

    def all_red(x):
        parts = [x]
        for shift in range(1, n_red):
            pairs = [(i, (i + shift) % n_red) for i in range(n_red)]
            parts.append(lax.ppermute(x, "red", pairs))
        return parts

    def sum_red(x):
        return sum(a.astype(F32) for a in all_red(x))

    def collect(kept, got, width):
        core, chip = lax.axis_index("tok"), lax.axis_index("wide")
        terms = jnp.concatenate([kept, got], axis=1)

        def block(at):
            start = ((at // half_wide) ^ core) * half_wide + at % half_wide
            return lax.dynamic_slice_in_dim(terms, start * width, width, axis=1)

        total = block(chip).astype(F32)
        for k in range(n_wide - 1, 0, -1):
            pairs = [(i, i ^ k) for i in range(n_wide)]
            total = total + lax.ppermute(block(chip ^ k), "wide", pairs).astype(F32)
        return total

    def body(tokens, ln_gain, q_gain, k_gain, w_qkv, w_up, w_attn, w_down):
        core = lax.axis_index("tok")
        width = tokens.shape[1]
        qkv_rows = w_qkv.reshape(w_qkv.shape[0], w_qkv.shape[1] * w_qkv.shape[2])
        attn_rows = w_attn.reshape(w_attn.shape[0] * w_attn.shape[1], w_attn.shape[2])
        depth, units = w_up.shape
        cuts = slices(tokens.shape[0], SHARES)
        pieces = slices(units, PIECES)
        n = len(cuts)

        gain_rows = jnp.broadcast_to(ln_gain[None], (GAIN_ROWS, width))
        raw = jnp.concatenate([gain_rows, tokens], axis=0)
        raw = lax.all_gather(raw, "wide", axis=1, tiled=True)
        floats = raw[GAIN_ROWS:].astype(F32)
        sums = jnp.stack([jnp.sum(floats, axis=1), jnp.sum(floats * floats, axis=1)])
        sums = sum_red(sums)[:, :, None] / D
        normed = normalize(floats, sums[0], sums[1], raw[:1]).astype(BF16)
        own = lax.dynamic_slice_in_dim(normed, core * depth, depth, axis=1)
        other = lax.dynamic_slice_in_dim(normed, (1 - core) * depth, depth, axis=1)
        other = swap(other)

        every = slice(0, qkv_rows.shape[1])
        far_qkv = project_far(other, qkv_rows, every)
        fars, earlier = [], far_qkv
        for piece in pieces:
            fars.append(project_far(other, w_up, piece, [earlier]))
            earlier = fars[-1]
        (qkv,) = project_near(
            own, qkv_rows, every, swap(far_qkv), [slice(0, tokens.shape[0])], [earlier]
        )
        earlier = qkv
        sums = []
        for piece, far in zip(pieces, fars):
            sums.append(project_near(own, w_up, piece, swap(far), cuts, [earlier]))
            earlier = sums[-1][-1]

        order = [(c, p) for c in range(n) for p in range(len(pieces))]
        outs, scattered = [], []
        terms, waiting = (), None
        earlier = [earlier]

        def output(at, have, terms, earlier):
            c, p = order[at]
            attention = (attended[cuts[c]], attended_other[cuts[c]], attn_rows)
            return project_hidden(
                have,
                swap(have),
                w_down,
                pieces[p],
                terms if p else (),
                () if p else attention,
                p == len(pieces) - 1,
                earlier,
            )

        def scatter(kept, got):
            lower = jnp.where(core == 0, kept, got)
            upper = jnp.where(core == 0, got, kept)
            full = jnp.concatenate([lower, upper], axis=1)
            scattered.append(lax.psum_scatter(full, "wide", scatter_dimension=1, tiled=True))
            return full

        hidden = None
        for at, (c, p) in enumerate(order):
            arrived = gelu_sum(all_red(sums[p][c]), earlier)
            earlier = [arrived]
            if at == 0:
                attended = attend(sum_red(qkv) + nothing(arrived), q_gain, k_gain)
                attended_other = swap(attended)
                earlier = [attended]
            if waiting is not None:
                earlier.append(scatter(*waiting))
                waiting = None
            if at:
                terms = output(at - 1, hidden, terms, earlier)
                earlier = [terms[0]]
                if p == 0:
                    waiting = (terms[0], swap(terms[1]))
            hidden = arrived
        if waiting is not None:
            earlier.append(scatter(*waiting))
        terms = output(len(order) - 1, hidden, terms, earlier + scattered[:1])
        for cut, summed in zip(cuts, scattered):
            outs.append(tokens[cut].astype(F32) + summed.astype(F32))
        outs.append(tokens[cuts[-1]].astype(F32) + collect(terms[0], swap(terms[1]), width))
        return jnp.concatenate(outs, axis=0)

    return body


def solution(mesh):
    return jax.shard_map(
        make_body(mesh),
        mesh=mesh,
        in_specs=(
            P(("grp", "tok"), ("red", "wide")),
            P(("red", "wide")),
            P("wide", None),
            P("wide", None),
            P(("red", "tok"), "wide", None),
            P(("red", "tok"), "wide"),
            P("wide", None, ("red", "tok")),
            P("wide", ("red", "tok")),
        ),
        out_specs=P(("grp", "tok"), ("red", "wide")),
        check_vma=False,
    )
```

profile of v0, /device:TPU:0, one launch (start us, length us, event | category | flops | bytes accessed | tf_op | source)
XLA Modules:
  0.0 208.5 jit_solution(9840616840361872357)
XLA Ops:
  7.2 1.8 pad_maximum_fusion.3
  9.1 40.7 %all-gather.2.cloned.1.call-done = bf16[264,3072]{1,0:T(8,128)(2,1)} async-done(((bf16[264,768]{1,0:T(8,128)(2,1)}), bf16[264,3072]{1,0:T(8,128)(2,1)}) %all-gather.2.cloned.1.call-update) | async-done | bytes 1622032 | tf_op jit(solution)/shard_map/all_gather | solution.py:241
  49.8 2.1 %convert_reduce_fusion = (f32[256]{0:T(256)S(1)}, f32[256]{0:T(256)S(1)}) fusion(bf16[264,3072]{1,0:T(8,128)(2,1)} %all-gather.2.cloned.1.call-done), kind=kLoop, calls=%fused_computation.2 | loop fusion | flops 3145216 | bytes 1574912 | tf_op jit(solution)/shard_map/reduce_sum | solution.py:243
  56.5 2.3 %collective-permute-done.1.refs_0_ = bf16[256,1536]{1,0:T(8,128)(2,1)S(1)} collective-permute-done((bf16[256,1536]{1,0:T(8,128)(2,1)S(1)}, bf16[256,1536]{1,0:T(8,128)(2,1)S(1)}, u32[]{:S(2)}, u32[]{:S(2)}) %collective-permute-start.1) | collective-permute-done | bytes 786464 | tf_op jit(solution)/shard_map/ppermute | solution.py:203
  59.4 6.8 %shard_map.83.refs_2_ = bf16[256,3072]{1,0:T(8,128)(2,1)S(1)} custom-call(bf16[256,1536]{1,0:T(8,128)(2,1)S(1)} %collective-permute-done.1.refs_0_, bf16[1536,6144]{1,0:T(8,128)(2,1)} %refs_1_.7, bf16[256,384]{1,0:T(8,128)(2,1)S(1)} %shard_map.82.refs_2_), custom_call_target="tpu_custom_call" | custom-call | tf_op jit(solution)/shard_map/pallas_call | solution.py:68
  66.4 6.8 %shard_map.84.refs_3_ = bf16[256,3072]{1,0:T(8,128)(2,1)S(1)} custom-call(bf16[256,1536]{1,0:T(8,128)(2,1)S(1)} %collective-permute-done.1.refs_0_, bf16[1536,6144]{1,0:T(8,128)(2,1)} %refs_1_.7, bf16[256,3072]{1,0:T(8,128)(2,1)S(1)} %shard_map.83.refs_2_), custom_call_target="tpu_custom_call" | custom-call | tf_op jit(solution)/shard_map/pallas_call | solution.py:68
  73.8 3.2 %collective-permute-done.4.refs_2_ = bf16[256,384]{1,0:T(8,128)(2,1)S(1)} collective-permute-done((bf16[256,384]{1,0:T(8,128)(2,1)S(1)}, bf16[256,384]{1,0:T(8,128)(2,1)S(1)}, u32[]{:S(2)}, u32[]{:S(2)}) %collective-permute-start.4) | collective-permute-done | bytes 196640 | tf_op jit(solution)/shard_map/ppermute | solution.py:203
  77.6 6.9 %shard_map.86 = (bf16[112,3072]{1,0:T(8,128)(2,1)S(1)}, bf16[80,3072]{1,0:T(8,128)(2,1)S(1)}, bf16[64,3072]{1,0:T(8,128)(2,1)S(1)}) custom-call(bf16[256,1536]{1,0:T(8,128)(2,1)S(1)} %get-tuple-element.48.refs_0_, bf16[1536,6144]{1,0:T(8,128)(2,1)} %refs_1_.7, bf16[256,3072]{1,0:T(8,128)(2,1)S(1)} %collective-permute-done.3.refs_2_, ...), custom_call_target="tpu_custom_call" | custom-call | tf_op jit(solution)/shard_map/pallas_call | solution.py:68
  84.5 1.5 collective-permute-start.7
  86.6 6.9 %shard_map.87 = (bf16[112,3072]{1,0:T(8,128)(2,1)S(1)}, bf16[80,3072]{1,0:T(8,128)(2,1)S(1)}, bf16[64,3072]{1,0:T(8,128)(2,1)S(1)}) custom-call(bf16[256,1536]{1,0:T(8,128)(2,1)S(1)} %get-tuple-element.48.refs_0_, bf16[1536,6144]{1,0:T(8,128)(2,1)} %refs_1_.7, bf16[256,3072]{1,0:T(8,128)(2,1)S(1)} %collective-permute-done.2.refs_2_, ...), custom_call_target="tpu_custom_call" | custom-call | tf_op jit(solution)/shard_map/pallas_call | solution.py:68
  95.0 7.8 %collective-permute-done.7.refs_1_ = bf16[112,3072]{1,0:T(8,128)(2,1)S(1)} collective-permute-done((bf16[112,3072]{1,0:T(8,128)(2,1)S(1)}, bf16[112,3072]{1,0:T(8,128)(2,1)S(1)}, u32[]{:S(2)}, u32[]{:S(2)}) %collective-permute-start.7) | collective-permute-done | bytes 688160 | tf_op jit(solution)/shard_map/ppermute | solution.py:209
  104.7 2.4 %collective-permute-done.6 = bf16[256,384]{1,0:T(8,128)(2,1)S(1)} collective-permute-done((bf16[256,384]{1,0:T(8,128)(2,1)S(1)}, bf16[256,384]{1,0:T(8,128)(2,1)S(1)}, u32[]{:S(2)}, u32[]{:S(2)}) %collective-permute-start.6) | collective-permute-done | bytes 196640 | tf_op jit(solution)/shard_map/ppermute | solution.py:209
  108.2 13.0 %collective-permute-done.5.refs_1_ = bf16[112,3072]{1,0:T(8,128)(2,1)S(1)} collective-permute-done((bf16[112,3072]{1,0:T(8,128)(2,1)S(1)}, bf16[112,3072]{1,0:T(8,128)(2,1)S(1)}, u32[]{:S(2)}, u32[]{:S(2)}) %collective-permute-start.5) | collective-permute-done | bytes 688160 | tf_op jit(solution)/shard_map/ppermute | solution.py:209
  125.3 7.5 %shard_map.90 = (f32[112,1536]{1,0:T(8,128)S(1)}, f32[112,1536]{1,0:T(8,128)S(1)}) custom-call(bf16[112,3072]{1,0:T(8,128)(2,1)S(1)} %shard_map.88.refs_0_, bf16[112,3072]{1,0:T(8,128)(2,1)S(1)} %collective-permute-done.9.refs_1_, bf16[6144,1536]{1,0:T(8,128)(2,1)} %refs_2_.11, bf16[112,128]{1,0:T(8,128)(2,1)S(1)} %slice_bitcast_fusion.refs_3_, ...), custom_call_target="tpu_custom_call" | custom-call | tf_op jit(solution)/shard_map/pallas_call | solution.py:68
  132.9 3.2 %collective-permute-done.11.refs_1_ = bf16[80,3072]{1,0:T(8,128)(2,1)S(1)} collective-permute-done((bf16[80,3072]{1,0:T(8,128)(2,1)S(1)}, bf16[80,3072]{1,0:T(8,128)(2,1)S(1)}, u32[]{:S(2)}, u32[]{:S(2)}) %collective-permute-start.11) | collective-permute-done | bytes 491552 | tf_op jit(solution)/shard_map/ppermute | solution.py:209
  136.6 8.0 %shard_map.92 = (bf16[112,1536]{1,0:T(8,128)(2,1)S(1)}, bf16[112,1536]{1,0:T(8,128)(2,1)}) custom-call(bf16[112,3072]{1,0:T(8,128)(2,1)S(1)} %shard_map.89.refs_6_.refs_0_, bf16[112,3072]{1,0:T(8,128)(2,1)S(1)} %collective-permute-done.8.refs_1_, bf16[6144,1536]{1,0:T(8,128)(2,1)} %refs_2_.11, f32[112,1536]{1,0:T(8,128)S(1)} %get-tuple-element.27.refs_2_.refs_3_, ...), custom_call_target="tpu_custom_call" | custom-call | tf_op jit(solution)/shard_map/pallas_call | solution.py:68
  152.3 7.1 %shard_map.94 = (f32[80,1536]{1,0:T(8,128)S(1)}, f32[80,1536]{1,0:T(8,128)S(1)}) custom-call(bf16[80,3072]{1,0:T(8,128)(2,1)S(1)} %shard_map.91.refs_5_.refs_0_, bf16[80,3072]{1,0:T(8,128)(2,1)} %collective-permute-done.15.refs_1_, bf16[6144,1536]{1,0:T(8,128)(2,1)} %refs_2_.11, bf16[80,128]{1,0:T(8,128)(2,1)S(1)} %slice_bitcast_fusion.1.refs_3_, ...), custom_call_target="tpu_custom_call" | custom-call | tf_op jit(solution)/shard_map/pallas_call | solution.py:68
  159.4 2.8 %shard_map.95.refs_5_.refs_0_ = bf16[64,3072]{1,0:T(8,128)(2,1)S(1)} custom-call(bf16[64,3072]{1,0:T(8,128)(2,1)S(1)} %get-tuple-element.23.refs_3_.refs_0_, bf16[64,3072]{1,0:T(8,128)(2,1)} %collective-permute-done.16.refs_1_, f32[80,1536]{1,0:T(8,128)S(1)} %get-tuple-element.33.refs_2_.refs_3_), custom_call_target="tpu_custom_call" | custom-call | tf_op jit(solution)/shard_map/pallas_call | solution.py:68
  162.3 7.4 %shard_map.96 = (bf16[80,1536]{1,0:T(8,128)(2,1)S(1)}, bf16[80,1536]{1,0:T(8,128)(2,1)}) custom-call(bf16[80,3072]{1,0:T(8,128)(2,1)S(1)} %shard_map.93.refs_6_.refs_0_, bf16[80,3072]{1,0:T(8,128)(2,1)S(1)} %collective-permute-done.14.refs_1_, bf16[6144,1536]{1,0:T(8,128)(2,1)} %refs_2_.11, f32[80,1536]{1,0:T(8,128)S(1)} %get-tuple-element.33.refs_2_.refs_3_, ...), custom_call_target="tpu_custom_call" | custom-call | tf_op jit(solution)/shard_map/pallas_call | solution.py:68
  174.1 6.7 %shard_map.98 = (f32[64,1536]{1,0:T(8,128)S(1)}, f32[64,1536]{1,0:T(8,128)S(1)}) custom-call(bf16[64,3072]{1,0:T(8,128)(2,1)S(1)} %shard_map.95.refs_5_.refs_0_, bf16[64,3072]{1,0:T(8,128)(2,1)S(1)} %collective-permute-done.20.refs_1_, bf16[6144,1536]{1,0:T(8,128)(2,1)} %refs_2_.11, bf16[64,128]{1,0:T(8,128)(2,1)S(1)} %slice_bitcast_fusion.2.refs_3_, ...), custom_call_target="tpu_custom_call" | custom-call | tf_op jit(solution)/shard_map/pallas_call | solution.py:68
  181.8 6.5 %shard_map.99 = (bf16[64,1536]{1,0:T(8,128)(2,1)S(1)}, bf16[64,1536]{1,0:T(8,128)(2,1)S(1)}) custom-call(bf16[64,3072]{1,0:T(8,128)(2,1)S(1)} %shard_map.97.refs_6_.refs_0_, bf16[64,3072]{1,0:T(8,128)(2,1)S(1)} %collective-permute-done.19.refs_1_, bf16[6144,1536]{1,0:T(8,128)(2,1)} %refs_2_.11, f32[64,1536]{1,0:T(8,128)S(1)} %get-tuple-element.37.refs_3_.refs_5_, ...), custom_call_target="tpu_custom_call" | custom-call | tf_op jit(solution)/shard_map/pallas_call | solution.py:68
  191.7 2.5 %collective-permute-start.24 = (bf16[64,768]{1,0:T(8,128)(2,1)S(1)}, bf16[64,768]{1,0:T(8,128)(2,1)S(1)}, u32[]{:S(2)}, u32[]{:S(2)}) collective-permute-start(bf16[64,768]{1,0:T(8,128)(2,1)S(1)} %get-tuple-element.54), channel_id=1, source_target_pairs={{0,4},{4,0},{8,12},{12,8},{1,5},{5,1},{9,13},{13,9},{2,6},{6,2},{1... | collective-permute-start | bytes 294920 | tf_op jit(solution)/shard_map/ppermute | solution.py:226
  195.2 2.2 %collective-permute-done.22 = bf16[64,768]{1,0:T(8,128)(2,1)S(1)} collective-permute-done((bf16[64,768]{1,0:T(8,128)(2,1)S(1)}, bf16[64,768]{1,0:T(8,128)(2,1)S(1)}, u32[]{:S(2)}, u32[]{:S(2)}) %collective-permute-start.22) | collective-permute-done | bytes 98336 | tf_op jit(solution)/shard_map/ppermute | solution.py:226
  197.4 3.5 %collective-permute-done.23 = bf16[64,768]{1,0:T(8,128)(2,1)S(1)} collective-permute-done((bf16[64,768]{1,0:T(8,128)(2,1)S(1)}, bf16[64,768]{1,0:T(8,128)(2,1)S(1)}, u32[]{:S(2)}, u32[]{:S(2)}) %collective-permute-start.23) | collective-permute-done | bytes 98336 | tf_op jit(solution)/shard_map/ppermute | solution.py:226
  (111 shorter events, 34.6 us)
Async XLA Ops:
  6.5 43.2 %all-gather.2.cloned.1.call-start = ((), (), s32[]{:S(2)}) async-start(), calls=%async_computation.2 | async-start | bytes 2027520 | tf_op jit(solution)/shard_map/all_gather | solution.py:241
  9.0 171.8 %reduce-scatter.3.cloned.1.call-start = ((), (), s32[]{:S(2)}) async-start(), calls=%async_computation.3 | async-start | bytes 860160 | tf_op jit(solution)/shard_map/reduce_scatter | solution.py:288
  51.9 3.7 %collective-permute-start = (f32[2,256]{1,0:T(2,128)S(1)}, f32[2,256]{1,0:T(2,128)S(1)}, u32[]{:S(2)}, u32[]{:S(2)}) collective-permute-start(f32[2,256]{1,0:T(2,128)S(1)} %pad_maximum_fusion.4), channel_id=1, source_target_pairs={{0,2},{2,0},{1,3},{3,1},{4,6},{6,4},{5,7},{7,5},{8,10},{10,8},{9,1... | collective-permute-start | bytes 6152 | tf_op jit(solution)/shard_map/ppermute | solution.py:209
  66.2 11.4 %collective-permute-start.3 = (bf16[256,3072]{1,0:T(8,128)(2,1)S(1)}, bf16[256,3072]{1,0:T(8,128)(2,1)S(1)}, u32[]{:S(2)}, u32[]{:S(2)}) collective-permute-start(bf16[256,3072]{1,0:T(8,128)(2,1)S(1)} %shard_map.83.refs_2_), channel_id=1, source_target_pairs={{0,1},{1,0},{2,3},{3,2},{4,5},{5,4},{6,7},{7,6},{8,9},{9,8},{10,11... | collective-permute-start | bytes 4718600 | tf_op jit(solution)/shard_map/ppermute | solution.py:203
  73.2 13.3 %collective-permute-start.2 = (bf16[256,3072]{1,0:T(8,128)(2,1)S(1)}, bf16[256,3072]{1,0:T(8,128)(2,1)S(1)}, u32[]{:S(2)}, u32[]{:S(2)}) collective-permute-start(bf16[256,3072]{1,0:T(8,128)(2,1)S(1)} %shard_map.84.refs_3_), channel_id=1, source_target_pairs={{0,1},{1,0},{2,3},{3,2},{4,5},{5,4},{6,7},{7,6},{8,9},{9,8},{10,11... | collective-permute-start | bytes 4718600 | tf_op jit(solution)/shard_map/ppermute | solution.py:203
  73.7 3.3 %collective-permute-start.4 = (bf16[256,384]{1,0:T(8,128)(2,1)S(1)}, bf16[256,384]{1,0:T(8,128)(2,1)S(1)}, u32[]{:S(2)}, u32[]{:S(2)}) collective-permute-start(bf16[256,384]{1,0:T(8,128)(2,1)S(1)} %shard_map.82.refs_2_), channel_id=1, source_target_pairs={{0,1},{1,0},{2,3},{3,2},{4,5},{5,4},{6,7},{7,6},{8,9},{9,8},{10,11... | collective-permute-start | bytes 589832 | tf_op jit(solution)/shard_map/ppermute | solution.py:203
  84.5 18.3 %collective-permute-start.7 = (bf16[112,3072]{1,0:T(8,128)(2,1)S(1)}, bf16[112,3072]{1,0:T(8,128)(2,1)S(1)}, u32[]{:S(2)}, u32[]{:S(2)}) collective-permute-start(bf16[112,3072]{1,0:T(8,128)(2,1)S(1)} %get-tuple-element.25.refs_0_), channel_id=1, source_target_pairs={{0,2},{2,0},{1,3},{3,1},{4,6},{6,4},{5,7},{7,5},{8,10},{10,8},{9,1... | collective-permute-start | bytes 2064392 | tf_op jit(solution)/shard_map/ppermute | solution.py:209
  86.0 21.0 %collective-permute-start.6 = (bf16[256,384]{1,0:T(8,128)(2,1)S(1)}, bf16[256,384]{1,0:T(8,128)(2,1)S(1)}, u32[]{:S(2)}, u32[]{:S(2)}) collective-permute-start(bf16[256,384]{1,0:T(8,128)(2,1)S(1)} %shard_map.85.refs_3_), channel_id=1, source_target_pairs={{0,2},{2,0},{1,3},{3,1},{4,6},{6,4},{5,7},{7,5},{8,10},{10,8},{9,1... | collective-permute-start | bytes 589832 | tf_op jit(solution)/shard_map/ppermute | solution.py:209
  93.5 27.7 %collective-permute-start.5 = (bf16[112,3072]{1,0:T(8,128)(2,1)S(1)}, bf16[112,3072]{1,0:T(8,128)(2,1)S(1)}, u32[]{:S(2)}, u32[]{:S(2)}) collective-permute-start(bf16[112,3072]{1,0:T(8,128)(2,1)S(1)} %get-tuple-element.24.refs_0_), channel_id=1, source_target_pairs={{0,2},{2,0},{1,3},{3,1},{4,6},{6,4},{5,7},{7,5},{8,10},{10,8},{9,1... | collective-permute-start | bytes 2064392 | tf_op jit(solution)/shard_map/ppermute | solution.py:209
  104.0 21.3 %collective-permute-start.9 = (bf16[112,3072]{1,0:T(8,128)(2,1)S(1)}, bf16[112,3072]{1,0:T(8,128)(2,1)S(1)}, u32[]{:S(2)}, u32[]{:S(2)}) collective-permute-start(bf16[112,3072]{1,0:T(8,128)(2,1)S(1)} %shard_map.88.refs_0_), channel_id=1, source_target_pairs={{0,1},{1,0},{2,3},{3,2},{4,5},{5,4},{6,7},{7,6},{8,9},{9,8},{10,11... | collective-permute-start | bytes 2064392 | tf_op jit(solution)/shard_map/ppermute | solution.py:203
  121.9 14.7 %collective-permute-start.8 = (bf16[112,3072]{1,0:T(8,128)(2,1)S(1)}, bf16[112,3072]{1,0:T(8,128)(2,1)S(1)}, u32[]{:S(2)}, u32[]{:S(2)}) collective-permute-start(bf16[112,3072]{1,0:T(8,128)(2,1)S(1)} %shard_map.89.refs_6_.refs_0_), channel_id=1, source_target_pairs={{0,1},{1,0},{2,3},{3,2},{4,5},{5,4},{6,7},{7,6},{8,9},{9,8},{10,11... | collective-permute-start | bytes 2064392 | tf_op jit(solution)/shard_map/ppermute | solution.py:203
  122.0 14.1 %collective-permute-start.11 = (bf16[80,3072]{1,0:T(8,128)(2,1)S(1)}, bf16[80,3072]{1,0:T(8,128)(2,1)S(1)}, u32[]{:S(2)}, u32[]{:S(2)}) collective-permute-start(bf16[80,3072]{1,0:T(8,128)(2,1)S(1)} %get-tuple-element.29.refs_0_), channel_id=1, source_target_pairs={{0,2},{2,0},{1,3},{3,1},{4,6},{6,4},{5,7},{7,5},{8,10},{10,8},{9,1... | collective-permute-start | bytes 1474568 | tf_op jit(solution)/shard_map/ppermute | solution.py:209
  123.5 22.8 %collective-permute-start.13 = (bf16[80,3072]{1,0:T(8,128)(2,1)S(1)}, bf16[80,3072]{1,0:T(8,128)(2,1)S(1)}, u32[]{:S(2)}, u32[]{:S(2)}) collective-permute-start(bf16[80,3072]{1,0:T(8,128)(2,1)S(1)} %get-tuple-element.32.refs_0_), channel_id=1, source_target_pairs={{0,2},{2,0},{1,3},{3,1},{4,6},{6,4},{5,7},{7,5},{8,10},{10,8},{9,1... | collective-permute-start | bytes 1474568 | tf_op jit(solution)/shard_map/ppermute | solution.py:209
  144.6 2.6 %collective-permute-start.12 = (bf16[112,1536]{1,0:T(8,128)(2,1)}, bf16[112,1536]{1,0:T(8,128)(2,1)}, u32[]{:S(2)}, u32[]{:S(2)}) collective-permute-start(bf16[112,1536]{1,0:T(8,128)(2,1)} %get-tuple-element.31), channel_id=1, source_target_pairs={{0,1},{1,0},{2,3},{3,2},{4,5},{5,4},{6,7},{7,6},{8,9},{9,8},{10,11... | collective-permute-start | bytes 1032200 | tf_op jit(solution)/shard_map/ppermute | solution.py:203
  144.6 14.8 %collective-permute-start.16 = (bf16[64,3072]{1,0:T(8,128)(2,1)S(1)}, bf16[64,3072]{1,0:T(8,128)(2,1)}, u32[]{:S(2)}, u32[]{:S(2)}) collective-permute-start(bf16[64,3072]{1,0:T(8,128)(2,1)S(1)} %get-tuple-element.23.refs_3_.refs_0_), channel_id=1, source_target_pairs={{0,2},{2,0},{1,3},{3,1},{4,6},{6,4},{5,7},{7,5},{8,10},{10,8},{9,1... | collective-permute-start | bytes 1179656 | tf_op jit(solution)/shard_map/ppermute | solution.py:209
  146.1 5.1 %collective-permute-start.15 = (bf16[80,3072]{1,0:T(8,128)(2,1)S(1)}, bf16[80,3072]{1,0:T(8,128)(2,1)}, u32[]{:S(2)}, u32[]{:S(2)}) collective-permute-start(bf16[80,3072]{1,0:T(8,128)(2,1)S(1)} %shard_map.91.refs_5_.refs_0_), channel_id=1, source_target_pairs={{0,1},{1,0},{2,3},{3,2},{4,5},{5,4},{6,7},{7,6},{8,9},{9,8},{10,11... | collective-permute-start | bytes 1474568 | tf_op jit(solution)/shard_map/ppermute | solution.py:203
  146.9 15.4 %collective-permute-start.14 = (bf16[80,3072]{1,0:T(8,128)(2,1)S(1)}, bf16[80,3072]{1,0:T(8,128)(2,1)S(1)}, u32[]{:S(2)}, u32[]{:S(2)}) collective-permute-start(bf16[80,3072]{1,0:T(8,128)(2,1)S(1)} %shard_map.93.refs_6_.refs_0_), channel_id=1, source_target_pairs={{0,1},{1,0},{2,3},{3,2},{4,5},{5,4},{6,7},{7,6},{8,9},{9,8},{10,11... | collective-permute-start | bytes 1474568 | tf_op jit(solution)/shard_map/ppermute | solution.py:203
  149.2 45.1 %reduce-scatter.5.cloned.1.call-start = ((), (), s32[]{:S(2)}) async-start(), calls=%async_computation.4 | async-start | bytes 614400 | tf_op jit(solution)/shard_map/reduce_scatter | solution.py:288
  149.4 20.8 %collective-permute-start.18 = (bf16[64,3072]{1,0:T(8,128)(2,1)S(1)}, bf16[64,3072]{1,0:T(8,128)(2,1)S(1)}, u32[]{:S(2)}, u32[]{:S(2)}) collective-permute-start(bf16[64,3072]{1,0:T(8,128)(2,1)S(1)} %get-tuple-element.26.refs_2_.refs_0_), channel_id=1, source_target_pairs={{0,2},{2,0},{1,3},{3,1},{4,6},{6,4},{5,7},{7,5},{8,10},{10,8},{9,1... | collective-permute-start | bytes 1179656 | tf_op jit(solution)/shard_map/ppermute | solution.py:209
  169.9 3.2 %collective-permute-start.20 = (bf16[64,3072]{1,0:T(8,128)(2,1)S(1)}, bf16[64,3072]{1,0:T(8,128)(2,1)S(1)}, u32[]{:S(2)}, u32[]{:S(2)}) collective-permute-start(bf16[64,3072]{1,0:T(8,128)(2,1)S(1)} %shard_map.95.refs_5_.refs_0_), channel_id=1, source_target_pairs={{0,1},{1,0},{2,3},{3,2},{4,5},{5,4},{6,7},{7,6},{8,9},{9,8},{10,11... | collective-permute-start | bytes 1179656 | tf_op jit(solution)/shard_map/ppermute | solution.py:203
  170.7 10.1 %collective-permute-start.19 = (bf16[64,3072]{1,0:T(8,128)(2,1)S(1)}, bf16[64,3072]{1,0:T(8,128)(2,1)S(1)}, u32[]{:S(2)}, u32[]{:S(2)}) collective-permute-start(bf16[64,3072]{1,0:T(8,128)(2,1)S(1)} %shard_map.97.refs_6_.refs_0_), channel_id=1, source_target_pairs={{0,1},{1,0},{2,3},{3,2},{4,5},{5,4},{6,7},{7,6},{8,9},{9,8},{10,11... | collective-permute-start | bytes 1179656 | tf_op jit(solution)/shard_map/ppermute | solution.py:203
  189.8 7.6 %collective-permute-start.22 = (bf16[64,768]{1,0:T(8,128)(2,1)S(1)}, bf16[64,768]{1,0:T(8,128)(2,1)S(1)}, u32[]{:S(2)}, u32[]{:S(2)}) collective-permute-start(bf16[64,768]{1,0:T(8,128)(2,1)S(1)} %get-tuple-element.53), channel_id=1, source_target_pairs={{0,12},{4,8},{8,4},{12,0},{1,13},{5,9},{9,5},{13,1},{2,14},{6,10},... | collective-permute-start | bytes 294920 | tf_op jit(solution)/shard_map/ppermute | solution.py:226
  191.1 9.8 %collective-permute-start.23 = (bf16[64,768]{1,0:T(8,128)(2,1)S(1)}, bf16[64,768]{1,0:T(8,128)(2,1)S(1)}, u32[]{:S(2)}, u32[]{:S(2)}) collective-permute-start(bf16[64,768]{1,0:T(8,128)(2,1)S(1)} %get-tuple-element.55), channel_id=1, source_target_pairs={{0,8},{4,12},{8,0},{12,4},{1,9},{5,13},{9,1},{13,5},{2,10},{6,14},... | collective-permute-start | bytes 294920 | tf_op jit(solution)/shard_map/ppermute | solution.py:226
  191.7 9.2 %collective-permute-start.24 = (bf16[64,768]{1,0:T(8,128)(2,1)S(1)}, bf16[64,768]{1,0:T(8,128)(2,1)S(1)}, u32[]{:S(2)}, u32[]{:S(2)}) collective-permute-start(bf16[64,768]{1,0:T(8,128)(2,1)S(1)} %get-tuple-element.54), channel_id=1, source_target_pairs={{0,4},{4,0},{8,12},{12,8},{1,5},{5,1},{9,13},{13,9},{2,6},{6,2},{1... | collective-permute-start | bytes 294920 | tf_op jit(solution)/shard_map/ppermute | solution.py:226
  (16 other events, 80.0 us)
Sparse Core Ops, SparseCore 0:
  9.1 40.5 all-gather.1
  149.3 21.0 reduce-scatter.2
  172.8 20.2 reduce-scatter.4
where the time goes:
time: 210 us; the launch traced here: 208 us
  waiting for transfers between devices  82.6 us (39%)
  Pallas kernels  77.5 us (37%)
  starting transfers between devices  17 us (8%)
  between operations  14.2 us (7%)
  other arithmetic  10.6 us (5%)
  local copies, waits for them, and re-layouts  5.93 us (3%)
    pallas_call x18, Pallas kernels, call(): pl.pallas_call(body, in_specs=list(specs) + [WHOLE] * len(earlier), compi...  77.5 us
    all_gather x1, waiting for transfers between devices, body(): raw = lax.all_gather(raw, 'wide', axis=1, tiled=True)  40.7 us
    ppermute x8, waiting for transfers between devices, all_red(): parts.append(lax.ppermute(x, 'red', pairs))  27.7 us
    ppermute x8, starting transfers between devices, all_red(): parts.append(lax.ppermute(x, 'red', pairs))  9.8 us
    ppermute x14, waiting for transfers between devices, swap(): return lax.ppermute(x, 'tok', [(0, 1), (1, 0)])  8.41 us
    ppermute x3, waiting for transfers between devices, collect(): total = total + lax.ppermute(block(chip ^ k), 'wide', pairs).astype(F32)  5.76 us
    ppermute x3, starting transfers between devices, collect(): total = total + lax.ppermute(block(chip ^ k), 'wide', pairs).astype(F32)  4.45 us
  transfers between devices with their start and end apart: 28, of which 13 were waited for; matrix products, arithmetic and copies ran while one was open for 4% of the time, Pallas kernels for 34%

commit v1 on v0

--- a/solution.py
+++ b/solution.py
@@ -13,7 +13,7 @@
 EPS = 1e-06
 SHARES = (7, 5, 4)
 PIECES = (1, 1)
-GAIN_ROWS = 8
+PARTS = 4
 BF16, F32 = jnp.bfloat16, jnp.float32
 PARAMS = pltpu.CompilerParams(vmem_limit_bytes=44 * 2**20)
 SOON = pl.CostEstimate(flops=0, bytes_accessed=0, transcendentals=0)
@@ -54,10 +54,28 @@
     return [slice(a, b) for a, b in zip([0] + ends[:-1], ends)]
 
 
-def steps_of(piece):
+def steps_of(piece, blocks=(512, 384, 256, 128)):
     size = math.gcd(piece.stop - piece.start, piece.start)
-    block = next(b for b in (512, 384, 256, 128) if size % b == 0)
+    block = next(b for b in blocks if size % b == 0)
     return block, (piece.stop - piece.start) // block, piece.start // block
+
+
+def row_parts(block, columns, index):
+    return [
+        pl.BlockSpec(
+            (block // PARTS, columns),
+            lambda j, part=part: (PARTS * index(j)[0] + part, index(j)[1]),
+        )
+        for part in range(PARTS)
+    ]
+
+
+def dot_parts(x, weights):
+    depth = x.shape[1] // PARTS
+    return sum(
+        jnp.dot(x[:, at * depth : (at + 1) * depth], w[...], preferred_element_type=F32)
+        for at, w in enumerate(weights)
+    )
 
 
 def call(kernel, earlier, operands, specs, **options):
@@ -79,17 +97,14 @@
     block, steps, skipped = steps_of(piece)
 
     def kernel(ins, outs):
-        part = jnp.dot(ins[0][...], ins[1][...], preferred_element_type=F32)
-        outs[0][...] = part.astype(BF16)
+        outs[0][...] = dot_parts(ins[0][...], ins[1:]).astype(BF16)
 
     return call(
         kernel,
         earlier,
-        (other, weight),
-        [
-            pl.BlockSpec((rows, depth), lambda j: (0, 0)),
-            pl.BlockSpec((depth, block), lambda j: (0, skipped + j)),
-        ],
+        (other, *[weight] * PARTS),
+        [pl.BlockSpec((rows, depth), lambda j: (0, 0))]
+        + row_parts(depth, block, lambda j: (0, skipped + j)),
         grid=(steps,),
         out_specs=pl.BlockSpec((rows, block), lambda j: (0, j)),
         out_shape=jax.ShapeDtypeStruct((rows, block * steps), BF16),
@@ -101,8 +116,8 @@
     block, steps, skipped = steps_of(piece)
 
     def kernel(ins, outs):
-        part = jnp.dot(ins[0][...], ins[1][...], preferred_element_type=F32)
-        part = (part + ins[2][...].astype(F32)).astype(BF16)
+        part = dot_parts(ins[0][...], ins[2:])
+        part = (part + ins[1][...].astype(F32)).astype(BF16)
         for cut, out in zip(cuts, outs):
             out[...] = part[cut]
 
@@ -110,12 +125,12 @@
     return call(
         kernel,
         earlier,
-        (own, weight, far),
+        (own, far, *[weight] * PARTS),
         [
             pl.BlockSpec((rows, depth), lambda j: (0, 0)),
-            pl.BlockSpec((depth, block), lambda j: (0, skipped + j)),
             pl.BlockSpec((rows, block), lambda j: (0, j)),
-        ],
+        ]
+        + row_parts(depth, block, lambda j: (0, skipped + j)),
         grid=(steps,),
         out_specs=[pl.BlockSpec((height, block), lambda j: (0, j)) for height in heights],
         out_shape=[jax.ShapeDtypeStruct((height, block * steps), BF16) for height in heights],
@@ -147,10 +162,10 @@
 def project_hidden(own, other, weight, piece, added, attention, last, earlier=()):
     rows = own.shape[0]
     columns = weight.shape[1]
-    block, steps, skipped = steps_of(piece)
+    block, steps, skipped = steps_of(piece, (1024, 768, 512, 384, 256, 128))
     whole = pl.BlockSpec((rows, columns), lambda k: (0, 0))
     part = pl.BlockSpec((rows, block), lambda k: (0, k))
-    specs = [part, part, pl.BlockSpec((block, columns), lambda k: (skipped + k, 0))]
+    specs = [part, part, *row_parts(block, columns, lambda k: (skipped + k, 0))]
     specs += [whole] * len(added)
     specs += [pl.BlockSpec(a.shape, lambda k: (0, 0)) for a in attention]
 
@@ -158,7 +173,7 @@
         outs, totals = refs[:2], refs[2:]
         k = pl.program_id(0)
         both = jnp.concatenate([ins[0][...], ins[1][...]], axis=0)
-        product = jnp.dot(both, ins[2][...], preferred_element_type=F32)
+        product = dot_parts(both, ins[2 : 2 + PARTS])
         halves = [product[:rows], product[rows:]]
 
         @pl.when(k == 0)
@@ -166,7 +181,7 @@
             first = list(halves)
             for at in range(2):
                 if added:
-                    first[at] = first[at] + ins[3 + at][...]
+                    first[at] = first[at] + ins[2 + PARTS + at][...]
                 if attention:
                     first[at] = first[at] + jnp.dot(
                         ins[-3 + at][...], ins[-1][...], preferred_element_type=F32
@@ -186,7 +201,7 @@
     return call(
         kernel,
         earlier,
-        (own, other, weight, *added, *attention),
+        (own, other, *[weight] * PARTS, *added, *attention),
         specs,
         grid=(steps,),
         out_specs=[whole] * 2,
@@ -236,13 +251,12 @@
         pieces = slices(units, PIECES)
         n = len(cuts)
 
-        gain_rows = jnp.broadcast_to(ln_gain[None], (GAIN_ROWS, width))
-        raw = jnp.concatenate([gain_rows, tokens], axis=0)
-        raw = lax.all_gather(raw, "wide", axis=1, tiled=True)
-        floats = raw[GAIN_ROWS:].astype(F32)
+        raw = lax.all_gather(tokens, "wide", axis=1, tiled=True)
+        gain = lax.all_gather(ln_gain, "wide", axis=0, tiled=True)
+        floats = tokens.astype(F32)
         sums = jnp.stack([jnp.sum(floats, axis=1), jnp.sum(floats * floats, axis=1)])
-        sums = sum_red(sums)[:, :, None] / D
-        normed = normalize(floats, sums[0], sums[1], raw[:1]).astype(BF16)
+        sums = lax.psum(sums, ("wide", "red"))[:, :, None] / D
+        normed = normalize(raw.astype(F32), sums[0], sums[1], gain).astype(BF16)
         own = lax.dynamic_slice_in_dim(normed, core * depth, depth, axis=1)
         other = lax.dynamic_slice_in_dim(normed, (1 - core) * depth, depth, axis=1)
         other = swap(other)

time: 210 us -> 203 us (0.967)
  blocking collectives: 0 us -> 36.8 us
  waiting for transfers between devices: 82.6 us -> 48.6 us
  Pallas kernels: 77.5 us -> 71.6 us
    all_gather x1, waiting for transfers between devices: 40.7 us -> 2.93 us  [body(): raw = lax.all_gather(tokens, 'wide', axis=1, tiled=True)]
    psum x0 -> x1, blocking collectives: none -> 22.1 us  [body(): sums = lax.psum(sums, ('wide', 'red'))[:, :, None] / D]
    all_gather x0 -> x1, blocking collectives: none -> 14.7 us  [body(): gain = lax.all_gather(ln_gain, 'wide', axis=0, tiled=True)]
    reduce_scatter x2, waiting for transfers between devices: 0.02 us -> 5.94 us  [scatter(): lax.psum_scatter(full, 'wide', scatter_dimension=1, tiled=True)]
    pallas_call x18, Pallas kernels: 77.5 us -> 71.6 us  [call(): pl.pallas_call(body, in_specs=list(specs) + [WHOLE] * len(earlier), compi...]
    ppermute x3, waiting for transfers between devices: 5.76 us -> 2.31 us  [collect(): total = total + lax.ppermute(block(chip ^ k), 'wide', pairs).astype(F32)]
    ppermute x8 -> x7, starting transfers between devices: 9.8 us -> 9 us  [all_red(): parts.append(lax.ppermute(x, 'red', pairs))]
    ppermute x8 -> x7, waiting for transfers between devices: 27.7 us -> 28.2 us  [all_red(): parts.append(lax.ppermute(x, 'red', pairs))]
  transfers between devices with their start and end apart: 28 -> 27, of which waited for: 13 -> 13; matrix products, arithmetic and copies ran while one was open for 4% -> 4% of each run, Pallas kernels for 34% -> 32%
where the time goes in v1:
time: 203 us; the launch traced here: 202 us
  Pallas kernels  71.6 us (35%)
  waiting for transfers between devices  48.6 us (24%)
  blocking collectives  36.8 us (18%)
  starting transfers between devices  16 us (8%)
  between operations  14.2 us (7%)
  other arithmetic  9.43 us (5%)
  local copies, waits for them, and re-layouts  4.47 us (2%)
    pallas_call x18, Pallas kernels, call(): pl.pallas_call(body, in_specs=list(specs) + [WHOLE] * len(earlier), compi...  71.6 us
    ppermute x7, waiting for transfers between devices, all_red(): parts.append(lax.ppermute(x, 'red', pairs))  28.2 us
    psum x1, blocking collectives, body(): sums = lax.psum(sums, ('wide', 'red'))[:, :, None] / D  22.1 us
    all_gather x1, blocking collectives, body(): gain = lax.all_gather(ln_gain, 'wide', axis=0, tiled=True)  14.7 us
    ppermute x7, starting transfers between devices, all_red(): parts.append(lax.ppermute(x, 'red', pairs))  9 us
    ppermute x14, waiting for transfers between devices, swap(): return lax.ppermute(x, 'tok', [(0, 1), (1, 0)])  8.51 us
    reduce_scatter x2, waiting for transfers between devices, scatter(): lax.psum_scatter(full, 'wide', scatter_dimension=1, tiled=True)  5.94 us
    ppermute x3, starting transfers between devices, collect(): total = total + lax.ppermute(block(chip ^ k), 'wide', pairs).astype(F32)  4.45 us
  transfers between devices with their start and end apart: 27, of which 13 were waited for; matrix products, arithmetic and copies ran while one was open for 4% of the time, Pallas kernels for 32%

profile of v1, /device:TPU:0, one launch (start us, length us, event | category | flops | bytes accessed | tf_op | source)
XLA Modules:
  0.0 201.9 jit_solution(4465233339062631355)
XLA Ops:
  8.0 14.7 %all-gather = bf16[4,1,768]{2,1,0:T(2,128)(2,1)S(1)} all-gather(bf16[1,1,768]{2,1,0:T(2,128)(2,1)S(1)} %reshape.109), channel_id=1, replica_groups=mesh['grp'=2,'wide'=4,'red'=2,'tok'=2] {'wide'}, dimensions={0}, use_global_device_ids=true | all-gather | bytes 7680 | tf_op jit(solution)/shard_map/all_gather | solution.py:255
  24.0 22.1 %psum.7 = f32[2,256]{1,0:T(2,128)S(1)} all-reduce(f32[2,256]{1,0:T(2,128)S(1)} %pad_maximum_fusion.3), channel_id=1, replica_groups=mesh['grp'=2,'wide'=4,'red'=2,'tok'=2] {'wide','red'}, use_global_device_ids=true, to_apply=%region_2.0 | all-reduce | flops 512 | bytes 4096 | tf_op jit(solution)/shard_map/psum | solution.py:258
  46.1 2.9 %all-gather.3.cloned.1.call-done = bf16[256,3072]{1,0:T(8,128)(2,1)} async-done(((bf16[256,768]{1,0:T(8,128)(2,1)}), bf16[256,3072]{1,0:T(8,128)(2,1)}) %all-gather.3.cloned.1.call-update) | async-done | bytes 1572880 | tf_op jit(solution)/shard_map/all_gather | solution.py:254
  49.0 2.1 %multiply_convert_fusion = bf16[256,3072]{1,0:T(8,128)(2,1)S(1)} fusion(bf16[256,3072]{1,0:T(8,128)(2,1)} %all-gather.3.cloned.1.call-done, f32[3072]{0:T(1024)S(1)} %bitcast.31, f32[256]{0:T(256)S(1)} %add_rsqrt_fusion.2, f32[256]{0:T(256)S(1)} %bitcast.33), kind=kLoop, calls=%fused_computation | loop fusion | flops 3932160 | bytes 3160064 | tf_op jit(solution)/shard_map/convert_element_type | solution.py:259
  51.3 2.3 %collective-permute-done.refs_0_ = bf16[256,1536]{1,0:T(8,128)(2,1)S(1)} collective-permute-done((bf16[256,1536]{1,0:T(8,128)(2,1)S(1)}, bf16[256,1536]{1,0:T(8,128)(2,1)S(1)}, u32[]{:S(2)}, u32[]{:S(2)}) %collective-permute-start) | collective-permute-done | bytes 786464 | tf_op jit(solution)/shard_map/ppermute | solution.py:218
  54.2 7.2 %shard_map.83.refs_5_ = bf16[256,3072]{1,0:T(8,128)(2,1)S(1)} custom-call(bf16[256,1536]{1,0:T(8,128)(2,1)S(1)} %collective-permute-done.refs_0_, bf16[1536,6144]{1,0:T(8,128)(2,1)} %refs_5_.9, bf16[1536,6144]{1,0:T(8,128)(2,1)} %refs_5_.9, bf16[1536,6144]{1,0:T(8,128)(2,1)} %refs_5_.9, bf16[1536,6144]{1,0:T(8,128)(2,1)} %refs_5_.9, ...), custom_call_target="tpu_custom_call" | custom-call | tf_op jit(solution)/shard_map/pallas_call | solution.py:86
  61.7 7.2 %shard_map.84.refs_6_ = bf16[256,3072]{1,0:T(8,128)(2,1)S(1)} custom-call(bf16[256,1536]{1,0:T(8,128)(2,1)S(1)} %collective-permute-done.refs_0_, bf16[1536,6144]{1,0:T(8,128)(2,1)} %refs_5_.9, bf16[1536,6144]{1,0:T(8,128)(2,1)} %refs_5_.9, bf16[1536,6144]{1,0:T(8,128)(2,1)} %refs_5_.9, bf16[1536,6144]{1,0:T(8,128)(2,1)} %refs_5_.9, ...), custom_call_target="tpu_custom_call" | custom-call | tf_op jit(solution)/shard_map/pallas_call | solution.py:86
  69.5 3.2 %collective-permute-done.3.refs_1_ = bf16[256,384]{1,0:T(8,128)(2,1)S(1)} collective-permute-done((bf16[256,384]{1,0:T(8,128)(2,1)S(1)}, bf16[256,384]{1,0:T(8,128)(2,1)S(1)}, u32[]{:S(2)}, u32[]{:S(2)}) %collective-permute-start.3) | collective-permute-done | bytes 196640 | tf_op jit(solution)/shard_map/ppermute | solution.py:218
  73.3 7.4 %shard_map.86 = (bf16[112,3072]{1,0:T(8,128)(2,1)S(1)}, bf16[80,3072]{1,0:T(8,128)(2,1)S(1)}, bf16[64,3072]{1,0:T(8,128)(2,1)S(1)}) custom-call(bf16[256,1536]{1,0:T(8,128)(2,1)S(1)} %get-tuple-element.48.refs_0_, bf16[256,3072]{1,0:T(8,128)(2,1)S(1)} %collective-permute-done.2.refs_1_, bf16[1536,6144]{1,0:T(8,128)(2,1)} %refs_5_.9, ...), custom_call_target="tpu_custom_call" | custom-call | tf_op jit(solution)/shard_map/pallas_call | solution.py:86
  82.8 7.4 %shard_map.87 = (bf16[112,3072]{1,0:T(8,128)(2,1)S(1)}, bf16[80,3072]{1,0:T(8,128)(2,1)S(1)}, bf16[64,3072]{1,0:T(8,128)(2,1)S(1)}) custom-call(bf16[256,1536]{1,0:T(8,128)(2,1)S(1)} %get-tuple-element.48.refs_0_, bf16[256,3072]{1,0:T(8,128)(2,1)S(1)} %collective-permute-done.1.refs_1_, bf16[1536,6144]{1,0:T(8,128)(2,1)} %refs_5_.9, ...), custom_call_target="tpu_custom_call" | custom-call | tf_op jit(solution)/shard_map/pallas_call | solution.py:86
  91.8 7.2 %collective-permute-done.6.refs_1_ = bf16[112,3072]{1,0:T(8,128)(2,1)S(1)} collective-permute-done((bf16[112,3072]{1,0:T(8,128)(2,1)S(1)}, bf16[112,3072]{1,0:T(8,128)(2,1)S(1)}, u32[]{:S(2)}, u32[]{:S(2)}) %collective-permute-start.6) | collective-permute-done | bytes 688160 | tf_op jit(solution)/shard_map/ppermute | solution.py:224
  100.9 2.4 %collective-permute-done.5 = bf16[256,384]{1,0:T(8,128)(2,1)S(1)} collective-permute-done((bf16[256,384]{1,0:T(8,128)(2,1)S(1)}, bf16[256,384]{1,0:T(8,128)(2,1)S(1)}, u32[]{:S(2)}, u32[]{:S(2)}) %collective-permute-start.5) | collective-permute-done | bytes 196640 | tf_op jit(solution)/shard_map/ppermute | solution.py:224
  104.4 13.0 %collective-permute-done.4.refs_1_ = bf16[112,3072]{1,0:T(8,128)(2,1)S(1)} collective-permute-done((bf16[112,3072]{1,0:T(8,128)(2,1)S(1)}, bf16[112,3072]{1,0:T(8,128)(2,1)S(1)}, u32[]{:S(2)}, u32[]{:S(2)}) %collective-permute-start.4) | collective-permute-done | bytes 688160 | tf_op jit(solution)/shard_map/ppermute | solution.py:224
  121.6 6.2 %shard_map.90 = (f32[112,1536]{1,0:T(8,128)S(1)}, f32[112,1536]{1,0:T(8,128)S(1)}) custom-call(bf16[112,3072]{1,0:T(8,128)(2,1)S(1)} %shard_map.88.refs_0_, bf16[112,3072]{1,0:T(8,128)(2,1)S(1)} %collective-permute-done.8.refs_1_, bf16[6144,1536]{1,0:T(8,128)(2,1)} %refs_5_.15, bf16[6144,1536]{1,0:T(8,128)(2,1)} %refs_5_.15, bf16[6144,1536]{1,0:T(8,128)(2,1)} %refs_5_.15, ...), custom_call_target="tpu_custom_call" | custom-call | tf_op jit(solution)/shard_map/pallas_call | solution.py:86
  127.8 4.5 %collective-permute-done.10.refs_1_ = bf16[80,3072]{1,0:T(8,128)(2,1)S(1)} collective-permute-done((bf16[80,3072]{1,0:T(8,128)(2,1)S(1)}, bf16[80,3072]{1,0:T(8,128)(2,1)S(1)}, u32[]{:S(2)}, u32[]{:S(2)}) %collective-permute-start.10) | collective-permute-done | bytes 491552 | tf_op jit(solution)/shard_map/ppermute | solution.py:224
  132.8 6.7 %shard_map.92 = (bf16[112,1536]{1,0:T(8,128)(2,1)S(1)}, bf16[112,1536]{1,0:T(8,128)(2,1)}) custom-call(bf16[112,3072]{1,0:T(8,128)(2,1)S(1)} %shard_map.89.refs_9_.refs_0_, bf16[112,3072]{1,0:T(8,128)(2,1)S(1)} %collective-permute-done.7.refs_1_, bf16[6144,1536]{1,0:T(8,128)(2,1)} %refs_5_.15, bf16[6144,1536]{1,0:T(8,128)(2,1)} %refs_5_.15, ...), custom_call_target="tpu_custom_call" | custom-call | tf_op jit(solution)/shard_map/pallas_call | solution.py:86
  148.0 5.7 %shard_map.94 = (f32[80,1536]{1,0:T(8,128)S(1)}, f32[80,1536]{1,0:T(8,128)S(1)}) custom-call(bf16[80,3072]{1,0:T(8,128)(2,1)S(1)} %shard_map.91.refs_8_.refs_0_, bf16[80,3072]{1,0:T(8,128)(2,1)} %collective-permute-done.14.refs_1_, bf16[6144,1536]{1,0:T(8,128)(2,1)} %refs_5_.15, bf16[6144,1536]{1,0:T(8,128)(2,1)} %refs_5_.15, bf16[6144,1536]{1,0:T(8,128)(2,1)} %refs_5_.15, ...), custom_call_target="tpu_custom_call" | custom-call | tf_op jit(solution)/shard_map/pallas_call | solution.py:86
  153.7 2.8 %shard_map.95.refs_8_.refs_0_ = bf16[64,3072]{1,0:T(8,128)(2,1)S(1)} custom-call(bf16[64,3072]{1,0:T(8,128)(2,1)S(1)} %get-tuple-element.23.refs_6_.refs_0_, bf16[64,3072]{1,0:T(8,128)(2,1)} %collective-permute-done.15.refs_1_, f32[80,1536]{1,0:T(8,128)S(1)} %get-tuple-element.33.refs_2_.refs_6_), custom_call_target="tpu_custom_call" | custom-call | tf_op jit(solution)/shard_map/pallas_call | solution.py:86
  156.5 6.2 %shard_map.96 = (bf16[80,1536]{1,0:T(8,128)(2,1)S(1)}, bf16[80,1536]{1,0:T(8,128)(2,1)}) custom-call(bf16[80,3072]{1,0:T(8,128)(2,1)S(1)} %shard_map.93.refs_9_.refs_0_, bf16[80,3072]{1,0:T(8,128)(2,1)S(1)} %collective-permute-done.13.refs_1_, bf16[6144,1536]{1,0:T(8,128)(2,1)} %refs_5_.15, bf16[6144,1536]{1,0:T(8,128)(2,1)} %refs_5_.15, ...), custom_call_target="tpu_custom_call" | custom-call | tf_op jit(solution)/shard_map/pallas_call | solution.py:86
  167.5 5.4 %shard_map.98 = (f32[64,1536]{1,0:T(8,128)S(1)}, f32[64,1536]{1,0:T(8,128)S(1)}) custom-call(bf16[64,3072]{1,0:T(8,128)(2,1)S(1)} %shard_map.95.refs_8_.refs_0_, bf16[64,3072]{1,0:T(8,128)(2,1)S(1)} %collective-permute-done.19.refs_1_, bf16[6144,1536]{1,0:T(8,128)(2,1)} %refs_5_.15, bf16[6144,1536]{1,0:T(8,128)(2,1)} %refs_5_.15, ...), custom_call_target="tpu_custom_call" | custom-call | tf_op jit(solution)/shard_map/pallas_call | solution.py:86
  173.9 5.3 %shard_map.99 = (bf16[64,1536]{1,0:T(8,128)(2,1)S(1)}, bf16[64,1536]{1,0:T(8,128)(2,1)S(1)}) custom-call(bf16[64,3072]{1,0:T(8,128)(2,1)S(1)} %shard_map.97.refs_9_.refs_0_, bf16[64,3072]{1,0:T(8,128)(2,1)S(1)} %collective-permute-done.18.refs_1_, bf16[6144,1536]{1,0:T(8,128)(2,1)} %refs_5_.15, bf16[6144,1536]{1,0:T(8,128)(2,1)} %refs_5_.15, ...), custom_call_target="tpu_custom_call" | custom-call | tf_op jit(solution)/shard_map/pallas_call | solution.py:86
  182.8 2.4 %collective-permute-start.23 = (bf16[64,768]{1,0:T(8,128)(2,1)S(1)}, bf16[64,768]{1,0:T(8,128)(2,1)S(1)}, u32[]{:S(2)}, u32[]{:S(2)}) collective-permute-start(bf16[64,768]{1,0:T(8,128)(2,1)S(1)} %get-tuple-element.54), channel_id=1, source_target_pairs={{0,4},{4,0},{8,12},{12,8},{1,5},{5,1},{9,13},{13,9},{2,6},{6,2},{1... | collective-permute-start | bytes 294920 | tf_op jit(solution)/shard_map/ppermute | solution.py:241
  185.2 5.9 %reduce-scatter.5.cloned.1.call-done = bf16[80,768]{1,0:T(8,128)(2,1)} async-done(((bf16[80,3072]{1,0:T(8,128)(2,1)}), bf16[80,768]{1,0:T(8,128)(2,1)}) %reduce-scatter.5.cloned.1.call-update) | async-done | bytes 122896 | tf_op jit(solution)/shard_map/reduce_scatter | solution.py:302
  192.0 2.3 %collective-permute-done.22 = bf16[64,768]{1,0:T(8,128)(2,1)S(1)} collective-permute-done((bf16[64,768]{1,0:T(8,128)(2,1)S(1)}, bf16[64,768]{1,0:T(8,128)(2,1)S(1)}, u32[]{:S(2)}, u32[]{:S(2)}) %collective-permute-start.22) | collective-permute-done | bytes 98336 | tf_op jit(solution)/shard_map/ppermute | solution.py:241
  (106 shorter events, 35.2 us)
Async XLA Ops:
  6.5 42.5 %all-gather.3.cloned.1.call-start = ((), (), s32[]{:S(2)}) async-start(), calls=%async_computation.2 | async-start | bytes 1966080 | tf_op jit(solution)/shard_map/all_gather | solution.py:254
  7.3 165.7 %reduce-scatter.3.cloned.1.call-start = ((), (), s32[]{:S(2)}) async-start(), calls=%async_computation.3 | async-start | bytes 860160 | tf_op jit(solution)/shard_map/reduce_scatter | solution.py:302
  51.2 2.4 %collective-permute-start = (bf16[256,1536]{1,0:T(8,128)(2,1)S(1)}, bf16[256,1536]{1,0:T(8,128)(2,1)S(1)}, u32[]{:S(2)}, u32[]{:S(2)}) collective-permute-start(bf16[256,1536]{1,0:T(8,128)(2,1)S(1)} %get-tuple-element.47), channel_id=1, source_target_pairs={{0,1},{1,0},{2,3},{3,2},{4,5},{5,4},{6,7},{7,6},{8,9},{9,8},{10,11... | collective-permute-start | bytes 2359304 | tf_op jit(solution)/shard_map/ppermute | solution.py:218
  61.5 11.8 %collective-permute-start.2 = (bf16[256,3072]{1,0:T(8,128)(2,1)S(1)}, bf16[256,3072]{1,0:T(8,128)(2,1)S(1)}, u32[]{:S(2)}, u32[]{:S(2)}) collective-permute-start(bf16[256,3072]{1,0:T(8,128)(2,1)S(1)} %shard_map.83.refs_5_), channel_id=1, source_target_pairs={{0,1},{1,0},{2,3},{3,2},{4,5},{5,4},{6,7},{7,6},{8,9},{9,8},{10,11... | collective-permute-start | bytes 4718600 | tf_op jit(solution)/shard_map/ppermute | solution.py:218
  68.9 13.9 %collective-permute-start.1 = (bf16[256,3072]{1,0:T(8,128)(2,1)S(1)}, bf16[256,3072]{1,0:T(8,128)(2,1)S(1)}, u32[]{:S(2)}, u32[]{:S(2)}) collective-permute-start(bf16[256,3072]{1,0:T(8,128)(2,1)S(1)} %shard_map.84.refs_6_), channel_id=1, source_target_pairs={{0,1},{1,0},{2,3},{3,2},{4,5},{5,4},{6,7},{7,6},{8,9},{9,8},{10,11... | collective-permute-start | bytes 4718600 | tf_op jit(solution)/shard_map/ppermute | solution.py:218
  69.4 3.3 %collective-permute-start.3 = (bf16[256,384]{1,0:T(8,128)(2,1)S(1)}, bf16[256,384]{1,0:T(8,128)(2,1)S(1)}, u32[]{:S(2)}, u32[]{:S(2)}) collective-permute-start(bf16[256,384]{1,0:T(8,128)(2,1)S(1)} %shard_map.82.refs_5_), channel_id=1, source_target_pairs={{0,1},{1,0},{2,3},{3,2},{4,5},{5,4},{6,7},{7,6},{8,9},{9,8},{10,11... | collective-permute-start | bytes 589832 | tf_op jit(solution)/shard_map/ppermute | solution.py:218
  80.7 18.3 %collective-permute-start.6 = (bf16[112,3072]{1,0:T(8,128)(2,1)S(1)}, bf16[112,3072]{1,0:T(8,128)(2,1)S(1)}, u32[]{:S(2)}, u32[]{:S(2)}) collective-permute-start(bf16[112,3072]{1,0:T(8,128)(2,1)S(1)} %get-tuple-element.25.refs_0_), channel_id=1, source_target_pairs={{0,2},{2,0},{1,3},{3,1},{4,6},{6,4},{5,7},{7,5},{8,10},{10,8},{9,1... | collective-permute-start | bytes 2064392 | tf_op jit(solution)/shard_map/ppermute | solution.py:224
  82.4 20.9 %collective-permute-start.5 = (bf16[256,384]{1,0:T(8,128)(2,1)S(1)}, bf16[256,384]{1,0:T(8,128)(2,1)S(1)}, u32[]{:S(2)}, u32[]{:S(2)}) collective-permute-start(bf16[256,384]{1,0:T(8,128)(2,1)S(1)} %shard_map.85.refs_6_), channel_id=1, source_target_pairs={{0,2},{2,0},{1,3},{3,1},{4,6},{6,4},{5,7},{7,5},{8,10},{10,8},{9,1... | collective-permute-start | bytes 589832 | tf_op jit(solution)/shard_map/ppermute | solution.py:224
  90.2 27.2 %collective-permute-start.4 = (bf16[112,3072]{1,0:T(8,128)(2,1)S(1)}, bf16[112,3072]{1,0:T(8,128)(2,1)S(1)}, u32[]{:S(2)}, u32[]{:S(2)}) collective-permute-start(bf16[112,3072]{1,0:T(8,128)(2,1)S(1)} %get-tuple-element.24.refs_0_), channel_id=1, source_target_pairs={{0,2},{2,0},{1,3},{3,1},{4,6},{6,4},{5,7},{7,5},{8,10},{10,8},{9,1... | collective-permute-start | bytes 2064392 | tf_op jit(solution)/shard_map/ppermute | solution.py:224
  100.2 21.3 %collective-permute-start.8 = (bf16[112,3072]{1,0:T(8,128)(2,1)S(1)}, bf16[112,3072]{1,0:T(8,128)(2,1)S(1)}, u32[]{:S(2)}, u32[]{:S(2)}) collective-permute-start(bf16[112,3072]{1,0:T(8,128)(2,1)S(1)} %shard_map.88.refs_0_), channel_id=1, source_target_pairs={{0,1},{1,0},{2,3},{3,2},{4,5},{5,4},{6,7},{7,6},{8,9},{9,8},{10,11... | collective-permute-start | bytes 2064392 | tf_op jit(solution)/shard_map/ppermute | solution.py:218
  118.1 14.7 %collective-permute-start.7 = (bf16[112,3072]{1,0:T(8,128)(2,1)S(1)}, bf16[112,3072]{1,0:T(8,128)(2,1)S(1)}, u32[]{:S(2)}, u32[]{:S(2)}) collective-permute-start(bf16[112,3072]{1,0:T(8,128)(2,1)S(1)} %shard_map.89.refs_9_.refs_0_), channel_id=1, source_target_pairs={{0,1},{1,0},{2,3},{3,2},{4,5},{5,4},{6,7},{7,6},{8,9},{9,8},{10,11... | collective-permute-start | bytes 2064392 | tf_op jit(solution)/shard_map/ppermute | solution.py:218
  118.2 14.1 %collective-permute-start.10 = (bf16[80,3072]{1,0:T(8,128)(2,1)S(1)}, bf16[80,3072]{1,0:T(8,128)(2,1)S(1)}, u32[]{:S(2)}, u32[]{:S(2)}) collective-permute-start(bf16[80,3072]{1,0:T(8,128)(2,1)S(1)} %get-tuple-element.29.refs_0_), channel_id=1, source_target_pairs={{0,2},{2,0},{1,3},{3,1},{4,6},{6,4},{5,7},{7,5},{8,10},{10,8},{9,1... | collective-permute-start | bytes 1474568 | tf_op jit(solution)/shard_map/ppermute | solution.py:224
  119.8 22.5 %collective-permute-start.12 = (bf16[80,3072]{1,0:T(8,128)(2,1)S(1)}, bf16[80,3072]{1,0:T(8,128)(2,1)S(1)}, u32[]{:S(2)}, u32[]{:S(2)}) collective-permute-start(bf16[80,3072]{1,0:T(8,128)(2,1)S(1)} %get-tuple-element.32.refs_0_), channel_id=1, source_target_pairs={{0,2},{2,0},{1,3},{3,1},{4,6},{6,4},{5,7},{7,5},{8,10},{10,8},{9,1... | collective-permute-start | bytes 1474568 | tf_op jit(solution)/shard_map/ppermute | solution.py:224
  139.5 3.5 %collective-permute-start.11 = (bf16[112,1536]{1,0:T(8,128)(2,1)}, bf16[112,1536]{1,0:T(8,128)(2,1)}, u32[]{:S(2)}, u32[]{:S(2)}) collective-permute-start(bf16[112,1536]{1,0:T(8,128)(2,1)} %get-tuple-element.31), channel_id=1, source_target_pairs={{0,1},{1,0},{2,3},{3,2},{4,5},{5,4},{6,7},{7,6},{8,9},{9,8},{10,11... | collective-permute-start | bytes 1032200 | tf_op jit(solution)/shard_map/ppermute | solution.py:218
  139.5 14.2 %collective-permute-start.15 = (bf16[64,3072]{1,0:T(8,128)(2,1)S(1)}, bf16[64,3072]{1,0:T(8,128)(2,1)}, u32[]{:S(2)}, u32[]{:S(2)}) collective-permute-start(bf16[64,3072]{1,0:T(8,128)(2,1)S(1)} %get-tuple-element.23.refs_6_.refs_0_), channel_id=1, source_target_pairs={{0,2},{2,0},{1,3},{3,1},{4,6},{6,4},{5,7},{7,5},{8,10},{10,8},{9,1... | collective-permute-start | bytes 1179656 | tf_op jit(solution)/shard_map/ppermute | solution.py:224
  141.1 5.8 %collective-permute-start.14 = (bf16[80,3072]{1,0:T(8,128)(2,1)S(1)}, bf16[80,3072]{1,0:T(8,128)(2,1)}, u32[]{:S(2)}, u32[]{:S(2)}) collective-permute-start(bf16[80,3072]{1,0:T(8,128)(2,1)S(1)} %shard_map.91.refs_8_.refs_0_), channel_id=1, source_target_pairs={{0,1},{1,0},{2,3},{3,2},{4,5},{5,4},{6,7},{7,6},{8,9},{9,8},{10,11... | collective-permute-start | bytes 1474568 | tf_op jit(solution)/shard_map/ppermute | solution.py:218
  142.9 13.6 %collective-permute-start.13 = (bf16[80,3072]{1,0:T(8,128)(2,1)S(1)}, bf16[80,3072]{1,0:T(8,128)(2,1)S(1)}, u32[]{:S(2)}, u32[]{:S(2)}) collective-permute-start(bf16[80,3072]{1,0:T(8,128)(2,1)S(1)} %shard_map.93.refs_9_.refs_0_), channel_id=1, source_target_pairs={{0,1},{1,0},{2,3},{3,2},{4,5},{5,4},{6,7},{7,6},{8,9},{9,8},{10,11... | collective-permute-start | bytes 1474568 | tf_op jit(solution)/shard_map/ppermute | solution.py:218
  145.0 46.1 %reduce-scatter.5.cloned.1.call-start = ((), (), s32[]{:S(2)}) async-start(), calls=%async_computation.4 | async-start | bytes 614400 | tf_op jit(solution)/shard_map/reduce_scatter | solution.py:302
  145.2 18.1 %collective-permute-start.17 = (bf16[64,3072]{1,0:T(8,128)(2,1)S(1)}, bf16[64,3072]{1,0:T(8,128)(2,1)S(1)}, u32[]{:S(2)}, u32[]{:S(2)}) collective-permute-start(bf16[64,3072]{1,0:T(8,128)(2,1)S(1)} %get-tuple-element.26.refs_2_.refs_0_), channel_id=1, source_target_pairs={{0,2},{2,0},{1,3},{3,1},{4,6},{6,4},{5,7},{7,5},{8,10},{10,8},{9,1... | collective-permute-start | bytes 1179656 | tf_op jit(solution)/shard_map/ppermute | solution.py:224
  163.0 3.5 %collective-permute-start.19 = (bf16[64,3072]{1,0:T(8,128)(2,1)S(1)}, bf16[64,3072]{1,0:T(8,128)(2,1)S(1)}, u32[]{:S(2)}, u32[]{:S(2)}) collective-permute-start(bf16[64,3072]{1,0:T(8,128)(2,1)S(1)} %shard_map.95.refs_8_.refs_0_), channel_id=1, source_target_pairs={{0,1},{1,0},{2,3},{3,2},{4,5},{5,4},{6,7},{7,6},{8,9},{9,8},{10,11... | collective-permute-start | bytes 1179656 | tf_op jit(solution)/shard_map/ppermute | solution.py:218
  163.7 9.2 %collective-permute-start.18 = (bf16[64,3072]{1,0:T(8,128)(2,1)S(1)}, bf16[64,3072]{1,0:T(8,128)(2,1)S(1)}, u32[]{:S(2)}, u32[]{:S(2)}) collective-permute-start(bf16[64,3072]{1,0:T(8,128)(2,1)S(1)} %shard_map.97.refs_9_.refs_0_), channel_id=1, source_target_pairs={{0,1},{1,0},{2,3},{3,2},{4,5},{5,4},{6,7},{7,6},{8,9},{9,8},{10,11... | collective-permute-start | bytes 1179656 | tf_op jit(solution)/shard_map/ppermute | solution.py:218
  180.7 11.3 %collective-permute-start.21 = (bf16[64,768]{1,0:T(8,128)(2,1)S(1)}, bf16[64,768]{1,0:T(8,128)(2,1)S(1)}, u32[]{:S(2)}, u32[]{:S(2)}) collective-permute-start(bf16[64,768]{1,0:T(8,128)(2,1)S(1)} %get-tuple-element.53), channel_id=1, source_target_pairs={{0,12},{4,8},{8,4},{12,0},{1,13},{5,9},{9,5},{13,1},{2,14},{6,10},... | collective-permute-start | bytes 294920 | tf_op jit(solution)/shard_map/ppermute | solution.py:241
  182.1 12.3 %collective-permute-start.22 = (bf16[64,768]{1,0:T(8,128)(2,1)S(1)}, bf16[64,768]{1,0:T(8,128)(2,1)S(1)}, u32[]{:S(2)}, u32[]{:S(2)}) collective-permute-start(bf16[64,768]{1,0:T(8,128)(2,1)S(1)} %get-tuple-element.55), channel_id=1, source_target_pairs={{0,8},{4,12},{8,0},{12,4},{1,9},{5,13},{9,1},{13,5},{2,10},{6,14},... | collective-permute-start | bytes 294920 | tf_op jit(solution)/shard_map/ppermute | solution.py:241
  182.8 11.5 %collective-permute-start.23 = (bf16[64,768]{1,0:T(8,128)(2,1)S(1)}, bf16[64,768]{1,0:T(8,128)(2,1)S(1)}, u32[]{:S(2)}, u32[]{:S(2)}) collective-permute-start(bf16[64,768]{1,0:T(8,128)(2,1)S(1)} %get-tuple-element.54), channel_id=1, source_target_pairs={{0,4},{4,0},{8,12},{12,8},{1,5},{5,1},{9,13},{13,9},{2,6},{6,2},{1... | collective-permute-start | bytes 294920 | tf_op jit(solution)/shard_map/ppermute | solution.py:241
  (13 other events, 52.5 us)
Sparse Core Ops, SparseCore 0:
  8.9 40.0 all-gather.2
  145.1 21.5 reduce-scatter.2
  169.1 21.9 reduce-scatter.4

commit v2 on v1

--- a/solution.py
+++ b/solution.py
@@ -15,9 +15,8 @@
 PIECES = (1, 1)
 PARTS = 4
 BF16, F32 = jnp.bfloat16, jnp.float32
-PARAMS = pltpu.CompilerParams(vmem_limit_bytes=44 * 2**20)
+PARAMS = pltpu.CompilerParams(vmem_limit_bytes=32 * 2**20)
 SOON = pl.CostEstimate(flops=0, bytes_accessed=0, transcendentals=0)
-WHOLE = pl.BlockSpec(memory_space=pl.ANY)
 
 
 def normalize(values, mean, meansq, gain):
@@ -78,6 +77,11 @@
     )
 
 
+def corner_of(x):
+    shape = (min(16, x.shape[0]), min(128, x.shape[1]))
+    return pl.BlockSpec(shape, lambda *_: (0, 0))
+
+
 def call(kernel, earlier, operands, specs, **options):
     def body(*refs):
         n = len(operands)
@@ -85,56 +89,11 @@
 
     return pl.pallas_call(
         body,
-        in_specs=list(specs) + [WHOLE] * len(earlier),
+        in_specs=list(specs) + [corner_of(a) for a in earlier],
         compiler_params=PARAMS,
         cost_estimate=SOON,
         **options,
     )(*operands, *earlier)
-
-
-def project_far(other, weight, piece, earlier=()):
-    rows, depth = other.shape
-    block, steps, skipped = steps_of(piece)
-
-    def kernel(ins, outs):
-        outs[0][...] = dot_parts(ins[0][...], ins[1:]).astype(BF16)
-
-    return call(
-        kernel,
-        earlier,
-        (other, *[weight] * PARTS),
-        [pl.BlockSpec((rows, depth), lambda j: (0, 0))]
-        + row_parts(depth, block, lambda j: (0, skipped + j)),
-        grid=(steps,),
-        out_specs=pl.BlockSpec((rows, block), lambda j: (0, j)),
-        out_shape=jax.ShapeDtypeStruct((rows, block * steps), BF16),
-    )
-
-
-def project_near(own, weight, piece, far, cuts, earlier=()):
-    rows, depth = own.shape
-    block, steps, skipped = steps_of(piece)
-
-    def kernel(ins, outs):
-        part = dot_parts(ins[0][...], ins[2:])
-        part = (part + ins[1][...].astype(F32)).astype(BF16)
-        for cut, out in zip(cuts, outs):
-            out[...] = part[cut]
-
-    heights = [cut.stop - cut.start for cut in cuts]
-    return call(
-        kernel,
-        earlier,
-        (own, far, *[weight] * PARTS),
-        [
-            pl.BlockSpec((rows, depth), lambda j: (0, 0)),
-            pl.BlockSpec((rows, block), lambda j: (0, j)),
-        ]
-        + row_parts(depth, block, lambda j: (0, skipped + j)),
-        grid=(steps,),
-        out_specs=[pl.BlockSpec((height, block), lambda j: (0, j)) for height in heights],
-        out_shape=[jax.ShapeDtypeStruct((height, block * steps), BF16) for height in heights],
-    )
 
 
 def gelu_sum(parts, earlier=()):
@@ -261,25 +220,23 @@
         other = lax.dynamic_slice_in_dim(normed, (1 - core) * depth, depth, axis=1)
         other = swap(other)
 
-        every = slice(0, qkv_rows.shape[1])
-        far_qkv = project_far(other, qkv_rows, every)
-        fars, earlier = [], far_qkv
-        for piece in pieces:
-            fars.append(project_far(other, w_up, piece, [earlier]))
-            earlier = fars[-1]
-        (qkv,) = project_near(
-            own, qkv_rows, every, swap(far_qkv), [slice(0, tokens.shape[0])], [earlier]
-        )
-        earlier = qkv
-        sums = []
-        for piece, far in zip(pieces, fars):
-            sums.append(project_near(own, w_up, piece, swap(far), cuts, [earlier]))
-            earlier = sums[-1][-1]
+        both = jnp.concatenate([own, other], axis=0)
+        rows = tokens.shape[0]
+
+        def project(weight):
+            part = jnp.dot(both, weight, preferred_element_type=F32).astype(BF16)
+            return part[:rows], swap(part[rows:])
+
+        def block_sum(parts, start=0.0):
+            return (parts[0].astype(F32) + parts[1].astype(F32) + start).astype(BF16)
+
+        halves = [project(w_up[:, piece]) for piece in pieces]
+        qkv = block_sum(project(qkv_rows))
 
         order = [(c, p) for c in range(n) for p in range(len(pieces))]
         outs, scattered = [], []
-        terms, waiting = (), None
-        earlier = [earlier]
+        terms, waiting, firsts = (), None, []
+        earlier = ()
 
         def output(at, have, terms, earlier):
             c, p = order[at]
@@ -304,8 +261,12 @@
 
         hidden = None
         for at, (c, p) in enumerate(order):
-            arrived = gelu_sum(all_red(sums[p][c]), earlier)
+            start = nothing(firsts[c - 1]) if c else 0.0
+            parts = all_red(block_sum([a[cuts[c]] for a in halves[p]], start))
+            arrived = gelu_sum(parts, earlier)
             earlier = [arrived]
+            if p == 0:
+                firsts.append(arrived)
             if at == 0:
                 attended = attend(sum_red(qkv) + nothing(arrived), q_gain, k_gain)
                 attended_other = swap(attended)
@@ -313,6 +274,8 @@
             if waiting is not None:
                 earlier.append(scatter(*waiting))
                 waiting = None
+            if at == len(order) - 1:
+                earlier += scattered[:1]
             if at:
                 terms = output(at - 1, hidden, terms, earlier)
                 earlier = [terms[0]]
@@ -321,7 +284,7 @@
             hidden = arrived
         if waiting is not None:
             earlier.append(scatter(*waiting))
-        terms = output(len(order) - 1, hidden, terms, earlier + scattered[:1])
+        terms = output(len(order) - 1, hidden, terms, earlier)
         for cut, summed in zip(cuts, scattered):
             outs.append(tokens[cut].astype(F32) + summed.astype(F32))
         outs.append(tokens[cuts[-1]].astype(F32) + collect(terms[0], swap(terms[1]), width))

time: 203 us -> 207 us (1.020)
  Pallas kernels: 71.6 us -> 25.5 us
  local copies, waits for them, and re-layouts: 4.47 us -> 40 us
  matrix products: 0.73 us -> 16.3 us
  waiting for transfers between devices: 48.6 us -> 39.8 us
  other arithmetic: 9.43 us -> 15.4 us
    pallas_call x18 -> x12, Pallas kernels: 71.6 us -> 25.5 us  [call(): pl.pallas_call(body, in_specs=list(specs) + [corner_of(a) for a in earlie...]
    unnamed x22 -> x44, local copies, waits for them, and re-layouts: 3.77 us -> 37.3 us
    dot_general x0 -> x3, matrix products: none -> 15.6 us  [project(): part = jnp.dot(both, weight, preferred_element_type=F32).astype(BF16)]
    convert_element_type x0 -> x7, other arithmetic: none -> 8.1 us  [block_sum(): return (parts[0].astype(F32) + parts[1].astype(F32) + start).astype(BF16)]
    reduce_scatter x2, waiting for transfers between devices: 5.94 us -> 0.46 us  [scatter(): lax.psum_scatter(full, 'wide', scatter_dimension=1, tiled=True)]
    ppermute x7, waiting for transfers between devices: 28.2 us -> 24.2 us  [all_red(): parts.append(lax.ppermute(x, 'red', pairs))]
    ppermute x3, waiting for transfers between devices: 2.31 us -> 5.79 us  [collect(): total = total + lax.ppermute(block(chip ^ k), 'wide', pairs).astype(F32)]
    ppermute x14, waiting for transfers between devices: 8.51 us -> 5.66 us  [swap(): return lax.ppermute(x, 'tok', [(0, 1), (1, 0)])]
  transfers between devices with their start and end apart: 27 -> 27, of which waited for: 13 -> 9; matrix products, arithmetic and copies ran while one was open for 4% -> 10% of each run, Pallas kernels for 32% -> 12%
where the time goes in v2:
time: 207 us; the launch traced here: 206 us
  local copies, waits for them, and re-layouts  40 us (19%)
  waiting for transfers between devices  39.8 us (19%)
  blocking collectives  36.8 us (18%)
  Pallas kernels  25.5 us (12%)
  starting transfers between devices  17.2 us (8%)
  matrix products  16.3 us (8%)
  other arithmetic  15.4 us (7%)
  between operations  15 us (7%)
    unnamed x44, local copies, waits for them, and re-layouts  37.3 us
    pallas_call x12, Pallas kernels, call(): pl.pallas_call(body, in_specs=list(specs) + [corner_of(a) for a in earlie...  25.5 us
    ppermute x7, waiting for transfers between devices, all_red(): parts.append(lax.ppermute(x, 'red', pairs))  24.2 us
    psum x1, blocking collectives, body(): sums = lax.psum(sums, ('wide', 'red'))[:, :, None] / D  22.1 us
    dot_general x3, matrix products, project(): part = jnp.dot(both, weight, preferred_element_type=F32).astype(BF16)  15.6 us
    all_gather x1, blocking collectives, body(): gain = lax.all_gather(ln_gain, 'wide', axis=0, tiled=True)  14.7 us
    ppermute x7, starting transfers between devices, all_red(): parts.append(lax.ppermute(x, 'red', pairs))  9.19 us
    convert_element_type x7, other arithmetic, block_sum(): return (parts[0].astype(F32) + parts[1].astype(F32) + start).astype(BF16)  8.1 us
  transfers between devices with their start and end apart: 27, of which 9 were waited for; matrix products, arithmetic and copies ran while one was open for 10% of the time, Pallas kernels for 12%

profile of v2, /device:TPU:0, one launch (start us, length us, event | category | flops | bytes accessed | tf_op | source)
XLA Modules:
  0.0 206.1 jit_solution(15254504545991037789)
XLA Ops:
  8.0 14.7 %all-gather = bf16[4,1,768]{2,1,0:T(2,128)(2,1)S(1)} all-gather(bf16[1,1,768]{2,1,0:T(2,128)(2,1)S(1)} %reshape.115), channel_id=1, replica_groups=mesh['grp'=2,'wide'=4,'red'=2,'tok'=2] {'wide'}, dimensions={0}, use_global_device_ids=true | all-gather | bytes 7680 | tf_op jit(solution)/shard_map/all_gather | solution.py:214
  24.0 22.1 %psum.7 = f32[2,256]{1,0:T(2,128)S(1)} all-reduce(f32[2,256]{1,0:T(2,128)S(1)} %pad_maximum_fusion.7), channel_id=1, replica_groups=mesh['grp'=2,'wide'=4,'red'=2,'tok'=2] {'wide','red'}, use_global_device_ids=true, to_apply=%region_2.0 | all-reduce | flops 512 | bytes 4096 | tf_op jit(solution)/shard_map/psum | solution.py:217
  46.1 2.9 %all-gather.3.cloned.1.call-done = bf16[256,3072]{1,0:T(8,128)(2,1)} async-done(((bf16[256,768]{1,0:T(8,128)(2,1)}), bf16[256,3072]{1,0:T(8,128)(2,1)}) %all-gather.3.cloned.1.call-update) | async-done | bytes 1572880 | tf_op jit(solution)/shard_map/all_gather | solution.py:213
  51.3 2.3 %collective-permute-done = bf16[256,1536]{1,0:T(8,128)(2,1)S(1)} collective-permute-done((bf16[256,1536]{1,0:T(8,128)(2,1)S(1)}, bf16[256,1536]{1,0:T(8,128)(2,1)S(1)}, u32[]{:S(2)}, u32[]{:S(2)}) %collective-permute-start) | collective-permute-done | bytes 786464 | tf_op jit(solution)/shard_map/ppermute | solution.py:177
  53.6 9.5 %fusion.7 = bf16[512,3072]{1,0:T(8,128)(2,1)S(1)} fusion(bf16[1536,6144]{1,0:T(8,128)(2,1)} %param.13, bf16[256,1536]{1,0:T(8,128)(2,1)S(1)} %collective-permute-done, bf16[256,1536]{1,0:T(8,128)(2,1)S(1)} %get-tuple-element.35), kind=kOutput, calls=%fused_computation.5 | convolution fusion | flops 4836556800 | bytes 14155776 | tf_op jit(solution)/shard_map/dot_general | solution.py:227
  65.5 5.3 %fusion.4 = bf16[512,3072]{1,0:T(8,128)(2,1)S(1)} fusion(bf16[1536,6144]{1,0:T(8,128)(2,1)S(1)} %bitcast.35, bf16[256,1536]{1,0:T(8,128)(2,1)S(1)} %collective-permute-done, bf16[256,1536]{1,0:T(8,128)(2,1)S(1)} %get-tuple-element.35), kind=kOutput, calls=%fused_computation.4 | convolution fusion | flops 4836556800 | bytes 14155776 | tf_op jit(solution)/shard_map/dot_general | solution.py:227
  74.0 2.3 %collective-permute-done.3 = bf16[256,384]{0,1:T(8,128)(2,1)S(1)} collective-permute-done((bf16[256,384]{0,1:T(8,128)(2,1)S(1)}, bf16[256,384]{0,1:T(8,128)(2,1)S(1)}, u32[]{:S(2)}, u32[]{:S(2)}) %collective-permute-start.3) | collective-permute-done | bytes 196640 | tf_op jit(solution)/shard_map/ppermute | solution.py:177
  83.1 15.8 %collective-permute-done.6.refs_1_ = bf16[112,3072]{1,0:T(8,128)(2,1)S(1)} collective-permute-done((bf16[112,3072]{1,0:T(8,128)(2,1)S(1)}, bf16[112,3072]{1,0:T(8,128)(2,1)S(1)}, u32[]{:S(2)}, u32[]{:S(2)}) %collective-permute-start.6) | collective-permute-done | bytes 688160 | tf_op jit(solution)/shard_map/ppermute | solution.py:183
  105.2 8.4 %collective-permute-done.2.refs_1_ = bf16[112,3072]{1,0:T(8,128)(2,1)S(1)} collective-permute-done((bf16[112,3072]{1,0:T(8,128)(2,1)S(1)}, bf16[112,3072]{1,0:T(8,128)(2,1)S(1)}, u32[]{:S(2)}, u32[]{:S(2)}) %collective-permute-start.2) | collective-permute-done | bytes 688160 | tf_op jit(solution)/shard_map/ppermute | solution.py:183
  117.3 6.4 %copy-done.2 = bf16[6144,1536]{1,0:T(8,128)(2,1)S(1)} copy-done((bf16[6144,1536]{1,0:T(8,128)(2,1)S(1)}, bf16[6144,1536]{1,0:T(8,128)(2,1)}, u32[]{:S(2)}) %copy-start.2) | copy-done | bytes 18874392
  123.7 3.5 %shard_map.84 = (f32[112,1536]{1,0:T(8,128)S(1)}, f32[112,1536]{1,0:T(8,128)S(1)}) custom-call(bf16[112,3072]{1,0:T(8,128)(2,1)S(1)} %shard_map.82.refs_0_, bf16[112,3072]{1,0:T(8,128)(2,1)S(1)} %collective-permute-done.8.refs_1_, bf16[6144,1536]{1,0:T(8,128)(2,1)S(1)} %copy-done.2, bf16[6144,1536]{1,0:T(8,128)(2,1)S(1)} %copy-done.2, ...), custom_call_target="tpu_custom_call" | custom-call | tf_op jit(solution)/shard_map/pallas_call | solution.py:90
  129.2 6.4 %copy-done.3 = bf16[6144,1536]{1,0:T(8,128)(2,1)S(1)} copy-done((bf16[6144,1536]{1,0:T(8,128)(2,1)S(1)}, bf16[6144,1536]{1,0:T(8,128)(2,1)}, u32[]{:S(2)}) %copy-start.3) | copy-done | bytes 18874392
  135.5 3.3 %shard_map.86 = (bf16[112,1536]{1,0:T(8,128)(2,1)S(1)}, bf16[112,1536]{1,0:T(8,128)(2,1)S(1)}) custom-call(bf16[112,3072]{1,0:T(8,128)(2,1)S(1)} %shard_map.83.refs_9_.refs_0_, bf16[112,3072]{1,0:T(8,128)(2,1)S(1)} %collective-permute-done.7.refs_1_, bf16[6144,1536]{1,0:T(8,128)(2,1)S(1)} %copy-done.3, bf16[6144,1536]{1,0:T(8,128)(2,1)S(1)} %copy-done.3, ...), custom_call_target="tpu_custom_call" | custom-call | tf_op jit(solution)/shard_map/pallas_call | solution.py:90
  145.7 6.5 %copy-done.4 = bf16[6144,1536]{1,0:T(8,128)(2,1)S(1)} copy-done((bf16[6144,1536]{1,0:T(8,128)(2,1)S(1)}, bf16[6144,1536]{1,0:T(8,128)(2,1)}, u32[]{:S(2)}) %copy-start.4) | copy-done | bytes 18874392
  152.2 3.7 %shard_map.88 = (f32[80,1536]{1,0:T(8,128)S(1)}, f32[80,1536]{1,0:T(8,128)S(1)}) custom-call(bf16[80,3072]{1,0:T(8,128)(2,1)S(1)} %shard_map.85.refs_8_.refs_0_, bf16[80,3072]{1,0:T(8,128)(2,1)} %collective-permute-done.14.refs_1_, bf16[6144,1536]{1,0:T(8,128)(2,1)S(1)} %copy-done.4, bf16[6144,1536]{1,0:T(8,128)(2,1)S(1)} %copy-done.4, ...), custom_call_target="tpu_custom_call" | custom-call | tf_op jit(solution)/shard_map/pallas_call | solution.py:90
  155.9 2.8 %shard_map.89.refs_8_.refs_0_ = bf16[64,3072]{1,0:T(8,128)(2,1)S(1)} custom-call(bf16[64,3072]{1,0:T(8,128)(2,1)S(1)} %add_convert_fusion.5.refs_0_, bf16[64,3072]{1,0:T(8,128)(2,1)} %collective-permute-done.15.refs_1_, f32[80,1536]{1,0:T(8,128)S(1)} %get-tuple-element.21.refs_2_.refs_6_), custom_call_target="tpu_custom_call" | custom-call | tf_op jit(solution)/shard_map/pallas_call | solution.py:90
  158.8 6.4 %copy-done.5 = bf16[6144,1536]{1,0:T(8,128)(2,1)S(1)} copy-done((bf16[6144,1536]{1,0:T(8,128)(2,1)S(1)}, bf16[6144,1536]{1,0:T(8,128)(2,1)}, u32[]{:S(2)}) %copy-start.5) | copy-done | bytes 18874392
  165.2 2.5 %shard_map.90 = (bf16[80,1536]{1,0:T(8,128)(2,1)S(1)}, bf16[80,1536]{1,0:T(8,128)(2,1)S(1)}) custom-call(bf16[80,3072]{1,0:T(8,128)(2,1)S(1)} %shard_map.87.refs_9_.refs_0_, bf16[80,3072]{1,0:T(8,128)(2,1)S(1)} %collective-permute-done.13.refs_1_, bf16[6144,1536]{1,0:T(8,128)(2,1)S(1)} %copy-done.5, bf16[6144,1536]{1,0:T(8,128)(2,1)S(1)} %copy-done.5, ...), custom_call_target="tpu_custom_call" | custom-call | tf_op jit(solution)/shard_map/pallas_call | solution.py:90
  168.3 2.8 %shard_map.91.refs_9_.refs_0_ = bf16[64,3072]{1,0:T(8,128)(2,1)S(1)} custom-call(bf16[64,3072]{1,0:T(8,128)(2,1)S(1)} %add_convert_fusion.4.refs_0_, bf16[64,3072]{1,0:T(8,128)(2,1)} %collective-permute-done.17.refs_1_, bf16[80,1536]{1,0:T(8,128)(2,1)S(1)} %get-tuple-element.23.refs_2_), custom_call_target="tpu_custom_call" | custom-call | tf_op jit(solution)/shard_map/pallas_call | solution.py:90
  172.4 6.5 %copy-done.6 = bf16[6144,1536]{1,0:T(8,128)(2,1)S(1)} copy-done((bf16[6144,1536]{1,0:T(8,128)(2,1)S(1)}, bf16[6144,1536]{1,0:T(8,128)(2,1)}, u32[]{:S(2)}) %copy-start.6) | copy-done | bytes 18874392
  180.8 2.3 %shard_map.92 = (f32[64,1536]{1,0:T(8,128)S(1)}, f32[64,1536]{1,0:T(8,128)S(1)}) custom-call(bf16[64,3072]{1,0:T(8,128)(2,1)S(1)} %shard_map.89.refs_8_.refs_0_, bf16[64,3072]{1,0:T(8,128)(2,1)S(1)} %collective-permute-done.19.refs_1_, bf16[6144,1536]{1,0:T(8,128)(2,1)S(1)} %copy-done.6, bf16[6144,1536]{1,0:T(8,128)(2,1)S(1)} %copy-done.6, ...), custom_call_target="tpu_custom_call" | custom-call | tf_op jit(solution)/shard_map/pallas_call | solution.py:90
  183.2 2.1 %shard_map.93 = (bf16[64,1536]{1,0:T(8,128)(2,1)S(1)}, bf16[64,1536]{1,0:T(8,128)(2,1)S(1)}) custom-call(bf16[64,3072]{1,0:T(8,128)(2,1)S(1)} %shard_map.91.refs_9_.refs_0_, bf16[64,3072]{1,0:T(8,128)(2,1)S(1)} %collective-permute-done.18.refs_1_, bf16[6144,1536]{1,0:T(8,128)(2,1)S(1)} %copy-done.6, bf16[6144,1536]{1,0:T(8,128)(2,1)S(1)} %copy-done.6, ...), custom_call_target="tpu_custom_call" | custom-call | tf_op jit(solution)/shard_map/pallas_call | solution.py:90
  188.9 2.5 %collective-permute-start.23 = (bf16[64,768]{1,0:T(8,128)(2,1)S(1)}, bf16[64,768]{1,0:T(8,128)(2,1)S(1)}, u32[]{:S(2)}, u32[]{:S(2)}) collective-permute-start(bf16[64,768]{1,0:T(8,128)(2,1)S(1)} %get-tuple-element.42), channel_id=1, source_target_pairs={{0,4},{4,0},{8,12},{12,8},{1,5},{5,1},{9,13},{13,9},{2,6},{6,2},{1... | collective-permute-start | bytes 294920 | tf_op jit(solution)/shard_map/ppermute | solution.py:200
  194.5 4.0 %collective-permute-done.22 = bf16[64,768]{1,0:T(8,128)(2,1)S(1)} collective-permute-done((bf16[64,768]{1,0:T(8,128)(2,1)S(1)}, bf16[64,768]{1,0:T(8,128)(2,1)S(1)}, u32[]{:S(2)}, u32[]{:S(2)}) %collective-permute-start.22) | collective-permute-done | bytes 98336 | tf_op jit(solution)/shard_map/ppermute | solution.py:200
  (137 shorter events, 46.1 us)
Async XLA Ops:
  6.5 42.5 %all-gather.3.cloned.1.call-start = ((), (), s32[]{:S(2)}) async-start(), calls=%async_computation.2 | async-start | bytes 1966080 | tf_op jit(solution)/shard_map/all_gather | solution.py:213
  7.3 165.1 %reduce-scatter.3.cloned.1.call-start = ((), (), s32[]{:S(2)}) async-start(), calls=%async_computation.3 | async-start | bytes 860160 | tf_op jit(solution)/shard_map/reduce_scatter | solution.py:259
  65.3 12.6 %collective-permute-start.5 = (bf16[256,3072]{1,0:T(8,128)(2,1)}, bf16[256,3072]{1,0:T(8,128)(2,1)}, u32[]{:S(2)}, u32[]{:S(2)}) collective-permute-start(bf16[256,3072]{1,0:T(8,128)(2,1)} %slice.170), channel_id=1, source_target_pairs={{0,1},{1,0},{2,3},{3,2},{4,5},{5,4},{6,7},{7,6},{8,9},{9,8},{10,11... | collective-permute-start | bytes 4718600 | tf_op jit(solution)/shard_map/ppermute | solution.py:177
  72.5 7.5 %collective-permute-start.1 = (bf16[256,3072]{1,0:T(8,128)(2,1)S(1)}, bf16[256,3072]{1,0:T(8,128)(2,1)}, u32[]{:S(2)}, u32[]{:S(2)}) collective-permute-start(bf16[256,3072]{1,0:T(8,128)(2,1)S(1)} %slice.165), channel_id=1, source_target_pairs={{0,1},{1,0},{2,3},{3,2},{4,5},{5,4},{6,7},{7,6},{8,9},{9,8},{10,11... | collective-permute-start | bytes 4718600 | tf_op jit(solution)/shard_map/ppermute | solution.py:177
  76.3 24.4 %collective-permute-start.4 = (bf16[256,384]{0,1:T(8,128)(2,1)S(1)}, bf16[256,384]{0,1:T(8,128)(2,1)S(1)}, u32[]{:S(2)}, u32[]{:S(2)}) collective-permute-start(bf16[256,384]{0,1:T(8,128)(2,1)S(1)} %add_convert_fusion.6), channel_id=1, source_target_pairs={{0,2},{2,0},{1,3},{3,1},{4,6},{6,4},{5,7},{7,5},{8,10},{10,8},{9,1... | collective-permute-start | bytes 589832 | tf_op jit(solution)/shard_map/ppermute | solution.py:183
  79.4 19.4 %collective-permute-start.6 = (bf16[112,3072]{1,0:T(8,128)(2,1)S(1)}, bf16[112,3072]{1,0:T(8,128)(2,1)S(1)}, u32[]{:S(2)}, u32[]{:S(2)}) collective-permute-start(bf16[112,3072]{1,0:T(8,128)(2,1)S(1)} %add_convert_fusion.refs_0_), channel_id=1, source_target_pairs={{0,2},{2,0},{1,3},{3,1},{4,6},{6,4},{5,7},{7,5},{8,10},{10,8},{9,1... | collective-permute-start | bytes 2064392 | tf_op jit(solution)/shard_map/ppermute | solution.py:183
  81.4 32.1 %collective-permute-start.2 = (bf16[112,3072]{1,0:T(8,128)(2,1)S(1)}, bf16[112,3072]{1,0:T(8,128)(2,1)S(1)}, u32[]{:S(2)}, u32[]{:S(2)}) collective-permute-start(bf16[112,3072]{1,0:T(8,128)(2,1)S(1)} %add_convert_fusion.1.refs_0_), channel_id=1, source_target_pairs={{0,2},{2,0},{1,3},{3,1},{4,6},{6,4},{5,7},{7,5},{8,10},{10,8},{9,1... | collective-permute-start | bytes 2064392 | tf_op jit(solution)/shard_map/ppermute | solution.py:183
  100.0 17.3 %collective-permute-start.8 = (bf16[112,3072]{1,0:T(8,128)(2,1)S(1)}, bf16[112,3072]{1,0:T(8,128)(2,1)S(1)}, u32[]{:S(2)}, u32[]{:S(2)}) collective-permute-start(bf16[112,3072]{1,0:T(8,128)(2,1)S(1)} %shard_map.82.refs_0_), channel_id=1, source_target_pairs={{0,1},{1,0},{2,3},{3,2},{4,5},{5,4},{6,7},{7,6},{8,9},{9,8},{10,11... | collective-permute-start | bytes 2064392 | tf_op jit(solution)/shard_map/ppermute | solution.py:177
  101.7 15.7 %collective-permute-start.9 = (bf16[256,128]{1,0:T(8,128)(2,1)S(1)}, bf16[256,128]{1,0:T(8,128)(2,1)S(1)}, u32[]{:S(2)}, u32[]{:S(2)}) collective-permute-start(bf16[256,128]{1,0:T(8,128)(2,1)S(1)} %fusion.11.refs_2_), channel_id=1, source_target_pairs={{0,1},{1,0},{2,3},{3,2},{4,5},{5,4},{6,7},{7,6},{8,9},{9,8},{10,11... | collective-permute-start | bytes 196616 | tf_op jit(solution)/shard_map/ppermute | solution.py:177
  103.6 23.6 %collective-permute-start.10 = (bf16[80,3072]{1,0:T(8,128)(2,1)S(1)}, bf16[80,3072]{1,0:T(8,128)(2,1)S(1)}, u32[]{:S(2)}, u32[]{:S(2)}) collective-permute-start(bf16[80,3072]{1,0:T(8,128)(2,1)S(1)} %add_convert_fusion.3.refs_0_), channel_id=1, source_target_pairs={{0,2},{2,0},{1,3},{3,1},{4,6},{6,4},{5,7},{7,5},{8,10},{10,8},{9,1... | collective-permute-start | bytes 1474568 | tf_op jit(solution)/shard_map/ppermute | solution.py:183
  114.3 14.9 %collective-permute-start.7 = (bf16[112,3072]{1,0:T(8,128)(2,1)S(1)}, bf16[112,3072]{1,0:T(8,128)(2,1)S(1)}, u32[]{:S(2)}, u32[]{:S(2)}) collective-permute-start(bf16[112,3072]{1,0:T(8,128)(2,1)S(1)} %shard_map.83.refs_9_.refs_0_), channel_id=1, source_target_pairs={{0,1},{1,0},{2,3},{3,2},{4,5},{5,4},{6,7},{7,6},{8,9},{9,8},{10,11... | collective-permute-start | bytes 2064392 | tf_op jit(solution)/shard_map/ppermute | solution.py:177
  115.7 25.3 %collective-permute-start.12 = (bf16[80,3072]{1,0:T(8,128)(2,1)S(1)}, bf16[80,3072]{1,0:T(8,128)(2,1)S(1)}, u32[]{:S(2)}, u32[]{:S(2)}) collective-permute-start(bf16[80,3072]{1,0:T(8,128)(2,1)S(1)} %add_convert_fusion.2.refs_0_), channel_id=1, source_target_pairs={{0,2},{2,0},{1,3},{3,1},{4,6},{6,4},{5,7},{7,5},{8,10},{10,8},{9,1... | collective-permute-start | bytes 1474568 | tf_op jit(solution)/shard_map/ppermute | solution.py:183
  128.3 17.4 %collective-permute-start.14 = (bf16[80,3072]{1,0:T(8,128)(2,1)S(1)}, bf16[80,3072]{1,0:T(8,128)(2,1)}, u32[]{:S(2)}, u32[]{:S(2)}) collective-permute-start(bf16[80,3072]{1,0:T(8,128)(2,1)S(1)} %shard_map.85.refs_8_.refs_0_), channel_id=1, source_target_pairs={{0,1},{1,0},{2,3},{3,2},{4,5},{5,4},{6,7},{7,6},{8,9},{9,8},{10,11... | collective-permute-start | bytes 1474568 | tf_op jit(solution)/shard_map/ppermute | solution.py:177
  138.8 2.8 %collective-permute-start.11 = (bf16[112,1536]{1,0:T(8,128)(2,1)S(1)}, bf16[112,1536]{1,0:T(8,128)(2,1)S(1)}, u32[]{:S(2)}, u32[]{:S(2)}) collective-permute-start(bf16[112,1536]{1,0:T(8,128)(2,1)S(1)} %get-tuple-element.20), channel_id=1, source_target_pairs={{0,1},{1,0},{2,3},{3,2},{4,5},{5,4},{6,7},{7,6},{8,9},{9,8},{10,11... | collective-permute-start | bytes 1032200 | tf_op jit(solution)/shard_map/ppermute | solution.py:177
  140.4 15.5 %collective-permute-start.15 = (bf16[64,3072]{1,0:T(8,128)(2,1)S(1)}, bf16[64,3072]{1,0:T(8,128)(2,1)}, u32[]{:S(2)}, u32[]{:S(2)}) collective-permute-start(bf16[64,3072]{1,0:T(8,128)(2,1)S(1)} %add_convert_fusion.5.refs_0_), channel_id=1, source_target_pairs={{0,2},{2,0},{1,3},{3,1},{4,6},{6,4},{5,7},{7,5},{8,10},{10,8},{9,1... | collective-permute-start | bytes 1179656 | tf_op jit(solution)/shard_map/ppermute | solution.py:183
  141.5 17.3 %collective-permute-start.13 = (bf16[80,3072]{1,0:T(8,128)(2,1)S(1)}, bf16[80,3072]{1,0:T(8,128)(2,1)S(1)}, u32[]{:S(2)}, u32[]{:S(2)}) collective-permute-start(bf16[80,3072]{1,0:T(8,128)(2,1)S(1)} %shard_map.87.refs_9_.refs_0_), channel_id=1, source_target_pairs={{0,1},{1,0},{2,3},{3,2},{4,5},{5,4},{6,7},{7,6},{8,9},{9,8},{10,11... | collective-permute-start | bytes 1474568 | tf_op jit(solution)/shard_map/ppermute | solution.py:177
  142.6 49.2 %reduce-scatter.5.cloned.1.call-start = ((), (), s32[]{:S(2)}) async-start(), calls=%async_computation.4 | async-start | bytes 614400 | tf_op jit(solution)/shard_map/reduce_scatter | solution.py:259
  144.0 24.3 %collective-permute-start.17 = (bf16[64,3072]{1,0:T(8,128)(2,1)S(1)}, bf16[64,3072]{1,0:T(8,128)(2,1)}, u32[]{:S(2)}, u32[]{:S(2)}) collective-permute-start(bf16[64,3072]{1,0:T(8,128)(2,1)S(1)} %add_convert_fusion.4.refs_0_), channel_id=1, source_target_pairs={{0,2},{2,0},{1,3},{3,1},{4,6},{6,4},{5,7},{7,5},{8,10},{10,8},{9,1... | collective-permute-start | bytes 1179656 | tf_op jit(solution)/shard_map/ppermute | solution.py:183
  167.8 3.7 %collective-permute-start.16 = (bf16[80,1536]{1,0:T(8,128)(2,1)S(1)}, bf16[80,1536]{1,0:T(8,128)(2,1)S(1)}, u32[]{:S(2)}, u32[]{:S(2)}) collective-permute-start(bf16[80,1536]{1,0:T(8,128)(2,1)S(1)} %get-tuple-element.24), channel_id=1, source_target_pairs={{0,1},{1,0},{2,3},{3,2},{4,5},{5,4},{6,7},{7,6},{8,9},{9,8},{10,11... | collective-permute-start | bytes 737288 | tf_op jit(solution)/shard_map/ppermute | solution.py:177
  168.0 4.3 %collective-permute-start.19 = (bf16[64,3072]{1,0:T(8,128)(2,1)S(1)}, bf16[64,3072]{1,0:T(8,128)(2,1)S(1)}, u32[]{:S(2)}, u32[]{:S(2)}) collective-permute-start(bf16[64,3072]{1,0:T(8,128)(2,1)S(1)} %shard_map.89.refs_8_.refs_0_), channel_id=1, source_target_pairs={{0,1},{1,0},{2,3},{3,2},{4,5},{5,4},{6,7},{7,6},{8,9},{9,8},{10,11... | collective-permute-start | bytes 1179656 | tf_op jit(solution)/shard_map/ppermute | solution.py:177
  171.2 12.0 %collective-permute-start.18 = (bf16[64,3072]{1,0:T(8,128)(2,1)S(1)}, bf16[64,3072]{1,0:T(8,128)(2,1)S(1)}, u32[]{:S(2)}, u32[]{:S(2)}) collective-permute-start(bf16[64,3072]{1,0:T(8,128)(2,1)S(1)} %shard_map.91.refs_9_.refs_0_), channel_id=1, source_target_pairs={{0,1},{1,0},{2,3},{3,2},{4,5},{5,4},{6,7},{7,6},{8,9},{9,8},{10,11... | collective-permute-start | bytes 1179656 | tf_op jit(solution)/shard_map/ppermute | solution.py:177
  186.9 7.6 %collective-permute-start.21 = (bf16[64,768]{1,0:T(8,128)(2,1)S(1)}, bf16[64,768]{1,0:T(8,128)(2,1)S(1)}, u32[]{:S(2)}, u32[]{:S(2)}) collective-permute-start(bf16[64,768]{1,0:T(8,128)(2,1)S(1)} %get-tuple-element.41), channel_id=1, source_target_pairs={{0,12},{4,8},{8,4},{12,0},{1,13},{5,9},{9,5},{13,1},{2,14},{6,10},... | collective-permute-start | bytes 294920 | tf_op jit(solution)/shard_map/ppermute | solution.py:200
  188.2 10.3 %collective-permute-start.22 = (bf16[64,768]{1,0:T(8,128)(2,1)S(1)}, bf16[64,768]{1,0:T(8,128)(2,1)S(1)}, u32[]{:S(2)}, u32[]{:S(2)}) collective-permute-start(bf16[64,768]{1,0:T(8,128)(2,1)S(1)} %get-tuple-element.43), channel_id=1, source_target_pairs={{0,8},{4,12},{8,0},{12,4},{1,9},{5,13},{9,1},{13,5},{2,10},{6,14},... | collective-permute-start | bytes 294920 | tf_op jit(solution)/shard_map/ppermute | solution.py:200
  188.9 9.6 %collective-permute-start.23 = (bf16[64,768]{1,0:T(8,128)(2,1)S(1)}, bf16[64,768]{1,0:T(8,128)(2,1)S(1)}, u32[]{:S(2)}, u32[]{:S(2)}) collective-permute-start(bf16[64,768]{1,0:T(8,128)(2,1)S(1)} %get-tuple-element.42), channel_id=1, source_target_pairs={{0,4},{4,0},{8,12},{12,8},{1,5},{5,1},{9,13},{13,9},{2,6},{6,2},{1... | collective-permute-start | bytes 294920 | tf_op jit(solution)/shard_map/ppermute | solution.py:200
  (24 other events, 243.3 us)
Sparse Core Ops, SparseCore 0:
  8.9 40.0 all-gather.2
  142.7 21.5 reduce-scatter.2
  172.5 19.3 reduce-scatter.4

commit v3 on v2

--- a/solution.py
+++ b/solution.py
@@ -13,9 +13,9 @@
 EPS = 1e-06
 SHARES = (7, 5, 4)
 PIECES = (1, 1)
-PARTS = 4
+AHEAD = 4
 BF16, F32 = jnp.bfloat16, jnp.float32
-PARAMS = pltpu.CompilerParams(vmem_limit_bytes=32 * 2**20)
+PARAMS = pltpu.CompilerParams(vmem_limit_bytes=48 * 2**20)
 SOON = pl.CostEstimate(flops=0, bytes_accessed=0, transcendentals=0)
 
 
@@ -53,28 +53,10 @@
     return [slice(a, b) for a, b in zip([0] + ends[:-1], ends)]
 
 
-def steps_of(piece, blocks=(512, 384, 256, 128)):
+def steps_of(piece):
     size = math.gcd(piece.stop - piece.start, piece.start)
-    block = next(b for b in blocks if size % b == 0)
+    block = next(b for b in (512, 384, 256, 128) if size % b == 0)
     return block, (piece.stop - piece.start) // block, piece.start // block
-
-
-def row_parts(block, columns, index):
-    return [
-        pl.BlockSpec(
-            (block // PARTS, columns),
-            lambda j, part=part: (PARTS * index(j)[0] + part, index(j)[1]),
-        )
-        for part in range(PARTS)
-    ]
-
-
-def dot_parts(x, weights):
-    depth = x.shape[1] // PARTS
-    return sum(
-        jnp.dot(x[:, at * depth : (at + 1) * depth], w[...], preferred_element_type=F32)
-        for at, w in enumerate(weights)
-    )
 
 
 def corner_of(x):
@@ -118,54 +100,115 @@
     )
 
 
-def project_hidden(own, other, weight, piece, added, attention, last, earlier=()):
-    rows = own.shape[0]
-    columns = weight.shape[1]
-    block, steps, skipped = steps_of(piece, (1024, 768, 512, 384, 256, 128))
-    whole = pl.BlockSpec((rows, columns), lambda k: (0, 0))
-    part = pl.BlockSpec((rows, block), lambda k: (0, k))
-    specs = [part, part, *row_parts(block, columns, lambda k: (skipped + k, 0))]
-    specs += [whole] * len(added)
-    specs += [pl.BlockSpec(a.shape, lambda k: (0, 0)) for a in attention]
+def project_rows(own, other, weight, piece, earlier=()):
+    rows, depth = own.shape
+    columns = piece.stop - piece.start
+    block, steps, _ = steps_of(piece)
+    whole = pl.BlockSpec((rows, depth), lambda *_: (0, 0))
+    out = pl.BlockSpec((rows, columns), lambda *_: (0, 0))
 
     def kernel(ins, refs):
-        outs, totals = refs[:2], refs[2:]
-        k = pl.program_id(0)
-        both = jnp.concatenate([ins[0][...], ins[1][...]], axis=0)
-        product = dot_parts(both, ins[2 : 2 + PARTS])
-        halves = [product[:rows], product[rows:]]
-
-        @pl.when(k == 0)
-        def _():
-            first = list(halves)
-            for at in range(2):
-                if added:
-                    first[at] = first[at] + ins[2 + PARTS + at][...]
-                if attention:
-                    first[at] = first[at] + jnp.dot(
-                        ins[-3 + at][...], ins[-1][...], preferred_element_type=F32
-                    )
-                totals[at][...] = first[at]
-
-        @pl.when(k > 0)
-        def _():
-            for at in range(2):
-                totals[at][...] += halves[at]
-
-        @pl.when(k == steps - 1)
-        def _():
-            for at in range(2):
-                outs[at][...] = totals[at][...].astype(outs[at].dtype)
+        near, far, both, landed, sems = refs
+
+        def bring(at):
+            start = pl.multiple_of(piece.start + at * block, block)
+            source = ins[2].at[:, pl.ds(start, block)]
+            return pltpu.make_async_copy(source, landed.at[at], sems.at[at])
+
+        for at in range(min(AHEAD, steps)):
+            bring(at).start()
+        both[:rows] = ins[0][...]
+        both[rows:] = ins[1][...]
+
+        @pl.loop(0, steps)
+        def _(at):
+            bring(at).wait()
+
+            @pl.when(at + AHEAD < steps)
+            def _():
+                bring(at + AHEAD).start()
+
+            part = jnp.dot(both[...], landed[at], preferred_element_type=F32).astype(BF16)
+            here = pl.ds(pl.multiple_of(at * block, block), block)
+            near[:, here] = part[:rows]
+            far[:, here] = part[rows:]
 
     return call(
         kernel,
         earlier,
-        (own, other, *[weight] * PARTS, *added, *attention),
+        (own, other, weight),
+        [whole, whole, pl.BlockSpec(memory_space=pltpu.HBM)],
+        grid=(1,),
+        out_specs=[out] * 2,
+        out_shape=[jax.ShapeDtypeStruct((rows, columns), BF16)] * 2,
+        scratch_shapes=[
+            pltpu.VMEM((2 * rows, depth), BF16),
+            pltpu.VMEM((steps, depth, block), BF16),
+            pltpu.SemaphoreType.DMA((steps,)),
+        ],
+    )
+
+
+def project_hidden(own, other, weight, piece, added, attention, last, earlier=()):
+    rows, units = own.shape
+    columns = weight.shape[1]
+    block, steps, _ = steps_of(piece)
+    whole = pl.BlockSpec((rows, columns), lambda *_: (0, 0))
+    part = pl.BlockSpec((rows, units), lambda *_: (0, 0))
+    specs = [part, part, pl.BlockSpec(memory_space=pltpu.HBM)]
+    specs += [whole] * len(added)
+    specs += [pl.BlockSpec(a.shape, lambda *_: (0, 0)) for a in attention]
+
+    def kernel(ins, refs):
+        outs, (both, total, landed, sems) = refs[:2], refs[2:]
+
+        def bring(at):
+            start = pl.multiple_of(piece.start + at * block, block)
+            source = ins[2].at[pl.ds(start, block), :]
+            return pltpu.make_async_copy(source, landed.at[at], sems.at[at])
+
+        for at in range(min(AHEAD, steps)):
+            bring(at).start()
+        halves = (slice(0, rows), slice(rows, 2 * rows))
+        for at, half in enumerate(halves):
+            both[half] = ins[at][...]
+            first = jnp.zeros((rows, columns), F32)
+            if added:
+                first = ins[3 + at][...]
+            if attention:
+                first = first + jnp.dot(
+                    ins[-3 + at][...], ins[-1][...], preferred_element_type=F32
+                )
+            total[half] = first
+
+        @pl.loop(0, steps)
+        def _(at):
+            bring(at).wait()
+
+            @pl.when(at + AHEAD < steps)
+            def _():
+                bring(at + AHEAD).start()
+
+            here = pl.ds(pl.multiple_of(at * block, block), block)
+            total[...] += jnp.dot(both[:, here], landed[at], preferred_element_type=F32)
+
+        for out, half in zip(outs, halves):
+            out[...] = total[half].astype(out.dtype)
+
+    return call(
+        kernel,
+        earlier,
+        (own, other, weight, *added, *attention),
         specs,
-        grid=(steps,),
+        grid=(1,),
         out_specs=[whole] * 2,
         out_shape=[jax.ShapeDtypeStruct((rows, columns), BF16 if last else F32)] * 2,
-        scratch_shapes=[pltpu.VMEM((rows, columns), F32)] * 2,
+        scratch_shapes=[
+            pltpu.VMEM((2 * rows, units), BF16),
+            pltpu.VMEM((2 * rows, columns), F32),
+            pltpu.VMEM((steps, block, columns), BF16),
+            pltpu.SemaphoreType.DMA((steps,)),
+        ],
     )
 
 
@@ -220,18 +263,18 @@
         other = lax.dynamic_slice_in_dim(normed, (1 - core) * depth, depth, axis=1)
         other = swap(other)
 
-        both = jnp.concatenate([own, other], axis=0)
-        rows = tokens.shape[0]
-
-        def project(weight):
-            part = jnp.dot(both, weight, preferred_element_type=F32).astype(BF16)
-            return part[:rows], swap(part[rows:])
+        def project(weight, piece, earlier):
+            near, far = project_rows(own, other, weight, piece, earlier)
+            return near, swap(far)
 
         def block_sum(parts, start=0.0):
             return (parts[0].astype(F32) + parts[1].astype(F32) + start).astype(BF16)
 
-        halves = [project(w_up[:, piece]) for piece in pieces]
-        qkv = block_sum(project(qkv_rows))
+        halves, earlier = [], ()
+        for piece in pieces:
+            halves.append(project(w_up, piece, earlier))
+            earlier = [halves[-1][0]]
+        qkv = block_sum(project(qkv_rows, slice(0, qkv_rows.shape[1]), earlier))
 
         order = [(c, p) for c in range(n) for p in range(len(pieces))]
         outs, scattered = [], []

time: 207 us -> 200 us (0.966)
  Pallas kernels: 25.5 us -> 59.7 us
  local copies, waits for them, and re-layouts: 40 us -> 11 us
  matrix products: 16.3 us -> 0.74 us
    pallas_call x12 -> x15, Pallas kernels: 25.5 us -> 59.7 us  [call(): pl.pallas_call(body, in_specs=list(specs) + [corner_of(a) for a in earlie...]
    unnamed x44 -> x30, local copies, waits for them, and re-layouts: 37.3 us -> 6.25 us
    dot_general x3 -> x0, matrix products: 15.6 us -> none  [project(): part = jnp.dot(both, weight, preferred_element_type=F32).astype(BF16)]
    slice x6, local copies, waits for them, and re-layouts: 0.02 us -> 2.91 us  [output(): attention = (attended[cuts[c]], attended_other[cuts[c]], attn_rows)]
  transfers between devices with their start and end apart: 27 -> 27, of which waited for: 9 -> 9; matrix products, arithmetic and copies ran while one was open for 10% -> 10% of each run, Pallas kernels for 12% -> 26%
where the time goes in v3:
time: 200 us; the launch traced here: 199 us
  Pallas kernels  59.7 us (30%)
  waiting for transfers between devices  41.6 us (21%)
  blocking collectives  36.8 us (18%)
  starting transfers between devices  17.2 us (9%)
  other arithmetic  17.1 us (9%)
  between operations  14.9 us (7%)
  local copies, waits for them, and re-layouts  11 us (6%)
    pallas_call x15, Pallas kernels, call(): pl.pallas_call(body, in_specs=list(specs) + [corner_of(a) for a in earlie...  59.7 us
    ppermute x7, waiting for transfers between devices, all_red(): parts.append(lax.ppermute(x, 'red', pairs))  25.9 us
    psum x1, blocking collectives, body(): sums = lax.psum(sums, ('wide', 'red'))[:, :, None] / D  22.1 us
    all_gather x1, blocking collectives, body(): gain = lax.all_gather(ln_gain, 'wide', axis=0, tiled=True)  14.7 us
    convert_element_type x7, other arithmetic, block_sum(): return (parts[0].astype(F32) + parts[1].astype(F32) + start).astype(BF16)  9.59 us
    ppermute x7, starting transfers between devices, all_red(): parts.append(lax.ppermute(x, 'red', pairs))  9.06 us
    unnamed x30, local copies, waits for them, and re-layouts  6.25 us
    ppermute x14, waiting for transfers between devices, swap(): return lax.ppermute(x, 'tok', [(0, 1), (1, 0)])  5.33 us
  transfers between devices with their start and end apart: 27, of which 9 were waited for; matrix products, arithmetic and copies ran while one was open for 10% of the time, Pallas kernels for 26%

profile of v3, /device:TPU:0, one launch (start us, length us, event | category | flops | bytes accessed | tf_op | source)
XLA Modules:
  0.0 199.0 jit_solution(3560112777102889127)
XLA Ops:
  8.0 14.7 %all-gather = bf16[4,1,768]{2,1,0:T(2,128)(2,1)S(1)} all-gather(bf16[1,1,768]{2,1,0:T(2,128)(2,1)S(1)} %reshape.115), channel_id=1, replica_groups=mesh['grp'=2,'wide'=4,'red'=2,'tok'=2] {'wide'}, dimensions={0}, use_global_device_ids=true | all-gather | bytes 7680 | tf_op jit(solution)/shard_map/all_gather | solution.py:257
  24.0 22.1 %psum.7 = f32[2,256]{1,0:T(2,128)S(1)} all-reduce(f32[2,256]{1,0:T(2,128)S(1)} %pad_maximum_fusion.3), channel_id=1, replica_groups=mesh['grp'=2,'wide'=4,'red'=2,'tok'=2] {'wide','red'}, use_global_device_ids=true, to_apply=%region_2.0 | all-reduce | flops 512 | bytes 4096 | tf_op jit(solution)/shard_map/psum | solution.py:260
  46.1 2.9 %all-gather.3.cloned.1.call-done = bf16[256,3072]{1,0:T(8,128)(2,1)} async-done(((bf16[256,768]{1,0:T(8,128)(2,1)}), bf16[256,3072]{1,0:T(8,128)(2,1)}) %all-gather.3.cloned.1.call-update) | async-done | bytes 1572880 | tf_op jit(solution)/shard_map/all_gather | solution.py:256
  49.0 2.1 %multiply_convert_fusion = bf16[256,3072]{1,0:T(8,128)(2,1)S(1)} fusion(bf16[256,3072]{1,0:T(8,128)(2,1)} %all-gather.3.cloned.1.call-done, f32[3072]{0:T(1024)S(1)} %bitcast.25, f32[256]{0:T(256)S(1)} %add_rsqrt_fusion.2, f32[256]{0:T(256)S(1)} %bitcast.27), kind=kLoop, calls=%fused_computation | loop fusion | flops 3932160 | bytes 3160064 | tf_op jit(solution)/shard_map/convert_element_type | solution.py:261
  51.3 2.3 %collective-permute-done.refs_1_ = bf16[256,1536]{1,0:T(8,128)(2,1)S(1)} collective-permute-done((bf16[256,1536]{1,0:T(8,128)(2,1)S(1)}, bf16[256,1536]{1,0:T(8,128)(2,1)S(1)}, u32[]{:S(2)}, u32[]{:S(2)}) %collective-permute-start) | collective-permute-done | bytes 786464 | tf_op jit(solution)/shard_map/ppermute | solution.py:220
  53.6 8.5 %shard_map.82 = (bf16[256,3072]{1,0:T(8,128)(2,1)S(1)}, bf16[256,3072]{1,0:T(8,128)(2,1)}) custom-call(bf16[256,1536]{1,0:T(8,128)(2,1)S(1)} %get-tuple-element.48.refs_0_, bf16[256,1536]{1,0:T(8,128)(2,1)S(1)} %collective-permute-done.refs_1_, bf16[1536,6144]{1,0:T(8,128)(2,1)} %refs_2_.9), custom_call_target="tpu_custom_call" | custom-call | tf_op jit(solution)/shard_map/pallas_call | solution.py:72
  63.4 9.3 %shard_map.83 = (bf16[256,3072]{1,0:T(8,128)(2,1)S(1)}, bf16[256,3072]{1,0:T(8,128)(2,1)}) custom-call(bf16[256,1536]{1,0:T(8,128)(2,1)S(1)} %get-tuple-element.48.refs_0_, bf16[256,1536]{1,0:T(8,128)(2,1)S(1)} %collective-permute-done.refs_1_, bf16[1536,6144]{1,0:T(8,128)(2,1)} %refs_2_.9, bf16[256,3072]{1,0:T(8,128)(2,1)} %copy-done), custom_call_target="tpu_custom_call" | custom-call | tf_op jit(solution)/shard_map/pallas_call | solution.py:72
  74.7 1.9 collective-permute-done.3
  83.9 16.2 %collective-permute-done.6.refs_1_ = bf16[112,3072]{1,0:T(8,128)(2,1)S(1)} collective-permute-done((bf16[112,3072]{1,0:T(8,128)(2,1)S(1)}, bf16[112,3072]{1,0:T(8,128)(2,1)S(1)}, u32[]{:S(2)}, u32[]{:S(2)}) %collective-permute-start.6) | collective-permute-done | bytes 688160 | tf_op jit(solution)/shard_map/ppermute | solution.py:226
  106.5 8.3 %collective-permute-done.2.refs_1_ = bf16[112,3072]{1,0:T(8,128)(2,1)S(1)} collective-permute-done((bf16[112,3072]{1,0:T(8,128)(2,1)S(1)}, bf16[112,3072]{1,0:T(8,128)(2,1)S(1)}, u32[]{:S(2)}, u32[]{:S(2)}) %collective-permute-start.2) | collective-permute-done | bytes 688160 | tf_op jit(solution)/shard_map/ppermute | solution.py:226
  119.1 4.9 %shard_map.87 = (f32[112,1536]{1,0:T(8,128)S(1)}, f32[112,1536]{1,0:T(8,128)S(1)}) custom-call(bf16[112,3072]{1,0:T(8,128)(2,1)S(1)} %shard_map.85.refs_0_, bf16[112,3072]{1,0:T(8,128)(2,1)S(1)} %collective-permute-done.8.refs_1_, bf16[6144,1536]{1,0:T(8,128)(2,1)} %refs_2_.15, bf16[112,128]{1,0:T(8,128)(2,1)S(1)} %slice_bitcast_fusion.refs_3_, ...), custom_call_target="tpu_custom_call" | custom-call | tf_op jit(solution)/shard_map/pallas_call | solution.py:72
  125.4 2.3 %shard_map.88.refs_5_.refs_0_ = bf16[80,3072]{1,0:T(8,128)(2,1)} custom-call(bf16[80,3072]{1,0:T(8,128)(2,1)S(1)} %add_convert_fusion.3.refs_0_, bf16[80,3072]{1,0:T(8,128)(2,1)S(1)} %collective-permute-done.10.refs_1_, f32[112,1536]{1,0:T(8,128)S(1)} %get-tuple-element.29.refs_2_.refs_3_), custom_call_target="tpu_custom_call" | custom-call | tf_op jit(solution)/shard_map/pallas_call | solution.py:72
  129.5 5.4 %shard_map.89 = (bf16[112,1536]{1,0:T(8,128)(2,1)S(1)}, bf16[112,1536]{1,0:T(8,128)(2,1)S(1)}) custom-call(bf16[112,3072]{1,0:T(8,128)(2,1)S(1)} %shard_map.86.refs_6_.refs_0_, bf16[112,3072]{1,0:T(8,128)(2,1)S(1)} %collective-permute-done.7.refs_1_, bf16[6144,1536]{1,0:T(8,128)(2,1)} %refs_2_.15, f32[112,1536]{1,0:T(8,128)S(1)} %get-tuple-element.29.refs_2_.refs_3_, ...), custom_call_target="tpu_custom_call" | custom-call | tf_op jit(solution)/shard_map/pallas_call | solution.py:72
  135.5 1.9 add_convert_fusion.5.refs_0_
  140.8 1.9 add_convert_fusion.4.refs_0_
  144.6 5.8 %shard_map.91 = (f32[80,1536]{1,0:T(8,128)S(1)}, f32[80,1536]{1,0:T(8,128)S(1)}) custom-call(bf16[80,3072]{1,0:T(8,128)(2,1)} %shard_map.88.refs_5_.refs_0_, bf16[80,3072]{1,0:T(8,128)(2,1)} %collective-permute-done.14.refs_1_, bf16[6144,1536]{1,0:T(8,128)(2,1)} %refs_2_.15, bf16[80,128]{1,0:T(8,128)(2,1)S(1)} %slice_bitcast_fusion.1.refs_3_, ...), custom_call_target="tpu_custom_call" | custom-call | tf_op jit(solution)/shard_map/pallas_call | solution.py:72
  152.2 2.8 %shard_map.92.refs_5_.refs_0_ = bf16[64,3072]{1,0:T(8,128)(2,1)S(1)} custom-call(bf16[64,3072]{1,0:T(8,128)(2,1)} %add_convert_fusion.5.refs_0_, bf16[64,3072]{1,0:T(8,128)(2,1)S(1)} %copy-done.8, f32[80,1536]{1,0:T(8,128)S(1)} %get-tuple-element.33.refs_2_.refs_3_), custom_call_target="tpu_custom_call" | custom-call | tf_op jit(solution)/shard_map/pallas_call | solution.py:72
  155.0 5.5 %shard_map.93 = (bf16[80,1536]{1,0:T(8,128)(2,1)S(1)}, bf16[80,1536]{1,0:T(8,128)(2,1)S(1)}) custom-call(bf16[80,3072]{1,0:T(8,128)(2,1)S(1)} %shard_map.90.refs_6_.refs_0_, bf16[80,3072]{1,0:T(8,128)(2,1)} %collective-permute-done.13.refs_1_, bf16[6144,1536]{1,0:T(8,128)(2,1)} %refs_2_.15, f32[80,1536]{1,0:T(8,128)S(1)} %get-tuple-element.33.refs_2_.refs_3_, ...), custom_call_target="tpu_custom_call" | custom-call | tf_op jit(solution)/shard_map/pallas_call | solution.py:72
  161.2 2.8 %shard_map.94.refs_6_.refs_0_ = bf16[64,3072]{1,0:T(8,128)(2,1)S(1)} custom-call(bf16[64,3072]{1,0:T(8,128)(2,1)} %add_convert_fusion.4.refs_0_, bf16[64,3072]{1,0:T(8,128)(2,1)S(1)} %collective-permute-done.17.refs_1_, bf16[80,1536]{1,0:T(8,128)(2,1)S(1)} %get-tuple-element.35.refs_2_), custom_call_target="tpu_custom_call" | custom-call | tf_op jit(solution)/shard_map/pallas_call | solution.py:72
  168.6 4.7 %shard_map.95 = (f32[64,1536]{1,0:T(8,128)S(1)}, f32[64,1536]{1,0:T(8,128)S(1)}) custom-call(bf16[64,3072]{1,0:T(8,128)(2,1)S(1)} %shard_map.92.refs_5_.refs_0_, bf16[64,3072]{1,0:T(8,128)(2,1)S(1)} %collective-permute-done.19.refs_1_, bf16[6144,1536]{1,0:T(8,128)(2,1)} %refs_2_.15, bf16[64,128]{1,0:T(8,128)(2,1)S(1)} %slice_bitcast_fusion.2.refs_3_, ...), custom_call_target="tpu_custom_call" | custom-call | tf_op jit(solution)/shard_map/pallas_call | solution.py:72
  173.3 4.5 %shard_map.96 = (bf16[64,1536]{1,0:T(8,128)(2,1)S(1)}, bf16[64,1536]{1,0:T(8,128)(2,1)S(1)}) custom-call(bf16[64,3072]{1,0:T(8,128)(2,1)S(1)} %shard_map.94.refs_6_.refs_0_, bf16[64,3072]{1,0:T(8,128)(2,1)S(1)} %collective-permute-done.18.refs_1_, bf16[6144,1536]{1,0:T(8,128)(2,1)} %refs_2_.15, f32[64,1536]{1,0:T(8,128)S(1)} %get-tuple-element.37.refs_3_.refs_5_, ...), custom_call_target="tpu_custom_call" | custom-call | tf_op jit(solution)/shard_map/pallas_call | solution.py:72
  181.4 2.5 %collective-permute-start.23 = (bf16[64,768]{1,0:T(8,128)(2,1)S(1)}, bf16[64,768]{1,0:T(8,128)(2,1)S(1)}, u32[]{:S(2)}, u32[]{:S(2)}) collective-permute-start(bf16[64,768]{1,0:T(8,128)(2,1)S(1)} %get-tuple-element.54), channel_id=1, source_target_pairs={{0,4},{4,0},{8,12},{12,8},{1,5},{5,1},{9,13},{13,9},{2,6},{6,2},{1... | collective-permute-start | bytes 294920 | tf_op jit(solution)/shard_map/ppermute | solution.py:243
  183.8 2.4 %reduce-scatter.5.cloned.1.call-done = bf16[80,768]{1,0:T(8,128)(2,1)} async-done(((bf16[80,3072]{1,0:T(8,128)(2,1)}), bf16[80,768]{1,0:T(8,128)(2,1)}) %reduce-scatter.5.cloned.1.call-update) | async-done | bytes 122896 | tf_op jit(solution)/shard_map/reduce_scatter | solution.py:302
  187.2 4.3 %collective-permute-done.22 = bf16[64,768]{1,0:T(8,128)(2,1)S(1)} collective-permute-done((bf16[64,768]{1,0:T(8,128)(2,1)S(1)}, bf16[64,768]{1,0:T(8,128)(2,1)S(1)}, u32[]{:S(2)}, u32[]{:S(2)}) %collective-permute-start.22) | collective-permute-done | bytes 98336 | tf_op jit(solution)/shard_map/ppermute | solution.py:243
  (119 shorter events, 44.2 us)
Async XLA Ops:
  6.5 42.5 %all-gather.3.cloned.1.call-start = ((), (), s32[]{:S(2)}) async-start(), calls=%async_computation.2 | async-start | bytes 1966080 | tf_op jit(solution)/shard_map/all_gather | solution.py:256
  7.3 159.4 %reduce-scatter.3.cloned.1.call-start = ((), (), s32[]{:S(2)}) async-start(), calls=%async_computation.3 | async-start | bytes 860160 | tf_op jit(solution)/shard_map/reduce_scatter | solution.py:302
  63.3 15.9 %collective-permute-start.5 = (bf16[256,3072]{1,0:T(8,128)(2,1)}, bf16[256,3072]{1,0:T(8,128)(2,1)}, u32[]{:S(2)}, u32[]{:S(2)}) collective-permute-start(bf16[256,3072]{1,0:T(8,128)(2,1)} %get-tuple-element.28), channel_id=1, source_target_pairs={{0,1},{1,0},{2,3},{3,2},{4,5},{5,4},{6,7},{7,6},{8,9},{9,8},{10,11... | collective-permute-start | bytes 4718600 | tf_op jit(solution)/shard_map/ppermute | solution.py:220
  72.7 8.3 %collective-permute-start.1 = (bf16[256,3072]{1,0:T(8,128)(2,1)}, bf16[256,3072]{1,0:T(8,128)(2,1)}, u32[]{:S(2)}, u32[]{:S(2)}) collective-permute-start(bf16[256,3072]{1,0:T(8,128)(2,1)} %get-tuple-element.25), channel_id=1, source_target_pairs={{0,1},{1,0},{2,3},{3,2},{4,5},{5,4},{6,7},{7,6},{8,9},{9,8},{10,11... | collective-permute-start | bytes 4718600 | tf_op jit(solution)/shard_map/ppermute | solution.py:220
  77.6 24.4 %collective-permute-start.4 = (bf16[256,384]{1,0:T(8,128)(2,1)S(1)}, bf16[256,384]{1,0:T(8,128)(2,1)S(1)}, u32[]{:S(2)}, u32[]{:S(2)}) collective-permute-start(bf16[256,384]{1,0:T(8,128)(2,1)S(1)} %add_convert_fusion.6), channel_id=1, source_target_pairs={{0,2},{2,0},{1,3},{3,1},{4,6},{6,4},{5,7},{7,5},{8,10},{10,8},{9,1... | collective-permute-start | bytes 589832 | tf_op jit(solution)/shard_map/ppermute | solution.py:226
  80.5 19.6 %collective-permute-start.6 = (bf16[112,3072]{1,0:T(8,128)(2,1)S(1)}, bf16[112,3072]{1,0:T(8,128)(2,1)S(1)}, u32[]{:S(2)}, u32[]{:S(2)}) collective-permute-start(bf16[112,3072]{1,0:T(8,128)(2,1)S(1)} %add_convert_fusion.refs_0_), channel_id=1, source_target_pairs={{0,2},{2,0},{1,3},{3,1},{4,6},{6,4},{5,7},{7,5},{8,10},{10,8},{9,1... | collective-permute-start | bytes 2064392 | tf_op jit(solution)/shard_map/ppermute | solution.py:226
  82.3 32.6 %collective-permute-start.2 = (bf16[112,3072]{1,0:T(8,128)(2,1)S(1)}, bf16[112,3072]{1,0:T(8,128)(2,1)S(1)}, u32[]{:S(2)}, u32[]{:S(2)}) collective-permute-start(bf16[112,3072]{1,0:T(8,128)(2,1)S(1)} %add_convert_fusion.1.refs_0_), channel_id=1, source_target_pairs={{0,2},{2,0},{1,3},{3,1},{4,6},{6,4},{5,7},{7,5},{8,10},{10,8},{9,1... | collective-permute-start | bytes 2064392 | tf_op jit(solution)/shard_map/ppermute | solution.py:226
  101.3 17.2 %collective-permute-start.8 = (bf16[112,3072]{1,0:T(8,128)(2,1)S(1)}, bf16[112,3072]{1,0:T(8,128)(2,1)S(1)}, u32[]{:S(2)}, u32[]{:S(2)}) collective-permute-start(bf16[112,3072]{1,0:T(8,128)(2,1)S(1)} %shard_map.85.refs_0_), channel_id=1, source_target_pairs={{0,1},{1,0},{2,3},{3,2},{4,5},{5,4},{6,7},{7,6},{8,9},{9,8},{10,11... | collective-permute-start | bytes 2064392 | tf_op jit(solution)/shard_map/ppermute | solution.py:220
  103.1 15.3 %collective-permute-start.9 = (bf16[256,128]{1,0:T(8,128)(2,1)S(1)}, bf16[256,128]{1,0:T(8,128)(2,1)S(1)}, u32[]{:S(2)}, u32[]{:S(2)}) collective-permute-start(bf16[256,128]{1,0:T(8,128)(2,1)S(1)} %fusion.refs_2_), channel_id=1, source_target_pairs={{0,1},{1,0},{2,3},{3,2},{4,5},{5,4},{6,7},{7,6},{8,9},{9,8},{10,11... | collective-permute-start | bytes 196616 | tf_op jit(solution)/shard_map/ppermute | solution.py:220
  104.9 20.5 %collective-permute-start.10 = (bf16[80,3072]{1,0:T(8,128)(2,1)S(1)}, bf16[80,3072]{1,0:T(8,128)(2,1)S(1)}, u32[]{:S(2)}, u32[]{:S(2)}) collective-permute-start(bf16[80,3072]{1,0:T(8,128)(2,1)S(1)} %add_convert_fusion.3.refs_0_), channel_id=1, source_target_pairs={{0,2},{2,0},{1,3},{3,1},{4,6},{6,4},{5,7},{7,5},{8,10},{10,8},{9,1... | collective-permute-start | bytes 1474568 | tf_op jit(solution)/shard_map/ppermute | solution.py:226
  115.5 14.0 %collective-permute-start.7 = (bf16[112,3072]{1,0:T(8,128)(2,1)S(1)}, bf16[112,3072]{1,0:T(8,128)(2,1)S(1)}, u32[]{:S(2)}, u32[]{:S(2)}) collective-permute-start(bf16[112,3072]{1,0:T(8,128)(2,1)S(1)} %shard_map.86.refs_6_.refs_0_), channel_id=1, source_target_pairs={{0,1},{1,0},{2,3},{3,2},{4,5},{5,4},{6,7},{7,6},{8,9},{9,8},{10,11... | collective-permute-start | bytes 2064392 | tf_op jit(solution)/shard_map/ppermute | solution.py:220
  116.8 22.1 %collective-permute-start.12 = (bf16[80,3072]{1,0:T(8,128)(2,1)S(1)}, bf16[80,3072]{1,0:T(8,128)(2,1)S(1)}, u32[]{:S(2)}, u32[]{:S(2)}) collective-permute-start(bf16[80,3072]{1,0:T(8,128)(2,1)S(1)} %add_convert_fusion.2.refs_0_), channel_id=1, source_target_pairs={{0,2},{2,0},{1,3},{3,1},{4,6},{6,4},{5,7},{7,5},{8,10},{10,8},{9,1... | collective-permute-start | bytes 1474568 | tf_op jit(solution)/shard_map/ppermute | solution.py:226
  128.9 15.8 %collective-permute-start.14 = (bf16[80,3072]{1,0:T(8,128)(2,1)}, bf16[80,3072]{1,0:T(8,128)(2,1)}, u32[]{:S(2)}, u32[]{:S(2)}) collective-permute-start(bf16[80,3072]{1,0:T(8,128)(2,1)} %shard_map.88.refs_5_.refs_0_), channel_id=1, source_target_pairs={{0,1},{1,0},{2,3},{3,2},{4,5},{5,4},{6,7},{7,6},{8,9},{9,8},{10,11... | collective-permute-start | bytes 1474568 | tf_op jit(solution)/shard_map/ppermute | solution.py:220
  134.9 4.7 %collective-permute-start.11 = (bf16[112,1536]{1,0:T(8,128)(2,1)S(1)}, bf16[112,1536]{1,0:T(8,128)(2,1)S(1)}, u32[]{:S(2)}, u32[]{:S(2)}) collective-permute-start(bf16[112,1536]{1,0:T(8,128)(2,1)S(1)} %get-tuple-element.32), channel_id=1, source_target_pairs={{0,1},{1,0},{2,3},{3,2},{4,5},{5,4},{6,7},{7,6},{8,9},{9,8},{10,11... | collective-permute-start | bytes 1032200 | tf_op jit(solution)/shard_map/ppermute | solution.py:220
  137.4 13.1 %collective-permute-start.15 = (bf16[64,3072]{1,0:T(8,128)(2,1)}, bf16[64,3072]{1,0:T(8,128)(2,1)S(1)}, u32[]{:S(2)}, u32[]{:S(2)}) collective-permute-start(bf16[64,3072]{1,0:T(8,128)(2,1)} %add_convert_fusion.5.refs_0_), channel_id=1, source_target_pairs={{0,2},{2,0},{1,3},{3,1},{4,6},{6,4},{5,7},{7,5},{8,10},{10,8},{9,1... | collective-permute-start | bytes 1179656 | tf_op jit(solution)/shard_map/ppermute | solution.py:226
  139.5 15.5 %collective-permute-start.13 = (bf16[80,3072]{1,0:T(8,128)(2,1)S(1)}, bf16[80,3072]{1,0:T(8,128)(2,1)}, u32[]{:S(2)}, u32[]{:S(2)}) collective-permute-start(bf16[80,3072]{1,0:T(8,128)(2,1)S(1)} %shard_map.90.refs_6_.refs_0_), channel_id=1, source_target_pairs={{0,1},{1,0},{2,3},{3,2},{4,5},{5,4},{6,7},{7,6},{8,9},{9,8},{10,11... | collective-permute-start | bytes 1474568 | tf_op jit(solution)/shard_map/ppermute | solution.py:220
  140.6 45.6 %reduce-scatter.5.cloned.1.call-start = ((), (), s32[]{:S(2)}) async-start(), calls=%async_computation.4 | async-start | bytes 614400 | tf_op jit(solution)/shard_map/reduce_scatter | solution.py:302
  142.7 18.5 %collective-permute-start.17 = (bf16[64,3072]{1,0:T(8,128)(2,1)}, bf16[64,3072]{1,0:T(8,128)(2,1)S(1)}, u32[]{:S(2)}, u32[]{:S(2)}) collective-permute-start(bf16[64,3072]{1,0:T(8,128)(2,1)} %add_convert_fusion.4.refs_0_), channel_id=1, source_target_pairs={{0,2},{2,0},{1,3},{3,1},{4,6},{6,4},{5,7},{7,5},{8,10},{10,8},{9,1... | collective-permute-start | bytes 1179656 | tf_op jit(solution)/shard_map/ppermute | solution.py:226
  160.6 3.7 %collective-permute-start.16 = (bf16[80,1536]{1,0:T(8,128)(2,1)S(1)}, bf16[80,1536]{1,0:T(8,128)(2,1)S(1)}, u32[]{:S(2)}, u32[]{:S(2)}) collective-permute-start(bf16[80,1536]{1,0:T(8,128)(2,1)S(1)} %get-tuple-element.36), channel_id=1, source_target_pairs={{0,1},{1,0},{2,3},{3,2},{4,5},{5,4},{6,7},{7,6},{8,9},{9,8},{10,11... | collective-permute-start | bytes 737288 | tf_op jit(solution)/shard_map/ppermute | solution.py:220
  160.9 5.7 %collective-permute-start.19 = (bf16[64,3072]{1,0:T(8,128)(2,1)S(1)}, bf16[64,3072]{1,0:T(8,128)(2,1)S(1)}, u32[]{:S(2)}, u32[]{:S(2)}) collective-permute-start(bf16[64,3072]{1,0:T(8,128)(2,1)S(1)} %shard_map.92.refs_5_.refs_0_), channel_id=1, source_target_pairs={{0,1},{1,0},{2,3},{3,2},{4,5},{5,4},{6,7},{7,6},{8,9},{9,8},{10,11... | collective-permute-start | bytes 1179656 | tf_op jit(solution)/shard_map/ppermute | solution.py:220
  164.0 9.3 %collective-permute-start.18 = (bf16[64,3072]{1,0:T(8,128)(2,1)S(1)}, bf16[64,3072]{1,0:T(8,128)(2,1)S(1)}, u32[]{:S(2)}, u32[]{:S(2)}) collective-permute-start(bf16[64,3072]{1,0:T(8,128)(2,1)S(1)} %shard_map.94.refs_6_.refs_0_), channel_id=1, source_target_pairs={{0,1},{1,0},{2,3},{3,2},{4,5},{5,4},{6,7},{7,6},{8,9},{9,8},{10,11... | collective-permute-start | bytes 1179656 | tf_op jit(solution)/shard_map/ppermute | solution.py:220
  179.4 7.8 %collective-permute-start.21 = (bf16[64,768]{1,0:T(8,128)(2,1)S(1)}, bf16[64,768]{1,0:T(8,128)(2,1)S(1)}, u32[]{:S(2)}, u32[]{:S(2)}) collective-permute-start(bf16[64,768]{1,0:T(8,128)(2,1)S(1)} %get-tuple-element.53), channel_id=1, source_target_pairs={{0,12},{4,8},{8,4},{12,0},{1,13},{5,9},{9,5},{13,1},{2,14},{6,10},... | collective-permute-start | bytes 294920 | tf_op jit(solution)/shard_map/ppermute | solution.py:243
  180.7 10.7 %collective-permute-start.22 = (bf16[64,768]{1,0:T(8,128)(2,1)S(1)}, bf16[64,768]{1,0:T(8,128)(2,1)S(1)}, u32[]{:S(2)}, u32[]{:S(2)}) collective-permute-start(bf16[64,768]{1,0:T(8,128)(2,1)S(1)} %get-tuple-element.55), channel_id=1, source_target_pairs={{0,8},{4,12},{8,0},{12,4},{1,9},{5,13},{9,1},{13,5},{2,10},{6,14},... | collective-permute-start | bytes 294920 | tf_op jit(solution)/shard_map/ppermute | solution.py:243
  181.4 10.1 %collective-permute-start.23 = (bf16[64,768]{1,0:T(8,128)(2,1)S(1)}, bf16[64,768]{1,0:T(8,128)(2,1)S(1)}, u32[]{:S(2)}, u32[]{:S(2)}) collective-permute-start(bf16[64,768]{1,0:T(8,128)(2,1)S(1)} %get-tuple-element.54), channel_id=1, source_target_pairs={{0,4},{4,0},{8,12},{12,8},{1,5},{5,1},{9,13},{13,9},{2,6},{6,2},{1... | collective-permute-start | bytes 294920 | tf_op jit(solution)/shard_map/ppermute | solution.py:243
  (17 other events, 104.1 us)
Sparse Core Ops, SparseCore 0:
  8.9 40.0 all-gather.2
  140.7 20.6 reduce-scatter.2
  165.3 20.8 reduce-scatter.4

commit v4 on v3

--- a/solution.py
+++ b/solution.py
@@ -16,6 +16,8 @@
 AHEAD = 4
 BF16, F32 = jnp.bfloat16, jnp.float32
 PARAMS = pltpu.CompilerParams(vmem_limit_bytes=48 * 2**20)
+SMALL = pltpu.CompilerParams(vmem_limit_bytes=8 * 2**20)
+LONG = pl.CostEstimate(flops=0, bytes_accessed=10**8, transcendentals=0)
 SOON = pl.CostEstimate(flops=0, bytes_accessed=0, transcendentals=0)
 
 
@@ -64,7 +66,7 @@
     return pl.BlockSpec(shape, lambda *_: (0, 0))
 
 
-def call(kernel, earlier, operands, specs, **options):
+def call(kernel, earlier, operands, specs, params=None, cost=None, **options):
     def body(*refs):
         n = len(operands)
         kernel(refs[:n], refs[n + len(earlier) :])
@@ -72,10 +74,31 @@
     return pl.pallas_call(
         body,
         in_specs=list(specs) + [corner_of(a) for a in earlier],
-        compiler_params=PARAMS,
-        cost_estimate=SOON,
+        compiler_params=params or PARAMS,
+        cost_estimate=cost or SOON,
         **options,
     )(*operands, *earlier)
+
+
+def token_sums(tokens):
+    rows = tokens.shape[0]
+
+    def kernel(ins, outs):
+        floats = ins[0][...].astype(F32)
+        outs[0][...] = jnp.sum(floats, axis=1, keepdims=True)
+        outs[1][...] = jnp.sum(floats * floats, axis=1, keepdims=True)
+
+    return call(
+        kernel,
+        (),
+        (tokens,),
+        [pl.BlockSpec(tokens.shape, lambda *_: (0, 0))],
+        params=SMALL,
+        cost=LONG,
+        grid=(1,),
+        out_specs=[pl.BlockSpec((rows, 1), lambda *_: (0, 0))] * 2,
+        out_shape=[jax.ShapeDtypeStruct((rows, 1), F32)] * 2,
+    )
 
 
 def gelu_sum(parts, earlier=()):
@@ -94,58 +117,10 @@
         earlier,
         parts,
         [spec] * len(parts),
+        params=SMALL,
         grid=(steps,),
         out_specs=spec,
         out_shape=jax.ShapeDtypeStruct((rows, units), BF16),
-    )
-
-
-def project_rows(own, other, weight, piece, earlier=()):
-    rows, depth = own.shape
-    columns = piece.stop - piece.start
-    block, steps, _ = steps_of(piece)
-    whole = pl.BlockSpec((rows, depth), lambda *_: (0, 0))
-    out = pl.BlockSpec((rows, columns), lambda *_: (0, 0))
-
-    def kernel(ins, refs):
-        near, far, both, landed, sems = refs
-
-        def bring(at):
-            start = pl.multiple_of(piece.start + at * block, block)
-            source = ins[2].at[:, pl.ds(start, block)]
-            return pltpu.make_async_copy(source, landed.at[at], sems.at[at])
-
-        for at in range(min(AHEAD, steps)):
-            bring(at).start()
-        both[:rows] = ins[0][...]
-        both[rows:] = ins[1][...]
-
-        @pl.loop(0, steps)
-        def _(at):
-            bring(at).wait()
-
-            @pl.when(at + AHEAD < steps)
-            def _():
-                bring(at + AHEAD).start()
-
-            part = jnp.dot(both[...], landed[at], preferred_element_type=F32).astype(BF16)
-            here = pl.ds(pl.multiple_of(at * block, block), block)
-            near[:, here] = part[:rows]
-            far[:, here] = part[rows:]
-
-    return call(
-        kernel,
-        earlier,
-        (own, other, weight),
-        [whole, whole, pl.BlockSpec(memory_space=pltpu.HBM)],
-        grid=(1,),
-        out_specs=[out] * 2,
-        out_shape=[jax.ShapeDtypeStruct((rows, columns), BF16)] * 2,
-        scratch_shapes=[
-            pltpu.VMEM((2 * rows, depth), BF16),
-            pltpu.VMEM((steps, depth, block), BF16),
-            pltpu.SemaphoreType.DMA((steps,)),
-        ],
     )
 
 
@@ -255,26 +230,26 @@
 
         raw = lax.all_gather(tokens, "wide", axis=1, tiled=True)
         gain = lax.all_gather(ln_gain, "wide", axis=0, tiled=True)
-        floats = tokens.astype(F32)
-        sums = jnp.stack([jnp.sum(floats, axis=1), jnp.sum(floats * floats, axis=1)])
-        sums = lax.psum(sums, ("wide", "red"))[:, :, None] / D
+        sums = lax.psum(jnp.stack(token_sums(tokens)), ("wide", "red")) / D
         normed = normalize(raw.astype(F32), sums[0], sums[1], gain).astype(BF16)
         own = lax.dynamic_slice_in_dim(normed, core * depth, depth, axis=1)
         other = lax.dynamic_slice_in_dim(normed, (1 - core) * depth, depth, axis=1)
         other = swap(other)
 
-        def project(weight, piece, earlier):
-            near, far = project_rows(own, other, weight, piece, earlier)
-            return near, swap(far)
-
-        def block_sum(parts, start=0.0):
-            return (parts[0].astype(F32) + parts[1].astype(F32) + start).astype(BF16)
-
-        halves, earlier = [], ()
-        for piece in pieces:
-            halves.append(project(w_up, piece, earlier))
-            earlier = [halves[-1][0]]
-        qkv = block_sum(project(qkv_rows, slice(0, qkv_rows.shape[1]), earlier))
+        def far_part(weight):
+            return swap(jnp.dot(other, weight, preferred_element_type=F32).astype(BF16))
+
+        def near_sum(cut, weight, far):
+            near = jnp.dot(own[cut], weight, preferred_element_type=F32)
+            return (near + far[cut].astype(F32)).astype(BF16)
+
+        rows = slice(0, tokens.shape[0])
+        rest = slice(cuts[0].stop, rows.stop)
+        weights = [w_up[:, piece] for piece in pieces]
+        fars = [far_part(weight) for weight in weights]
+        leads = [near_sum(cuts[0], weight, far) for weight, far in zip(weights, fars)]
+        rests = [near_sum(rest, weight, far) for weight, far in zip(weights, fars)]
+        qkv = near_sum(rows, qkv_rows, far_part(qkv_rows))
 
         order = [(c, p) for c in range(n) for p in range(len(pieces))]
         outs, scattered = [], []
@@ -304,8 +279,11 @@
 
         hidden = None
         for at, (c, p) in enumerate(order):
-            start = nothing(firsts[c - 1]) if c else 0.0
-            parts = all_red(block_sum([a[cuts[c]] for a in halves[p]], start))
+            if c:
+                part = slice(cuts[c].start - rest.start, cuts[c].stop - rest.start)
+                parts = all_red(rests[p][part] + nothing(firsts[c - 1]).astype(BF16))
+            else:
+                parts = all_red(leads[p])
             arrived = gelu_sum(parts, earlier)
             earlier = [arrived]
             if p == 0:

time: 200 us -> 197 us (0.985)
  matrix products: 0.74 us -> 34.8 us
  Pallas kernels: 59.7 us -> 39.9 us
  other arithmetic: 17.1 us -> 11.4 us
  waiting for transfers between devices: 41.6 us -> 36.9 us
  local copies, waits for them, and re-layouts: 11 us -> 6.33 us
  starting transfers between devices: 17.2 us -> 15.2 us
    dot_general x0 -> x8, matrix products: none -> 34.1 us  [the longest x5 21.6 us: near_sum(): near = jnp.dot(own[cut], weight, preferred_element_type=F32)]
    pallas_call x15 -> x13, Pallas kernels: 59.7 us -> 39.9 us  [call(): pl.pallas_call(body, in_specs=list(specs) + [corner_of(a) for a in earlie...]
    convert_element_type x7 -> x1, other arithmetic: 9.59 us -> 0.71 us  [near_sum(): return (near + far[cut].astype(F32)).astype(BF16)]
    ppermute x7, waiting for transfers between devices: 25.9 us -> 20.3 us  [all_red(): parts.append(lax.ppermute(x, 'red', pairs))]
    add x0 -> x4, other arithmetic: none -> 3.21 us  [body(): parts = all_red(rests[p][part] + nothing(firsts[c - 1]).astype(BF16))]
    reduce_scatter x2, waiting for transfers between devices: 2.41 us -> 5.28 us  [scatter(): lax.psum_scatter(full, 'wide', scatter_dimension=1, tiled=True)]
    unnamed x30 -> x42, local copies, waits for them, and re-layouts: 6.25 us -> 3.72 us
  transfers between devices with their start and end apart: 27 -> 27, of which waited for: 9 -> 11; matrix products, arithmetic and copies ran while one was open for 10% -> 19% of each run, Pallas kernels for 26% -> 20%
where the time goes in v4:
time: 197 us; the launch traced here: 196 us
  Pallas kernels  39.9 us (20%)
  waiting for transfers between devices  36.9 us (19%)
  blocking collectives  36.8 us (19%)
  matrix products  34.8 us (18%)
  starting transfers between devices  15.2 us (8%)
  between operations  15 us (8%)
  other arithmetic  11.4 us (6%)
  local copies, waits for them, and re-layouts  6.33 us (3%)
    pallas_call x13, Pallas kernels, call(): pl.pallas_call(body, in_specs=list(specs) + [corner_of(a) for a in earlie...  39.9 us
    psum x1, blocking collectives, body(): sums = lax.psum(jnp.stack(token_sums(tokens)), ('wide', 'red')) / D  21.9 us
    dot_general x5, matrix products, near_sum(): near = jnp.dot(own[cut], weight, preferred_element_type=F32)  21.6 us
    ppermute x7, waiting for transfers between devices, all_red(): parts.append(lax.ppermute(x, 'red', pairs))  20.3 us
    all_gather x1, blocking collectives, body(): gain = lax.all_gather(ln_gain, 'wide', axis=0, tiled=True)  14.9 us
    dot_general x3, matrix products, far_part(): return swap(jnp.dot(other, weight, preferred_element_type=F32).astype(BF16))  12.5 us
    ppermute x7, starting transfers between devices, all_red(): parts.append(lax.ppermute(x, 'red', pairs))  7.5 us
    ppermute x14, waiting for transfers between devices, swap(): return lax.ppermute(x, 'tok', [(0, 1), (1, 0)])  5.34 us
  transfers between devices with their start and end apart: 27, of which 11 were waited for; matrix products, arithmetic and copies ran while one was open for 19% of the time, Pallas kernels for 20%

profile of v4, /device:TPU:0, one launch (start us, length us, event | category | flops | bytes accessed | tf_op | source)
XLA Modules:
  0.0 196.4 jit_solution(11994211386275144071)
XLA Ops:
  9.2 14.9 %all-gather = bf16[4,1,768]{2,1,0:T(2,128)(2,1)S(1)} all-gather(bf16[1,1,768]{2,1,0:T(2,128)(2,1)S(1)} %reshape.110), channel_id=1, replica_groups=mesh['grp'=2,'wide'=4,'red'=2,'tok'=2] {'wide'}, dimensions={0}, use_global_device_ids=true | all-gather | bytes 7680 | tf_op jit(solution)/shard_map/all_gather | solution.py:232
  24.3 21.9 %psum.7 = f32[2,256,1]{1,2,0:T(1,128)S(1)} all-reduce(f32[2,256,1]{1,2,0:T(1,128)S(1)} %pad_maximum_fusion.3), channel_id=1, replica_groups=mesh['grp'=2,'wide'=4,'red'=2,'tok'=2] {'wide','red'}, use_global_device_ids=true, to_apply=%region_0.0 | all-reduce | flops 512 | bytes 4096 | tf_op jit(solution)/shard_map/psum | solution.py:233
  46.3 2.8 %all-gather.3.cloned.1.call-done = bf16[256,3072]{1,0:T(8,128)(2,1)} async-done(((bf16[256,768]{1,0:T(8,128)(2,1)}), bf16[256,3072]{1,0:T(8,128)(2,1)}) %all-gather.3.cloned.1.call-update) | async-done | bytes 1572880 | tf_op jit(solution)/shard_map/all_gather | solution.py:231
  51.3 2.3 %collective-permute-done = bf16[256,1536]{1,0:T(8,128)(2,1)S(1)} collective-permute-done((bf16[256,1536]{1,0:T(8,128)(2,1)S(1)}, bf16[256,1536]{1,0:T(8,128)(2,1)S(1)}, u32[]{:S(2)}, u32[]{:S(2)}) %collective-permute-start) | collective-permute-done | bytes 786464 | tf_op jit(solution)/shard_map/ppermute | solution.py:195
  53.6 8.3 %fusion.12 = bf16[256,3072]{1,0:T(8,128)(2,1)} fusion(bf16[256,1536]{1,0:T(8,128)(2,1)S(1)} %collective-permute-done, bf16[1536,6144]{1,0:T(8,128)(2,1)} %param.13), kind=kOutput, calls=%fused_computation.12 | convolution fusion | flops 2416705536 | bytes 11796480 | tf_op jit(solution)/shard_map/dot_general | solution.py:240
  62.0 3.7 %fusion.15 = bf16[256,3072]{1,0:T(8,128)(2,1)} fusion(bf16[256,1536]{1,0:T(8,128)(2,1)S(1)} %collective-permute-done, bf16[1536,6144]{1,0:T(8,128)(2,1)S(1)} %copy-done.14), kind=kOutput, calls=%fused_computation.13 | convolution fusion | flops 2416705536 | bytes 11796480 | tf_op jit(solution)/shard_map/dot_general | solution.py:240
  71.7 5.5 %add_convert_fusion.3.refs_0_ = bf16[112,3072]{1,0:T(8,128)(2,1)S(1)} fusion(bf16[256,3072]{1,0:T(8,128)(2,1)} %collective-permute-done.1, bf16[1536,6144]{1,0:T(8,128)(2,1)} %param.13, bf16[256,3072]{1,0:T(8,128)(2,1)S(1)} %multiply_convert_fusion, s32[]{:T(128)S(6)} %select_n.75), kind=kOutput, calls=%fused_computation.18 | convolution fusion | flops 1057996800 | bytes 11157508 | tf_op jit(solution)/shard_map/dot_general | solution.py:243
  77.7 5.6 %add_convert_fusion.2.refs_0_ = bf16[112,3072]{1,0:T(8,128)(2,1)S(1)} fusion(bf16[256,3072]{1,0:T(8,128)(2,1)} %collective-permute-done.5, bf16[1536,6144]{1,0:T(8,128)(2,1)} %param.13, bf16[256,3072]{1,0:T(8,128)(2,1)} %copy-done.8, s32[]{:T(128)S(6)} %select_n.75), kind=kOutput, calls=%fused_computation.17 | convolution fusion | flops 1057996800 | bytes 11157508 | tf_op jit(solution)/shard_map/dot_general | solution.py:243
  83.3 2.1 %collective-permute-start.6 = (bf16[112,3072]{1,0:T(8,128)(2,1)S(1)}, bf16[112,3072]{1,0:T(8,128)(2,1)S(1)}, u32[]{:S(2)}, u32[]{:S(2)}) collective-permute-start(bf16[112,3072]{1,0:T(8,128)(2,1)S(1)} %add_convert_fusion.2.refs_0_), channel_id=1, source_target_pairs={{0,2},{2,0},{1,3},{3,1},{4,6},{6,4},{5,7},{7,5},{8,10},{10,8},{9,1... | collective-permute-start | bytes 2064392 | tf_op jit(solution)/shard_map/ppermute | solution.py:201
  85.5 6.3 %add_convert_fusion = bf16[144,3072]{1,0:T(8,128)(2,1)} fusion(bf16[256,3072]{1,0:T(8,128)(2,1)} %collective-permute-done.1, bf16[1536,6144]{1,0:T(8,128)(2,1)} %param.13, bf16[256,3072]{1,0:T(8,128)(2,1)S(1)} %copy-done.9, s32[]{:T(128)S(6)} %add.178, s32[]{:T(128)S(6)} %select_n.75), kind=kOutput, calls=%fused_computation.15 | convolution fusion | flops 1360281600 | bytes 11649032 | tf_op jit(solution)/shard_map/dot_general | solution.py:243
  91.8 3.6 %add_convert_fusion.1 = bf16[144,3072]{1,0:T(8,128)(2,1)} fusion(bf16[256,3072]{1,0:T(8,128)(2,1)} %collective-permute-done.5, bf16[1536,6144]{1,0:T(8,128)(2,1)S(1)} %bitcast.42, bf16[256,3072]{1,0:T(8,128)(2,1)S(1)} %copy-done.9, s32[]{:T(128)S(6)} %add.178, s32[]{:T(128)S(6)} %select_n.75), kind=kOutput, calls=%fused_computation.16 | convolution fusion | flops 1360281600 | bytes 11649032 | tf_op jit(solution)/shard_map/dot_general | solution.py:243
  95.4 14.0 %collective-permute-done.6.refs_1_ = bf16[112,3072]{1,0:T(8,128)(2,1)S(1)} collective-permute-done((bf16[112,3072]{1,0:T(8,128)(2,1)S(1)}, bf16[112,3072]{1,0:T(8,128)(2,1)S(1)}, u32[]{:S(2)}, u32[]{:S(2)}) %collective-permute-start.6) | collective-permute-done | bytes 688160 | tf_op jit(solution)/shard_map/ppermute | solution.py:201
  115.5 3.3 %shard_map.84.refs_6_.refs_0_ = bf16[112,3072]{1,0:T(8,128)(2,1)S(1)} custom-call(bf16[112,3072]{1,0:T(8,128)(2,1)S(1)} %add_convert_fusion.3.refs_0_, bf16[112,3072]{1,0:T(8,128)(2,1)} %collective-permute-done.2.refs_1_, bf16[256,128]{1,0:T(8,128)(2,1)S(1)} %fusion.25.refs_2_), custom_call_target="tpu_custom_call" | custom-call | tf_op jit(solution)/shard_map/pallas_call | solution.py:74
  120.6 4.9 %shard_map.85 = (f32[112,1536]{1,0:T(8,128)S(1)}, f32[112,1536]{1,0:T(8,128)S(1)}) custom-call(bf16[112,3072]{1,0:T(8,128)(2,1)S(1)} %shard_map.83.refs_0_, bf16[112,3072]{1,0:T(8,128)(2,1)S(1)} %collective-permute-done.8.refs_1_, bf16[6144,1536]{1,0:T(8,128)(2,1)} %refs_2_.11, bf16[112,128]{1,0:T(8,128)(2,1)S(1)} %slice_bitcast_fusion.refs_3_, ...), custom_call_target="tpu_custom_call" | custom-call | tf_op jit(solution)/shard_map/pallas_call | solution.py:74
  125.6 3.6 %collective-permute-done.10.refs_1_ = bf16[80,3072]{1,0:T(8,128)(2,1)S(1)} collective-permute-done((bf16[80,3072]{1,0:T(8,128)(2,1)S(1)}, bf16[80,3072]{1,0:T(8,128)(2,1)S(1)}, u32[]{:S(2)}, u32[]{:S(2)}) %collective-permute-start.10) | collective-permute-done | bytes 491552 | tf_op jit(solution)/shard_map/ppermute | solution.py:201
  130.9 4.7 %shard_map.87 = (bf16[112,1536]{1,0:T(8,128)(2,1)S(1)}, bf16[112,1536]{1,0:T(8,128)(2,1)S(1)}) custom-call(bf16[112,3072]{1,0:T(8,128)(2,1)S(1)} %shard_map.84.refs_6_.refs_0_, bf16[112,3072]{1,0:T(8,128)(2,1)S(1)} %collective-permute-done.7.refs_1_, bf16[6144,1536]{1,0:T(8,128)(2,1)} %refs_2_.11, f32[112,1536]{1,0:T(8,128)S(1)} %get-tuple-element.21.refs_2_.refs_3_, ...), custom_call_target="tpu_custom_call" | custom-call | tf_op jit(solution)/shard_map/pallas_call | solution.py:74
  142.9 4.8 %shard_map.89 = (f32[80,1536]{1,0:T(8,128)S(1)}, f32[80,1536]{1,0:T(8,128)S(1)}) custom-call(bf16[80,3072]{1,0:T(8,128)(2,1)S(1)} %shard_map.86.refs_5_.refs_0_, bf16[80,3072]{1,0:T(8,128)(2,1)S(1)} %collective-permute-done.14.refs_1_, bf16[6144,1536]{1,0:T(8,128)(2,1)} %refs_2_.11, bf16[80,128]{1,0:T(8,128)(2,1)S(1)} %slice_bitcast_fusion.1.refs_3_, ...), custom_call_target="tpu_custom_call" | custom-call | tf_op jit(solution)/shard_map/pallas_call | solution.py:74
  149.4 2.8 %shard_map.90.refs_5_.refs_0_ = bf16[64,3072]{1,0:T(8,128)(2,1)S(1)} custom-call(bf16[64,3072]{1,0:T(8,128)(2,1)S(1)} %slice_add_fusion.3.refs_0_, bf16[64,3072]{1,0:T(8,128)(2,1)} %collective-permute-done.15.refs_1_, f32[80,1536]{1,0:T(8,128)S(1)} %get-tuple-element.25.refs_2_.refs_3_), custom_call_target="tpu_custom_call" | custom-call | tf_op jit(solution)/shard_map/pallas_call | solution.py:74
  152.2 5.6 %shard_map.91 = (bf16[80,1536]{1,0:T(8,128)(2,1)S(1)}, bf16[80,1536]{1,0:T(8,128)(2,1)S(1)}) custom-call(bf16[80,3072]{1,0:T(8,128)(2,1)S(1)} %shard_map.88.refs_6_.refs_0_, bf16[80,3072]{1,0:T(8,128)(2,1)} %collective-permute-done.13.refs_1_, bf16[6144,1536]{1,0:T(8,128)(2,1)} %refs_2_.11, f32[80,1536]{1,0:T(8,128)S(1)} %get-tuple-element.25.refs_2_.refs_3_, ...), custom_call_target="tpu_custom_call" | custom-call | tf_op jit(solution)/shard_map/pallas_call | solution.py:74
  158.3 2.8 %shard_map.92.refs_6_.refs_0_ = bf16[64,3072]{1,0:T(8,128)(2,1)S(1)} custom-call(bf16[64,3072]{1,0:T(8,128)(2,1)S(1)} %slice_add_fusion.2.refs_0_, bf16[64,3072]{1,0:T(8,128)(2,1)} %collective-permute-done.17.refs_1_, bf16[80,1536]{1,0:T(8,128)(2,1)S(1)} %get-tuple-element.27.refs_2_), custom_call_target="tpu_custom_call" | custom-call | tf_op jit(solution)/shard_map/pallas_call | solution.py:74
  165.0 4.6 %shard_map.93 = (f32[64,1536]{1,0:T(8,128)S(1)}, f32[64,1536]{1,0:T(8,128)S(1)}) custom-call(bf16[64,3072]{1,0:T(8,128)(2,1)S(1)} %shard_map.90.refs_5_.refs_0_, bf16[64,3072]{1,0:T(8,128)(2,1)S(1)} %collective-permute-done.19.refs_1_, bf16[6144,1536]{1,0:T(8,128)(2,1)} %refs_2_.11, bf16[64,128]{1,0:T(8,128)(2,1)S(1)} %slice_bitcast_fusion.2.refs_3_, ...), custom_call_target="tpu_custom_call" | custom-call | tf_op jit(solution)/shard_map/pallas_call | solution.py:74
  169.7 4.5 %shard_map.94 = (bf16[64,1536]{1,0:T(8,128)(2,1)S(1)}, bf16[64,1536]{1,0:T(8,128)(2,1)S(1)}) custom-call(bf16[64,3072]{1,0:T(8,128)(2,1)S(1)} %shard_map.92.refs_6_.refs_0_, bf16[64,3072]{1,0:T(8,128)(2,1)S(1)} %collective-permute-done.18.refs_1_, bf16[6144,1536]{1,0:T(8,128)(2,1)} %refs_2_.11, f32[64,1536]{1,0:T(8,128)S(1)} %get-tuple-element.29.refs_3_.refs_5_, ...), custom_call_target="tpu_custom_call" | custom-call | tf_op jit(solution)/shard_map/pallas_call | solution.py:74
  177.6 2.6 %collective-permute-start.22 = (bf16[64,768]{1,0:T(8,128)(2,1)S(1)}, bf16[64,768]{1,0:T(8,128)(2,1)S(1)}, u32[]{:S(2)}, u32[]{:S(2)}) collective-permute-start(bf16[64,768]{1,0:T(8,128)(2,1)S(1)} %get-tuple-element.43), channel_id=1, source_target_pairs={{0,8},{4,12},{8,0},{12,4},{1,9},{5,13},{9,1},{13,5},{2,10},{6,14},... | collective-permute-start | bytes 294920 | tf_op jit(solution)/shard_map/ppermute | solution.py:218
  180.2 5.3 %reduce-scatter.5.cloned.1.call-done = bf16[80,768]{1,0:T(8,128)(2,1)} async-done(((bf16[80,3072]{1,0:T(8,128)(2,1)}), bf16[80,768]{1,0:T(8,128)(2,1)}) %reduce-scatter.5.cloned.1.call-update) | async-done | bytes 122896 | tf_op jit(solution)/shard_map/reduce_scatter | solution.py:277
  (137 shorter events, 41.0 us)
Async XLA Ops:
  6.5 42.5 %all-gather.3.cloned.1.call-start = ((), (), s32[]{:S(2)}) async-start(), calls=%async_computation.2 | async-start | bytes 1966080 | tf_op jit(solution)/shard_map/all_gather | solution.py:231
  7.3 155.8 %reduce-scatter.3.cloned.1.call-start = ((), (), s32[]{:S(2)}) async-start(), calls=%async_computation.3 | async-start | bytes 860160 | tf_op jit(solution)/shard_map/reduce_scatter | solution.py:277
  61.8 9.8 %collective-permute-start.1 = (bf16[256,3072]{1,0:T(8,128)(2,1)}, bf16[256,3072]{1,0:T(8,128)(2,1)}, u32[]{:S(2)}, u32[]{:S(2)}) collective-permute-start(bf16[256,3072]{1,0:T(8,128)(2,1)} %fusion.12), channel_id=1, source_target_pairs={{0,1},{1,0},{2,3},{3,2},{4,5},{5,4},{6,7},{7,6},{8,9},{9,8},{10,11... | collective-permute-start | bytes 4718600 | tf_op jit(solution)/shard_map/ppermute | solution.py:195
  65.7 12.0 %collective-permute-start.5 = (bf16[256,3072]{1,0:T(8,128)(2,1)}, bf16[256,3072]{1,0:T(8,128)(2,1)}, u32[]{:S(2)}, u32[]{:S(2)}) collective-permute-start(bf16[256,3072]{1,0:T(8,128)(2,1)} %fusion.15), channel_id=1, source_target_pairs={{0,1},{1,0},{2,3},{3,2},{4,5},{5,4},{6,7},{7,6},{8,9},{9,8},{10,11... | collective-permute-start | bytes 4718600 | tf_op jit(solution)/shard_map/ppermute | solution.py:195
  70.1 41.1 %collective-permute-start.4 = (bf16[256,384]{1,0:T(8,128)(2,1)}, bf16[256,384]{1,0:T(8,128)(2,1)}, u32[]{:S(2)}, u32[]{:S(2)}) collective-permute-start(bf16[256,384]{1,0:T(8,128)(2,1)} %add_convert_fusion.4), channel_id=1, source_target_pairs={{0,2},{2,0},{1,3},{3,1},{4,6},{6,4},{5,7},{7,5},{8,10},{10,8},{9,1... | collective-permute-start | bytes 589832 | tf_op jit(solution)/shard_map/ppermute | solution.py:201
  77.2 38.3 %collective-permute-start.2 = (bf16[112,3072]{1,0:T(8,128)(2,1)S(1)}, bf16[112,3072]{1,0:T(8,128)(2,1)}, u32[]{:S(2)}, u32[]{:S(2)}) collective-permute-start(bf16[112,3072]{1,0:T(8,128)(2,1)S(1)} %add_convert_fusion.3.refs_0_), channel_id=1, source_target_pairs={{0,2},{2,0},{1,3},{3,1},{4,6},{6,4},{5,7},{7,5},{8,10},{10,8},{9,1... | collective-permute-start | bytes 2064392 | tf_op jit(solution)/shard_map/ppermute | solution.py:201
  83.3 26.1 %collective-permute-start.6 = (bf16[112,3072]{1,0:T(8,128)(2,1)S(1)}, bf16[112,3072]{1,0:T(8,128)(2,1)S(1)}, u32[]{:S(2)}, u32[]{:S(2)}) collective-permute-start(bf16[112,3072]{1,0:T(8,128)(2,1)S(1)} %add_convert_fusion.2.refs_0_), channel_id=1, source_target_pairs={{0,2},{2,0},{1,3},{3,1},{4,6},{6,4},{5,7},{7,5},{8,10},{10,8},{9,1... | collective-permute-start | bytes 2064392 | tf_op jit(solution)/shard_map/ppermute | solution.py:201
  110.6 10.0 %collective-permute-start.8 = (bf16[112,3072]{1,0:T(8,128)(2,1)S(1)}, bf16[112,3072]{1,0:T(8,128)(2,1)S(1)}, u32[]{:S(2)}, u32[]{:S(2)}) collective-permute-start(bf16[112,3072]{1,0:T(8,128)(2,1)S(1)} %shard_map.83.refs_0_), channel_id=1, source_target_pairs={{0,1},{1,0},{2,3},{3,2},{4,5},{5,4},{6,7},{7,6},{8,9},{9,8},{10,11... | collective-permute-start | bytes 2064392 | tf_op jit(solution)/shard_map/ppermute | solution.py:195
  113.4 7.3 %collective-permute-start.9 = (bf16[256,128]{1,0:T(8,128)(2,1)S(1)}, bf16[256,128]{1,0:T(8,128)(2,1)S(1)}, u32[]{:S(2)}, u32[]{:S(2)}) collective-permute-start(bf16[256,128]{1,0:T(8,128)(2,1)S(1)} %fusion.25.refs_2_), channel_id=1, source_target_pairs={{0,1},{1,0},{2,3},{3,2},{4,5},{5,4},{6,7},{7,6},{8,9},{9,8},{10,11... | collective-permute-start | bytes 196616 | tf_op jit(solution)/shard_map/ppermute | solution.py:195
  115.0 14.1 %collective-permute-start.10 = (bf16[80,3072]{1,0:T(8,128)(2,1)S(1)}, bf16[80,3072]{1,0:T(8,128)(2,1)S(1)}, u32[]{:S(2)}, u32[]{:S(2)}) collective-permute-start(bf16[80,3072]{1,0:T(8,128)(2,1)S(1)} %slice_add_fusion.1.refs_0_), channel_id=1, source_target_pairs={{0,2},{2,0},{1,3},{3,1},{4,6},{6,4},{5,7},{7,5},{8,10},{10,8},{9,1... | collective-permute-start | bytes 1474568 | tf_op jit(solution)/shard_map/ppermute | solution.py:201
  118.8 12.0 %collective-permute-start.7 = (bf16[112,3072]{1,0:T(8,128)(2,1)S(1)}, bf16[112,3072]{1,0:T(8,128)(2,1)S(1)}, u32[]{:S(2)}, u32[]{:S(2)}) collective-permute-start(bf16[112,3072]{1,0:T(8,128)(2,1)S(1)} %shard_map.84.refs_6_.refs_0_), channel_id=1, source_target_pairs={{0,1},{1,0},{2,3},{3,2},{4,5},{5,4},{6,7},{7,6},{8,9},{9,8},{10,11... | collective-permute-start | bytes 2064392 | tf_op jit(solution)/shard_map/ppermute | solution.py:195
  119.0 19.8 %collective-permute-start.12 = (bf16[80,3072]{1,0:T(8,128)(2,1)S(1)}, bf16[80,3072]{1,0:T(8,128)(2,1)S(1)}, u32[]{:S(2)}, u32[]{:S(2)}) collective-permute-start(bf16[80,3072]{1,0:T(8,128)(2,1)S(1)} %slice_add_fusion.refs_0_), channel_id=1, source_target_pairs={{0,2},{2,0},{1,3},{3,1},{4,6},{6,4},{5,7},{7,5},{8,10},{10,8},{9,1... | collective-permute-start | bytes 1474568 | tf_op jit(solution)/shard_map/ppermute | solution.py:201
  130.2 12.7 %collective-permute-start.14 = (bf16[80,3072]{1,0:T(8,128)(2,1)S(1)}, bf16[80,3072]{1,0:T(8,128)(2,1)S(1)}, u32[]{:S(2)}, u32[]{:S(2)}) collective-permute-start(bf16[80,3072]{1,0:T(8,128)(2,1)S(1)} %shard_map.86.refs_5_.refs_0_), channel_id=1, source_target_pairs={{0,1},{1,0},{2,3},{3,2},{4,5},{5,4},{6,7},{7,6},{8,9},{9,8},{10,11... | collective-permute-start | bytes 1474568 | tf_op jit(solution)/shard_map/ppermute | solution.py:195
  135.6 3.8 %collective-permute-start.11 = (bf16[112,1536]{1,0:T(8,128)(2,1)S(1)}, bf16[112,1536]{1,0:T(8,128)(2,1)S(1)}, u32[]{:S(2)}, u32[]{:S(2)}) collective-permute-start(bf16[112,1536]{1,0:T(8,128)(2,1)S(1)} %get-tuple-element.24), channel_id=1, source_target_pairs={{0,1},{1,0},{2,3},{3,2},{4,5},{5,4},{6,7},{7,6},{8,9},{9,8},{10,11... | collective-permute-start | bytes 1032200 | tf_op jit(solution)/shard_map/ppermute | solution.py:195
  137.2 12.1 %collective-permute-start.15 = (bf16[64,3072]{1,0:T(8,128)(2,1)S(1)}, bf16[64,3072]{1,0:T(8,128)(2,1)}, u32[]{:S(2)}, u32[]{:S(2)}) collective-permute-start(bf16[64,3072]{1,0:T(8,128)(2,1)S(1)} %slice_add_fusion.3.refs_0_), channel_id=1, source_target_pairs={{0,2},{2,0},{1,3},{3,1},{4,6},{6,4},{5,7},{7,5},{8,10},{10,8},{9,1... | collective-permute-start | bytes 1179656 | tf_op jit(solution)/shard_map/ppermute | solution.py:201
  139.3 12.9 %collective-permute-start.13 = (bf16[80,3072]{1,0:T(8,128)(2,1)S(1)}, bf16[80,3072]{1,0:T(8,128)(2,1)}, u32[]{:S(2)}, u32[]{:S(2)}) collective-permute-start(bf16[80,3072]{1,0:T(8,128)(2,1)S(1)} %shard_map.88.refs_6_.refs_0_), channel_id=1, source_target_pairs={{0,1},{1,0},{2,3},{3,2},{4,5},{5,4},{6,7},{7,6},{8,9},{9,8},{10,11... | collective-permute-start | bytes 1474568 | tf_op jit(solution)/shard_map/ppermute | solution.py:195
  140.4 45.1 %reduce-scatter.5.cloned.1.call-start = ((), (), s32[]{:S(2)}) async-start(), calls=%async_computation.4 | async-start | bytes 614400 | tf_op jit(solution)/shard_map/reduce_scatter | solution.py:277
  141.5 16.8 %collective-permute-start.17 = (bf16[64,3072]{1,0:T(8,128)(2,1)S(1)}, bf16[64,3072]{1,0:T(8,128)(2,1)}, u32[]{:S(2)}, u32[]{:S(2)}) collective-permute-start(bf16[64,3072]{1,0:T(8,128)(2,1)S(1)} %slice_add_fusion.2.refs_0_), channel_id=1, source_target_pairs={{0,2},{2,0},{1,3},{3,1},{4,6},{6,4},{5,7},{7,5},{8,10},{10,8},{9,1... | collective-permute-start | bytes 1179656 | tf_op jit(solution)/shard_map/ppermute | solution.py:201
  157.8 3.7 %collective-permute-start.16 = (bf16[80,1536]{1,0:T(8,128)(2,1)S(1)}, bf16[80,1536]{1,0:T(8,128)(2,1)S(1)}, u32[]{:S(2)}, u32[]{:S(2)}) collective-permute-start(bf16[80,1536]{1,0:T(8,128)(2,1)S(1)} %get-tuple-element.28), channel_id=1, source_target_pairs={{0,1},{1,0},{2,3},{3,2},{4,5},{5,4},{6,7},{7,6},{8,9},{9,8},{10,11... | collective-permute-start | bytes 737288 | tf_op jit(solution)/shard_map/ppermute | solution.py:195
  158.0 5.1 %collective-permute-start.19 = (bf16[64,3072]{1,0:T(8,128)(2,1)S(1)}, bf16[64,3072]{1,0:T(8,128)(2,1)S(1)}, u32[]{:S(2)}, u32[]{:S(2)}) collective-permute-start(bf16[64,3072]{1,0:T(8,128)(2,1)S(1)} %shard_map.90.refs_5_.refs_0_), channel_id=1, source_target_pairs={{0,1},{1,0},{2,3},{3,2},{4,5},{5,4},{6,7},{7,6},{8,9},{9,8},{10,11... | collective-permute-start | bytes 1179656 | tf_op jit(solution)/shard_map/ppermute | solution.py:195
  161.2 8.5 %collective-permute-start.18 = (bf16[64,3072]{1,0:T(8,128)(2,1)S(1)}, bf16[64,3072]{1,0:T(8,128)(2,1)S(1)}, u32[]{:S(2)}, u32[]{:S(2)}) collective-permute-start(bf16[64,3072]{1,0:T(8,128)(2,1)S(1)} %shard_map.92.refs_6_.refs_0_), channel_id=1, source_target_pairs={{0,1},{1,0},{2,3},{3,2},{4,5},{5,4},{6,7},{7,6},{8,9},{9,8},{10,11... | collective-permute-start | bytes 1179656 | tf_op jit(solution)/shard_map/ppermute | solution.py:195
  175.7 10.7 %collective-permute-start.21 = (bf16[64,768]{1,0:T(8,128)(2,1)S(1)}, bf16[64,768]{1,0:T(8,128)(2,1)S(1)}, u32[]{:S(2)}, u32[]{:S(2)}) collective-permute-start(bf16[64,768]{1,0:T(8,128)(2,1)S(1)} %get-tuple-element.41), channel_id=1, source_target_pairs={{0,12},{4,8},{8,4},{12,0},{1,13},{5,9},{9,5},{13,1},{2,14},{6,10},... | collective-permute-start | bytes 294920 | tf_op jit(solution)/shard_map/ppermute | solution.py:218
  177.1 9.9 %collective-permute-start.23 = (bf16[64,768]{1,0:T(8,128)(2,1)S(1)}, bf16[64,768]{1,0:T(8,128)(2,1)S(1)}, u32[]{:S(2)}, u32[]{:S(2)}) collective-permute-start(bf16[64,768]{1,0:T(8,128)(2,1)S(1)} %get-tuple-element.42), channel_id=1, source_target_pairs={{0,4},{4,0},{8,12},{12,8},{1,5},{5,1},{9,13},{13,9},{2,6},{6,2},{1... | collective-permute-start | bytes 294920 | tf_op jit(solution)/shard_map/ppermute | solution.py:218
  177.6 11.3 %collective-permute-start.22 = (bf16[64,768]{1,0:T(8,128)(2,1)S(1)}, bf16[64,768]{1,0:T(8,128)(2,1)S(1)}, u32[]{:S(2)}, u32[]{:S(2)}) collective-permute-start(bf16[64,768]{1,0:T(8,128)(2,1)S(1)} %get-tuple-element.43), channel_id=1, source_target_pairs={{0,8},{4,12},{8,0},{12,4},{1,9},{5,13},{9,1},{13,5},{2,10},{6,14},... | collective-permute-start | bytes 294920 | tf_op jit(solution)/shard_map/ppermute | solution.py:218
  (23 other events, 259.1 us)
Sparse Core Ops, SparseCore 0:
  8.9 40.0 all-gather.2
  140.5 20.6 reduce-scatter.2
  163.6 21.8 reduce-scatter.4

commit v5 on v4

--- a/solution.py
+++ b/solution.py
@@ -11,13 +11,13 @@
 D = 6144
 PATCHES = 256
 EPS = 1e-06
-SHARES = (7, 5, 4)
+SHARES = (8, 4, 4)
 PIECES = (1, 1)
 AHEAD = 4
+GAIN_ROWS = 8
 BF16, F32 = jnp.bfloat16, jnp.float32
 PARAMS = pltpu.CompilerParams(vmem_limit_bytes=48 * 2**20)
 SMALL = pltpu.CompilerParams(vmem_limit_bytes=8 * 2**20)
-LONG = pl.CostEstimate(flops=0, bytes_accessed=10**8, transcendentals=0)
 SOON = pl.CostEstimate(flops=0, bytes_accessed=0, transcendentals=0)
 
 
@@ -66,7 +66,7 @@
     return pl.BlockSpec(shape, lambda *_: (0, 0))
 
 
-def call(kernel, earlier, operands, specs, params=None, cost=None, **options):
+def call(kernel, earlier, operands, specs, params=None, **options):
     def body(*refs):
         n = len(operands)
         kernel(refs[:n], refs[n + len(earlier) :])
@@ -75,30 +75,9 @@
         body,
         in_specs=list(specs) + [corner_of(a) for a in earlier],
         compiler_params=params or PARAMS,
-        cost_estimate=cost or SOON,
+        cost_estimate=SOON,
         **options,
     )(*operands, *earlier)
-
-
-def token_sums(tokens):
-    rows = tokens.shape[0]
-
-    def kernel(ins, outs):
-        floats = ins[0][...].astype(F32)
-        outs[0][...] = jnp.sum(floats, axis=1, keepdims=True)
-        outs[1][...] = jnp.sum(floats * floats, axis=1, keepdims=True)
-
-    return call(
-        kernel,
-        (),
-        (tokens,),
-        [pl.BlockSpec(tokens.shape, lambda *_: (0, 0))],
-        params=SMALL,
-        cost=LONG,
-        grid=(1,),
-        out_specs=[pl.BlockSpec((rows, 1), lambda *_: (0, 0))] * 2,
-        out_shape=[jax.ShapeDtypeStruct((rows, 1), F32)] * 2,
-    )
 
 
 def gelu_sum(parts, earlier=()):
@@ -228,44 +207,56 @@
         pieces = slices(units, PIECES)
         n = len(cuts)
 
-        raw = lax.all_gather(tokens, "wide", axis=1, tiled=True)
-        gain = lax.all_gather(ln_gain, "wide", axis=0, tiled=True)
-        sums = lax.psum(jnp.stack(token_sums(tokens)), ("wide", "red")) / D
-        normed = normalize(raw.astype(F32), sums[0], sums[1], gain).astype(BF16)
-        own = lax.dynamic_slice_in_dim(normed, core * depth, depth, axis=1)
-        other = lax.dynamic_slice_in_dim(normed, (1 - core) * depth, depth, axis=1)
-        other = swap(other)
-
-        def far_part(weight):
-            return swap(jnp.dot(other, weight, preferred_element_type=F32).astype(BF16))
-
-        def near_sum(cut, weight, far):
-            near = jnp.dot(own[cut], weight, preferred_element_type=F32)
-            return (near + far[cut].astype(F32)).astype(BF16)
-
-        rows = slice(0, tokens.shape[0])
-        rest = slice(cuts[0].stop, rows.stop)
+        first = cuts[0].stop
+        gain_rows = jnp.broadcast_to(ln_gain[None], (GAIN_ROWS, width))
+        lead = jnp.concatenate([gain_rows, tokens[:first]], axis=0)
+        lead = lax.all_gather(lead, "wide", axis=1, tiled=True)
+        gain = lead[:1]
+
+        def normed(floats):
+            sums = jnp.stack([jnp.sum(floats, axis=1), jnp.sum(floats * floats, axis=1)])
+            sums = sum_red(sums)[:, :, None] / D
+            values = normalize(floats, sums[0], sums[1], gain).astype(BF16)
+            mine = lax.dynamic_slice_in_dim(values, core * depth, depth, axis=1)
+            theirs = lax.dynamic_slice_in_dim(values, (1 - core) * depth, depth, axis=1)
+            return mine, swap(theirs)
+
+        def project(pair, weight):
+            both = jnp.concatenate(pair, axis=0)
+            half = both.shape[0] // 2
+            part = jnp.dot(both, weight, preferred_element_type=F32)
+            far = swap(part[half:].astype(BF16)).astype(F32)
+            return (part[:half] + far).astype(BF16)
+
         weights = [w_up[:, piece] for piece in pieces]
-        fars = [far_part(weight) for weight in weights]
-        leads = [near_sum(cuts[0], weight, far) for weight, far in zip(weights, fars)]
-        rests = [near_sum(rest, weight, far) for weight, far in zip(weights, fars)]
-        qkv = near_sum(rows, qkv_rows, far_part(qkv_rows))
+        lead_pair = normed(lead[GAIN_ROWS:].astype(F32))
+        leads = [project(lead_pair, weight) for weight in weights]
+        lead_parts = [all_red(x) for x in leads]
+        arrived = gelu_sum(lead_parts[0])
+
+        rest = tokens[first:] + nothing(leads[-1]).astype(BF16)
+        rest = lax.all_gather(rest, "wide", axis=1, tiled=True)
+        rest_pair = normed(rest.astype(F32) + nothing(arrived))
+        qkv = project([jnp.concatenate(p, axis=0) for p in zip(lead_pair, rest_pair)], qkv_rows)
+        rests = [project(rest_pair, weight) for weight in weights]
 
         order = [(c, p) for c in range(n) for p in range(len(pieces))]
         outs, scattered = [], []
         terms, waiting, firsts = (), None, []
-        earlier = ()
+        earlier = [rests[-1]]
 
         def output(at, have, terms, earlier):
             c, p = order[at]
-            attention = (attended[cuts[c]], attended_other[cuts[c]], attn_rows)
+            attention = ()
+            if p == len(pieces) - 1:
+                attention = (attended[cuts[c]], attended_other[cuts[c]], attn_rows)
             return project_hidden(
                 have,
                 swap(have),
                 w_down,
                 pieces[p],
                 terms if p else (),
-                () if p else attention,
+                attention,
                 p == len(pieces) - 1,
                 earlier,
             )
@@ -280,15 +271,16 @@
         hidden = None
         for at, (c, p) in enumerate(order):
             if c:
-                part = slice(cuts[c].start - rest.start, cuts[c].stop - rest.start)
+                part = slice(cuts[c].start - first, cuts[c].stop - first)
                 parts = all_red(rests[p][part] + nothing(firsts[c - 1]).astype(BF16))
             else:
-                parts = all_red(leads[p])
-            arrived = gelu_sum(parts, earlier)
-            earlier = [arrived]
+                parts = lead_parts[p]
+            if at:
+                arrived = gelu_sum(parts, earlier)
+                earlier = [arrived]
             if p == 0:
                 firsts.append(arrived)
-            if at == 0:
+            if at == 1:
                 attended = attend(sum_red(qkv) + nothing(arrived), q_gain, k_gain)
                 attended_other = swap(attended)
                 earlier = [attended]

time: 197 us -> 186 us (0.944)
  matrix products: 34.8 us -> 21.2 us
  starting transfers between devices: 15.2 us -> 21.7 us
  local copies, waits for them, and re-layouts: 6.33 us -> 12.6 us
  Pallas kernels: 39.9 us -> 33.9 us
  waiting for transfers between devices: 36.9 us -> 32.2 us
  other arithmetic: 11.4 us -> 7.24 us
  blocking collectives: 36.8 us -> 40 us
    all_gather x1 -> x2, blocking collectives: 14.9 us -> 40 us  [the longest x1 21.9 us: body(): lead = lax.all_gather(lead, 'wide', axis=1, tiled=True)]
    psum x1 -> x0, blocking collectives: 21.9 us -> none  [body(): sums = lax.psum(jnp.stack(token_sums(tokens)), ('wide', 'red')) / D]
    dot_general x8 -> x5, matrix products: 34.1 us -> 20.5 us  [project(): part = jnp.dot(both, weight, preferred_element_type=F32)]
    ppermute x7 -> x9, starting transfers between devices: 7.5 us -> 13.9 us  [all_red(): parts.append(lax.ppermute(x, 'red', pairs))]
    pallas_call x13 -> x12, Pallas kernels: 39.9 us -> 33.9 us  [call(): pl.pallas_call(body, in_specs=list(specs) + [corner_of(a) for a in earlie...]
    unnamed x42 -> x41, local copies, waits for them, and re-layouts: 3.72 us -> 7.39 us
    all_gather x1 -> x0, waiting for transfers between devices: 2.8 us -> none  [body(): raw = lax.all_gather(tokens, 'wide', axis=1, tiled=True)]
    add x4 -> x3, other arithmetic: 3.21 us -> 1.18 us  [body(): parts = all_red(rests[p][part] + nothing(firsts[c - 1]).astype(BF16))]
  transfers between devices with their start and end apart: 27 -> 31, of which waited for: 11 -> 14; matrix products, arithmetic and copies ran while one was open for 19% -> 12% of each run, Pallas kernels for 20% -> 15%
where the time goes in v5:
time: 186 us
  blocking collectives  40 us (22%)
  Pallas kernels  33.9 us (18%)
  waiting for transfers between devices  32.2 us (17%)
  starting transfers between devices  21.7 us (12%)
  matrix products  21.2 us (11%)
  between operations  16.9 us (9%)
  local copies, waits for them, and re-layouts  12.6 us (7%)
  other arithmetic  7.24 us (4%)
    pallas_call x12, Pallas kernels, call(): pl.pallas_call(body, in_specs=list(specs) + [corner_of(a) for a in earlie...  33.9 us
    all_gather x1, blocking collectives, body(): lead = lax.all_gather(lead, 'wide', axis=1, tiled=True)  21.9 us
    ppermute x9, waiting for transfers between devices, all_red(): parts.append(lax.ppermute(x, 'red', pairs))  20.6 us
    dot_general x5, matrix products, project(): part = jnp.dot(both, weight, preferred_element_type=F32)  20.5 us
    all_gather x1, blocking collectives, body(): rest = lax.all_gather(rest, 'wide', axis=1, tiled=True)  18.2 us
    ppermute x9, starting transfers between devices, all_red(): parts.append(lax.ppermute(x, 'red', pairs))  13.9 us
    unnamed x41, local copies, waits for them, and re-layouts  7.39 us
    ppermute x3, starting transfers between devices, collect(): total = total + lax.ppermute(block(chip ^ k), 'wide', pairs).astype(F32)  4.47 us
  transfers between devices with their start and end apart: 31, of which 14 were waited for; matrix products, arithmetic and copies ran while one was open for 12% of the time, Pallas kernels for 15%

profile of v5, /device:TPU:0, one launch (start us, length us, event | category | flops | bytes accessed | tf_op | source)
XLA Modules:
  0.0 185.7 jit_solution(17384265799127169101)
XLA Ops:
  8.3 21.9 %all_gather.6 = bf16[136,3072]{1,0:T(8,128)(2,1)S(1)} all-gather(bf16[136,768]{1,0:T(8,128)(2,1)S(1)} %pad_maximum_fusion.9), channel_id=1, replica_groups=mesh['grp'=2,'wide'=4,'red'=2,'tok'=2] {'wide'}, dimensions={1}, use_global_device_ids=true | all-gather | bytes 1044480 | tf_op jit(solution)/shard_map/all_gather | solution.py:213
  32.0 2.1 %collective-permute-done = f32[2,128]{1,0:T(2,128)S(1)} collective-permute-done((f32[2,128]{1,0:T(2,128)S(1)}, f32[2,128]{1,0:T(2,128)S(1)}, u32[]{:S(2)}, u32[]{:S(2)}) %collective-permute-start) | collective-permute-done | bytes 1056 | tf_op jit(solution)/shard_map/ppermute | solution.py:180
  36.3 5.4 %fusion.2 = f32[256,3072]{1,0:T(8,128)S(1)} fusion(bf16[1536,6144]{1,0:T(8,128)(2,1)} %param.13, bf16[128,1536]{1,0:T(8,128)(2,1)S(1)} %collective-permute-done.1, bf16[128,1536]{1,0:T(8,128)(2,1)S(1)} %get-tuple-element.43), kind=kOutput, calls=%fused_computation.2 | convolution fusion | flops 2417491968 | bytes 13369344 | tf_op jit(solution)/shard_map/dot_general | solution.py:227
  42.0 3.6 %copy-done.17 = bf16[1536,6144]{1,0:T(8,128)(2,1)S(1)} copy-done((bf16[1536,6144]{1,0:T(8,128)(2,1)S(1)}, bf16[1536,6144]{1,0:T(8,128)(2,1)}, u32[]{:S(2)}) %copy-start.17) | copy-done | bytes 18874392
  45.6 2.6 %fusion.6 = f32[256,3072]{1,0:T(8,128)S(1)} fusion(bf16[1536,6144]{1,0:T(8,128)(2,1)S(1)} %copy-done.17, bf16[128,1536]{1,0:T(8,128)(2,1)S(1)} %collective-permute-done.1, bf16[128,1536]{1,0:T(8,128)(2,1)S(1)} %get-tuple-element.43), kind=kOutput, calls=%fused_computation.6 | convolution fusion | flops 2417491968 | bytes 13369344 | tf_op jit(solution)/shard_map/dot_general | solution.py:227
  52.1 18.2 %all_gather.7 = bf16[128,3072]{1,0:T(8,128)(2,1)S(1)} all-gather(bf16[128,768]{1,0:T(8,128)(2,1)S(1)} %slice_add_fusion.9), channel_id=1, replica_groups=mesh['grp'=2,'wide'=4,'red'=2,'tok'=2] {'wide'}, dimensions={1}, use_global_device_ids=true | all-gather | bytes 983040 | tf_op jit(solution)/shard_map/all_gather | solution.py:238
  74.1 2.1 %collective-permute-done.6 = f32[2,128]{1,0:T(2,128)S(1)} collective-permute-done((f32[2,128]{1,0:T(2,128)S(1)}, f32[2,128]{1,0:T(2,128)S(1)}, u32[]{:S(2)}, u32[]{:S(2)}) %collective-permute-start.6) | collective-permute-done | bytes 1056 | tf_op jit(solution)/shard_map/ppermute | solution.py:180
  79.5 5.4 %fusion.4 = f32[256,3072]{1,0:T(8,128)S(1)} fusion(bf16[1536,6144]{1,0:T(8,128)(2,1)} %param.13, bf16[128,1536]{1,0:T(8,128)(2,1)} %collective-permute-done.7, bf16[128,1536]{1,0:T(8,128)(2,1)} %get-tuple-element.41), kind=kOutput, calls=%fused_computation.4 | convolution fusion | flops 2417491968 | bytes 13369344 | tf_op jit(solution)/shard_map/dot_general | solution.py:227
  88.2 5.3 %fusion = f32[256,3072]{1,0:T(8,128)S(1)} fusion(bf16[1536,6144]{1,0:T(8,128)(2,1)} %param.13, bf16[128,1536]{1,0:T(8,128)(2,1)} %collective-permute-done.7, bf16[128,1536]{1,0:T(8,128)(2,1)S(1)} %copy-done.14), kind=kOutput, calls=%fused_computation | convolution fusion | flops 2417491968 | bytes 13369344 | tf_op jit(solution)/shard_map/dot_general | solution.py:227
  95.9 2.0 %collective-permute-done.3.refs_1_ = bf16[128,3072]{1,0:T(8,128)(2,1)} collective-permute-done((bf16[128,3072]{1,0:T(8,128)(2,1)S(1)}, bf16[128,3072]{1,0:T(8,128)(2,1)}, u32[]{:S(2)}, u32[]{:S(2)}) %collective-permute-start.3) | collective-permute-done | bytes 786464 | tf_op jit(solution)/shard_map/ppermute | solution.py:180
  97.9 3.2 %shard_map.83.refs_0_ = bf16[128,3072]{1,0:T(8,128)(2,1)S(1)} custom-call(bf16[128,3072]{1,0:T(8,128)(2,1)S(1)} %fusion.15.refs_0_, bf16[128,3072]{1,0:T(8,128)(2,1)} %collective-permute-done.3.refs_1_, bf16[128,3072]{1,0:T(8,128)(2,1)S(1)} %fusion.13.refs_2_), custom_call_target="tpu_custom_call" | custom-call | tf_op jit(solution)/shard_map/pallas_call | solution.py:74
  106.2 5.0 %shard_map.84 = (f32[128,1536]{1,0:T(8,128)S(1)}, f32[128,1536]{1,0:T(8,128)S(1)}) custom-call(bf16[128,3072]{1,0:T(8,128)(2,1)S(1)} %shard_map.82.refs_0_, bf16[128,3072]{1,0:T(8,128)(2,1)S(1)} %collective-permute-done.10.refs_1_, bf16[6144,1536]{1,0:T(8,128)(2,1)} %refs_2_.11, bf16[256,128]{1,0:T(8,128)(2,1)S(1)} %fusion.26.refs_3_), custom_call_target="tpu_custom_call" | custom-call | tf_op jit(solution)/shard_map/pallas_call | solution.py:74
  111.3 3.8 %collective-permute-done.15.refs_1_ = bf16[64,3072]{1,0:T(8,128)(2,1)S(1)} collective-permute-done((bf16[64,3072]{1,0:T(8,128)(2,1)S(1)}, bf16[64,3072]{1,0:T(8,128)(2,1)S(1)}, u32[]{:S(2)}, u32[]{:S(2)}) %collective-permute-start.15) | collective-permute-done | bytes 393248 | tf_op jit(solution)/shard_map/ppermute | solution.py:180
  116.7 5.1 %shard_map.86 = (bf16[128,1536]{1,0:T(8,128)(2,1)S(1)}, bf16[128,1536]{1,0:T(8,128)(2,1)S(1)}) custom-call(bf16[128,3072]{1,0:T(8,128)(2,1)S(1)} %shard_map.83.refs_0_, bf16[128,3072]{1,0:T(8,128)(2,1)S(1)} %collective-permute-done.9.refs_1_, bf16[6144,1536]{1,0:T(8,128)(2,1)} %refs_2_.11, f32[128,1536]{1,0:T(8,128)S(1)} %get-tuple-element.17.refs_2_.refs_3_, ...), custom_call_target="tpu_custom_call" | custom-call | tf_op jit(solution)/shard_map/pallas_call | solution.py:74
  127.5 6.4 %collective-permute-done.17.refs_1_ = bf16[64,3072]{1,0:T(8,128)(2,1)S(1)} collective-permute-done((bf16[64,3072]{1,0:T(8,128)(2,1)S(1)}, bf16[64,3072]{1,0:T(8,128)(2,1)S(1)}, u32[]{:S(2)}, u32[]{:S(2)}) %collective-permute-start.17) | collective-permute-done | bytes 393248 | tf_op jit(solution)/shard_map/ppermute | solution.py:180
  136.1 4.5 %shard_map.88 = (f32[64,1536]{1,0:T(8,128)S(1)}, f32[64,1536]{1,0:T(8,128)S(1)}) custom-call(bf16[64,3072]{1,0:T(8,128)(2,1)S(1)} %shard_map.85.refs_8_.refs_0_, bf16[64,3072]{1,0:T(8,128)(2,1)S(1)} %collective-permute-done.19.refs_1_, bf16[6144,1536]{1,0:T(8,128)(2,1)} %refs_2_.11, bf16[64,3072]{1,0:T(8,128)(2,1)S(1)} %shard_map.87.refs_3_.refs_0_, ...), custom_call_target="tpu_custom_call" | custom-call | tf_op jit(solution)/shard_map/pallas_call | solution.py:74
  142.8 4.5 %shard_map.90 = (bf16[64,1536]{1,0:T(8,128)(2,1)S(1)}, bf16[64,1536]{1,0:T(8,128)(2,1)S(1)}) custom-call(bf16[64,3072]{1,0:T(8,128)(2,1)S(1)} %shard_map.87.refs_3_.refs_0_, bf16[64,3072]{1,0:T(8,128)(2,1)S(1)} %collective-permute-done.18.refs_1_, bf16[6144,1536]{1,0:T(8,128)(2,1)} %refs_2_.11, f32[64,1536]{1,0:T(8,128)S(1)} %get-tuple-element.21.refs_2_.refs_3_, ...), custom_call_target="tpu_custom_call" | custom-call | tf_op jit(solution)/shard_map/pallas_call | solution.py:74
  147.9 2.5 %collective-permute-done.22.refs_1_ = bf16[64,3072]{1,0:T(8,128)(2,1)S(1)} collective-permute-done((bf16[64,3072]{1,0:T(8,128)(2,1)S(1)}, bf16[64,3072]{1,0:T(8,128)(2,1)S(1)}, u32[]{:S(2)}, u32[]{:S(2)}) %collective-permute-start.22) | collective-permute-done | bytes 393248 | tf_op jit(solution)/shard_map/ppermute | solution.py:180
  153.8 4.5 %shard_map.92 = (f32[64,1536]{1,0:T(8,128)S(1)}, f32[64,1536]{1,0:T(8,128)S(1)}) custom-call(bf16[64,3072]{1,0:T(8,128)(2,1)S(1)} %shard_map.89.refs_8_.refs_0_, bf16[64,3072]{1,0:T(8,128)(2,1)S(1)} %collective-permute-done.24.refs_1_, bf16[6144,1536]{1,0:T(8,128)(2,1)} %refs_2_.11, bf16[64,3072]{1,0:T(8,128)(2,1)S(1)} %shard_map.91.refs_3_.refs_0_, ...), custom_call_target="tpu_custom_call" | custom-call | tf_op jit(solution)/shard_map/pallas_call | solution.py:74
  158.3 4.6 %shard_map.93 = (bf16[64,1536]{1,0:T(8,128)(2,1)S(1)}, bf16[64,1536]{1,0:T(8,128)(2,1)S(1)}) custom-call(bf16[64,3072]{1,0:T(8,128)(2,1)S(1)} %shard_map.91.refs_3_.refs_0_, bf16[64,3072]{1,0:T(8,128)(2,1)S(1)} %collective-permute-done.23.refs_1_, bf16[6144,1536]{1,0:T(8,128)(2,1)} %refs_2_.11, f32[64,1536]{1,0:T(8,128)S(1)} %get-tuple-element.25.refs_3_.refs_8_, ...), custom_call_target="tpu_custom_call" | custom-call | tf_op jit(solution)/shard_map/pallas_call | solution.py:74
  164.6 1.9 %collective-permute-start.26 = (bf16[64,768]{1,0:T(8,128)(2,1)S(1)}, bf16[64,768]{1,0:T(8,128)(2,1)S(1)}, u32[]{:S(2)}, u32[]{:S(2)}) collective-permute-start(bf16[64,768]{1,0:T(8,128)(2,1)S(1)} %get-tuple-element.47), channel_id=1, source_target_pairs={{0,12},{4,8},{8,4},{12,0},{1,13},{5,9},{9,5},{13,1},{2,14},{6,10},... | collective-permute-start | bytes 294920 | tf_op jit(solution)/shard_map/ppermute | solution.py:197
  166.5 2.5 %collective-permute-start.28 = (bf16[64,768]{1,0:T(8,128)(2,1)S(1)}, bf16[64,768]{1,0:T(8,128)(2,1)S(1)}, u32[]{:S(2)}, u32[]{:S(2)}) collective-permute-start(bf16[64,768]{1,0:T(8,128)(2,1)S(1)} %get-tuple-element.48), channel_id=1, source_target_pairs={{0,4},{4,0},{8,12},{12,8},{1,5},{5,1},{9,13},{13,9},{2,6},{6,2},{1... | collective-permute-start | bytes 294920 | tf_op jit(solution)/shard_map/ppermute | solution.py:197
  169.1 4.2 %reduce-scatter.5.cloned.1.call-done = bf16[64,768]{1,0:T(8,128)(2,1)} async-done(((bf16[64,3072]{1,0:T(8,128)(2,1)}), bf16[64,768]{1,0:T(8,128)(2,1)}) %reduce-scatter.5.cloned.1.call-update) | async-done | bytes 98320 | tf_op jit(solution)/shard_map/reduce_scatter | solution.py:268
  173.3 3.7 %collective-permute-done.27 = bf16[64,768]{1,0:T(8,128)(2,1)S(1)} collective-permute-done((bf16[64,768]{1,0:T(8,128)(2,1)S(1)}, bf16[64,768]{1,0:T(8,128)(2,1)S(1)}, u32[]{:S(2)}, u32[]{:S(2)}) %collective-permute-start.27) | collective-permute-done | bytes 98336 | tf_op jit(solution)/shard_map/ppermute | solution.py:197
  (155 shorter events, 44.0 us)
Async XLA Ops:
  6.5 145.3 %reduce-scatter.3.cloned.1.call-start = ((), (), s32[]{:S(2)}) async-start(), calls=%async_computation.2 | async-start | bytes 983040 | tf_op jit(solution)/shard_map/reduce_scatter | solution.py:268
  41.8 6.7 %collective-permute-start.4 = (bf16[128,3072]{1,0:T(8,128)(2,1)S(1)}, bf16[128,3072]{1,0:T(8,128)(2,1)S(1)}, u32[]{:S(2)}, u32[]{:S(2)}) collective-permute-start(bf16[128,3072]{1,0:T(8,128)(2,1)S(1)} %slice.274), channel_id=1, source_target_pairs={{0,1},{1,0},{2,3},{3,2},{4,5},{5,4},{6,7},{7,6},{8,9},{9,8},{10,11... | collective-permute-start | bytes 2359304 | tf_op jit(solution)/shard_map/ppermute | solution.py:174
  48.7 21.5 %collective-permute-start.5 = (bf16[128,3072]{1,0:T(8,128)(2,1)S(1)}, bf16[128,3072]{1,0:T(8,128)(2,1)S(1)}, u32[]{:S(2)}, u32[]{:S(2)}) collective-permute-start(bf16[128,3072]{1,0:T(8,128)(2,1)S(1)} %fusion.14.refs_0_), channel_id=1, source_target_pairs={{0,2},{2,0},{1,3},{3,1},{4,6},{6,4},{5,7},{7,5},{8,10},{10,8},{9,1... | collective-permute-start | bytes 2359304 | tf_op jit(solution)/shard_map/ppermute | solution.py:180
  77.4 20.4 %collective-permute-start.3 = (bf16[128,3072]{1,0:T(8,128)(2,1)S(1)}, bf16[128,3072]{1,0:T(8,128)(2,1)}, u32[]{:S(2)}, u32[]{:S(2)}) collective-permute-start(bf16[128,3072]{1,0:T(8,128)(2,1)S(1)} %fusion.15.refs_0_), channel_id=1, source_target_pairs={{0,2},{2,0},{1,3},{3,1},{4,6},{6,4},{5,7},{7,5},{8,10},{10,8},{9,1... | collective-permute-start | bytes 2359304 | tf_op jit(solution)/shard_map/ppermute | solution.py:180
  78.9 27.3 %collective-permute-start.10 = (bf16[128,3072]{1,0:T(8,128)(2,1)S(1)}, bf16[128,3072]{1,0:T(8,128)(2,1)S(1)}, u32[]{:S(2)}, u32[]{:S(2)}) collective-permute-start(bf16[128,3072]{1,0:T(8,128)(2,1)S(1)} %shard_map.82.refs_0_), channel_id=1, source_target_pairs={{0,1},{1,0},{2,3},{3,2},{4,5},{5,4},{6,7},{7,6},{8,9},{9,8},{10,11... | collective-permute-start | bytes 2359304 | tf_op jit(solution)/shard_map/ppermute | solution.py:174
  85.1 10.6 %collective-permute-start.8 = (bf16[128,3072]{1,0:T(8,128)(2,1)S(1)}, bf16[128,3072]{1,0:T(8,128)(2,1)S(1)}, u32[]{:S(2)}, u32[]{:S(2)}) collective-permute-start(bf16[128,3072]{1,0:T(8,128)(2,1)S(1)} %slice.273), channel_id=1, source_target_pairs={{0,1},{1,0},{2,3},{3,2},{4,5},{5,4},{6,7},{7,6},{8,9},{9,8},{10,11... | collective-permute-start | bytes 2359304 | tf_op jit(solution)/shard_map/ppermute | solution.py:174
  88.0 6.1 %collective-permute-start.11 = (bf16[256,384]{0,1:T(8,128)(2,1)S(1)}, bf16[256,384]{0,1:T(8,128)(2,1)S(1)}, u32[]{:S(2)}, u32[]{:S(2)}) collective-permute-start(bf16[256,384]{0,1:T(8,128)(2,1)S(1)} %slice.276), channel_id=1, source_target_pairs={{0,1},{1,0},{2,3},{3,2},{4,5},{5,4},{6,7},{7,6},{8,9},{9,8},{10,11... | collective-permute-start | bytes 589832 | tf_op jit(solution)/shard_map/ppermute | solution.py:174
  93.6 8.8 %collective-permute-start.14 = (bf16[128,3072]{1,0:T(8,128)(2,1)S(1)}, bf16[128,3072]{1,0:T(8,128)(2,1)S(1)}, u32[]{:S(2)}, u32[]{:S(2)}) collective-permute-start(bf16[128,3072]{1,0:T(8,128)(2,1)S(1)} %slice.272), channel_id=1, source_target_pairs={{0,1},{1,0},{2,3},{3,2},{4,5},{5,4},{6,7},{7,6},{8,9},{9,8},{10,11... | collective-permute-start | bytes 2359304 | tf_op jit(solution)/shard_map/ppermute | solution.py:174
  94.2 8.1 %collective-permute-start.12 = (bf16[256,384]{0,1:T(8,128)(2,1)S(1)}, bf16[256,384]{0,1:T(8,128)(2,1)S(1)}, u32[]{:S(2)}, u32[]{:S(2)}) collective-permute-start(bf16[256,384]{0,1:T(8,128)(2,1)S(1)} %fusion.27), channel_id=1, source_target_pairs={{0,2},{2,0},{1,3},{3,1},{4,6},{6,4},{5,7},{7,5},{8,10},{10,8},{9,1... | collective-permute-start | bytes 589832 | tf_op jit(solution)/shard_map/ppermute | solution.py:180
  101.6 15.1 %collective-permute-start.9 = (bf16[128,3072]{1,0:T(8,128)(2,1)S(1)}, bf16[128,3072]{1,0:T(8,128)(2,1)S(1)}, u32[]{:S(2)}, u32[]{:S(2)}) collective-permute-start(bf16[128,3072]{1,0:T(8,128)(2,1)S(1)} %shard_map.83.refs_0_), channel_id=1, source_target_pairs={{0,1},{1,0},{2,3},{3,2},{4,5},{5,4},{6,7},{7,6},{8,9},{9,8},{10,11... | collective-permute-start | bytes 2359304 | tf_op jit(solution)/shard_map/ppermute | solution.py:174
  103.5 11.6 %collective-permute-start.15 = (bf16[64,3072]{1,0:T(8,128)(2,1)S(1)}, bf16[64,3072]{1,0:T(8,128)(2,1)S(1)}, u32[]{:S(2)}, u32[]{:S(2)}) collective-permute-start(bf16[64,3072]{1,0:T(8,128)(2,1)S(1)} %slice_add_fusion.7.refs_0_), channel_id=1, source_target_pairs={{0,2},{2,0},{1,3},{3,1},{4,6},{6,4},{5,7},{7,5},{8,10},{10,8},{9,1... | collective-permute-start | bytes 1179656 | tf_op jit(solution)/shard_map/ppermute | solution.py:180
  105.9 5.4 %collective-permute-start.13 = (bf16[256,128]{1,0:T(8,128)(2,1)S(1)}, bf16[256,128]{1,0:T(8,128)(2,1)S(1)}, u32[]{:S(2)}, u32[]{:S(2)}) collective-permute-start(bf16[256,128]{1,0:T(8,128)(2,1)S(1)} %fusion.26.refs_3_), channel_id=1, source_target_pairs={{0,1},{1,0},{2,3},{3,2},{4,5},{5,4},{6,7},{7,6},{8,9},{9,8},{10,11... | collective-permute-start | bytes 196616 | tf_op jit(solution)/shard_map/ppermute | solution.py:174
  122.0 12.0 %collective-permute-start.17 = (bf16[64,3072]{1,0:T(8,128)(2,1)S(1)}, bf16[64,3072]{1,0:T(8,128)(2,1)S(1)}, u32[]{:S(2)}, u32[]{:S(2)}) collective-permute-start(bf16[64,3072]{1,0:T(8,128)(2,1)S(1)} %get-tuple-element.39.refs_0_), channel_id=1, source_target_pairs={{0,2},{2,0},{1,3},{3,1},{4,6},{6,4},{5,7},{7,5},{8,10},{10,8},{9,1... | collective-permute-start | bytes 1179656 | tf_op jit(solution)/shard_map/ppermute | solution.py:180
  124.7 48.6 %reduce-scatter.5.cloned.1.call-start = ((), (), s32[]{:S(2)}) async-start(), calls=%async_computation.3 | async-start | bytes 491520 | tf_op jit(solution)/shard_map/reduce_scatter | solution.py:268
  125.8 10.3 %collective-permute-start.19 = (bf16[64,3072]{1,0:T(8,128)(2,1)S(1)}, bf16[64,3072]{1,0:T(8,128)(2,1)S(1)}, u32[]{:S(2)}, u32[]{:S(2)}) collective-permute-start(bf16[64,3072]{1,0:T(8,128)(2,1)S(1)} %shard_map.85.refs_8_.refs_0_), channel_id=1, source_target_pairs={{0,1},{1,0},{2,3},{3,2},{4,5},{5,4},{6,7},{7,6},{8,9},{9,8},{10,11... | collective-permute-start | bytes 1179656 | tf_op jit(solution)/shard_map/ppermute | solution.py:174
  126.0 16.4 %collective-permute-start.20 = (bf16[64,3072]{1,0:T(8,128)(2,1)S(1)}, bf16[64,3072]{1,0:T(8,128)(2,1)S(1)}, u32[]{:S(2)}, u32[]{:S(2)}) collective-permute-start(bf16[64,3072]{1,0:T(8,128)(2,1)S(1)} %slice_add_fusion.5.refs_0_), channel_id=1, source_target_pairs={{0,2},{2,0},{1,3},{3,1},{4,6},{6,4},{5,7},{7,5},{8,10},{10,8},{9,1... | collective-permute-start | bytes 1179656 | tf_op jit(solution)/shard_map/ppermute | solution.py:180
  134.4 8.4 %collective-permute-start.18 = (bf16[64,3072]{1,0:T(8,128)(2,1)S(1)}, bf16[64,3072]{1,0:T(8,128)(2,1)S(1)}, u32[]{:S(2)}, u32[]{:S(2)}) collective-permute-start(bf16[64,3072]{1,0:T(8,128)(2,1)S(1)} %shard_map.87.refs_3_.refs_0_), channel_id=1, source_target_pairs={{0,1},{1,0},{2,3},{3,2},{4,5},{5,4},{6,7},{7,6},{8,9},{9,8},{10,11... | collective-permute-start | bytes 1179656 | tf_op jit(solution)/shard_map/ppermute | solution.py:174
  134.5 15.9 %collective-permute-start.22 = (bf16[64,3072]{1,0:T(8,128)(2,1)S(1)}, bf16[64,3072]{1,0:T(8,128)(2,1)S(1)}, u32[]{:S(2)}, u32[]{:S(2)}) collective-permute-start(bf16[64,3072]{1,0:T(8,128)(2,1)S(1)} %get-tuple-element.40.refs_0_), channel_id=1, source_target_pairs={{0,2},{2,0},{1,3},{3,1},{4,6},{6,4},{5,7},{7,5},{8,10},{10,8},{9,1... | collective-permute-start | bytes 1179656 | tf_op jit(solution)/shard_map/ppermute | solution.py:180
  147.3 3.7 %collective-permute-start.21 = (bf16[64,1536]{1,0:T(8,128)(2,1)S(1)}, bf16[64,1536]{1,0:T(8,128)(2,1)S(1)}, u32[]{:S(2)}, u32[]{:S(2)}) collective-permute-start(bf16[64,1536]{1,0:T(8,128)(2,1)S(1)} %get-tuple-element.24), channel_id=1, source_target_pairs={{0,1},{1,0},{2,3},{3,2},{4,5},{5,4},{6,7},{7,6},{8,9},{9,8},{10,11... | collective-permute-start | bytes 589832 | tf_op jit(solution)/shard_map/ppermute | solution.py:174
  147.5 4.3 %collective-permute-start.24 = (bf16[64,3072]{1,0:T(8,128)(2,1)S(1)}, bf16[64,3072]{1,0:T(8,128)(2,1)S(1)}, u32[]{:S(2)}, u32[]{:S(2)}) collective-permute-start(bf16[64,3072]{1,0:T(8,128)(2,1)S(1)} %shard_map.89.refs_8_.refs_0_), channel_id=1, source_target_pairs={{0,1},{1,0},{2,3},{3,2},{4,5},{5,4},{6,7},{7,6},{8,9},{9,8},{10,11... | collective-permute-start | bytes 1179656 | tf_op jit(solution)/shard_map/ppermute | solution.py:174
  150.9 7.4 %collective-permute-start.23 = (bf16[64,3072]{1,0:T(8,128)(2,1)S(1)}, bf16[64,3072]{1,0:T(8,128)(2,1)S(1)}, u32[]{:S(2)}, u32[]{:S(2)}) collective-permute-start(bf16[64,3072]{1,0:T(8,128)(2,1)S(1)} %shard_map.91.refs_3_.refs_0_), channel_id=1, source_target_pairs={{0,1},{1,0},{2,3},{3,2},{4,5},{5,4},{6,7},{7,6},{8,9},{9,8},{10,11... | collective-permute-start | bytes 1179656 | tf_op jit(solution)/shard_map/ppermute | solution.py:174
  164.6 8.7 %collective-permute-start.26 = (bf16[64,768]{1,0:T(8,128)(2,1)S(1)}, bf16[64,768]{1,0:T(8,128)(2,1)S(1)}, u32[]{:S(2)}, u32[]{:S(2)}) collective-permute-start(bf16[64,768]{1,0:T(8,128)(2,1)S(1)} %get-tuple-element.47), channel_id=1, source_target_pairs={{0,12},{4,8},{8,4},{12,0},{1,13},{5,9},{9,5},{13,1},{2,14},{6,10},... | collective-permute-start | bytes 294920 | tf_op jit(solution)/shard_map/ppermute | solution.py:197
  166.5 10.5 %collective-permute-start.27 = (bf16[64,768]{1,0:T(8,128)(2,1)S(1)}, bf16[64,768]{1,0:T(8,128)(2,1)S(1)}, u32[]{:S(2)}, u32[]{:S(2)}) collective-permute-start(bf16[64,768]{1,0:T(8,128)(2,1)S(1)} %get-tuple-element.49), channel_id=1, source_target_pairs={{0,8},{4,12},{8,0},{12,4},{1,9},{5,13},{9,1},{13,5},{2,10},{6,14},... | collective-permute-start | bytes 294920 | tf_op jit(solution)/shard_map/ppermute | solution.py:197
  166.5 10.4 %collective-permute-start.28 = (bf16[64,768]{1,0:T(8,128)(2,1)S(1)}, bf16[64,768]{1,0:T(8,128)(2,1)S(1)}, u32[]{:S(2)}, u32[]{:S(2)}) collective-permute-start(bf16[64,768]{1,0:T(8,128)(2,1)S(1)} %get-tuple-element.48), channel_id=1, source_target_pairs={{0,4},{4,0},{8,12},{12,8},{1,5},{5,1},{9,13},{13,9},{2,6},{6,2},{1... | collective-permute-start | bytes 294920 | tf_op jit(solution)/shard_map/ppermute | solution.py:197
  (27 other events, 199.2 us)
Sparse Core Ops, SparseCore 0:
  124.8 22.7 reduce-scatter.2
  151.9 21.3 reduce-scatter.4

commit v6 on v5

--- a/solution.py
+++ b/solution.py
@@ -11,7 +11,7 @@
 D = 6144
 PATCHES = 256
 EPS = 1e-06
-SHARES = (8, 4, 4)
+SHARES = (9, 4, 3)
 PIECES = (1, 1)
 AHEAD = 4
 GAIN_ROWS = 8
@@ -31,20 +31,6 @@
     return normalize(values, mean, meansq, gain)
 
 
-def attend(qkv, q_gain, k_gain):
-    width = q_gain.shape[1]
-    query = head_norm(qkv[:, :width], q_gain[0]).astype(BF16)
-    key = head_norm(qkv[:, width : 2 * width], k_gain[0]).astype(BF16)
-    value = qkv[:, 2 * width :].astype(BF16)
-    query, key, value = (a.reshape(-1, PATCHES, width) for a in (query, key, value))
-    scores = jnp.einsum("ipd,iqd->ipq", query, key, preferred_element_type=F32)
-    scores = scores * width ** (-0.5)
-    weights = jnp.exp(scores - jnp.max(scores, axis=-1, keepdims=True))
-    total = jnp.sum(weights, axis=-1, keepdims=True)
-    acc = jnp.einsum("ipq,iqd->ipd", weights, value.astype(F32), precision=lax.Precision.HIGHEST)
-    return (acc / total).astype(BF16).reshape(-1, width)
-
-
 def nothing(x):
     corner = x[(0,) * x.ndim].astype(jnp.int32)
     return lax.shift_right_logical(corner & 1, 1).astype(F32)
@@ -100,6 +86,136 @@
         grid=(steps,),
         out_specs=spec,
         out_shape=jax.ShapeDtypeStruct((rows, units), BF16),
+    )
+
+
+def sum_rows(near, far, cut, earlier=()):
+    spec = pl.BlockSpec(near.shape, lambda *_: (0, 0))
+    shape = (cut.stop - cut.start, near.shape[1])
+
+    def kernel(ins, outs):
+        outs[0][...] = (ins[0][cut].astype(F32) + ins[1][cut].astype(F32)).astype(BF16)
+
+    return call(
+        kernel,
+        earlier,
+        (near, far),
+        [spec, spec],
+        params=SMALL,
+        grid=(1,),
+        out_specs=pl.BlockSpec(shape, lambda *_: (0, 0)),
+        out_shape=jax.ShapeDtypeStruct(shape, BF16),
+    )
+
+
+def side_by_side(kept, got, core, earlier=()):
+    rows, columns = kept.shape
+    spec = pl.BlockSpec(kept.shape, lambda *_: (0, 0))
+
+    def kernel(ins, outs):
+        first = ins[2][0] == 0
+        outs[0][:, :columns] = jnp.where(first, ins[0][...], ins[1][...])
+        outs[0][:, columns:] = jnp.where(first, ins[1][...], ins[0][...])
+
+    return call(
+        kernel,
+        earlier,
+        (kept, got, core.reshape(1)),
+        [spec, spec, pl.BlockSpec(memory_space=pltpu.SMEM)],
+        params=SMALL,
+        grid=(1,),
+        out_specs=pl.BlockSpec((rows, 2 * columns), lambda *_: (0, 0)),
+        out_shape=jax.ShapeDtypeStruct((rows, 2 * columns), kept.dtype),
+    )
+
+
+def attend(parts, q_gain, k_gain, earlier=()):
+    rows, width = parts[0].shape[0], q_gain.shape[1]
+    n = len(parts)
+
+    def kernel(ins, outs):
+        def columns(at):
+            here = slice(at * width, (at + 1) * width)
+            return sum(part[:, here].astype(F32) for part in ins[:n])
+
+        query = head_norm(columns(0), ins[n][...]).astype(BF16)
+        key = head_norm(columns(1), ins[n + 1][...]).astype(BF16)
+        value = columns(2).astype(BF16).astype(F32)
+        for at in range(0, rows, PATCHES):
+            image = slice(at, at + PATCHES)
+            scores = lax.dot_general(
+                query[image], key[image], (((1,), (1,)), ((), ())), preferred_element_type=F32
+            )
+            scores = scores * width ** (-0.5)
+            weights = jnp.exp(scores - jnp.max(scores, axis=-1, keepdims=True))
+            total = jnp.sum(weights, axis=-1, keepdims=True)
+            acc = jnp.dot(
+                weights,
+                value[image],
+                precision=lax.Precision.HIGHEST,
+                preferred_element_type=F32,
+            )
+            outs[0][image] = (acc / total).astype(BF16)
+
+    whole = [pl.BlockSpec(a.shape, lambda *_: (0, 0)) for a in (*parts, q_gain, k_gain)]
+    return call(
+        kernel,
+        earlier,
+        (*parts, q_gain, k_gain),
+        whole,
+        params=SMALL,
+        grid=(1,),
+        out_specs=pl.BlockSpec((rows, width), lambda *_: (0, 0)),
+        out_shape=jax.ShapeDtypeStruct((rows, width), BF16),
+    )
+
+
+def project_rows(own, other, weight, piece, earlier=()):
+    rows, depth = own.shape
+    columns = piece.stop - piece.start
+    block, steps, _ = steps_of(piece)
+    whole = pl.BlockSpec((rows, depth), lambda *_: (0, 0))
+    out = pl.BlockSpec((rows, columns), lambda *_: (0, 0))
+
+    def kernel(ins, refs):
+        near, far, both, landed, sems = refs
+
+        def bring(at):
+            start = pl.multiple_of(piece.start + at * block, block)
+            source = ins[2].at[:, pl.ds(start, block)]
+            return pltpu.make_async_copy(source, landed.at[at], sems.at[at])
+
+        for at in range(min(AHEAD, steps)):
+            bring(at).start()
+        both[:rows] = ins[0][...]
+        both[rows:] = ins[1][...]
+
+        @pl.loop(0, steps)
+        def _(at):
+            bring(at).wait()
+
+            @pl.when(at + AHEAD < steps)
+            def _():
+                bring(at + AHEAD).start()
+
+            part = jnp.dot(both[...], landed[at], preferred_element_type=F32).astype(BF16)
+            here = pl.ds(pl.multiple_of(at * block, block), block)
+            near[:, here] = part[:rows]
+            far[:, here] = part[rows:]
+
+    return call(
+        kernel,
+        earlier,
+        (own, other, weight),
+        [whole, whole, pl.BlockSpec(memory_space=pltpu.HBM)],
+        grid=(1,),
+        out_specs=[out] * 2,
+        out_shape=[jax.ShapeDtypeStruct((rows, columns), BF16)] * 2,
+        scratch_shapes=[
+            pltpu.VMEM((2 * rows, depth), BF16),
+            pltpu.VMEM((steps, depth, block), BF16),
+            pltpu.SemaphoreType.DMA((steps,)),
+        ],
     )
 
 
@@ -237,13 +353,19 @@
         rest = tokens[first:] + nothing(leads[-1]).astype(BF16)
         rest = lax.all_gather(rest, "wide", axis=1, tiled=True)
         rest_pair = normed(rest.astype(F32) + nothing(arrived))
-        qkv = project([jnp.concatenate(p, axis=0) for p in zip(lead_pair, rest_pair)], qkv_rows)
-        rests = [project(rest_pair, weight) for weight in weights]
+        halves, before = [], []
+        for piece in pieces:
+            near, far = project_rows(*rest_pair, w_up, piece, before)
+            halves.append((near, swap(far)))
+            before = [near]
+        pair = [jnp.concatenate(p, axis=0) for p in zip(lead_pair, rest_pair)]
+        near, far = project_rows(*pair, qkv_rows, slice(0, qkv_rows.shape[1]), before)
+        qkv = sum_rows(near, swap(far), slice(0, tokens.shape[0]))
 
         order = [(c, p) for c in range(n) for p in range(len(pieces))]
         outs, scattered = [], []
         terms, waiting, firsts = (), None, []
-        earlier = [rests[-1]]
+        earlier = [near]
 
         def output(at, have, terms, earlier):
             c, p = order[at]
@@ -261,18 +383,22 @@
                 earlier,
             )
 
-        def scatter(kept, got):
-            lower = jnp.where(core == 0, kept, got)
-            upper = jnp.where(core == 0, got, kept)
-            full = jnp.concatenate([lower, upper], axis=1)
+        def scatter(kept, got, earlier):
+            full = side_by_side(kept, got, core, scattered[-1:] + earlier)
             scattered.append(lax.psum_scatter(full, "wide", scatter_dimension=1, tiled=True))
             return full
 
+        def sums_of(p, part, before):
+            return sum_rows(*halves[p], part, [before])
+
+        after_lead = [
+            sums_of(p, slice(0, cuts[1].stop - first), arrived) for p in range(len(pieces))
+        ]
         hidden = None
         for at, (c, p) in enumerate(order):
             if c:
                 part = slice(cuts[c].start - first, cuts[c].stop - first)
-                parts = all_red(rests[p][part] + nothing(firsts[c - 1]).astype(BF16))
+                parts = all_red(sums_of(p, part, firsts[c - 1]) if c > 1 else after_lead[p])
             else:
                 parts = lead_parts[p]
             if at:
@@ -281,22 +407,21 @@
             if p == 0:
                 firsts.append(arrived)
             if at == 1:
-                attended = attend(sum_red(qkv) + nothing(arrived), q_gain, k_gain)
+                attended = attend(all_red(qkv), q_gain, k_gain, earlier)
                 attended_other = swap(attended)
-                earlier = [attended]
-            if waiting is not None:
-                earlier.append(scatter(*waiting))
+                earlier = [attended, *after_lead]
+            if waiting is not None and not scattered:
+                earlier.append(scatter(*waiting, []))
                 waiting = None
-            if at == len(order) - 1:
-                earlier += scattered[:1]
             if at:
                 terms = output(at - 1, hidden, terms, earlier)
                 earlier = [terms[0]]
-                if p == 0:
-                    waiting = (terms[0], swap(terms[1]))
+            if waiting is not None:
+                earlier = [scatter(*waiting, earlier)]
+                waiting = None
+            if at and p == 0:
+                waiting = (terms[0], swap(terms[1]))
             hidden = arrived
-        if waiting is not None:
-            earlier.append(scatter(*waiting))
         terms = output(len(order) - 1, hidden, terms, earlier)
         for cut, summed in zip(cuts, scattered):
             outs.append(tokens[cut].astype(F32) + summed.astype(F32))

time: 186 us -> 198 us (1.065)
  waiting for transfers between devices: 32.2 us -> 55 us
  Pallas kernels: 33.9 us -> 46.9 us
  matrix products: 21.2 us -> 8.53 us
  starting transfers between devices: 21.7 us -> 16.9 us
  other arithmetic: 7.24 us -> 4.82 us
  local copies, waits for them, and re-layouts: 12.6 us -> 10.5 us
    ppermute x9, waiting for transfers between devices: 20.6 us -> 34.7 us  [all_red(): parts.append(lax.ppermute(x, 'red', pairs))]
    pallas_call x12 -> x23, Pallas kernels: 33.9 us -> 46.9 us  [call(): pl.pallas_call(body, in_specs=list(specs) + [corner_of(a) for a in earlie...]
    dot_general x5 -> x2, matrix products: 20.5 us -> 8.53 us  [project(): part = jnp.dot(both, weight, preferred_element_type=F32)]
    ppermute x17, waiting for transfers between devices: 3.62 us -> 9.97 us  [swap(): return lax.ppermute(x, 'tok', [(0, 1), (1, 0)])]
    ppermute x3, waiting for transfers between devices: 3.69 us -> 9 us  [collect(): total = total + lax.ppermute(block(chip ^ k), 'wide', pairs).astype(F32)]
    ppermute x9, starting transfers between devices: 13.9 us -> 9.18 us  [all_red(): parts.append(lax.ppermute(x, 'red', pairs))]
    reduce_scatter x2, waiting for transfers between devices: 4.18 us -> 1.33 us  [scatter(): lax.psum_scatter(full, 'wide', scatter_dimension=1, tiled=True)]
    unnamed x41 -> x37, local copies, waits for them, and re-layouts: 7.39 us -> 7.42 us
  transfers between devices with their start and end apart: 31 -> 31, of which waited for: 14 -> 18; matrix products, arithmetic and copies ran while one was open for 12% -> 3% of each run, Pallas kernels for 15% -> 20%
where the time goes in v6:
time: 198 us
  waiting for transfers between devices  55 us (28%)
  Pallas kernels  46.9 us (24%)
  blocking collectives  40.1 us (20%)
  starting transfers between devices  16.9 us (9%)
  between operations  15.2 us (8%)
  local copies, waits for them, and re-layouts  10.5 us (5%)
  matrix products  8.53 us (4%)
  other arithmetic  4.82 us (2%)
    pallas_call x23, Pallas kernels, call(): pl.pallas_call(body, in_specs=list(specs) + [corner_of(a) for a in earlie...  46.9 us
    ppermute x9, waiting for transfers between devices, all_red(): parts.append(lax.ppermute(x, 'red', pairs))  34.7 us
    all_gather x1, blocking collectives, body(): lead = lax.all_gather(lead, 'wide', axis=1, tiled=True)  23 us
    all_gather x1, blocking collectives, body(): rest = lax.all_gather(rest, 'wide', axis=1, tiled=True)  17.1 us
    ppermute x17, waiting for transfers between devices, swap(): return lax.ppermute(x, 'tok', [(0, 1), (1, 0)])  9.97 us
    ppermute x9, starting transfers between devices, all_red(): parts.append(lax.ppermute(x, 'red', pairs))  9.18 us
    ppermute x3, waiting for transfers between devices, collect(): total = total + lax.ppermute(block(chip ^ k), 'wide', pairs).astype(F32)  9 us
    dot_general x2, matrix products, project(): part = jnp.dot(both, weight, preferred_element_type=F32)  8.53 us
  transfers between devices with their start and end apart: 31, of which 18 were waited for; matrix products, arithmetic and copies ran while one was open for 3% of the time, Pallas kernels for 20%

profile of v6, /device:TPU:0, one launch (start us, length us, event | category | flops | bytes accessed | tf_op | source)
XLA Modules:
  0.0 197.9 jit_solution(2500068778096838971)
XLA Ops:
  8.2 23.0 %all_gather.6 = bf16[152,3072]{1,0:T(8,128)(2,1)S(1)} all-gather(bf16[152,768]{1,0:T(8,128)(2,1)S(1)} %pad_maximum_fusion.6), channel_id=1, replica_groups=mesh['grp'=2,'wide'=4,'red'=2,'tok'=2] {'wide'}, dimensions={1}, use_global_device_ids=true | all-gather | bytes 1167360 | tf_op jit(solution)/shard_map/all_gather | solution.py:329
  33.1 2.1 %collective-permute-done = f32[2,144]{1,0:T(2,128)S(1)} collective-permute-done((f32[2,144]{1,0:T(2,128)S(1)}, f32[2,144]{1,0:T(2,128)S(1)}, u32[]{:S(2)}, u32[]{:S(2)}) %collective-permute-start) | collective-permute-done | bytes 1184 | tf_op jit(solution)/shard_map/ppermute | solution.py:296
  35.8 1.8 collective-permute-done.1
  37.6 5.6 %fusion = f32[288,3072]{1,0:T(8,128)S(1)} fusion(bf16[1536,6144]{1,0:T(8,128)(2,1)} %refs_2_.10, bf16[144,1536]{1,0:T(8,128)(2,1)S(1)} %collective-permute-done.1, bf16[144,1536]{1,0:T(8,128)(2,1)S(1)} %get-tuple-element.45), kind=kOutput, calls=%fused_computation | convolution fusion | flops 2719678464 | bytes 13860864 | tf_op jit(solution)/shard_map/dot_general | solution.py:343
  45.8 2.9 %fusion.2 = f32[288,3072]{1,0:T(8,128)S(1)} fusion(bf16[1536,6144]{1,0:T(8,128)(2,1)S(1)} %bitcast.27, bf16[144,1536]{1,0:T(8,128)(2,1)S(1)} %collective-permute-done.1, bf16[144,1536]{1,0:T(8,128)(2,1)S(1)} %get-tuple-element.45), kind=kOutput, calls=%fused_computation.2 | convolution fusion | flops 2719678464 | bytes 13860864 | tf_op jit(solution)/shard_map/dot_general | solution.py:343
  53.6 17.1 %all_gather.7 = bf16[112,3072]{1,0:T(8,128)(2,1)S(1)} all-gather(bf16[112,768]{1,0:T(8,128)(2,1)S(1)} %slice_add_fusion.2), channel_id=1, replica_groups=mesh['grp'=2,'wide'=4,'red'=2,'tok'=2] {'wide'}, dimensions={1}, use_global_device_ids=true | all-gather | bytes 860160 | tf_op jit(solution)/shard_map/all_gather | solution.py:354
  79.2 4.7 %shard_map.83 = (bf16[112,3072]{1,0:T(8,128)(2,1)S(1)}, bf16[112,3072]{1,0:T(8,128)(2,1)S(1)}) custom-call(bf16[112,1536]{1,0:T(8,128)(2,1)S(1)} %get-tuple-element.48.refs_0_, bf16[112,1536]{1,0:T(8,128)(2,1)S(1)} %collective-permute-done.7.refs_1_, bf16[1536,6144]{1,0:T(8,128)(2,1)} %refs_2_.10), custom_call_target="tpu_custom_call" | custom-call | tf_op jit(solution)/shard_map/pallas_call | solution.py:60
  84.1 4.7 %shard_map.84 = (bf16[112,3072]{1,0:T(8,128)(2,1)S(1)}, bf16[112,3072]{1,0:T(8,128)(2,1)S(1)}) custom-call(bf16[112,1536]{1,0:T(8,128)(2,1)S(1)} %get-tuple-element.48.refs_0_, bf16[112,1536]{1,0:T(8,128)(2,1)S(1)} %collective-permute-done.7.refs_1_, bf16[1536,6144]{1,0:T(8,128)(2,1)} %refs_2_.10, bf16[112,3072]{1,0:T(8,128)(2,1)S(1)} %get-tuple-element.23.refs_3_.refs_0_), custom_call_target="tpu_custom_call" | custom-call | tf_op jit(solution)/shard_map/pallas_call | solution.py:60
  91.4 4.4 %collective-permute-done.3.refs_1_ = bf16[144,3072]{1,0:T(8,128)(2,1)S(1)} collective-permute-done((bf16[144,3072]{1,0:T(8,128)(2,1)S(1)}, bf16[144,3072]{1,0:T(8,128)(2,1)S(1)}, u32[]{:S(2)}, u32[]{:S(2)}) %collective-permute-start.3) | collective-permute-done | bytes 884768 | tf_op jit(solution)/shard_map/ppermute | solution.py:296
  98.0 2.4 %collective-permute-done.10.refs_1_ = bf16[256,384]{1,0:T(8,128)(2,1)S(1)} collective-permute-done((bf16[256,384]{1,0:T(8,128)(2,1)S(1)}, bf16[256,384]{1,0:T(8,128)(2,1)S(1)}, u32[]{:S(2)}, u32[]{:S(2)}) %collective-permute-start.10) | collective-permute-done | bytes 196640 | tf_op jit(solution)/shard_map/ppermute | solution.py:290
  101.1 12.1 %collective-permute-done.11.refs_1_ = bf16[256,384]{1,0:T(8,128)(2,1)S(1)} collective-permute-done((bf16[256,384]{1,0:T(8,128)(2,1)S(1)}, bf16[256,384]{1,0:T(8,128)(2,1)S(1)}, u32[]{:S(2)}, u32[]{:S(2)}) %collective-permute-start.11) | collective-permute-done | bytes 196640 | tf_op jit(solution)/shard_map/ppermute | solution.py:296
  116.1 5.4 %shard_map.91 = (f32[144,1536]{1,0:T(8,128)S(1)}, f32[144,1536]{1,0:T(8,128)S(1)}) custom-call(bf16[144,3072]{1,0:T(8,128)(2,1)S(1)} %shard_map.82.refs_2_.refs_0_, bf16[144,3072]{1,0:T(8,128)(2,1)S(1)} %collective-permute-done.9.refs_1_, bf16[6144,1536]{1,0:T(8,128)(2,1)} %refs_2_.17, bf16[256,128]{1,0:T(8,128)(2,1)S(1)} %shard_map.88.refs_3_, ...), custom_call_target="tpu_custom_call" | custom-call | tf_op jit(solution)/shard_map/pallas_call | solution.py:60
  122.5 5.3 %shard_map.93 = (bf16[144,1536]{1,0:T(8,128)(2,1)S(1)}, bf16[144,1536]{1,0:T(8,128)(2,1)S(1)}) custom-call(bf16[144,3072]{1,0:T(8,128)(2,1)S(1)} %shard_map.86.refs_4_.refs_0_, bf16[144,3072]{1,0:T(8,128)(2,1)S(1)} %collective-permute-done.8.refs_1_, bf16[6144,1536]{1,0:T(8,128)(2,1)} %refs_2_.17, f32[144,1536]{1,0:T(8,128)S(1)} %get-tuple-element.29.refs_2_.refs_3_, ...), custom_call_target="tpu_custom_call" | custom-call | tf_op jit(solution)/shard_map/pallas_call | solution.py:60
  128.1 1.6 collective-permute-done.16.refs_1_
  132.4 10.6 %collective-permute-done.17.refs_1_ = bf16[64,3072]{1,0:T(8,128)(2,1)S(1)} collective-permute-done((bf16[64,3072]{1,0:T(8,128)(2,1)S(1)}, bf16[64,3072]{1,0:T(8,128)(2,1)S(1)}, u32[]{:S(2)}, u32[]{:S(2)}) %collective-permute-start.17) | collective-permute-done | bytes 393248 | tf_op jit(solution)/shard_map/ppermute | solution.py:296
  146.9 5.2 %shard_map.96 = (f32[64,1536]{1,0:T(8,128)S(1)}, f32[64,1536]{1,0:T(8,128)S(1)}) custom-call(bf16[64,3072]{1,0:T(8,128)(2,1)S(1)} %shard_map.92.refs_8_.refs_0_.refs_2_, bf16[64,3072]{1,0:T(8,128)(2,1)S(1)} %collective-permute-done.19.refs_1_, bf16[6144,1536]{1,0:T(8,128)(2,1)} %refs_2_.17, bf16[64,3072]{1,0:T(8,128)(2,1)S(1)} %shard_map.95.refs_3_.refs_0_, ...), custom_call_target="tpu_custom_call" | custom-call | tf_op jit(solution)/shard_map/pallas_call | solution.py:60
  152.0 2.5 %collective-permute-done.20.refs_1_ = bf16[48,3072]{1,0:T(8,128)(2,1)S(1)} collective-permute-done((bf16[48,3072]{1,0:T(8,128)(2,1)S(1)}, bf16[48,3072]{1,0:T(8,128)(2,1)S(1)}, u32[]{:S(2)}, u32[]{:S(2)}) %collective-permute-start.20) | collective-permute-done | bytes 294944 | tf_op jit(solution)/shard_map/ppermute | solution.py:296
  155.0 4.4 %shard_map.99 = (bf16[64,1536]{1,0:T(8,128)(2,1)S(1)}, bf16[64,1536]{1,0:T(8,128)(2,1)S(1)}) custom-call(bf16[64,3072]{1,0:T(8,128)(2,1)S(1)} %shard_map.95.refs_3_.refs_0_, bf16[64,3072]{1,0:T(8,128)(2,1)S(1)} %collective-permute-done.18.refs_1_, bf16[6144,1536]{1,0:T(8,128)(2,1)} %refs_2_.17, f32[64,1536]{1,0:T(8,128)S(1)} %get-tuple-element.33.refs_2_.refs_3_, ...), custom_call_target="tpu_custom_call" | custom-call | tf_op jit(solution)/shard_map/pallas_call | solution.py:60
  161.4 4.4 %shard_map.102 = (f32[48,1536]{1,0:T(8,128)S(1)}, f32[48,1536]{1,0:T(8,128)S(1)}) custom-call(bf16[48,3072]{1,0:T(8,128)(2,1)S(1)} %shard_map.98.refs_8_.refs_0_, bf16[48,3072]{1,0:T(8,128)(2,1)S(1)} %collective-permute-done.22.refs_1_, bf16[6144,1536]{1,0:T(8,128)(2,1)} %refs_2_.17, bf16[48,3072]{1,0:T(8,128)(2,1)S(1)} %shard_map.101.refs_3_.refs_0_), custom_call_target="tpu_custom_call" | custom-call | tf_op jit(solution)/shard_map/pallas_call | solution.py:60
  167.7 5.2 %shard_map.104 = (bf16[48,1536]{1,0:T(8,128)(2,1)S(1)}, bf16[48,1536]{1,0:T(8,128)(2,1)S(1)}) custom-call(bf16[48,3072]{1,0:T(8,128)(2,1)S(1)} %shard_map.101.refs_3_.refs_0_, bf16[48,3072]{1,0:T(8,128)(2,1)S(1)} %collective-permute-done.24.refs_1_, bf16[6144,1536]{1,0:T(8,128)(2,1)} %refs_2_.17, f32[48,1536]{1,0:T(8,128)S(1)} %get-tuple-element.37.refs_4_.refs_3_, ...), custom_call_target="tpu_custom_call" | custom-call | tf_op jit(solution)/shard_map/pallas_call | solution.py:60
  174.4 2.0 %collective-permute-start.26 = (bf16[48,768]{1,0:T(8,128)(2,1)S(1)}, bf16[48,768]{1,0:T(8,128)(2,1)S(1)}, u32[]{:S(2)}, u32[]{:S(2)}) collective-permute-start(bf16[48,768]{1,0:T(8,128)(2,1)S(1)} %get-tuple-element.49), channel_id=1, source_target_pairs={{0,12},{4,8},{8,4},{12,0},{1,13},{5,9},{9,5},{13,1},{2,14},{6,10},... | collective-permute-start | bytes 221192 | tf_op jit(solution)/shard_map/ppermute | solution.py:313
  176.4 2.4 %collective-permute-start.28 = (bf16[48,768]{1,0:T(8,128)(2,1)S(1)}, bf16[48,768]{1,0:T(8,128)(2,1)S(1)}, u32[]{:S(2)}, u32[]{:S(2)}) collective-permute-start(bf16[48,768]{1,0:T(8,128)(2,1)S(1)} %get-tuple-element.50), channel_id=1, source_target_pairs={{0,4},{4,0},{8,12},{12,8},{1,5},{5,1},{9,13},{13,9},{2,6},{6,2},{1... | collective-permute-start | bytes 221192 | tf_op jit(solution)/shard_map/ppermute | solution.py:313
  178.9 3.5 %collective-permute-done.26 = bf16[48,768]{1,0:T(8,128)(2,1)S(1)} collective-permute-done((bf16[48,768]{1,0:T(8,128)(2,1)S(1)}, bf16[48,768]{1,0:T(8,128)(2,1)S(1)}, u32[]{:S(2)}, u32[]{:S(2)}) %collective-permute-start.26) | collective-permute-done | bytes 73760 | tf_op jit(solution)/shard_map/ppermute | solution.py:313
  182.4 5.5 %collective-permute-done.27 = bf16[48,768]{1,0:T(8,128)(2,1)S(1)} collective-permute-done((bf16[48,768]{1,0:T(8,128)(2,1)S(1)}, bf16[48,768]{1,0:T(8,128)(2,1)S(1)}, u32[]{:S(2)}, u32[]{:S(2)}) %collective-permute-start.27) | collective-permute-done | bytes 73760 | tf_op jit(solution)/shard_map/ppermute | solution.py:313
  (144 shorter events, 43.9 us)
Async XLA Ops:
  6.5 159.4 %reduce-scatter.3.cloned.1.call-start = ((), (), s32[]{:S(2)}) async-start(), calls=%async_computation.2 | async-start | bytes 1105920 | tf_op jit(solution)/shard_map/reduce_scatter | solution.py:388
  31.5 3.6 %collective-permute-start = (f32[2,144]{1,0:T(2,128)S(1)}, f32[2,144]{1,0:T(2,128)S(1)}, u32[]{:S(2)}, u32[]{:S(2)}) collective-permute-start(f32[2,144]{1,0:T(2,128)S(1)} %pad_maximum_fusion.7), channel_id=1, source_target_pairs={{0,2},{2,0},{1,3},{3,1},{4,6},{6,4},{5,7},{7,5},{8,10},{10,8},{9,1... | collective-permute-start | bytes 3464 | tf_op jit(solution)/shard_map/ppermute | solution.py:296
  43.4 5.6 %collective-permute-start.4 = (bf16[144,3072]{1,0:T(8,128)(2,1)S(1)}, bf16[144,3072]{1,0:T(8,128)(2,1)S(1)}, u32[]{:S(2)}, u32[]{:S(2)}) collective-permute-start(bf16[144,3072]{1,0:T(8,128)(2,1)S(1)} %slice.143), channel_id=1, source_target_pairs={{0,1},{1,0},{2,3},{3,2},{4,5},{5,4},{6,7},{7,6},{8,9},{9,8},{10,11... | collective-permute-start | bytes 2654216 | tf_op jit(solution)/shard_map/ppermute | solution.py:290
  49.2 22.0 %collective-permute-start.5 = (bf16[144,3072]{1,0:T(8,128)(2,1)S(1)}, bf16[144,3072]{1,0:T(8,128)(2,1)S(1)}, u32[]{:S(2)}, u32[]{:S(2)}) collective-permute-start(bf16[144,3072]{1,0:T(8,128)(2,1)S(1)} %fusion.8.refs_0_), channel_id=1, source_target_pairs={{0,2},{2,0},{1,3},{3,1},{4,6},{6,4},{5,7},{7,5},{8,10},{10,8},{9,1... | collective-permute-start | bytes 2654216 | tf_op jit(solution)/shard_map/ppermute | solution.py:296
  73.4 3.6 %collective-permute-start.6 = (f32[2,112]{1,0:T(2,128)S(1)}, f32[2,112]{1,0:T(2,128)S(1)}, u32[]{:S(2)}, u32[]{:S(2)}) collective-permute-start(f32[2,112]{1,0:T(2,128)S(1)} %pad_maximum_fusion.8), channel_id=1, source_target_pairs={{0,2},{2,0},{1,3},{3,1},{4,6},{6,4},{5,7},{7,5},{8,10},{10,8},{9,1... | collective-permute-start | bytes 2696 | tf_op jit(solution)/shard_map/ppermute | solution.py:296
  75.0 20.8 %collective-permute-start.3 = (bf16[144,3072]{1,0:T(8,128)(2,1)S(1)}, bf16[144,3072]{1,0:T(8,128)(2,1)S(1)}, u32[]{:S(2)}, u32[]{:S(2)}) collective-permute-start(bf16[144,3072]{1,0:T(8,128)(2,1)S(1)} %fusion.9.refs_0_), channel_id=1, source_target_pairs={{0,2},{2,0},{1,3},{3,1},{4,6},{6,4},{5,7},{7,5},{8,10},{10,8},{9,1... | collective-permute-start | bytes 2654216 | tf_op jit(solution)/shard_map/ppermute | solution.py:296
  77.6 38.6 %collective-permute-start.9 = (bf16[144,3072]{1,0:T(8,128)(2,1)S(1)}, bf16[144,3072]{1,0:T(8,128)(2,1)S(1)}, u32[]{:S(2)}, u32[]{:S(2)}) collective-permute-start(bf16[144,3072]{1,0:T(8,128)(2,1)S(1)} %shard_map.82.refs_2_.refs_0_), channel_id=1, source_target_pairs={{0,1},{1,0},{2,3},{3,2},{4,5},{5,4},{6,7},{7,6},{8,9},{9,8},{10,11... | collective-permute-start | bytes 2654216 | tf_op jit(solution)/shard_map/ppermute | solution.py:290
  83.9 13.5 %collective-permute-start.12 = (bf16[112,3072]{1,0:T(8,128)(2,1)S(1)}, bf16[112,3072]{1,0:T(8,128)(2,1)S(1)}, u32[]{:S(2)}, u32[]{:S(2)}) collective-permute-start(bf16[112,3072]{1,0:T(8,128)(2,1)S(1)} %get-tuple-element.27), channel_id=1, source_target_pairs={{0,1},{1,0},{2,3},{3,2},{4,5},{5,4},{6,7},{7,6},{8,9},{9,8},{10,11... | collective-permute-start | bytes 2064392 | tf_op jit(solution)/shard_map/ppermute | solution.py:290
  96.7 25.3 %collective-permute-start.8 = (bf16[144,3072]{1,0:T(8,128)(2,1)S(1)}, bf16[144,3072]{1,0:T(8,128)(2,1)S(1)}, u32[]{:S(2)}, u32[]{:S(2)}) collective-permute-start(bf16[144,3072]{1,0:T(8,128)(2,1)S(1)} %shard_map.86.refs_4_.refs_0_), channel_id=1, source_target_pairs={{0,1},{1,0},{2,3},{3,2},{4,5},{5,4},{6,7},{7,6},{8,9},{9,8},{10,11... | collective-permute-start | bytes 2654216 | tf_op jit(solution)/shard_map/ppermute | solution.py:290
  96.7 18.5 %collective-permute-start.13 = (bf16[112,3072]{1,0:T(8,128)(2,1)S(1)}, bf16[112,3072]{1,0:T(8,128)(2,1)S(1)}, u32[]{:S(2)}, u32[]{:S(2)}) collective-permute-start(bf16[112,3072]{1,0:T(8,128)(2,1)S(1)} %get-tuple-element.28), channel_id=1, source_target_pairs={{0,1},{1,0},{2,3},{3,2},{4,5},{5,4},{6,7},{7,6},{8,9},{9,8},{10,11... | collective-permute-start | bytes 2064392 | tf_op jit(solution)/shard_map/ppermute | solution.py:290
  97.4 24.1 %collective-permute-start.15 = (bf16[64,3072]{1,0:T(8,128)(2,1)S(1)}, bf16[64,3072]{1,0:T(8,128)(2,1)S(1)}, u32[]{:S(2)}, u32[]{:S(2)}) collective-permute-start(bf16[64,3072]{1,0:T(8,128)(2,1)S(1)} %shard_map.89.refs_4_.refs_0_), channel_id=1, source_target_pairs={{0,2},{2,0},{1,3},{3,1},{4,6},{6,4},{5,7},{7,5},{8,10},{10,8},{9,1... | collective-permute-start | bytes 1179656 | tf_op jit(solution)/shard_map/ppermute | solution.py:296
  100.5 12.7 %collective-permute-start.11 = (bf16[256,384]{1,0:T(8,128)(2,1)S(1)}, bf16[256,384]{1,0:T(8,128)(2,1)S(1)}, u32[]{:S(2)}, u32[]{:S(2)}) collective-permute-start(bf16[256,384]{1,0:T(8,128)(2,1)S(1)} %shard_map.87.refs_0_), channel_id=1, source_target_pairs={{0,2},{2,0},{1,3},{3,1},{4,6},{6,4},{5,7},{7,5},{8,10},{10,8},{9,1... | collective-permute-start | bytes 589832 | tf_op jit(solution)/shard_map/ppermute | solution.py:296
  131.5 57.7 %reduce-scatter.5.cloned.1.call-start = ((), (), s32[]{:S(2)}) async-start(), calls=%async_computation.3 | async-start | bytes 491520 | tf_op jit(solution)/shard_map/reduce_scatter | solution.py:388
  131.7 11.2 %collective-permute-start.17 = (bf16[64,3072]{1,0:T(8,128)(2,1)S(1)}, bf16[64,3072]{1,0:T(8,128)(2,1)S(1)}, u32[]{:S(2)}, u32[]{:S(2)}) collective-permute-start(bf16[64,3072]{1,0:T(8,128)(2,1)S(1)} %shard_map.90.refs_5_.refs_0_), channel_id=1, source_target_pairs={{0,2},{2,0},{1,3},{3,1},{4,6},{6,4},{5,7},{7,5},{8,10},{10,8},{9,1... | collective-permute-start | bytes 1179656 | tf_op jit(solution)/shard_map/ppermute | solution.py:296
  132.4 14.5 %collective-permute-start.19 = (bf16[64,3072]{1,0:T(8,128)(2,1)S(1)}, bf16[64,3072]{1,0:T(8,128)(2,1)S(1)}, u32[]{:S(2)}, u32[]{:S(2)}) collective-permute-start(bf16[64,3072]{1,0:T(8,128)(2,1)S(1)} %shard_map.92.refs_8_.refs_0_.refs_2_), channel_id=1, source_target_pairs={{0,1},{1,0},{2,3},{3,2},{4,5},{5,4},{6,7},{7,6},{8,9},{9,8},{10,11... | collective-permute-start | bytes 1179656 | tf_op jit(solution)/shard_map/ppermute | solution.py:290
  144.5 10.5 %collective-permute-start.18 = (bf16[64,3072]{1,0:T(8,128)(2,1)S(1)}, bf16[64,3072]{1,0:T(8,128)(2,1)S(1)}, u32[]{:S(2)}, u32[]{:S(2)}) collective-permute-start(bf16[64,3072]{1,0:T(8,128)(2,1)S(1)} %shard_map.95.refs_3_.refs_0_), channel_id=1, source_target_pairs={{0,1},{1,0},{2,3},{3,2},{4,5},{5,4},{6,7},{7,6},{8,9},{9,8},{10,11... | collective-permute-start | bytes 1179656 | tf_op jit(solution)/shard_map/ppermute | solution.py:290
  144.6 9.9 %collective-permute-start.20 = (bf16[48,3072]{1,0:T(8,128)(2,1)S(1)}, bf16[48,3072]{1,0:T(8,128)(2,1)S(1)}, u32[]{:S(2)}, u32[]{:S(2)}) collective-permute-start(bf16[48,3072]{1,0:T(8,128)(2,1)S(1)} %shard_map.97.refs_0_), channel_id=1, source_target_pairs={{0,2},{2,0},{1,3},{3,1},{4,6},{6,4},{5,7},{7,5},{8,10},{10,8},{9,1... | collective-permute-start | bytes 884744 | tf_op jit(solution)/shard_map/ppermute | solution.py:296
  145.3 15.1 %collective-permute-start.23 = (bf16[48,3072]{1,0:T(8,128)(2,1)S(1)}, bf16[48,3072]{1,0:T(8,128)(2,1)S(1)}, u32[]{:S(2)}, u32[]{:S(2)}) collective-permute-start(bf16[48,3072]{1,0:T(8,128)(2,1)S(1)} %shard_map.100.refs_0_), channel_id=1, source_target_pairs={{0,2},{2,0},{1,3},{3,1},{4,6},{6,4},{5,7},{7,5},{8,10},{10,8},{9,1... | collective-permute-start | bytes 884744 | tf_op jit(solution)/shard_map/ppermute | solution.py:296
  154.9 6.5 %collective-permute-start.22 = (bf16[48,3072]{1,0:T(8,128)(2,1)S(1)}, bf16[48,3072]{1,0:T(8,128)(2,1)S(1)}, u32[]{:S(2)}, u32[]{:S(2)}) collective-permute-start(bf16[48,3072]{1,0:T(8,128)(2,1)S(1)} %shard_map.98.refs_8_.refs_0_), channel_id=1, source_target_pairs={{0,1},{1,0},{2,3},{3,2},{4,5},{5,4},{6,7},{7,6},{8,9},{9,8},{10,11... | collective-permute-start | bytes 884744 | tf_op jit(solution)/shard_map/ppermute | solution.py:290
  160.8 6.8 %collective-permute-start.24 = (bf16[48,3072]{1,0:T(8,128)(2,1)S(1)}, bf16[48,3072]{1,0:T(8,128)(2,1)S(1)}, u32[]{:S(2)}, u32[]{:S(2)}) collective-permute-start(bf16[48,3072]{1,0:T(8,128)(2,1)S(1)} %shard_map.101.refs_3_.refs_0_), channel_id=1, source_target_pairs={{0,1},{1,0},{2,3},{3,2},{4,5},{5,4},{6,7},{7,6},{8,9},{9,8},{10,11... | collective-permute-start | bytes 884744 | tf_op jit(solution)/shard_map/ppermute | solution.py:290
  160.9 5.0 %collective-permute-start.21 = (bf16[64,1536]{1,0:T(8,128)(2,1)S(1)}, bf16[64,1536]{1,0:T(8,128)(2,1)S(1)}, u32[]{:S(2)}, u32[]{:S(2)}) collective-permute-start(bf16[64,1536]{1,0:T(8,128)(2,1)S(1)} %get-tuple-element.36), channel_id=1, source_target_pairs={{0,1},{1,0},{2,3},{3,2},{4,5},{5,4},{6,7},{7,6},{8,9},{9,8},{10,11... | collective-permute-start | bytes 589832 | tf_op jit(solution)/shard_map/ppermute | solution.py:290
  174.4 8.0 %collective-permute-start.26 = (bf16[48,768]{1,0:T(8,128)(2,1)S(1)}, bf16[48,768]{1,0:T(8,128)(2,1)S(1)}, u32[]{:S(2)}, u32[]{:S(2)}) collective-permute-start(bf16[48,768]{1,0:T(8,128)(2,1)S(1)} %get-tuple-element.49), channel_id=1, source_target_pairs={{0,12},{4,8},{8,4},{12,0},{1,13},{5,9},{9,5},{13,1},{2,14},{6,10},... | collective-permute-start | bytes 221192 | tf_op jit(solution)/shard_map/ppermute | solution.py:313
  176.4 11.5 %collective-permute-start.27 = (bf16[48,768]{1,0:T(8,128)(2,1)S(1)}, bf16[48,768]{1,0:T(8,128)(2,1)S(1)}, u32[]{:S(2)}, u32[]{:S(2)}) collective-permute-start(bf16[48,768]{1,0:T(8,128)(2,1)S(1)} %get-tuple-element.51), channel_id=1, source_target_pairs={{0,8},{4,12},{8,0},{12,4},{1,9},{5,13},{9,1},{13,5},{2,10},{6,14},... | collective-permute-start | bytes 221192 | tf_op jit(solution)/shard_map/ppermute | solution.py:313
  176.4 11.5 %collective-permute-start.28 = (bf16[48,768]{1,0:T(8,128)(2,1)S(1)}, bf16[48,768]{1,0:T(8,128)(2,1)S(1)}, u32[]{:S(2)}, u32[]{:S(2)}) collective-permute-start(bf16[48,768]{1,0:T(8,128)(2,1)S(1)} %get-tuple-element.50), channel_id=1, source_target_pairs={{0,4},{4,0},{8,12},{12,8},{1,5},{5,1},{9,13},{13,9},{2,6},{6,2},{1... | collective-permute-start | bytes 221192 | tf_op jit(solution)/shard_map/ppermute | solution.py:313
  (25 other events, 135.3 us)
Sparse Core Ops, SparseCore 0:
  131.6 23.2 reduce-scatter.2
  167.8 21.4 reduce-scatter.4

commit v7 on v6

--- a/solution.py
+++ b/solution.py
@@ -11,7 +11,7 @@
 D = 6144
 PATCHES = 256
 EPS = 1e-06
-SHARES = (9, 4, 3)
+SHARES = (8, 5, 3)
 PIECES = (1, 1)
 AHEAD = 4
 GAIN_ROWS = 8
@@ -353,19 +353,19 @@
         rest = tokens[first:] + nothing(leads[-1]).astype(BF16)
         rest = lax.all_gather(rest, "wide", axis=1, tiled=True)
         rest_pair = normed(rest.astype(F32) + nothing(arrived))
-        halves, before = [], []
+        pair = [jnp.concatenate(p, axis=0) for p in zip(lead_pair, rest_pair)]
+        near, far = project_rows(*pair, qkv_rows, slice(0, qkv_rows.shape[1]))
+        halves, before = [], [near]
+        qkv = sum_rows(near, swap(far), slice(0, tokens.shape[0]))
         for piece in pieces:
             near, far = project_rows(*rest_pair, w_up, piece, before)
             halves.append((near, swap(far)))
             before = [near]
-        pair = [jnp.concatenate(p, axis=0) for p in zip(lead_pair, rest_pair)]
-        near, far = project_rows(*pair, qkv_rows, slice(0, qkv_rows.shape[1]), before)
-        qkv = sum_rows(near, swap(far), slice(0, tokens.shape[0]))
 
         order = [(c, p) for c in range(n) for p in range(len(pieces))]
         outs, scattered = [], []
-        terms, waiting, firsts = (), None, []
-        earlier = [near]
+        terms, waiting = (), None
+        earlier = [near, qkv]
 
         def output(at, have, terms, earlier):
             c, p = order[at]
@@ -388,30 +388,24 @@
             scattered.append(lax.psum_scatter(full, "wide", scatter_dimension=1, tiled=True))
             return full
 
-        def sums_of(p, part, before):
-            return sum_rows(*halves[p], part, [before])
-
-        after_lead = [
-            sums_of(p, slice(0, cuts[1].stop - first), arrived) for p in range(len(pieces))
-        ]
-        hidden = None
+        hidden, ready = None, lead_parts
         for at, (c, p) in enumerate(order):
-            if c:
-                part = slice(cuts[c].start - first, cuts[c].stop - first)
-                parts = all_red(sums_of(p, part, firsts[c - 1]) if c > 1 else after_lead[p])
-            else:
-                parts = lead_parts[p]
             if at:
-                arrived = gelu_sum(parts, earlier)
+                arrived = gelu_sum(ready[p], earlier)
                 earlier = [arrived]
-            if p == 0:
-                firsts.append(arrived)
-            if at == 1:
+            if p == (0 if c else len(pieces) - 1) and c < n - 1:
+                part = slice(cuts[c + 1].start - first, cuts[c + 1].stop - first)
+                sums = [sum_rows(*half, part, [arrived]) for half in halves]
+                coming = [all_red(x) for x in sums]
+                earlier = earlier + sums
+            if at == len(pieces):
                 attended = attend(all_red(qkv), q_gain, k_gain, earlier)
                 attended_other = swap(attended)
-                earlier = [attended, *after_lead]
+                earlier = [attended]
+            if p == len(pieces) - 1 and c < n - 1:
+                ready = coming
             if waiting is not None and not scattered:
-                earlier.append(scatter(*waiting, []))
+                earlier.append(scatter(*waiting, earlier))
                 waiting = None
             if at:
                 terms = output(at - 1, hidden, terms, earlier)

time: 198 us -> 184 us (0.929)
  waiting for transfers between devices: 55 us -> 41.6 us
  starting transfers between devices: 16.9 us -> 20 us
    ppermute x9, waiting for transfers between devices: 34.7 us -> 23.2 us  [all_red(): parts.append(lax.ppermute(x, 'red', pairs))]
    ppermute x17, waiting for transfers between devices: 9.97 us -> 4.79 us  [swap(): return lax.ppermute(x, 'tok', [(0, 1), (1, 0)])]
    ppermute x9, starting transfers between devices: 9.18 us -> 12 us  [all_red(): parts.append(lax.ppermute(x, 'red', pairs))]
    unnamed x37 -> x19, local copies, waits for them, and re-layouts: 7.42 us -> 5.57 us
  transfers between devices with their start and end apart: 31 -> 31, of which waited for: 18 -> 17; matrix products, arithmetic and copies ran while one was open for 3% -> 2% of each run, Pallas kernels for 20% -> 25%
where the time goes in v7:
time: 184 us
  Pallas kernels  47.1 us (26%)
  waiting for transfers between devices  41.6 us (23%)
  blocking collectives  39.9 us (22%)
  starting transfers between devices  20 us (11%)
  between operations  15.2 us (8%)
  local copies, waits for them, and re-layouts  8.6 us (5%)
  matrix products  7.91 us (4%)
  other arithmetic  3.75 us (2%)
    pallas_call x23, Pallas kernels, call(): pl.pallas_call(body, in_specs=list(specs) + [corner_of(a) for a in earlie...  47.1 us
    ppermute x9, waiting for transfers between devices, all_red(): parts.append(lax.ppermute(x, 'red', pairs))  23.2 us
    all_gather x1, blocking collectives, body(): lead = lax.all_gather(lead, 'wide', axis=1, tiled=True)  21.9 us
    all_gather x1, blocking collectives, body(): rest = lax.all_gather(rest, 'wide', axis=1, tiled=True)  18 us
    ppermute x9, starting transfers between devices, all_red(): parts.append(lax.ppermute(x, 'red', pairs))  12 us
    ppermute x3, waiting for transfers between devices, collect(): total = total + lax.ppermute(block(chip ^ k), 'wide', pairs).astype(F32)  10.7 us
    dot_general x2, matrix products, project(): part = jnp.dot(both, weight, preferred_element_type=F32)  7.91 us
    unnamed x19, local copies, waits for them, and re-layouts  5.57 us
  transfers between devices with their start and end apart: 31, of which 17 were waited for; matrix products, arithmetic and copies ran while one was open for 2% of the time, Pallas kernels for 25%

profile of v7, /device:TPU:0, one launch (start us, length us, event | category | flops | bytes accessed | tf_op | source)
XLA Modules:
  0.0 184.0 jit_solution(3244002510687411620)
XLA Ops:
  8.2 21.9 %all_gather.6 = bf16[136,3072]{1,0:T(8,128)(2,1)S(1)} all-gather(bf16[136,768]{1,0:T(8,128)(2,1)S(1)} %pad_maximum_fusion.6), channel_id=1, replica_groups=mesh['grp'=2,'wide'=4,'red'=2,'tok'=2] {'wide'}, dimensions={1}, use_global_device_ids=true | all-gather | bytes 1044480 | tf_op jit(solution)/shard_map/all_gather | solution.py:329
  31.9 2.1 %collective-permute-done = f32[2,128]{1,0:T(2,128)S(1)} collective-permute-done((f32[2,128]{1,0:T(2,128)S(1)}, f32[2,128]{1,0:T(2,128)S(1)}, u32[]{:S(2)}, u32[]{:S(2)}) %collective-permute-start) | collective-permute-done | bytes 1056 | tf_op jit(solution)/shard_map/ppermute | solution.py:296
  36.2 5.3 %fusion = f32[256,3072]{1,0:T(8,128)S(1)} fusion(bf16[1536,6144]{1,0:T(8,128)(2,1)} %refs_2_.10, bf16[128,1536]{1,0:T(8,128)(2,1)S(1)} %get-tuple-element.48, bf16[128,1536]{1,0:T(8,128)(2,1)S(1)} %collective-permute-done.1), kind=kOutput, calls=%fused_computation | convolution fusion | flops 2417491968 | bytes 13369344 | tf_op jit(solution)/shard_map/dot_general | solution.py:343
  41.8 3.5 %copy-done.6 = bf16[1536,6144]{1,0:T(8,128)(2,1)S(1)} copy-done((bf16[1536,6144]{1,0:T(8,128)(2,1)S(1)}, bf16[1536,6144]{1,0:T(8,128)(2,1)}, u32[]{:S(2)}) %copy-start.6) | copy-done | bytes 18874392
  45.4 2.6 %fusion.2 = f32[256,3072]{1,0:T(8,128)S(1)} fusion(bf16[1536,6144]{1,0:T(8,128)(2,1)S(1)} %copy-done.6, bf16[128,1536]{1,0:T(8,128)(2,1)S(1)} %get-tuple-element.48, bf16[128,1536]{1,0:T(8,128)(2,1)S(1)} %collective-permute-done.1), kind=kOutput, calls=%fused_computation.2 | convolution fusion | flops 2417491968 | bytes 13369344 | tf_op jit(solution)/shard_map/dot_general | solution.py:343
  51.8 18.0 %all_gather.7 = bf16[128,3072]{1,0:T(8,128)(2,1)S(1)} all-gather(bf16[128,768]{1,0:T(8,128)(2,1)S(1)} %slice_add_fusion.2), channel_id=1, replica_groups=mesh['grp'=2,'wide'=4,'red'=2,'tok'=2] {'wide'}, dimensions={1}, use_global_device_ids=true | all-gather | bytes 983040 | tf_op jit(solution)/shard_map/all_gather | solution.py:354
  73.6 2.1 %collective-permute-done.6 = f32[2,128]{1,0:T(2,128)S(1)} collective-permute-done((f32[2,128]{1,0:T(2,128)S(1)}, f32[2,128]{1,0:T(2,128)S(1)}, u32[]{:S(2)}, u32[]{:S(2)}) %collective-permute-start.6) | collective-permute-done | bytes 1056 | tf_op jit(solution)/shard_map/ppermute | solution.py:296
  80.4 4.9 %shard_map.84 = (bf16[128,3072]{1,0:T(8,128)(2,1)S(1)}, bf16[128,3072]{1,0:T(8,128)(2,1)S(1)}) custom-call(bf16[128,1536]{1,0:T(8,128)(2,1)S(1)} %get-tuple-element.46.refs_0_, bf16[128,1536]{1,0:T(8,128)(2,1)S(1)} %collective-permute-done.7.refs_1_, bf16[1536,6144]{1,0:T(8,128)(2,1)} %refs_2_.10, bf16[256,384]{1,0:T(8,128)(2,1)S(1)} %get-tuple-element.23.refs_3_.refs_0_), custom_call_target="tpu_custom_call" | custom-call | tf_op jit(solution)/shard_map/pallas_call | solution.py:60
  85.9 4.9 %shard_map.85 = (bf16[128,3072]{1,0:T(8,128)(2,1)S(1)}, bf16[128,3072]{1,0:T(8,128)(2,1)S(1)}) custom-call(bf16[128,1536]{1,0:T(8,128)(2,1)S(1)} %get-tuple-element.46.refs_0_, bf16[128,1536]{1,0:T(8,128)(2,1)S(1)} %collective-permute-done.7.refs_1_, bf16[1536,6144]{1,0:T(8,128)(2,1)} %refs_2_.10, bf16[128,3072]{1,0:T(8,128)(2,1)S(1)} %get-tuple-element.24.refs_3_.refs_0_), custom_call_target="tpu_custom_call" | custom-call | tf_op jit(solution)/shard_map/pallas_call | solution.py:60
  91.4 4.8 %collective-permute-done.3.refs_1_ = bf16[128,3072]{1,0:T(8,128)(2,1)S(1)} collective-permute-done((bf16[128,3072]{1,0:T(8,128)(2,1)S(1)}, bf16[128,3072]{1,0:T(8,128)(2,1)S(1)}, u32[]{:S(2)}, u32[]{:S(2)}) %collective-permute-start.3) | collective-permute-done | bytes 786464 | tf_op jit(solution)/shard_map/ppermute | solution.py:296
  100.9 5.0 %shard_map.90 = (f32[128,1536]{1,0:T(8,128)S(1)}, f32[128,1536]{1,0:T(8,128)S(1)}) custom-call(bf16[128,3072]{1,0:T(8,128)(2,1)S(1)} %shard_map.82.refs_0_, bf16[128,3072]{1,0:T(8,128)(2,1)S(1)} %collective-permute-done.10.refs_1_, bf16[6144,1536]{1,0:T(8,128)(2,1)} %refs_2_.17, bf16[128,3072]{1,0:T(8,128)(2,1)S(1)} %shard_map.87.refs_2_.refs_3_.refs_0_, ...), custom_call_target="tpu_custom_call" | custom-call | tf_op jit(solution)/shard_map/pallas_call | solution.py:60
  105.9 5.2 %collective-permute-done.14.refs_1_ = bf16[80,3072]{1,0:T(8,128)(2,1)S(1)} collective-permute-done((bf16[80,3072]{1,0:T(8,128)(2,1)S(1)}, bf16[80,3072]{1,0:T(8,128)(2,1)S(1)}, u32[]{:S(2)}, u32[]{:S(2)}) %collective-permute-start.14) | collective-permute-done | bytes 491552 | tf_op jit(solution)/shard_map/ppermute | solution.py:296
  111.9 3.5 %collective-permute-done.13.refs_1_ = bf16[256,384]{1,0:T(8,128)(2,1)S(1)} collective-permute-done((bf16[256,384]{1,0:T(8,128)(2,1)S(1)}, bf16[256,384]{1,0:T(8,128)(2,1)S(1)}, u32[]{:S(2)}, u32[]{:S(2)}) %collective-permute-start.13) | collective-permute-done | bytes 196640 | tf_op jit(solution)/shard_map/ppermute | solution.py:296
  117.5 5.0 %shard_map.95 = (bf16[128,1536]{1,0:T(8,128)(2,1)S(1)}, bf16[128,1536]{1,0:T(8,128)(2,1)S(1)}) custom-call(bf16[128,3072]{1,0:T(8,128)(2,1)S(1)} %shard_map.87.refs_2_.refs_3_.refs_0_, bf16[128,3072]{1,0:T(8,128)(2,1)S(1)} %collective-permute-done.9.refs_1_, bf16[6144,1536]{1,0:T(8,128)(2,1)} %refs_2_.17, f32[128,1536]{1,0:T(8,128)S(1)} %get-tuple-element.29.refs_2_.refs_3_, ...), custom_call_target="tpu_custom_call" | custom-call | tf_op jit(solution)/shard_map/pallas_call | solution.py:60
  122.8 2.7 %collective-permute-done.17.refs_1_ = bf16[80,3072]{1,0:T(8,128)(2,1)S(1)} collective-permute-done((bf16[80,3072]{1,0:T(8,128)(2,1)S(1)}, bf16[80,3072]{1,0:T(8,128)(2,1)S(1)}, u32[]{:S(2)}, u32[]{:S(2)}) %collective-permute-start.17) | collective-permute-done | bytes 491552 | tf_op jit(solution)/shard_map/ppermute | solution.py:296
  129.9 5.3 %shard_map.98 = (f32[80,1536]{1,0:T(8,128)S(1)}, f32[80,1536]{1,0:T(8,128)S(1)}) custom-call(bf16[80,3072]{1,0:T(8,128)(2,1)S(1)} %shard_map.91.refs_2_.refs_4_.refs_0_, bf16[80,3072]{1,0:T(8,128)(2,1)S(1)} %collective-permute-done.19.refs_1_, bf16[6144,1536]{1,0:T(8,128)(2,1)} %refs_2_.17, bf16[80,3072]{1,0:T(8,128)(2,1)S(1)} %shard_map.96.refs_3_.refs_0_, ...), custom_call_target="tpu_custom_call" | custom-call | tf_op jit(solution)/shard_map/pallas_call | solution.py:60
  135.2 2.5 %collective-permute-done.20.refs_1_ = bf16[48,3072]{1,0:T(8,128)(2,1)S(1)} collective-permute-done((bf16[48,3072]{1,0:T(8,128)(2,1)S(1)}, bf16[48,3072]{1,0:T(8,128)(2,1)S(1)}, u32[]{:S(2)}, u32[]{:S(2)}) %collective-permute-start.20) | collective-permute-done | bytes 294944 | tf_op jit(solution)/shard_map/ppermute | solution.py:296
  138.2 4.7 %shard_map.100 = (bf16[80,1536]{1,0:T(8,128)(2,1)S(1)}, bf16[80,1536]{1,0:T(8,128)(2,1)S(1)}) custom-call(bf16[80,3072]{1,0:T(8,128)(2,1)S(1)} %shard_map.96.refs_3_.refs_0_, bf16[80,3072]{1,0:T(8,128)(2,1)S(1)} %collective-permute-done.18.refs_1_, bf16[6144,1536]{1,0:T(8,128)(2,1)} %refs_2_.17, f32[80,1536]{1,0:T(8,128)S(1)} %get-tuple-element.33.refs_2_.refs_3_, ...), custom_call_target="tpu_custom_call" | custom-call | tf_op jit(solution)/shard_map/pallas_call | solution.py:60
  144.2 4.5 %shard_map.102 = (f32[48,1536]{1,0:T(8,128)S(1)}, f32[48,1536]{1,0:T(8,128)S(1)}) custom-call(bf16[48,3072]{1,0:T(8,128)(2,1)S(1)} %shard_map.99.refs_8_.refs_0_, bf16[48,3072]{1,0:T(8,128)(2,1)S(1)} %collective-permute-done.22.refs_1_, bf16[6144,1536]{1,0:T(8,128)(2,1)} %refs_2_.17, bf16[48,3072]{1,0:T(8,128)(2,1)S(1)} %shard_map.101.refs_3_.refs_0_), custom_call_target="tpu_custom_call" | custom-call | tf_op jit(solution)/shard_map/pallas_call | solution.py:60
  151.7 5.2 %shard_map.104 = (bf16[48,1536]{1,0:T(8,128)(2,1)S(1)}, bf16[48,1536]{1,0:T(8,128)(2,1)S(1)}) custom-call(bf16[48,3072]{1,0:T(8,128)(2,1)S(1)} %shard_map.101.refs_3_.refs_0_, bf16[48,3072]{1,0:T(8,128)(2,1)S(1)} %collective-permute-done.24.refs_1_, bf16[6144,1536]{1,0:T(8,128)(2,1)} %refs_2_.17, f32[48,1536]{1,0:T(8,128)S(1)} %get-tuple-element.37.refs_4_.refs_3_, ...), custom_call_target="tpu_custom_call" | custom-call | tf_op jit(solution)/shard_map/pallas_call | solution.py:60
  158.4 1.7 collective-permute-start.26
  160.2 2.7 %collective-permute-start.28 = (bf16[48,768]{1,0:T(8,128)(2,1)S(1)}, bf16[48,768]{1,0:T(8,128)(2,1)S(1)}, u32[]{:S(2)}, u32[]{:S(2)}) collective-permute-start(bf16[48,768]{1,0:T(8,128)(2,1)S(1)} %get-tuple-element.50), channel_id=1, source_target_pairs={{0,4},{4,0},{8,12},{12,8},{1,5},{5,1},{9,13},{13,9},{2,6},{6,2},{1... | collective-permute-start | bytes 221192 | tf_op jit(solution)/shard_map/ppermute | solution.py:313
  162.9 4.0 %collective-permute-done.26 = bf16[48,768]{1,0:T(8,128)(2,1)S(1)} collective-permute-done((bf16[48,768]{1,0:T(8,128)(2,1)S(1)}, bf16[48,768]{1,0:T(8,128)(2,1)S(1)}, u32[]{:S(2)}, u32[]{:S(2)}) %collective-permute-start.26) | collective-permute-done | bytes 73760 | tf_op jit(solution)/shard_map/ppermute | solution.py:313
  167.0 6.6 %collective-permute-done.27 = bf16[48,768]{1,0:T(8,128)(2,1)S(1)} collective-permute-done((bf16[48,768]{1,0:T(8,128)(2,1)S(1)}, bf16[48,768]{1,0:T(8,128)(2,1)S(1)}, u32[]{:S(2)}, u32[]{:S(2)}) %collective-permute-start.27) | collective-permute-done | bytes 73760 | tf_op jit(solution)/shard_map/ppermute | solution.py:313
  (125 shorter events, 39.9 us)
Async XLA Ops:
  6.5 143.4 %reduce-scatter.3.cloned.1.call-start = ((), (), s32[]{:S(2)}) async-start(), calls=%async_computation.2 | async-start | bytes 983040 | tf_op jit(solution)/shard_map/reduce_scatter | solution.py:388
  30.4 3.6 %collective-permute-start = (f32[2,128]{1,0:T(2,128)S(1)}, f32[2,128]{1,0:T(2,128)S(1)}, u32[]{:S(2)}, u32[]{:S(2)}) collective-permute-start(f32[2,128]{1,0:T(2,128)S(1)} %pad_maximum_fusion.7), channel_id=1, source_target_pairs={{0,2},{2,0},{1,3},{3,1},{4,6},{6,4},{5,7},{7,5},{8,10},{10,8},{9,1... | collective-permute-start | bytes 3080 | tf_op jit(solution)/shard_map/ppermute | solution.py:296
  41.6 6.6 %collective-permute-start.4 = (bf16[128,3072]{1,0:T(8,128)(2,1)S(1)}, bf16[128,3072]{1,0:T(8,128)(2,1)S(1)}, u32[]{:S(2)}, u32[]{:S(2)}) collective-permute-start(bf16[128,3072]{1,0:T(8,128)(2,1)S(1)} %slice.145), channel_id=1, source_target_pairs={{0,1},{1,0},{2,3},{3,2},{4,5},{5,4},{6,7},{7,6},{8,9},{9,8},{10,11... | collective-permute-start | bytes 2359304 | tf_op jit(solution)/shard_map/ppermute | solution.py:290
  48.4 21.3 %collective-permute-start.5 = (bf16[128,3072]{1,0:T(8,128)(2,1)S(1)}, bf16[128,3072]{1,0:T(8,128)(2,1)S(1)}, u32[]{:S(2)}, u32[]{:S(2)}) collective-permute-start(bf16[128,3072]{1,0:T(8,128)(2,1)S(1)} %fusion.8.refs_0_), channel_id=1, source_target_pairs={{0,2},{2,0},{1,3},{3,1},{4,6},{6,4},{5,7},{7,5},{8,10},{10,8},{9,1... | collective-permute-start | bytes 2359304 | tf_op jit(solution)/shard_map/ppermute | solution.py:296
  72.0 3.6 %collective-permute-start.6 = (f32[2,128]{1,0:T(2,128)S(1)}, f32[2,128]{1,0:T(2,128)S(1)}, u32[]{:S(2)}, u32[]{:S(2)}) collective-permute-start(f32[2,128]{1,0:T(2,128)S(1)} %pad_maximum_fusion.8), channel_id=1, source_target_pairs={{0,2},{2,0},{1,3},{3,1},{4,6},{6,4},{5,7},{7,5},{8,10},{10,8},{9,1... | collective-permute-start | bytes 3080 | tf_op jit(solution)/shard_map/ppermute | solution.py:296
  76.2 20.0 %collective-permute-start.3 = (bf16[128,3072]{1,0:T(8,128)(2,1)S(1)}, bf16[128,3072]{1,0:T(8,128)(2,1)S(1)}, u32[]{:S(2)}, u32[]{:S(2)}) collective-permute-start(bf16[128,3072]{1,0:T(8,128)(2,1)S(1)} %fusion.9.refs_0_), channel_id=1, source_target_pairs={{0,2},{2,0},{1,3},{3,1},{4,6},{6,4},{5,7},{7,5},{8,10},{10,8},{9,1... | collective-permute-start | bytes 2359304 | tf_op jit(solution)/shard_map/ppermute | solution.py:296
  85.3 11.7 %collective-permute-start.11 = (bf16[128,3072]{1,0:T(8,128)(2,1)S(1)}, bf16[128,3072]{1,0:T(8,128)(2,1)S(1)}, u32[]{:S(2)}, u32[]{:S(2)}) collective-permute-start(bf16[128,3072]{1,0:T(8,128)(2,1)S(1)} %get-tuple-element.27), channel_id=1, source_target_pairs={{0,1},{1,0},{2,3},{3,2},{4,5},{5,4},{6,7},{7,6},{8,9},{9,8},{10,11... | collective-permute-start | bytes 2359304 | tf_op jit(solution)/shard_map/ppermute | solution.py:290
  85.5 5.8 %collective-permute-start.8 = (bf16[256,384]{1,0:T(8,128)(2,1)S(1)}, bf16[256,384]{1,0:T(8,128)(2,1)S(1)}, u32[]{:S(2)}, u32[]{:S(2)}) collective-permute-start(bf16[256,384]{1,0:T(8,128)(2,1)S(1)} %get-tuple-element.26), channel_id=1, source_target_pairs={{0,1},{1,0},{2,3},{3,2},{4,5},{5,4},{6,7},{7,6},{8,9},{9,8},{10,11... | collective-permute-start | bytes 589832 | tf_op jit(solution)/shard_map/ppermute | solution.py:290
  90.8 8.4 %collective-permute-start.12 = (bf16[128,3072]{1,0:T(8,128)(2,1)S(1)}, bf16[128,3072]{1,0:T(8,128)(2,1)S(1)}, u32[]{:S(2)}, u32[]{:S(2)}) collective-permute-start(bf16[128,3072]{1,0:T(8,128)(2,1)S(1)} %get-tuple-element.28), channel_id=1, source_target_pairs={{0,1},{1,0},{2,3},{3,2},{4,5},{5,4},{6,7},{7,6},{8,9},{9,8},{10,11... | collective-permute-start | bytes 2359304 | tf_op jit(solution)/shard_map/ppermute | solution.py:290
  91.0 9.9 %collective-permute-start.10 = (bf16[128,3072]{1,0:T(8,128)(2,1)S(1)}, bf16[128,3072]{1,0:T(8,128)(2,1)S(1)}, u32[]{:S(2)}, u32[]{:S(2)}) collective-permute-start(bf16[128,3072]{1,0:T(8,128)(2,1)S(1)} %shard_map.82.refs_0_), channel_id=1, source_target_pairs={{0,1},{1,0},{2,3},{3,2},{4,5},{5,4},{6,7},{7,6},{8,9},{9,8},{10,11... | collective-permute-start | bytes 2359304 | tf_op jit(solution)/shard_map/ppermute | solution.py:290
  96.9 20.6 %collective-permute-start.9 = (bf16[128,3072]{1,0:T(8,128)(2,1)S(1)}, bf16[128,3072]{1,0:T(8,128)(2,1)S(1)}, u32[]{:S(2)}, u32[]{:S(2)}) collective-permute-start(bf16[128,3072]{1,0:T(8,128)(2,1)S(1)} %shard_map.87.refs_2_.refs_3_.refs_0_), channel_id=1, source_target_pairs={{0,1},{1,0},{2,3},{3,2},{4,5},{5,4},{6,7},{7,6},{8,9},{9,8},{10,11... | collective-permute-start | bytes 2359304 | tf_op jit(solution)/shard_map/ppermute | solution.py:290
  97.1 14.1 %collective-permute-start.14 = (bf16[80,3072]{1,0:T(8,128)(2,1)S(1)}, bf16[80,3072]{1,0:T(8,128)(2,1)S(1)}, u32[]{:S(2)}, u32[]{:S(2)}) collective-permute-start(bf16[80,3072]{1,0:T(8,128)(2,1)S(1)} %shard_map.88.refs_4_.refs_0_), channel_id=1, source_target_pairs={{0,2},{2,0},{1,3},{3,1},{4,6},{6,4},{5,7},{7,5},{8,10},{10,8},{9,1... | collective-permute-start | bytes 1474568 | tf_op jit(solution)/shard_map/ppermute | solution.py:296
  98.7 16.7 %collective-permute-start.13 = (bf16[256,384]{1,0:T(8,128)(2,1)S(1)}, bf16[256,384]{1,0:T(8,128)(2,1)S(1)}, u32[]{:S(2)}, u32[]{:S(2)}) collective-permute-start(bf16[256,384]{1,0:T(8,128)(2,1)S(1)} %shard_map.86.refs_3_.refs_0_), channel_id=1, source_target_pairs={{0,2},{2,0},{1,3},{3,1},{4,6},{6,4},{5,7},{7,5},{8,10},{10,8},{9,1... | collective-permute-start | bytes 589832 | tf_op jit(solution)/shard_map/ppermute | solution.py:296
  99.3 26.2 %collective-permute-start.17 = (bf16[80,3072]{1,0:T(8,128)(2,1)S(1)}, bf16[80,3072]{1,0:T(8,128)(2,1)S(1)}, u32[]{:S(2)}, u32[]{:S(2)}) collective-permute-start(bf16[80,3072]{1,0:T(8,128)(2,1)S(1)} %shard_map.89.refs_5_.refs_0_), channel_id=1, source_target_pairs={{0,2},{2,0},{1,3},{3,1},{4,6},{6,4},{5,7},{7,5},{8,10},{10,8},{9,1... | collective-permute-start | bytes 1474568 | tf_op jit(solution)/shard_map/ppermute | solution.py:296
  127.0 48.2 %reduce-scatter.5.cloned.1.call-start = ((), (), s32[]{:S(2)}) async-start(), calls=%async_computation.3 | async-start | bytes 614400 | tf_op jit(solution)/shard_map/reduce_scatter | solution.py:388
  127.4 10.8 %collective-permute-start.18 = (bf16[80,3072]{1,0:T(8,128)(2,1)S(1)}, bf16[80,3072]{1,0:T(8,128)(2,1)S(1)}, u32[]{:S(2)}, u32[]{:S(2)}) collective-permute-start(bf16[80,3072]{1,0:T(8,128)(2,1)S(1)} %shard_map.96.refs_3_.refs_0_), channel_id=1, source_target_pairs={{0,1},{1,0},{2,3},{3,2},{4,5},{5,4},{6,7},{7,6},{8,9},{9,8},{10,11... | collective-permute-start | bytes 1474568 | tf_op jit(solution)/shard_map/ppermute | solution.py:290
  127.9 9.9 %collective-permute-start.20 = (bf16[48,3072]{1,0:T(8,128)(2,1)S(1)}, bf16[48,3072]{1,0:T(8,128)(2,1)S(1)}, u32[]{:S(2)}, u32[]{:S(2)}) collective-permute-start(bf16[48,3072]{1,0:T(8,128)(2,1)S(1)} %shard_map.92.refs_5_.refs_0_), channel_id=1, source_target_pairs={{0,2},{2,0},{1,3},{3,1},{4,6},{6,4},{5,7},{7,5},{8,10},{10,8},{9,1... | collective-permute-start | bytes 884744 | tf_op jit(solution)/shard_map/ppermute | solution.py:296
  129.4 13.8 %collective-permute-start.23 = (bf16[48,3072]{1,0:T(8,128)(2,1)S(1)}, bf16[48,3072]{1,0:T(8,128)(2,1)S(1)}, u32[]{:S(2)}, u32[]{:S(2)}) collective-permute-start(bf16[48,3072]{1,0:T(8,128)(2,1)S(1)} %shard_map.93.refs_6_.refs_0_), channel_id=1, source_target_pairs={{0,2},{2,0},{1,3},{3,1},{4,6},{6,4},{5,7},{7,5},{8,10},{10,8},{9,1... | collective-permute-start | bytes 884744 | tf_op jit(solution)/shard_map/ppermute | solution.py:296
  138.1 6.1 %collective-permute-start.22 = (bf16[48,3072]{1,0:T(8,128)(2,1)S(1)}, bf16[48,3072]{1,0:T(8,128)(2,1)S(1)}, u32[]{:S(2)}, u32[]{:S(2)}) collective-permute-start(bf16[48,3072]{1,0:T(8,128)(2,1)S(1)} %shard_map.99.refs_8_.refs_0_), channel_id=1, source_target_pairs={{0,1},{1,0},{2,3},{3,2},{4,5},{5,4},{6,7},{7,6},{8,9},{9,8},{10,11... | collective-permute-start | bytes 884744 | tf_op jit(solution)/shard_map/ppermute | solution.py:290
  143.6 8.1 %collective-permute-start.24 = (bf16[48,3072]{1,0:T(8,128)(2,1)S(1)}, bf16[48,3072]{1,0:T(8,128)(2,1)S(1)}, u32[]{:S(2)}, u32[]{:S(2)}) collective-permute-start(bf16[48,3072]{1,0:T(8,128)(2,1)S(1)} %shard_map.101.refs_3_.refs_0_), channel_id=1, source_target_pairs={{0,1},{1,0},{2,3},{3,2},{4,5},{5,4},{6,7},{7,6},{8,9},{9,8},{10,11... | collective-permute-start | bytes 884744 | tf_op jit(solution)/shard_map/ppermute | solution.py:290
  143.9 4.8 %collective-permute-start.21 = (bf16[80,1536]{1,0:T(8,128)(2,1)S(1)}, bf16[80,1536]{1,0:T(8,128)(2,1)S(1)}, u32[]{:S(2)}, u32[]{:S(2)}) collective-permute-start(bf16[80,1536]{1,0:T(8,128)(2,1)S(1)} %get-tuple-element.36), channel_id=1, source_target_pairs={{0,1},{1,0},{2,3},{3,2},{4,5},{5,4},{6,7},{7,6},{8,9},{9,8},{10,11... | collective-permute-start | bytes 737288 | tf_op jit(solution)/shard_map/ppermute | solution.py:290
  158.4 8.5 %collective-permute-start.26 = (bf16[48,768]{1,0:T(8,128)(2,1)S(1)}, bf16[48,768]{1,0:T(8,128)(2,1)S(1)}, u32[]{:S(2)}, u32[]{:S(2)}) collective-permute-start(bf16[48,768]{1,0:T(8,128)(2,1)S(1)} %get-tuple-element.49), channel_id=1, source_target_pairs={{0,12},{4,8},{8,4},{12,0},{1,13},{5,9},{9,5},{13,1},{2,14},{6,10},... | collective-permute-start | bytes 221192 | tf_op jit(solution)/shard_map/ppermute | solution.py:313
  160.2 13.4 %collective-permute-start.27 = (bf16[48,768]{1,0:T(8,128)(2,1)S(1)}, bf16[48,768]{1,0:T(8,128)(2,1)S(1)}, u32[]{:S(2)}, u32[]{:S(2)}) collective-permute-start(bf16[48,768]{1,0:T(8,128)(2,1)S(1)} %get-tuple-element.51), channel_id=1, source_target_pairs={{0,8},{4,12},{8,0},{12,4},{1,9},{5,13},{9,1},{13,5},{2,10},{6,14},... | collective-permute-start | bytes 221192 | tf_op jit(solution)/shard_map/ppermute | solution.py:313
  160.2 13.4 %collective-permute-start.28 = (bf16[48,768]{1,0:T(8,128)(2,1)S(1)}, bf16[48,768]{1,0:T(8,128)(2,1)S(1)}, u32[]{:S(2)}, u32[]{:S(2)}) collective-permute-start(bf16[48,768]{1,0:T(8,128)(2,1)S(1)} %get-tuple-element.50), channel_id=1, source_target_pairs={{0,4},{4,0},{8,12},{12,8},{1,5},{5,1},{9,13},{13,9},{2,6},{6,2},{1... | collective-permute-start | bytes 221192 | tf_op jit(solution)/shard_map/ppermute | solution.py:313
  (16 other events, 64.7 us)
Sparse Core Ops, SparseCore 0:
  127.2 22.7 reduce-scatter.2
  152.2 22.9 reduce-scatter.4

commit v8 on v7

--- a/solution.py
+++ b/solution.py
@@ -11,8 +11,9 @@
 D = 6144
 PATCHES = 256
 EPS = 1e-06
-SHARES = (8, 5, 3)
-PIECES = (1, 1)
+SHARES = (10, 6)
+LEAD_PIECES = (1, 1)
+REST_PIECES = (2, 1)
 AHEAD = 4
 GAIN_ROWS = 8
 BF16, F32 = jnp.bfloat16, jnp.float32
@@ -299,9 +300,9 @@
     def sum_red(x):
         return sum(a.astype(F32) for a in all_red(x))
 
-    def collect(kept, got, width):
+    def collect(kept, got, width, start):
         core, chip = lax.axis_index("tok"), lax.axis_index("wide")
-        terms = jnp.concatenate([kept, got], axis=1)
+        terms = jnp.concatenate([kept, got], axis=1) + start.astype(BF16)
 
         def block(at):
             start = ((at // half_wide) ^ core) * half_wide + at % half_wide
@@ -320,8 +321,7 @@
         attn_rows = w_attn.reshape(w_attn.shape[0] * w_attn.shape[1], w_attn.shape[2])
         depth, units = w_up.shape
         cuts = slices(tokens.shape[0], SHARES)
-        pieces = slices(units, PIECES)
-        n = len(cuts)
+        lead_pieces, rest_pieces = slices(units, LEAD_PIECES), slices(units, REST_PIECES)
 
         first = cuts[0].stop
         gain_rows = jnp.broadcast_to(ln_gain[None], (GAIN_ROWS, width))
@@ -344,7 +344,7 @@
             far = swap(part[half:].astype(BF16)).astype(F32)
             return (part[:half] + far).astype(BF16)
 
-        weights = [w_up[:, piece] for piece in pieces]
+        weights = [w_up[:, piece] for piece in lead_pieces]
         lead_pair = normed(lead[GAIN_ROWS:].astype(F32))
         leads = [project(lead_pair, weight) for weight in weights]
         lead_parts = [all_red(x) for x in leads]
@@ -357,69 +357,36 @@
         near, far = project_rows(*pair, qkv_rows, slice(0, qkv_rows.shape[1]))
         halves, before = [], [near]
         qkv = sum_rows(near, swap(far), slice(0, tokens.shape[0]))
-        for piece in pieces:
+        for piece in rest_pieces:
             near, far = project_rows(*rest_pair, w_up, piece, before)
             halves.append((near, swap(far)))
             before = [near]
 
-        order = [(c, p) for c in range(n) for p in range(len(pieces))]
-        outs, scattered = [], []
-        terms, waiting = (), None
-        earlier = [near, qkv]
-
-        def output(at, have, terms, earlier):
-            c, p = order[at]
-            attention = ()
-            if p == len(pieces) - 1:
-                attention = (attended[cuts[c]], attended_other[cuts[c]], attn_rows)
-            return project_hidden(
-                have,
-                swap(have),
-                w_down,
-                pieces[p],
-                terms if p else (),
-                attention,
-                p == len(pieces) - 1,
-                earlier,
-            )
-
-        def scatter(kept, got, earlier):
-            full = side_by_side(kept, got, core, scattered[-1:] + earlier)
-            scattered.append(lax.psum_scatter(full, "wide", scatter_dimension=1, tiled=True))
-            return full
-
-        hidden, ready = None, lead_parts
-        for at, (c, p) in enumerate(order):
-            if at:
-                arrived = gelu_sum(ready[p], earlier)
-                earlier = [arrived]
-            if p == (0 if c else len(pieces) - 1) and c < n - 1:
-                part = slice(cuts[c + 1].start - first, cuts[c + 1].stop - first)
-                sums = [sum_rows(*half, part, [arrived]) for half in halves]
-                coming = [all_red(x) for x in sums]
-                earlier = earlier + sums
-            if at == len(pieces):
-                attended = attend(all_red(qkv), q_gain, k_gain, earlier)
-                attended_other = swap(attended)
-                earlier = [attended]
-            if p == len(pieces) - 1 and c < n - 1:
-                ready = coming
-            if waiting is not None and not scattered:
-                earlier.append(scatter(*waiting, earlier))
-                waiting = None
-            if at:
-                terms = output(at - 1, hidden, terms, earlier)
-                earlier = [terms[0]]
-            if waiting is not None:
-                earlier = [scatter(*waiting, earlier)]
-                waiting = None
-            if at and p == 0:
-                waiting = (terms[0], swap(terms[1]))
-            hidden = arrived
-        terms = output(len(order) - 1, hidden, terms, earlier)
-        for cut, summed in zip(cuts, scattered):
-            outs.append(tokens[cut].astype(F32) + summed.astype(F32))
-        outs.append(tokens[cuts[-1]].astype(F32) + collect(terms[0], swap(terms[1]), width))
+        def output(have, piece, terms, cut, earlier=()):
+            last = piece.stop == units
+            attention = (attended[cut], attended_other[cut], attn_rows) if last else ()
+            return project_hidden(have, swap(have), w_down, piece, terms, attention, last, earlier)
+
+        second = gelu_sum(lead_parts[1], [halves[-1][0], qkv])
+        attended = attend(all_red(qkv), q_gain, k_gain, [second])
+        sums = [sum_rows(*half, slice(0, half[0].shape[0]), [attended]) for half in halves]
+        parts = [all_red(x) for x in sums]
+        attended_other = swap(attended)
+
+        terms = output(arrived, lead_pieces[0], (), cuts[0], sums)
+        terms = output(second, lead_pieces[1], terms, cuts[0])
+        full = side_by_side(terms[0], swap(terms[1]), core)
+        scattered = lax.psum_scatter(full, "wide", scatter_dimension=1, tiled=True)
+
+        hidden = gelu_sum(parts[0], [full])
+        terms = output(hidden, rest_pieces[0], (), cuts[1])
+        hidden = gelu_sum(parts[1], [terms[0]])
+        kept, got = output(hidden, rest_pieces[1], terms, cuts[1])
+        collected = collect(kept, swap(got), width, nothing(scattered))
+        outs = [
+            tokens[cuts[0]].astype(F32) + scattered.astype(F32),
+            tokens[cuts[1]].astype(F32) + collected,
+        ]
         return jnp.concatenate(outs, axis=0)
 
     return body

time: 184 us -> 189 us (1.027)
  waiting for transfers between devices: 41.6 us -> 63.4 us
  Pallas kernels: 47.1 us -> 36.4 us
  starting transfers between devices: 20 us -> 13.8 us
  local copies, waits for them, and re-layouts: 8.6 us -> 6.23 us
    ppermute x9 -> x7, waiting for transfers between devices: 23.2 us -> 42.8 us  [all_red(): parts.append(lax.ppermute(x, 'red', pairs))]
    pallas_call x23 -> x16, Pallas kernels: 47.1 us -> 36.4 us  [call(): pl.pallas_call(body, in_specs=list(specs) + [corner_of(a) for a in earlie...]
    ppermute x9 -> x7, starting transfers between devices: 12 us -> 6.86 us  [all_red(): parts.append(lax.ppermute(x, 'red', pairs))]
    ppermute x17 -> x14, waiting for transfers between devices: 4.79 us -> 9.62 us  [swap(): return lax.ppermute(x, 'tok', [(0, 1), (1, 0)])]
    unnamed x19 -> x22, local copies, waits for them, and re-layouts: 5.57 us -> 1.81 us
    reduce_scatter x2 -> x1, waiting for transfers between devices: 2.89 us -> 0.02 us  [body(): scattered = lax.psum_scatter(full, 'wide', scatter_dimension=1, tiled=True)]
    all_gather x1, blocking collectives: 21.9 us -> 24 us  [body(): lead = lax.all_gather(lead, 'wide', axis=1, tiled=True)]
  transfers between devices with their start and end apart: 31 -> 25, of which waited for: 17 -> 16; matrix products, arithmetic and copies ran while one was open for 2% -> 3% of each run, Pallas kernels for 25% -> 16%
where the time goes in v8:
time: 189 us; the launch traced here: 188 us
  waiting for transfers between devices  63.4 us (34%)
  blocking collectives  40.4 us (21%)
  Pallas kernels  36.4 us (19%)
  between operations  15.9 us (8%)
  starting transfers between devices  13.8 us (7%)
  matrix products  9.09 us (5%)
  local copies, waits for them, and re-layouts  6.23 us (3%)
  other arithmetic  3.19 us (2%)
    ppermute x7, waiting for transfers between devices, all_red(): parts.append(lax.ppermute(x, 'red', pairs))  42.8 us
    pallas_call x16, Pallas kernels, call(): pl.pallas_call(body, in_specs=list(specs) + [corner_of(a) for a in earlie...  36.4 us
    all_gather x1, blocking collectives, body(): lead = lax.all_gather(lead, 'wide', axis=1, tiled=True)  24 us
    all_gather x1, blocking collectives, body(): rest = lax.all_gather(rest, 'wide', axis=1, tiled=True)  16.4 us
    ppermute x3, waiting for transfers between devices, collect(): total = total + lax.ppermute(block(chip ^ k), 'wide', pairs).astype(F32)  10.9 us
    ppermute x14, waiting for transfers between devices, swap(): return lax.ppermute(x, 'tok', [(0, 1), (1, 0)])  9.62 us
    dot_general x2, matrix products, project(): part = jnp.dot(both, weight, preferred_element_type=F32)  9.09 us
    ppermute x7, starting transfers between devices, all_red(): parts.append(lax.ppermute(x, 'red', pairs))  6.86 us
  transfers between devices with their start and end apart: 25, of which 16 were waited for; matrix products, arithmetic and copies ran while one was open for 3% of the time, Pallas kernels for 16%

profile of v8, /device:TPU:0, one launch (start us, length us, event | category | flops | bytes accessed | tf_op | source)
XLA Modules:
  0.0 188.3 jit_solution(13685297642054752995)
XLA Ops:
  8.2 24.0 %all_gather.6 = bf16[168,3072]{1,0:T(8,128)(2,1)S(1)} all-gather(bf16[168,768]{1,0:T(8,128)(2,1)S(1)} %pad_maximum_fusion.6), channel_id=1, replica_groups=mesh['grp'=2,'wide'=4,'red'=2,'tok'=2] {'wide'}, dimensions={1}, use_global_device_ids=true | all-gather | bytes 1290240 | tf_op jit(solution)/shard_map/all_gather | solution.py:329
  34.2 2.1 %collective-permute-done = f32[2,160]{1,0:T(2,128)S(1)} collective-permute-done((f32[2,160]{1,0:T(2,128)S(1)}, f32[2,160]{1,0:T(2,128)S(1)}, u32[]{:S(2)}, u32[]{:S(2)}) %collective-permute-start) | collective-permute-done | bytes 1312 | tf_op jit(solution)/shard_map/ppermute | solution.py:297
  36.9 1.9 collective-permute-done.1
  38.7 5.9 %fusion = f32[320,3072]{1,0:T(8,128)S(1)} fusion(bf16[1536,6144]{1,0:T(8,128)(2,1)} %refs_2_.8, bf16[160,1536]{1,0:T(8,128)(2,1)S(1)} %collective-permute-done.1, bf16[160,1536]{1,0:T(8,128)(2,1)S(1)} %get-tuple-element.37), kind=kOutput, calls=%fused_computation | convolution fusion | flops 3021864960 | bytes 14352384 | tf_op jit(solution)/shard_map/dot_general | solution.py:343
  46.7 3.2 %fusion.2 = f32[320,3072]{1,0:T(8,128)S(1)} fusion(bf16[1536,6144]{1,0:T(8,128)(2,1)S(1)} %bitcast.27, bf16[160,1536]{1,0:T(8,128)(2,1)S(1)} %collective-permute-done.1, bf16[160,1536]{1,0:T(8,128)(2,1)S(1)} %get-tuple-element.37), kind=kOutput, calls=%fused_computation.2 | convolution fusion | flops 3021864960 | bytes 14352384 | tf_op jit(solution)/shard_map/dot_general | solution.py:343
  50.5 1.6 collective-permute-start.5
  54.2 16.4 %all_gather.7 = bf16[96,3072]{1,0:T(8,128)(2,1)S(1)} all-gather(bf16[96,768]{1,0:T(8,128)(2,1)S(1)} %slice_add_fusion.2), channel_id=1, replica_groups=mesh['grp'=2,'wide'=4,'red'=2,'tok'=2] {'wide'}, dimensions={1}, use_global_device_ids=true | all-gather | bytes 737280 | tf_op jit(solution)/shard_map/all_gather | solution.py:354
  70.6 4.0 %collective-permute-done.5.refs_1_ = bf16[160,3072]{1,0:T(8,128)(2,1)S(1)} collective-permute-done((bf16[160,3072]{1,0:T(8,128)(2,1)S(1)}, bf16[160,3072]{1,0:T(8,128)(2,1)S(1)}, u32[]{:S(2)}, u32[]{:S(2)}) %collective-permute-start.5) | collective-permute-done | bytes 983072 | tf_op jit(solution)/shard_map/ppermute | solution.py:297
  84.6 5.5 %shard_map.84 = (bf16[96,4096]{1,0:T(8,128)(2,1)S(1)}, bf16[96,4096]{1,0:T(8,128)(2,1)S(1)}) custom-call(bf16[96,1536]{1,0:T(8,128)(2,1)S(1)} %get-tuple-element.43.refs_0_, bf16[96,1536]{1,0:T(8,128)(2,1)S(1)} %collective-permute-done.7.refs_1_, bf16[1536,6144]{1,0:T(8,128)(2,1)} %refs_2_.8, bf16[256,384]{1,0:T(8,128)(2,1)S(1)} %get-tuple-element.19.refs_3_.refs_0_), custom_call_target="tpu_custom_call" | custom-call | tf_op jit(solution)/shard_map/pallas_call | solution.py:61
  90.2 3.4 %shard_map.85 = (bf16[96,2048]{1,0:T(8,128)(2,1)S(1)}, bf16[96,2048]{1,0:T(8,128)(2,1)S(1)}) custom-call(bf16[96,1536]{1,0:T(8,128)(2,1)S(1)} %get-tuple-element.43.refs_0_, bf16[96,1536]{1,0:T(8,128)(2,1)S(1)} %collective-permute-done.7.refs_1_, bf16[1536,6144]{1,0:T(8,128)(2,1)} %refs_2_.8, bf16[96,4096]{1,0:T(8,128)(2,1)S(1)} %get-tuple-element.20.refs_3_.refs_0_), custom_call_target="tpu_custom_call" | custom-call | tf_op jit(solution)/shard_map/pallas_call | solution.py:61
  93.6 7.8 %collective-permute-done.3.refs_1_ = bf16[160,3072]{1,0:T(8,128)(2,1)S(1)} collective-permute-done((bf16[160,3072]{1,0:T(8,128)(2,1)S(1)}, bf16[160,3072]{1,0:T(8,128)(2,1)S(1)}, u32[]{:S(2)}, u32[]{:S(2)}) %collective-permute-start.3) | collective-permute-done | bytes 983072 | tf_op jit(solution)/shard_map/ppermute | solution.py:297
  103.5 6.7 %collective-permute-done.12.refs_1_ = bf16[256,384]{1,0:T(8,128)(2,1)S(1)} collective-permute-done((bf16[256,384]{1,0:T(8,128)(2,1)S(1)}, bf16[256,384]{1,0:T(8,128)(2,1)S(1)}, u32[]{:S(2)}, u32[]{:S(2)}) %collective-permute-start.12) | collective-permute-done | bytes 196640 | tf_op jit(solution)/shard_map/ppermute | solution.py:297
  112.5 5.7 %shard_map.91 = (f32[160,1536]{1,0:T(8,128)S(1)}, f32[160,1536]{1,0:T(8,128)S(1)}) custom-call(bf16[160,3072]{1,0:T(8,128)(2,1)S(1)} %shard_map.82.refs_0_, bf16[160,3072]{1,0:T(8,128)(2,1)S(1)} %collective-permute-done.10.refs_1_, bf16[6144,1536]{1,0:T(8,128)(2,1)} %refs_2_.13, bf16[96,4096]{1,0:T(8,128)(2,1)S(1)} %shard_map.89.refs_3_.refs_0_, ...), custom_call_target="tpu_custom_call" | custom-call | tf_op jit(solution)/shard_map/pallas_call | solution.py:61
  118.3 5.7 %shard_map.92 = (bf16[160,1536]{1,0:T(8,128)(2,1)S(1)}, bf16[160,1536]{1,0:T(8,128)(2,1)S(1)}) custom-call(bf16[160,3072]{1,0:T(8,128)(2,1)S(1)} %shard_map.87.refs_4_.refs_0_, bf16[160,3072]{1,0:T(8,128)(2,1)S(1)} %collective-permute-done.9.refs_1_, bf16[6144,1536]{1,0:T(8,128)(2,1)} %refs_2_.13, f32[160,1536]{1,0:T(8,128)S(1)} %get-tuple-element.25.refs_3_, ...), custom_call_target="tpu_custom_call" | custom-call | tf_op jit(solution)/shard_map/pallas_call | solution.py:61
  126.9 17.0 %collective-permute-done.17.refs_1_ = bf16[96,4096]{1,0:T(8,128)(2,1)S(1)} collective-permute-done((bf16[96,4096]{1,0:T(8,128)(2,1)S(1)}, bf16[96,4096]{1,0:T(8,128)(2,1)S(1)}, u32[]{:S(2)}, u32[]{:S(2)}) %collective-permute-start.17) | collective-permute-done | bytes 786464 | tf_op jit(solution)/shard_map/ppermute | solution.py:297
  146.1 1.7 collective-permute-done.18.refs_1_
  147.8 5.6 %shard_map.95 = (f32[96,1536]{1,0:T(8,128)S(1)}, f32[96,1536]{1,0:T(8,128)S(1)}) custom-call(bf16[96,4096]{1,0:T(8,128)(2,1)S(1)} %shard_map.94.refs_0_, bf16[96,4096]{1,0:T(8,128)(2,1)S(1)} %collective-permute-done.18.refs_1_, bf16[6144,1536]{1,0:T(8,128)(2,1)} %refs_2_.13), custom_call_target="tpu_custom_call" | custom-call | tf_op jit(solution)/shard_map/pallas_call | solution.py:61
  153.4 3.6 %collective-permute-done.16.refs_1_ = bf16[96,2048]{1,0:T(8,128)(2,1)S(1)} collective-permute-done((bf16[96,2048]{1,0:T(8,128)(2,1)S(1)}, bf16[96,2048]{1,0:T(8,128)(2,1)S(1)}, u32[]{:S(2)}, u32[]{:S(2)}) %collective-permute-start.16) | collective-permute-done | bytes 393248 | tf_op jit(solution)/shard_map/ppermute | solution.py:297
  157.6 1.7 collective-permute-done.19.refs_1_
  159.2 3.4 %shard_map.97 = (bf16[96,1536]{1,0:T(8,128)(2,1)S(1)}, bf16[96,1536]{1,0:T(8,128)(2,1)S(1)}) custom-call(bf16[96,2048]{1,0:T(8,128)(2,1)S(1)} %shard_map.96.refs_0_, bf16[96,2048]{1,0:T(8,128)(2,1)S(1)} %collective-permute-done.19.refs_1_, bf16[6144,1536]{1,0:T(8,128)(2,1)} %refs_2_.13, f32[96,1536]{1,0:T(8,128)S(1)} %get-tuple-element.29.refs_2_.refs_3_, ...), custom_call_target="tpu_custom_call" | custom-call | tf_op jit(solution)/shard_map/pallas_call | solution.py:61
  165.0 2.5 %collective-permute-start.21 = (bf16[96,768]{1,0:T(8,128)(2,1)S(1)}, bf16[96,768]{1,0:T(8,128)(2,1)S(1)}, u32[]{:S(2)}, u32[]{:S(2)}) collective-permute-start(bf16[96,768]{1,0:T(8,128)(2,1)S(1)} %get-tuple-element.39), channel_id=1, source_target_pairs={{0,12},{4,8},{8,4},{12,0},{1,13},{5,9},{9,5},{13,1},{2,14},{6,10},... | collective-permute-start | bytes 442376 | tf_op jit(solution)/shard_map/ppermute | solution.py:314
  167.6 1.9 %collective-permute-start.23 = (bf16[96,768]{1,0:T(8,128)(2,1)S(1)}, bf16[96,768]{1,0:T(8,128)(2,1)S(1)}, u32[]{:S(2)}, u32[]{:S(2)}) collective-permute-start(bf16[96,768]{1,0:T(8,128)(2,1)S(1)} %get-tuple-element.40), channel_id=1, source_target_pairs={{0,4},{4,0},{8,12},{12,8},{1,5},{5,1},{9,13},{13,9},{2,6},{6,2},{1... | collective-permute-start | bytes 442376 | tf_op jit(solution)/shard_map/ppermute | solution.py:314
  169.5 4.2 %collective-permute-done.21 = bf16[96,768]{1,0:T(8,128)(2,1)S(1)} collective-permute-done((bf16[96,768]{1,0:T(8,128)(2,1)S(1)}, bf16[96,768]{1,0:T(8,128)(2,1)S(1)}, u32[]{:S(2)}, u32[]{:S(2)}) %collective-permute-start.21) | collective-permute-done | bytes 147488 | tf_op jit(solution)/shard_map/ppermute | solution.py:314
  173.7 6.7 %collective-permute-done.22 = bf16[96,768]{1,0:T(8,128)(2,1)S(1)} collective-permute-done((bf16[96,768]{1,0:T(8,128)(2,1)S(1)}, bf16[96,768]{1,0:T(8,128)(2,1)S(1)}, u32[]{:S(2)}, u32[]{:S(2)}) %collective-permute-start.22) | collective-permute-done | bytes 147488 | tf_op jit(solution)/shard_map/ppermute | solution.py:314
  (107 shorter events, 30.2 us)
Async XLA Ops:
  6.5 156.4 %reduce-scatter.2.cloned.1.call-start = ((), (), s32[]{:S(2)}) async-start(), calls=%async_computation.1 | async-start | bytes 1228800 | tf_op jit(solution)/shard_map/reduce_scatter | solution.py:379
  32.6 3.6 %collective-permute-start = (f32[2,160]{1,0:T(2,128)S(1)}, f32[2,160]{1,0:T(2,128)S(1)}, u32[]{:S(2)}, u32[]{:S(2)}) collective-permute-start(f32[2,160]{1,0:T(2,128)S(1)} %pad_maximum_fusion.7), channel_id=1, source_target_pairs={{0,2},{2,0},{1,3},{3,1},{4,6},{6,4},{5,7},{7,5},{8,10},{10,8},{9,1... | collective-permute-start | bytes 3848 | tf_op jit(solution)/shard_map/ppermute | solution.py:297
  36.8 1.9 %collective-permute-start.1 = (bf16[160,1536]{1,0:T(8,128)(2,1)S(1)}, bf16[160,1536]{1,0:T(8,128)(2,1)S(1)}, u32[]{:S(2)}, u32[]{:S(2)}) collective-permute-start(bf16[160,1536]{1,0:T(8,128)(2,1)S(1)} %get-tuple-element.38), channel_id=1, source_target_pairs={{0,1},{1,0},{2,3},{3,2},{4,5},{5,4},{6,7},{7,6},{8,9},{9,8},{10,11... | collective-permute-start | bytes 1474568 | tf_op jit(solution)/shard_map/ppermute | solution.py:291
  44.8 5.5 %collective-permute-start.4 = (bf16[160,3072]{1,0:T(8,128)(2,1)S(1)}, bf16[160,3072]{1,0:T(8,128)(2,1)S(1)}, u32[]{:S(2)}, u32[]{:S(2)}) collective-permute-start(bf16[160,3072]{1,0:T(8,128)(2,1)S(1)} %slice.130), channel_id=1, source_target_pairs={{0,1},{1,0},{2,3},{3,2},{4,5},{5,4},{6,7},{7,6},{8,9},{9,8},{10,11... | collective-permute-start | bytes 2949128 | tf_op jit(solution)/shard_map/ppermute | solution.py:291
  50.1 2.6 %collective-permute-start.2 = (bf16[160,3072]{1,0:T(8,128)(2,1)S(1)}, bf16[160,3072]{1,0:T(8,128)(2,1)S(1)}, u32[]{:S(2)}, u32[]{:S(2)}) collective-permute-start(bf16[160,3072]{1,0:T(8,128)(2,1)S(1)} %slice.131), channel_id=1, source_target_pairs={{0,1},{1,0},{2,3},{3,2},{4,5},{5,4},{6,7},{7,6},{8,9},{9,8},{10,11... | collective-permute-start | bytes 2949128 | tf_op jit(solution)/shard_map/ppermute | solution.py:291
  50.5 24.1 %collective-permute-start.5 = (bf16[160,3072]{1,0:T(8,128)(2,1)S(1)}, bf16[160,3072]{1,0:T(8,128)(2,1)S(1)}, u32[]{:S(2)}, u32[]{:S(2)}) collective-permute-start(bf16[160,3072]{1,0:T(8,128)(2,1)S(1)} %fusion.8.refs_0_), channel_id=1, source_target_pairs={{0,2},{2,0},{1,3},{3,1},{4,6},{6,4},{5,7},{7,5},{8,10},{10,8},{9,1... | collective-permute-start | bytes 2949128 | tf_op jit(solution)/shard_map/ppermute | solution.py:297
  77.0 3.6 %collective-permute-start.6 = (f32[2,96]{1,0:T(2,128)S(1)}, f32[2,96]{1,0:T(2,128)S(1)}, u32[]{:S(2)}, u32[]{:S(2)}) collective-permute-start(f32[2,96]{1,0:T(2,128)S(1)} %pad_maximum_fusion.8), channel_id=1, source_target_pairs={{0,2},{2,0},{1,3},{3,1},{4,6},{6,4},{5,7},{7,5},{8,10},{10,8},{9,1... | collective-permute-start | bytes 2312 | tf_op jit(solution)/shard_map/ppermute | solution.py:297
  78.5 22.9 %collective-permute-start.3 = (bf16[160,3072]{1,0:T(8,128)(2,1)S(1)}, bf16[160,3072]{1,0:T(8,128)(2,1)S(1)}, u32[]{:S(2)}, u32[]{:S(2)}) collective-permute-start(bf16[160,3072]{1,0:T(8,128)(2,1)S(1)} %fusion.9.refs_0_), channel_id=1, source_target_pairs={{0,2},{2,0},{1,3},{3,1},{4,6},{6,4},{5,7},{7,5},{8,10},{10,8},{9,1... | collective-permute-start | bytes 2949128 | tf_op jit(solution)/shard_map/ppermute | solution.py:297
  81.0 1.6 collective-permute-start.7
  84.0 9.5 %collective-permute-start.8 = (bf16[256,384]{1,0:T(8,128)(2,1)S(1)}, bf16[256,384]{1,0:T(8,128)(2,1)S(1)}, u32[]{:S(2)}, u32[]{:S(2)}) collective-permute-start(bf16[256,384]{1,0:T(8,128)(2,1)S(1)} %get-tuple-element.22), channel_id=1, source_target_pairs={{0,1},{1,0},{2,3},{3,2},{4,5},{5,4},{6,7},{7,6},{8,9},{9,8},{10,11... | collective-permute-start | bytes 589832 | tf_op jit(solution)/shard_map/ppermute | solution.py:291
  84.2 28.3 %collective-permute-start.10 = (bf16[160,3072]{1,0:T(8,128)(2,1)S(1)}, bf16[160,3072]{1,0:T(8,128)(2,1)S(1)}, u32[]{:S(2)}, u32[]{:S(2)}) collective-permute-start(bf16[160,3072]{1,0:T(8,128)(2,1)S(1)} %shard_map.82.refs_0_), channel_id=1, source_target_pairs={{0,1},{1,0},{2,3},{3,2},{4,5},{5,4},{6,7},{7,6},{8,9},{9,8},{10,11... | collective-permute-start | bytes 2949128 | tf_op jit(solution)/shard_map/ppermute | solution.py:291
  102.3 16.0 %collective-permute-start.9 = (bf16[160,3072]{1,0:T(8,128)(2,1)S(1)}, bf16[160,3072]{1,0:T(8,128)(2,1)S(1)}, u32[]{:S(2)}, u32[]{:S(2)}) collective-permute-start(bf16[160,3072]{1,0:T(8,128)(2,1)S(1)} %shard_map.87.refs_4_.refs_0_), channel_id=1, source_target_pairs={{0,1},{1,0},{2,3},{3,2},{4,5},{5,4},{6,7},{7,6},{8,9},{9,8},{10,11... | collective-permute-start | bytes 2949128 | tf_op jit(solution)/shard_map/ppermute | solution.py:291
  102.4 10.0 %collective-permute-start.11 = (bf16[96,4096]{1,0:T(8,128)(2,1)S(1)}, bf16[96,4096]{1,0:T(8,128)(2,1)S(1)}, u32[]{:S(2)}, u32[]{:S(2)}) collective-permute-start(bf16[96,4096]{1,0:T(8,128)(2,1)S(1)} %get-tuple-element.23), channel_id=1, source_target_pairs={{0,1},{1,0},{2,3},{3,2},{4,5},{5,4},{6,7},{7,6},{8,9},{9,8},{10,11... | collective-permute-start | bytes 2359304 | tf_op jit(solution)/shard_map/ppermute | solution.py:291
  102.9 8.2 %collective-permute-start.13 = (bf16[96,2048]{1,0:T(8,128)(2,1)S(1)}, bf16[96,2048]{1,0:T(8,128)(2,1)S(1)}, u32[]{:S(2)}, u32[]{:S(2)}) collective-permute-start(bf16[96,2048]{1,0:T(8,128)(2,1)S(1)} %get-tuple-element.24), channel_id=1, source_target_pairs={{0,1},{1,0},{2,3},{3,2},{4,5},{5,4},{6,7},{7,6},{8,9},{9,8},{10,11... | collective-permute-start | bytes 1179656 | tf_op jit(solution)/shard_map/ppermute | solution.py:291
  103.0 7.3 %collective-permute-start.12 = (bf16[256,384]{1,0:T(8,128)(2,1)S(1)}, bf16[256,384]{1,0:T(8,128)(2,1)S(1)}, u32[]{:S(2)}, u32[]{:S(2)}) collective-permute-start(bf16[256,384]{1,0:T(8,128)(2,1)S(1)} %shard_map.86.refs_3_.refs_0_), channel_id=1, source_target_pairs={{0,2},{2,0},{1,3},{3,1},{4,6},{6,4},{5,7},{7,5},{8,10},{10,8},{9,1... | collective-permute-start | bytes 589832 | tf_op jit(solution)/shard_map/ppermute | solution.py:297
  124.0 1.9 %collective-permute-start.15 = (bf16[160,1536]{1,0:T(8,128)(2,1)S(1)}, bf16[160,1536]{1,0:T(8,128)(2,1)S(1)}, u32[]{:S(2)}, u32[]{:S(2)}) collective-permute-start(bf16[160,1536]{1,0:T(8,128)(2,1)S(1)} %get-tuple-element.28), channel_id=1, source_target_pairs={{0,1},{1,0},{2,3},{3,2},{4,5},{5,4},{6,7},{7,6},{8,9},{9,8},{10,11... | collective-permute-start | bytes 1474568 | tf_op jit(solution)/shard_map/ppermute | solution.py:291
  124.2 19.8 %collective-permute-start.17 = (bf16[96,4096]{1,0:T(8,128)(2,1)S(1)}, bf16[96,4096]{1,0:T(8,128)(2,1)S(1)}, u32[]{:S(2)}, u32[]{:S(2)}) collective-permute-start(bf16[96,4096]{1,0:T(8,128)(2,1)S(1)} %shard_map.89.refs_3_.refs_0_), channel_id=1, source_target_pairs={{0,2},{2,0},{1,3},{3,1},{4,6},{6,4},{5,7},{7,5},{8,10},{10,8},{9,1... | collective-permute-start | bytes 2359304 | tf_op jit(solution)/shard_map/ppermute | solution.py:297
  145.4 2.4 %collective-permute-start.18 = (bf16[96,4096]{1,0:T(8,128)(2,1)S(1)}, bf16[96,4096]{1,0:T(8,128)(2,1)S(1)}, u32[]{:S(2)}, u32[]{:S(2)}) collective-permute-start(bf16[96,4096]{1,0:T(8,128)(2,1)S(1)} %shard_map.94.refs_0_), channel_id=1, source_target_pairs={{0,1},{1,0},{2,3},{3,2},{4,5},{5,4},{6,7},{7,6},{8,9},{9,8},{10,11... | collective-permute-start | bytes 2359304 | tf_op jit(solution)/shard_map/ppermute | solution.py:291
  145.5 11.5 %collective-permute-start.16 = (bf16[96,2048]{1,0:T(8,128)(2,1)S(1)}, bf16[96,2048]{1,0:T(8,128)(2,1)S(1)}, u32[]{:S(2)}, u32[]{:S(2)}) collective-permute-start(bf16[96,2048]{1,0:T(8,128)(2,1)S(1)} %shard_map.90.refs_4_.refs_0_), channel_id=1, source_target_pairs={{0,2},{2,0},{1,3},{3,1},{4,6},{6,4},{5,7},{7,5},{8,10},{10,8},{9,1... | collective-permute-start | bytes 1179656 | tf_op jit(solution)/shard_map/ppermute | solution.py:297
  157.5 1.8 collective-permute-start.19
  162.7 2.2 %collective-permute-start.20 = (bf16[96,1536]{1,0:T(8,128)(2,1)S(1)}, bf16[96,1536]{1,0:T(8,128)(2,1)S(1)}, u32[]{:S(2)}, u32[]{:S(2)}) collective-permute-start(bf16[96,1536]{1,0:T(8,128)(2,1)S(1)} %get-tuple-element.32), channel_id=1, source_target_pairs={{0,1},{1,0},{2,3},{3,2},{4,5},{5,4},{6,7},{7,6},{8,9},{9,8},{10,11... | collective-permute-start | bytes 884744 | tf_op jit(solution)/shard_map/ppermute | solution.py:291
  165.0 8.7 %collective-permute-start.21 = (bf16[96,768]{1,0:T(8,128)(2,1)S(1)}, bf16[96,768]{1,0:T(8,128)(2,1)S(1)}, u32[]{:S(2)}, u32[]{:S(2)}) collective-permute-start(bf16[96,768]{1,0:T(8,128)(2,1)S(1)} %get-tuple-element.39), channel_id=1, source_target_pairs={{0,12},{4,8},{8,4},{12,0},{1,13},{5,9},{9,5},{13,1},{2,14},{6,10},... | collective-permute-start | bytes 442376 | tf_op jit(solution)/shard_map/ppermute | solution.py:314
  167.6 12.9 %collective-permute-start.22 = (bf16[96,768]{1,0:T(8,128)(2,1)S(1)}, bf16[96,768]{1,0:T(8,128)(2,1)S(1)}, u32[]{:S(2)}, u32[]{:S(2)}) collective-permute-start(bf16[96,768]{1,0:T(8,128)(2,1)S(1)} %get-tuple-element.41), channel_id=1, source_target_pairs={{0,8},{4,12},{8,0},{12,4},{1,9},{5,13},{9,1},{13,5},{2,10},{6,14},... | collective-permute-start | bytes 442376 | tf_op jit(solution)/shard_map/ppermute | solution.py:314
  167.6 12.9 %collective-permute-start.23 = (bf16[96,768]{1,0:T(8,128)(2,1)S(1)}, bf16[96,768]{1,0:T(8,128)(2,1)S(1)}, u32[]{:S(2)}, u32[]{:S(2)}) collective-permute-start(bf16[96,768]{1,0:T(8,128)(2,1)S(1)} %get-tuple-element.40), channel_id=1, source_target_pairs={{0,4},{4,0},{8,12},{12,8},{1,5},{5,1},{9,13},{13,9},{2,6},{6,2},{1... | collective-permute-start | bytes 442376 | tf_op jit(solution)/shard_map/ppermute | solution.py:314
  (12 other events, 88.5 us)
Sparse Core Ops, SparseCore 0:
  127.1 25.3 reduce-scatter.1

commit v9 on v8

--- a/solution.py
+++ b/solution.py
@@ -11,9 +11,8 @@
 D = 6144
 PATCHES = 256
 EPS = 1e-06
-SHARES = (10, 6)
-LEAD_PIECES = (1, 1)
-REST_PIECES = (2, 1)
+SHARES = (8, 5, 3)
+PIECES = (1, 1)
 AHEAD = 4
 GAIN_ROWS = 8
 BF16, F32 = jnp.bfloat16, jnp.float32
@@ -300,9 +299,9 @@
     def sum_red(x):
         return sum(a.astype(F32) for a in all_red(x))
 
-    def collect(kept, got, width, start):
+    def collect(kept, got, width):
         core, chip = lax.axis_index("tok"), lax.axis_index("wide")
-        terms = jnp.concatenate([kept, got], axis=1) + start.astype(BF16)
+        terms = jnp.concatenate([kept, got], axis=1)
 
         def block(at):
             start = ((at // half_wide) ^ core) * half_wide + at % half_wide
@@ -321,7 +320,7 @@
         attn_rows = w_attn.reshape(w_attn.shape[0] * w_attn.shape[1], w_attn.shape[2])
         depth, units = w_up.shape
         cuts = slices(tokens.shape[0], SHARES)
-        lead_pieces, rest_pieces = slices(units, LEAD_PIECES), slices(units, REST_PIECES)
+        pieces = slices(units, PIECES)
 
         first = cuts[0].stop
         gain_rows = jnp.broadcast_to(ln_gain[None], (GAIN_ROWS, width))
@@ -344,7 +343,7 @@
             far = swap(part[half:].astype(BF16)).astype(F32)
             return (part[:half] + far).astype(BF16)
 
-        weights = [w_up[:, piece] for piece in lead_pieces]
+        weights = [w_up[:, piece] for piece in pieces]
         lead_pair = normed(lead[GAIN_ROWS:].astype(F32))
         leads = [project(lead_pair, weight) for weight in weights]
         lead_parts = [all_red(x) for x in leads]
@@ -357,7 +356,7 @@
         near, far = project_rows(*pair, qkv_rows, slice(0, qkv_rows.shape[1]))
         halves, before = [], [near]
         qkv = sum_rows(near, swap(far), slice(0, tokens.shape[0]))
-        for piece in rest_pieces:
+        for piece in pieces:
             near, far = project_rows(*rest_pair, w_up, piece, before)
             halves.append((near, swap(far)))
             before = [near]
@@ -367,26 +366,42 @@
             attention = (attended[cut], attended_other[cut], attn_rows) if last else ()
             return project_hidden(have, swap(have), w_down, piece, terms, attention, last, earlier)
 
-        second = gelu_sum(lead_parts[1], [halves[-1][0], qkv])
-        attended = attend(all_red(qkv), q_gain, k_gain, [second])
-        sums = [sum_rows(*half, slice(0, half[0].shape[0]), [attended]) for half in halves]
+        def chunk_sums(c, earlier):
+            part = slice(cuts[c].start - first, cuts[c].stop - first)
+            return [sum_rows(*half, part, [earlier]) for half in halves]
+
+        def scatter(kept, got, earlier):
+            full = side_by_side(kept, got, core, earlier)
+            return full, lax.psum_scatter(full, "wide", scatter_dimension=1, tiled=True)
+
+        attended = attend(all_red(qkv), q_gain, k_gain, [halves[-1][0]])
+        attended_other = swap(attended)
+        second = gelu_sum(lead_parts[1], [attended])
+        sums = chunk_sums(1, second)
         parts = [all_red(x) for x in sums]
-        attended_other = swap(attended)
-
-        terms = output(arrived, lead_pieces[0], (), cuts[0], sums)
-        terms = output(second, lead_pieces[1], terms, cuts[0])
-        full = side_by_side(terms[0], swap(terms[1]), core)
-        scattered = lax.psum_scatter(full, "wide", scatter_dimension=1, tiled=True)
-
-        hidden = gelu_sum(parts[0], [full])
-        terms = output(hidden, rest_pieces[0], (), cuts[1])
-        hidden = gelu_sum(parts[1], [terms[0]])
-        kept, got = output(hidden, rest_pieces[1], terms, cuts[1])
-        collected = collect(kept, swap(got), width, nothing(scattered))
-        outs = [
-            tokens[cuts[0]].astype(F32) + scattered.astype(F32),
-            tokens[cuts[1]].astype(F32) + collected,
-        ]
+        terms = output(arrived, pieces[0], (), cuts[0], sums)
+        terms = output(second, pieces[1], terms, cuts[0])
+        waiting = terms[0], swap(terms[1])
+
+        hidden = gelu_sum(parts[0], [terms[0]])
+        full, got = scatter(*waiting, [hidden])
+        scattered = [got]
+        sums = chunk_sums(2, hidden)
+        coming = [all_red(x) for x in sums]
+        second = gelu_sum(parts[1], [full, *sums])
+        terms = output(hidden, pieces[0], (), cuts[1], [second])
+
+        hidden = gelu_sum(coming[0], [terms[0]])
+        terms = output(second, pieces[1], terms, cuts[1], [hidden])
+        waiting = terms[0], swap(terms[1])
+
+        second = gelu_sum(coming[1], [terms[0]])
+        full, got = scatter(*waiting, [second, scattered[0]])
+        scattered.append(got)
+        terms = output(hidden, pieces[0], (), cuts[2], [full])
+        kept, sent = output(second, pieces[1], terms, cuts[2])
+        outs = [tokens[cut].astype(F32) + got.astype(F32) for cut, got in zip(cuts, scattered)]
+        outs.append(tokens[cuts[2]].astype(F32) + collect(kept, swap(sent), width))
         return jnp.concatenate(outs, axis=0)
 
     return body

time: 189 us -> 185 us (0.979)
  waiting for transfers between devices: 63.4 us -> 40.8 us
  Pallas kernels: 36.4 us -> 47.1 us
  starting transfers between devices: 13.8 us -> 19.1 us
  local copies, waits for them, and re-layouts: 6.23 us -> 10.8 us
    ppermute x7 -> x9, waiting for transfers between devices: 42.8 us -> 25.6 us  [all_red(): parts.append(lax.ppermute(x, 'red', pairs))]
    pallas_call x16 -> x23, Pallas kernels: 36.4 us -> 47.1 us  [call(): pl.pallas_call(body, in_specs=list(specs) + [corner_of(a) for a in earlie...]
    unnamed x22 -> x25, local copies, waits for them, and re-layouts: 1.81 us -> 7.75 us
    ppermute x7 -> x9, starting transfers between devices: 6.86 us -> 11.5 us  [all_red(): parts.append(lax.ppermute(x, 'red', pairs))]
    ppermute x3, waiting for transfers between devices: 10.9 us -> 7.08 us  [collect(): total = total + lax.ppermute(block(chip ^ k), 'wide', pairs).astype(F32)]
    all_gather x1, blocking collectives: 24 us -> 21.9 us  [body(): lead = lax.all_gather(lead, 'wide', axis=1, tiled=True)]
    ppermute x14 -> x17, waiting for transfers between devices: 9.62 us -> 8.04 us  [swap(): return lax.ppermute(x, 'tok', [(0, 1), (1, 0)])]
  transfers between devices with their start and end apart: 25 -> 31, of which waited for: 16 -> 17; matrix products, arithmetic and copies ran while one was open for 3% -> 2% of each run, Pallas kernels for 16% -> 25%
where the time goes in v9:
time: 185 us
  Pallas kernels  47.1 us (25%)
  waiting for transfers between devices  40.8 us (22%)
  blocking collectives  39.9 us (22%)
  starting transfers between devices  19.1 us (10%)
  between operations  15.3 us (8%)
  local copies, waits for them, and re-layouts  10.8 us (6%)
  matrix products  7.91 us (4%)
  other arithmetic  3.75 us (2%)
    pallas_call x23, Pallas kernels, call(): pl.pallas_call(body, in_specs=list(specs) + [corner_of(a) for a in earlie...  47.1 us
    ppermute x9, waiting for transfers between devices, all_red(): parts.append(lax.ppermute(x, 'red', pairs))  25.6 us
    all_gather x1, blocking collectives, body(): lead = lax.all_gather(lead, 'wide', axis=1, tiled=True)  21.9 us
    all_gather x1, blocking collectives, body(): rest = lax.all_gather(rest, 'wide', axis=1, tiled=True)  18 us
    ppermute x9, starting transfers between devices, all_red(): parts.append(lax.ppermute(x, 'red', pairs))  11.5 us
    ppermute x17, waiting for transfers between devices, swap(): return lax.ppermute(x, 'tok', [(0, 1), (1, 0)])  8.04 us
    dot_general x2, matrix products, project(): part = jnp.dot(both, weight, preferred_element_type=F32)  7.91 us
    unnamed x25, local copies, waits for them, and re-layouts  7.75 us
  transfers between devices with their start and end apart: 31, of which 17 were waited for; matrix products, arithmetic and copies ran while one was open for 2% of the time, Pallas kernels for 25%

profile of v9, /device:TPU:0, one launch (start us, length us, event | category | flops | bytes accessed | tf_op | source)
XLA Modules:
  0.0 184.6 jit_solution(9971832524712170061)
XLA Ops:
  8.2 21.9 %all_gather.6 = bf16[136,3072]{1,0:T(8,128)(2,1)S(1)} all-gather(bf16[136,768]{1,0:T(8,128)(2,1)S(1)} %pad_maximum_fusion.6), channel_id=1, replica_groups=mesh['grp'=2,'wide'=4,'red'=2,'tok'=2] {'wide'}, dimensions={1}, use_global_device_ids=true | all-gather | bytes 1044480 | tf_op jit(solution)/shard_map/all_gather | solution.py:328
  31.9 2.1 %collective-permute-done = f32[2,128]{1,0:T(2,128)S(1)} collective-permute-done((f32[2,128]{1,0:T(2,128)S(1)}, f32[2,128]{1,0:T(2,128)S(1)}, u32[]{:S(2)}, u32[]{:S(2)}) %collective-permute-start) | collective-permute-done | bytes 1056 | tf_op jit(solution)/shard_map/ppermute | solution.py:296
  34.5 1.7 collective-permute-done.1
  36.2 5.3 %fusion = f32[256,3072]{1,0:T(8,128)S(1)} fusion(bf16[1536,6144]{1,0:T(8,128)(2,1)} %refs_2_.10, bf16[128,1536]{1,0:T(8,128)(2,1)S(1)} %get-tuple-element.48, bf16[128,1536]{1,0:T(8,128)(2,1)S(1)} %collective-permute-done.1), kind=kOutput, calls=%fused_computation | convolution fusion | flops 2417491968 | bytes 13369344 | tf_op jit(solution)/shard_map/dot_general | solution.py:342
  41.8 3.5 %copy-done.10 = bf16[1536,6144]{1,0:T(8,128)(2,1)S(1)} copy-done((bf16[1536,6144]{1,0:T(8,128)(2,1)S(1)}, bf16[1536,6144]{1,0:T(8,128)(2,1)}, u32[]{:S(2)}) %copy-start.10) | copy-done | bytes 18874392
  45.4 2.6 %fusion.2 = f32[256,3072]{1,0:T(8,128)S(1)} fusion(bf16[1536,6144]{1,0:T(8,128)(2,1)S(1)} %copy-done.10, bf16[128,1536]{1,0:T(8,128)(2,1)S(1)} %get-tuple-element.48, bf16[128,1536]{1,0:T(8,128)(2,1)S(1)} %collective-permute-done.1), kind=kOutput, calls=%fused_computation.2 | convolution fusion | flops 2417491968 | bytes 13369344 | tf_op jit(solution)/shard_map/dot_general | solution.py:342
  48.4 1.6 collective-permute-start.5
  51.8 18.0 %all_gather.7 = bf16[128,3072]{1,0:T(8,128)(2,1)S(1)} all-gather(bf16[128,768]{1,0:T(8,128)(2,1)S(1)} %slice_add_fusion.2), channel_id=1, replica_groups=mesh['grp'=2,'wide'=4,'red'=2,'tok'=2] {'wide'}, dimensions={1}, use_global_device_ids=true | all-gather | bytes 983040 | tf_op jit(solution)/shard_map/all_gather | solution.py:353
  73.6 2.1 %collective-permute-done.6 = f32[2,128]{1,0:T(2,128)S(1)} collective-permute-done((f32[2,128]{1,0:T(2,128)S(1)}, f32[2,128]{1,0:T(2,128)S(1)}, u32[]{:S(2)}, u32[]{:S(2)}) %collective-permute-start.6) | collective-permute-done | bytes 1056 | tf_op jit(solution)/shard_map/ppermute | solution.py:296
  82.5 4.9 %shard_map.85 = (bf16[128,3072]{1,0:T(8,128)(2,1)S(1)}, bf16[128,3072]{1,0:T(8,128)(2,1)S(1)}) custom-call(bf16[128,1536]{1,0:T(8,128)(2,1)S(1)} %get-tuple-element.46.refs_0_, bf16[128,1536]{1,0:T(8,128)(2,1)S(1)} %collective-permute-done.7.refs_1_, bf16[1536,6144]{1,0:T(8,128)(2,1)} %refs_2_.10, bf16[256,384]{1,0:T(8,128)(2,1)S(1)} %get-tuple-element.23.refs_0_.refs_3_), custom_call_target="tpu_custom_call" | custom-call | tf_op jit(solution)/shard_map/pallas_call | solution.py:60
  88.0 4.9 %shard_map.86 = (bf16[128,3072]{1,0:T(8,128)(2,1)S(1)}, bf16[128,3072]{1,0:T(8,128)(2,1)S(1)}) custom-call(bf16[128,1536]{1,0:T(8,128)(2,1)S(1)} %get-tuple-element.46.refs_0_, bf16[128,1536]{1,0:T(8,128)(2,1)S(1)} %collective-permute-done.7.refs_1_, bf16[1536,6144]{1,0:T(8,128)(2,1)} %refs_2_.10, bf16[128,3072]{1,0:T(8,128)(2,1)S(1)} %get-tuple-element.25.refs_3_.refs_0_), custom_call_target="tpu_custom_call" | custom-call | tf_op jit(solution)/shard_map/pallas_call | solution.py:60
  93.1 7.3 %collective-permute-done.9.refs_1_ = bf16[256,384]{1,0:T(8,128)(2,1)S(1)} collective-permute-done((bf16[256,384]{1,0:T(8,128)(2,1)S(1)}, bf16[256,384]{1,0:T(8,128)(2,1)S(1)}, u32[]{:S(2)}, u32[]{:S(2)}) %collective-permute-start.9) | collective-permute-done | bytes 196640 | tf_op jit(solution)/shard_map/ppermute | solution.py:296
  105.1 5.2 %shard_map.91 = (f32[128,1536]{1,0:T(8,128)S(1)}, f32[128,1536]{1,0:T(8,128)S(1)}) custom-call(bf16[128,3072]{1,0:T(8,128)(2,1)S(1)} %shard_map.82.refs_0_, bf16[128,3072]{1,0:T(8,128)(2,1)S(1)} %collective-permute-done.11.refs_1_, bf16[6144,1536]{1,0:T(8,128)(2,1)} %refs_2_.17, bf16[80,3072]{1,0:T(8,128)(2,1)S(1)} %shard_map.89.refs_3_.refs_0_, ...), custom_call_target="tpu_custom_call" | custom-call | tf_op jit(solution)/shard_map/pallas_call | solution.py:60
  110.4 5.0 %shard_map.92 = (bf16[128,1536]{1,0:T(8,128)(2,1)S(1)}, bf16[128,1536]{1,0:T(8,128)(2,1)S(1)}) custom-call(bf16[128,3072]{1,0:T(8,128)(2,1)S(1)} %shard_map.88.refs_2_.refs_0_, bf16[128,3072]{1,0:T(8,128)(2,1)S(1)} %collective-permute-done.10.refs_1_, bf16[6144,1536]{1,0:T(8,128)(2,1)} %refs_2_.17, f32[128,1536]{1,0:T(8,128)S(1)} %get-tuple-element.29.refs_3_, ...), custom_call_target="tpu_custom_call" | custom-call | tf_op jit(solution)/shard_map/pallas_call | solution.py:60
  121.7 10.1 %collective-permute-done.17.refs_1_ = bf16[80,3072]{1,0:T(8,128)(2,1)S(1)} collective-permute-done((bf16[80,3072]{1,0:T(8,128)(2,1)S(1)}, bf16[80,3072]{1,0:T(8,128)(2,1)S(1)}, u32[]{:S(2)}, u32[]{:S(2)}) %collective-permute-start.17) | collective-permute-done | bytes 491552 | tf_op jit(solution)/shard_map/ppermute | solution.py:296
  135.2 4.5 %shard_map.98 = (f32[80,1536]{1,0:T(8,128)S(1)}, f32[80,1536]{1,0:T(8,128)S(1)}) custom-call(bf16[80,3072]{1,0:T(8,128)(2,1)S(1)} %shard_map.93.refs_3_.refs_2_.refs_0_, bf16[80,3072]{1,0:T(8,128)(2,1)S(1)} %collective-permute-done.19.refs_1_, bf16[6144,1536]{1,0:T(8,128)(2,1)} %refs_2_.17, bf16[80,3072]{1,0:T(8,128)(2,1)S(1)} %shard_map.97.refs_3_.refs_0_), custom_call_target="tpu_custom_call" | custom-call | tf_op jit(solution)/shard_map/pallas_call | solution.py:60
  139.7 3.2 %collective-permute-done.20.refs_1_ = bf16[48,3072]{1,0:T(8,128)(2,1)S(1)} collective-permute-done((bf16[48,3072]{1,0:T(8,128)(2,1)S(1)}, bf16[48,3072]{1,0:T(8,128)(2,1)S(1)}, u32[]{:S(2)}, u32[]{:S(2)}) %collective-permute-start.20) | collective-permute-done | bytes 294944 | tf_op jit(solution)/shard_map/ppermute | solution.py:296
  143.4 4.6 %shard_map.100 = (bf16[80,1536]{1,0:T(8,128)(2,1)S(1)}, bf16[80,1536]{1,0:T(8,128)(2,1)S(1)}) custom-call(bf16[80,3072]{1,0:T(8,128)(2,1)S(1)} %shard_map.97.refs_3_.refs_0_, bf16[80,3072]{1,0:T(8,128)(2,1)S(1)} %collective-permute-done.18.refs_1_, bf16[6144,1536]{1,0:T(8,128)(2,1)} %refs_2_.17, f32[80,1536]{1,0:T(8,128)S(1)} %get-tuple-element.33.refs_2_.refs_3_, ...), custom_call_target="tpu_custom_call" | custom-call | tf_op jit(solution)/shard_map/pallas_call | solution.py:60
  153.0 5.1 %shard_map.103 = (f32[48,1536]{1,0:T(8,128)S(1)}, f32[48,1536]{1,0:T(8,128)S(1)}) custom-call(bf16[48,3072]{1,0:T(8,128)(2,1)S(1)} %shard_map.99.refs_8_.refs_0_, bf16[48,3072]{1,0:T(8,128)(2,1)S(1)} %collective-permute-done.24.refs_1_, bf16[6144,1536]{1,0:T(8,128)(2,1)} %refs_2_.17, bf16[80,3072]{1,0:T(8,128)(2,1)} %shard_map.102.refs_3_), custom_call_target="tpu_custom_call" | custom-call | tf_op jit(solution)/shard_map/pallas_call | solution.py:60
  158.2 4.5 %shard_map.104 = (bf16[48,1536]{1,0:T(8,128)(2,1)S(1)}, bf16[48,1536]{1,0:T(8,128)(2,1)S(1)}) custom-call(bf16[48,3072]{1,0:T(8,128)(2,1)S(1)} %shard_map.101.refs_3_.refs_0_, bf16[48,3072]{1,0:T(8,128)(2,1)S(1)} %collective-permute-done.23.refs_1_, bf16[6144,1536]{1,0:T(8,128)(2,1)} %refs_2_.17, f32[48,1536]{1,0:T(8,128)S(1)} %get-tuple-element.37.refs_3_, ...), custom_call_target="tpu_custom_call" | custom-call | tf_op jit(solution)/shard_map/pallas_call | solution.py:60
  164.2 1.9 %collective-permute-start.26 = (bf16[48,768]{1,0:T(8,128)(2,1)S(1)}, bf16[48,768]{1,0:T(8,128)(2,1)S(1)}, u32[]{:S(2)}, u32[]{:S(2)}) collective-permute-start(bf16[48,768]{1,0:T(8,128)(2,1)S(1)} %get-tuple-element.49), channel_id=1, source_target_pairs={{0,12},{4,8},{8,4},{12,0},{1,13},{5,9},{9,5},{13,1},{2,14},{6,10},... | collective-permute-start | bytes 221192 | tf_op jit(solution)/shard_map/ppermute | solution.py:313
  166.2 2.5 %collective-permute-start.28 = (bf16[48,768]{1,0:T(8,128)(2,1)S(1)}, bf16[48,768]{1,0:T(8,128)(2,1)S(1)}, u32[]{:S(2)}, u32[]{:S(2)}) collective-permute-start(bf16[48,768]{1,0:T(8,128)(2,1)S(1)} %get-tuple-element.50), channel_id=1, source_target_pairs={{0,4},{4,0},{8,12},{12,8},{1,5},{5,1},{9,13},{13,9},{2,6},{6,2},{1... | collective-permute-start | bytes 221192 | tf_op jit(solution)/shard_map/ppermute | solution.py:313
  168.7 3.7 %collective-permute-done.26 = bf16[48,768]{1,0:T(8,128)(2,1)S(1)} collective-permute-done((bf16[48,768]{1,0:T(8,128)(2,1)S(1)}, bf16[48,768]{1,0:T(8,128)(2,1)S(1)}, u32[]{:S(2)}, u32[]{:S(2)}) %collective-permute-start.26) | collective-permute-done | bytes 73760 | tf_op jit(solution)/shard_map/ppermute | solution.py:313
  172.4 3.4 %collective-permute-done.27 = bf16[48,768]{1,0:T(8,128)(2,1)S(1)} collective-permute-done((bf16[48,768]{1,0:T(8,128)(2,1)S(1)}, bf16[48,768]{1,0:T(8,128)(2,1)S(1)}, u32[]{:S(2)}, u32[]{:S(2)}) %collective-permute-start.27) | collective-permute-done | bytes 73760 | tf_op jit(solution)/shard_map/ppermute | solution.py:313
  (131 shorter events, 39.6 us)
Async XLA Ops:
  6.5 144.7 %reduce-scatter.3.cloned.1.call-start = ((), (), s32[]{:S(2)}) async-start(), calls=%async_computation.2 | async-start | bytes 983040 | tf_op jit(solution)/shard_map/reduce_scatter | solution.py:375
  30.4 3.6 %collective-permute-start = (f32[2,128]{1,0:T(2,128)S(1)}, f32[2,128]{1,0:T(2,128)S(1)}, u32[]{:S(2)}, u32[]{:S(2)}) collective-permute-start(f32[2,128]{1,0:T(2,128)S(1)} %pad_maximum_fusion.7), channel_id=1, source_target_pairs={{0,2},{2,0},{1,3},{3,1},{4,6},{6,4},{5,7},{7,5},{8,10},{10,8},{9,1... | collective-permute-start | bytes 3080 | tf_op jit(solution)/shard_map/ppermute | solution.py:296
  41.6 6.6 %collective-permute-start.4 = (bf16[128,3072]{1,0:T(8,128)(2,1)S(1)}, bf16[128,3072]{1,0:T(8,128)(2,1)S(1)}, u32[]{:S(2)}, u32[]{:S(2)}) collective-permute-start(bf16[128,3072]{1,0:T(8,128)(2,1)S(1)} %slice.145), channel_id=1, source_target_pairs={{0,1},{1,0},{2,3},{3,2},{4,5},{5,4},{6,7},{7,6},{8,9},{9,8},{10,11... | collective-permute-start | bytes 2359304 | tf_op jit(solution)/shard_map/ppermute | solution.py:290
  48.1 2.4 %collective-permute-start.2 = (bf16[128,3072]{1,0:T(8,128)(2,1)S(1)}, bf16[128,3072]{1,0:T(8,128)(2,1)S(1)}, u32[]{:S(2)}, u32[]{:S(2)}) collective-permute-start(bf16[128,3072]{1,0:T(8,128)(2,1)S(1)} %slice.146), channel_id=1, source_target_pairs={{0,1},{1,0},{2,3},{3,2},{4,5},{5,4},{6,7},{7,6},{8,9},{9,8},{10,11... | collective-permute-start | bytes 2359304 | tf_op jit(solution)/shard_map/ppermute | solution.py:290
  48.4 21.3 %collective-permute-start.5 = (bf16[128,3072]{1,0:T(8,128)(2,1)S(1)}, bf16[128,3072]{1,0:T(8,128)(2,1)S(1)}, u32[]{:S(2)}, u32[]{:S(2)}) collective-permute-start(bf16[128,3072]{1,0:T(8,128)(2,1)S(1)} %fusion.8.refs_0_), channel_id=1, source_target_pairs={{0,2},{2,0},{1,3},{3,1},{4,6},{6,4},{5,7},{7,5},{8,10},{10,8},{9,1... | collective-permute-start | bytes 2359304 | tf_op jit(solution)/shard_map/ppermute | solution.py:296
  72.1 3.6 %collective-permute-start.6 = (f32[2,128]{1,0:T(2,128)S(1)}, f32[2,128]{1,0:T(2,128)S(1)}, u32[]{:S(2)}, u32[]{:S(2)}) collective-permute-start(f32[2,128]{1,0:T(2,128)S(1)} %pad_maximum_fusion.8), channel_id=1, source_target_pairs={{0,2},{2,0},{1,3},{3,1},{4,6},{6,4},{5,7},{7,5},{8,10},{10,8},{9,1... | collective-permute-start | bytes 3080 | tf_op jit(solution)/shard_map/ppermute | solution.py:296
  76.2 25.0 %collective-permute-start.3 = (bf16[128,3072]{1,0:T(8,128)(2,1)S(1)}, bf16[128,3072]{1,0:T(8,128)(2,1)S(1)}, u32[]{:S(2)}, u32[]{:S(2)}) collective-permute-start(bf16[128,3072]{1,0:T(8,128)(2,1)S(1)} %fusion.9.refs_0_), channel_id=1, source_target_pairs={{0,2},{2,0},{1,3},{3,1},{4,6},{6,4},{5,7},{7,5},{8,10},{10,8},{9,1... | collective-permute-start | bytes 2359304 | tf_op jit(solution)/shard_map/ppermute | solution.py:296
  81.9 18.5 %collective-permute-start.9 = (bf16[256,384]{1,0:T(8,128)(2,1)S(1)}, bf16[256,384]{1,0:T(8,128)(2,1)S(1)}, u32[]{:S(2)}, u32[]{:S(2)}) collective-permute-start(bf16[256,384]{1,0:T(8,128)(2,1)S(1)} %shard_map.84.refs_0_), channel_id=1, source_target_pairs={{0,2},{2,0},{1,3},{3,1},{4,6},{6,4},{5,7},{7,5},{8,10},{10,8},{9,1... | collective-permute-start | bytes 589832 | tf_op jit(solution)/shard_map/ppermute | solution.py:296
  87.4 14.6 %collective-permute-start.12 = (bf16[128,3072]{1,0:T(8,128)(2,1)S(1)}, bf16[128,3072]{1,0:T(8,128)(2,1)S(1)}, u32[]{:S(2)}, u32[]{:S(2)}) collective-permute-start(bf16[128,3072]{1,0:T(8,128)(2,1)S(1)} %get-tuple-element.27), channel_id=1, source_target_pairs={{0,1},{1,0},{2,3},{3,2},{4,5},{5,4},{6,7},{7,6},{8,9},{9,8},{10,11... | collective-permute-start | bytes 2359304 | tf_op jit(solution)/shard_map/ppermute | solution.py:290
  87.5 17.6 %collective-permute-start.11 = (bf16[128,3072]{1,0:T(8,128)(2,1)S(1)}, bf16[128,3072]{1,0:T(8,128)(2,1)S(1)}, u32[]{:S(2)}, u32[]{:S(2)}) collective-permute-start(bf16[128,3072]{1,0:T(8,128)(2,1)S(1)} %shard_map.82.refs_0_), channel_id=1, source_target_pairs={{0,1},{1,0},{2,3},{3,2},{4,5},{5,4},{6,7},{7,6},{8,9},{9,8},{10,11... | collective-permute-start | bytes 2359304 | tf_op jit(solution)/shard_map/ppermute | solution.py:290
  93.0 12.0 %collective-permute-start.13 = (bf16[128,3072]{1,0:T(8,128)(2,1)S(1)}, bf16[128,3072]{1,0:T(8,128)(2,1)S(1)}, u32[]{:S(2)}, u32[]{:S(2)}) collective-permute-start(bf16[128,3072]{1,0:T(8,128)(2,1)S(1)} %get-tuple-element.28), channel_id=1, source_target_pairs={{0,1},{1,0},{2,3},{3,2},{4,5},{5,4},{6,7},{7,6},{8,9},{9,8},{10,11... | collective-permute-start | bytes 2359304 | tf_op jit(solution)/shard_map/ppermute | solution.py:290
  101.9 8.4 %collective-permute-start.10 = (bf16[128,3072]{1,0:T(8,128)(2,1)S(1)}, bf16[128,3072]{1,0:T(8,128)(2,1)S(1)}, u32[]{:S(2)}, u32[]{:S(2)}) collective-permute-start(bf16[128,3072]{1,0:T(8,128)(2,1)S(1)} %shard_map.88.refs_2_.refs_0_), channel_id=1, source_target_pairs={{0,1},{1,0},{2,3},{3,2},{4,5},{5,4},{6,7},{7,6},{8,9},{9,8},{10,11... | collective-permute-start | bytes 2359304 | tf_op jit(solution)/shard_map/ppermute | solution.py:290
  102.1 13.7 %collective-permute-start.16 = (bf16[80,3072]{1,0:T(8,128)(2,1)S(1)}, bf16[80,3072]{1,0:T(8,128)(2,1)S(1)}, u32[]{:S(2)}, u32[]{:S(2)}) collective-permute-start(bf16[80,3072]{1,0:T(8,128)(2,1)S(1)} %shard_map.89.refs_3_.refs_0_), channel_id=1, source_target_pairs={{0,2},{2,0},{1,3},{3,1},{4,6},{6,4},{5,7},{7,5},{8,10},{10,8},{9,1... | collective-permute-start | bytes 1474568 | tf_op jit(solution)/shard_map/ppermute | solution.py:296
  118.2 57.7 %reduce-scatter.5.cloned.1.call-start = ((), (), s32[]{:S(2)}) async-start(), calls=%async_computation.3 | async-start | bytes 614400 | tf_op jit(solution)/shard_map/reduce_scatter | solution.py:375
  118.4 13.4 %collective-permute-start.17 = (bf16[80,3072]{1,0:T(8,128)(2,1)S(1)}, bf16[80,3072]{1,0:T(8,128)(2,1)S(1)}, u32[]{:S(2)}, u32[]{:S(2)}) collective-permute-start(bf16[80,3072]{1,0:T(8,128)(2,1)S(1)} %shard_map.90.refs_4_.refs_0_), channel_id=1, source_target_pairs={{0,2},{2,0},{1,3},{3,1},{4,6},{6,4},{5,7},{7,5},{8,10},{10,8},{9,1... | collective-permute-start | bytes 1474568 | tf_op jit(solution)/shard_map/ppermute | solution.py:296
  119.4 15.8 %collective-permute-start.19 = (bf16[80,3072]{1,0:T(8,128)(2,1)S(1)}, bf16[80,3072]{1,0:T(8,128)(2,1)S(1)}, u32[]{:S(2)}, u32[]{:S(2)}) collective-permute-start(bf16[80,3072]{1,0:T(8,128)(2,1)S(1)} %shard_map.93.refs_3_.refs_2_.refs_0_), channel_id=1, source_target_pairs={{0,1},{1,0},{2,3},{3,2},{4,5},{5,4},{6,7},{7,6},{8,9},{9,8},{10,11... | collective-permute-start | bytes 1474568 | tf_op jit(solution)/shard_map/ppermute | solution.py:290
  133.0 10.4 %collective-permute-start.18 = (bf16[80,3072]{1,0:T(8,128)(2,1)S(1)}, bf16[80,3072]{1,0:T(8,128)(2,1)S(1)}, u32[]{:S(2)}, u32[]{:S(2)}) collective-permute-start(bf16[80,3072]{1,0:T(8,128)(2,1)S(1)} %shard_map.97.refs_3_.refs_0_), channel_id=1, source_target_pairs={{0,1},{1,0},{2,3},{3,2},{4,5},{5,4},{6,7},{7,6},{8,9},{9,8},{10,11... | collective-permute-start | bytes 1474568 | tf_op jit(solution)/shard_map/ppermute | solution.py:290
  133.1 9.9 %collective-permute-start.20 = (bf16[48,3072]{1,0:T(8,128)(2,1)S(1)}, bf16[48,3072]{1,0:T(8,128)(2,1)S(1)}, u32[]{:S(2)}, u32[]{:S(2)}) collective-permute-start(bf16[48,3072]{1,0:T(8,128)(2,1)S(1)} %shard_map.95.refs_3_.refs_0_), channel_id=1, source_target_pairs={{0,2},{2,0},{1,3},{3,1},{4,6},{6,4},{5,7},{7,5},{8,10},{10,8},{9,1... | collective-permute-start | bytes 884744 | tf_op jit(solution)/shard_map/ppermute | solution.py:296
  134.0 14.8 %collective-permute-start.22 = (bf16[48,3072]{1,0:T(8,128)(2,1)S(1)}, bf16[48,3072]{1,0:T(8,128)(2,1)S(1)}, u32[]{:S(2)}, u32[]{:S(2)}) collective-permute-start(bf16[48,3072]{1,0:T(8,128)(2,1)S(1)} %shard_map.96.refs_4_.refs_0_), channel_id=1, source_target_pairs={{0,2},{2,0},{1,3},{3,1},{4,6},{6,4},{5,7},{7,5},{8,10},{10,8},{9,1... | collective-permute-start | bytes 884744 | tf_op jit(solution)/shard_map/ppermute | solution.py:296
  143.4 9.7 %collective-permute-start.24 = (bf16[48,3072]{1,0:T(8,128)(2,1)S(1)}, bf16[48,3072]{1,0:T(8,128)(2,1)S(1)}, u32[]{:S(2)}, u32[]{:S(2)}) collective-permute-start(bf16[48,3072]{1,0:T(8,128)(2,1)S(1)} %shard_map.99.refs_8_.refs_0_), channel_id=1, source_target_pairs={{0,1},{1,0},{2,3},{3,2},{4,5},{5,4},{6,7},{7,6},{8,9},{9,8},{10,11... | collective-permute-start | bytes 884744 | tf_op jit(solution)/shard_map/ppermute | solution.py:290
  149.3 8.9 %collective-permute-start.23 = (bf16[48,3072]{1,0:T(8,128)(2,1)S(1)}, bf16[48,3072]{1,0:T(8,128)(2,1)S(1)}, u32[]{:S(2)}, u32[]{:S(2)}) collective-permute-start(bf16[48,3072]{1,0:T(8,128)(2,1)S(1)} %shard_map.101.refs_3_.refs_0_), channel_id=1, source_target_pairs={{0,1},{1,0},{2,3},{3,2},{4,5},{5,4},{6,7},{7,6},{8,9},{9,8},{10,11... | collective-permute-start | bytes 884744 | tf_op jit(solution)/shard_map/ppermute | solution.py:290
  164.2 8.2 %collective-permute-start.26 = (bf16[48,768]{1,0:T(8,128)(2,1)S(1)}, bf16[48,768]{1,0:T(8,128)(2,1)S(1)}, u32[]{:S(2)}, u32[]{:S(2)}) collective-permute-start(bf16[48,768]{1,0:T(8,128)(2,1)S(1)} %get-tuple-element.49), channel_id=1, source_target_pairs={{0,12},{4,8},{8,4},{12,0},{1,13},{5,9},{9,5},{13,1},{2,14},{6,10},... | collective-permute-start | bytes 221192 | tf_op jit(solution)/shard_map/ppermute | solution.py:313
  166.2 9.6 %collective-permute-start.27 = (bf16[48,768]{1,0:T(8,128)(2,1)S(1)}, bf16[48,768]{1,0:T(8,128)(2,1)S(1)}, u32[]{:S(2)}, u32[]{:S(2)}) collective-permute-start(bf16[48,768]{1,0:T(8,128)(2,1)S(1)} %get-tuple-element.51), channel_id=1, source_target_pairs={{0,8},{4,12},{8,0},{12,4},{1,9},{5,13},{9,1},{13,5},{2,10},{6,14},... | collective-permute-start | bytes 221192 | tf_op jit(solution)/shard_map/ppermute | solution.py:313
  166.2 9.6 %collective-permute-start.28 = (bf16[48,768]{1,0:T(8,128)(2,1)S(1)}, bf16[48,768]{1,0:T(8,128)(2,1)S(1)}, u32[]{:S(2)}, u32[]{:S(2)}) collective-permute-start(bf16[48,768]{1,0:T(8,128)(2,1)S(1)} %get-tuple-element.50), channel_id=1, source_target_pairs={{0,4},{4,0},{8,12},{12,8},{1,5},{5,1},{9,13},{13,9},{2,6},{6,2},{1... | collective-permute-start | bytes 221192 | tf_op jit(solution)/shard_map/ppermute | solution.py:313
  (19 other events, 77.4 us)
Sparse Core Ops, SparseCore 0:
  118.3 22.1 reduce-scatter.2
  153.1 21.7 reduce-scatter.4

commit v10 on v9

--- a/solution.py
+++ b/solution.py
@@ -12,12 +12,14 @@
 PATCHES = 256
 EPS = 1e-06
 SHARES = (8, 5, 3)
-PIECES = (1, 1)
+LEAD_PIECES = (1, 1)
+REST_PIECES = (2, 1)
 AHEAD = 4
 GAIN_ROWS = 8
 BF16, F32 = jnp.bfloat16, jnp.float32
 PARAMS = pltpu.CompilerParams(vmem_limit_bytes=48 * 2**20)
 SMALL = pltpu.CompilerParams(vmem_limit_bytes=8 * 2**20)
+MIDDLE = pltpu.CompilerParams(vmem_limit_bytes=16 * 2**20)
 SOON = pl.CostEstimate(flops=0, bytes_accessed=0, transcendentals=0)
 
 
@@ -36,8 +38,9 @@
     return lax.shift_right_logical(corner & 1, 1).astype(F32)
 
 
-def slices(size, shares):
+def slices(size, shares, grain):
     ends = [sum(shares[: i + 1]) * size // sum(shares) for i in range(len(shares))]
+    ends = [end // grain * grain for end in ends]
     return [slice(a, b) for a, b in zip([0] + ends[:-1], ends)]
 
 
@@ -89,19 +92,24 @@
     )
 
 
-def sum_rows(near, far, cut, earlier=()):
-    spec = pl.BlockSpec(near.shape, lambda *_: (0, 0))
-    shape = (cut.stop - cut.start, near.shape[1])
+def sum_rows(pairs, cut, earlier=()):
+    widths = [near.shape[1] for near, _ in pairs]
+    shape = (cut.stop - cut.start, sum(widths))
 
     def kernel(ins, outs):
-        outs[0][...] = (ins[0][cut].astype(F32) + ins[1][cut].astype(F32)).astype(BF16)
-
-    return call(
-        kernel,
-        earlier,
-        (near, far),
-        [spec, spec],
-        params=SMALL,
+        start = 0
+        for at, width in enumerate(widths):
+            total = ins[2 * at][cut].astype(F32) + ins[2 * at + 1][cut].astype(F32)
+            outs[0][:, start : start + width] = total.astype(BF16)
+            start += width
+
+    operands = [part for pair in pairs for part in pair]
+    return call(
+        kernel,
+        earlier,
+        operands,
+        [pl.BlockSpec(part.shape, lambda *_: (0, 0)) for part in operands],
+        params=MIDDLE,
         grid=(1,),
         out_specs=pl.BlockSpec(shape, lambda *_: (0, 0)),
         out_shape=jax.ShapeDtypeStruct(shape, BF16),
@@ -319,8 +327,9 @@
         qkv_rows = w_qkv.reshape(w_qkv.shape[0], w_qkv.shape[1] * w_qkv.shape[2])
         attn_rows = w_attn.reshape(w_attn.shape[0] * w_attn.shape[1], w_attn.shape[2])
         depth, units = w_up.shape
-        cuts = slices(tokens.shape[0], SHARES)
-        pieces = slices(units, PIECES)
+        cuts = slices(tokens.shape[0], SHARES, 16)
+        pieces = slices(units, LEAD_PIECES, 128)
+        rest_pieces = slices(units, REST_PIECES, 128)
 
         first = cuts[0].stop
         gain_rows = jnp.broadcast_to(ln_gain[None], (GAIN_ROWS, width))
@@ -355,8 +364,8 @@
         pair = [jnp.concatenate(p, axis=0) for p in zip(lead_pair, rest_pair)]
         near, far = project_rows(*pair, qkv_rows, slice(0, qkv_rows.shape[1]))
         halves, before = [], [near]
-        qkv = sum_rows(near, swap(far), slice(0, tokens.shape[0]))
-        for piece in pieces:
+        qkv = sum_rows([(near, swap(far))], slice(0, tokens.shape[0]))
+        for piece in rest_pieces:
             near, far = project_rows(*rest_pair, w_up, piece, before)
             halves.append((near, swap(far)))
             before = [near]
@@ -366,9 +375,9 @@
             attention = (attended[cut], attended_other[cut], attn_rows) if last else ()
             return project_hidden(have, swap(have), w_down, piece, terms, attention, last, earlier)
 
-        def chunk_sums(c, earlier):
+        def chunk_sums(pairs, c, earlier):
             part = slice(cuts[c].start - first, cuts[c].stop - first)
-            return [sum_rows(*half, part, [earlier]) for half in halves]
+            return sum_rows(pairs, part, [earlier])
 
         def scatter(kept, got, earlier):
             full = side_by_side(kept, got, core, earlier)
@@ -377,29 +386,25 @@
         attended = attend(all_red(qkv), q_gain, k_gain, [halves[-1][0]])
         attended_other = swap(attended)
         second = gelu_sum(lead_parts[1], [attended])
-        sums = chunk_sums(1, second)
-        parts = [all_red(x) for x in sums]
-        terms = output(arrived, pieces[0], (), cuts[0], sums)
-        terms = output(second, pieces[1], terms, cuts[0])
+        sums = chunk_sums(halves, 1, second)
+        parts = all_red(sums)
+        terms = output(arrived, pieces[0], (), cuts[0], [sums])
+        coming = [chunk_sums([half], 2, terms[0]) for half in halves]
+        terms = output(second, pieces[1], terms, cuts[0], coming)
+        coming = [all_red(x) for x in coming]
+        full, got = scatter(terms[0], swap(terms[1]), [])
+        scattered = [got]
+
+        hidden = gelu_sum(parts, [full])
+        terms = output(hidden, slice(0, units), (), cuts[1])
         waiting = terms[0], swap(terms[1])
 
-        hidden = gelu_sum(parts[0], [terms[0]])
-        full, got = scatter(*waiting, [hidden])
-        scattered = [got]
-        sums = chunk_sums(2, hidden)
-        coming = [all_red(x) for x in sums]
-        second = gelu_sum(parts[1], [full, *sums])
-        terms = output(hidden, pieces[0], (), cuts[1], [second])
-
         hidden = gelu_sum(coming[0], [terms[0]])
-        terms = output(second, pieces[1], terms, cuts[1], [hidden])
-        waiting = terms[0], swap(terms[1])
-
-        second = gelu_sum(coming[1], [terms[0]])
-        full, got = scatter(*waiting, [second, scattered[0]])
+        full, got = scatter(*waiting, [hidden, scattered[0]])
         scattered.append(got)
-        terms = output(hidden, pieces[0], (), cuts[2], [full])
-        kept, sent = output(second, pieces[1], terms, cuts[2])
+        terms = output(hidden, rest_pieces[0], (), cuts[2], [full])
+        hidden = gelu_sum(coming[1], [terms[0]])
+        kept, sent = output(hidden, rest_pieces[1], terms, cuts[2])
         outs = [tokens[cut].astype(F32) + got.astype(F32) for cut, got in zip(cuts, scattered)]
         outs.append(tokens[cuts[2]].astype(F32) + collect(kept, swap(sent), width))
         return jnp.concatenate(outs, axis=0)

time: 185 us -> 183 us (0.989)
  Pallas kernels: 47.1 us -> 45 us
    ppermute x9 -> x8, waiting for transfers between devices: 25.6 us -> 18.7 us  [all_red(): parts.append(lax.ppermute(x, 'red', pairs))]
    ppermute x3, waiting for transfers between devices: 7.08 us -> 10.6 us  [collect(): total = total + lax.ppermute(block(chip ^ k), 'wide', pairs).astype(F32)]
    ppermute x17 -> x16, waiting for transfers between devices: 8.04 us -> 10.7 us  [swap(): return lax.ppermute(x, 'tok', [(0, 1), (1, 0)])]
    pallas_call x23 -> x20, Pallas kernels: 47.1 us -> 45 us  [call(): pl.pallas_call(body, in_specs=list(specs) + [corner_of(a) for a in earlie...]
    reduce_scatter x2, waiting for transfers between devices: 0.02 us -> 1.94 us  [scatter(): lax.psum_scatter(full, 'wide', scatter_dimension=1, tiled=True)]
    unnamed x25 -> x17, local copies, waits for them, and re-layouts: 7.75 us -> 6.47 us
    ppermute x9 -> x8, starting transfers between devices: 11.5 us -> 11.4 us  [all_red(): parts.append(lax.ppermute(x, 'red', pairs))]
  transfers between devices with their start and end apart: 31 -> 29, of which waited for: 17 -> 18; matrix products, arithmetic and copies ran while one was open for 2% -> 2% of each run, Pallas kernels for 25% -> 24%
where the time goes in v10:
time: 183 us
  Pallas kernels  45 us (25%)
  waiting for transfers between devices  42 us (23%)
  blocking collectives  39.8 us (22%)
  starting transfers between devices  19.4 us (11%)
  between operations  15.2 us (8%)
  local copies, waits for them, and re-layouts  9.5 us (5%)
  matrix products  7.91 us (4%)
  other arithmetic  3.79 us (2%)
    pallas_call x20, Pallas kernels, call(): pl.pallas_call(body, in_specs=list(specs) + [corner_of(a) for a in earlie...  45 us
    all_gather x1, blocking collectives, body(): lead = lax.all_gather(lead, 'wide', axis=1, tiled=True)  21.9 us
    ppermute x8, waiting for transfers between devices, all_red(): parts.append(lax.ppermute(x, 'red', pairs))  18.7 us
    all_gather x1, blocking collectives, body(): rest = lax.all_gather(rest, 'wide', axis=1, tiled=True)  18 us
    ppermute x8, starting transfers between devices, all_red(): parts.append(lax.ppermute(x, 'red', pairs))  11.4 us
    ppermute x16, waiting for transfers between devices, swap(): return lax.ppermute(x, 'tok', [(0, 1), (1, 0)])  10.7 us
    ppermute x3, waiting for transfers between devices, collect(): total = total + lax.ppermute(block(chip ^ k), 'wide', pairs).astype(F32)  10.6 us
    dot_general x2, matrix products, project(): part = jnp.dot(both, weight, preferred_element_type=F32)  7.91 us
  transfers between devices with their start and end apart: 29, of which 18 were waited for; matrix products, arithmetic and copies ran while one was open for 2% of the time, Pallas kernels for 24%

profile of v10, /device:TPU:0, one launch (start us, length us, event | category | flops | bytes accessed | tf_op | source)
XLA Modules:
  0.0 182.7 jit_solution(10296019037531720180)
XLA Ops:
  8.2 21.9 %all_gather.6 = bf16[136,3072]{1,0:T(8,128)(2,1)S(1)} all-gather(bf16[136,768]{1,0:T(8,128)(2,1)S(1)} %pad_maximum_fusion.6), channel_id=1, replica_groups=mesh['grp'=2,'wide'=4,'red'=2,'tok'=2] {'wide'}, dimensions={1}, use_global_device_ids=true | all-gather | bytes 1044480 | tf_op jit(solution)/shard_map/all_gather | solution.py:337
  31.9 2.1 %collective-permute-done = f32[2,128]{1,0:T(2,128)S(1)} collective-permute-done((f32[2,128]{1,0:T(2,128)S(1)}, f32[2,128]{1,0:T(2,128)S(1)}, u32[]{:S(2)}, u32[]{:S(2)}) %collective-permute-start) | collective-permute-done | bytes 1056 | tf_op jit(solution)/shard_map/ppermute | solution.py:304
  34.5 1.7 collective-permute-done.1
  36.2 5.3 %fusion = f32[256,3072]{1,0:T(8,128)S(1)} fusion(bf16[1536,6144]{1,0:T(8,128)(2,1)} %refs_2_.9, bf16[128,1536]{1,0:T(8,128)(2,1)S(1)} %get-tuple-element.44, bf16[128,1536]{1,0:T(8,128)(2,1)S(1)} %collective-permute-done.1), kind=kOutput, calls=%fused_computation | convolution fusion | flops 2417491968 | bytes 13369344 | tf_op jit(solution)/shard_map/dot_general | solution.py:351
  41.8 3.5 %copy-done.6 = bf16[1536,6144]{1,0:T(8,128)(2,1)S(1)} copy-done((bf16[1536,6144]{1,0:T(8,128)(2,1)S(1)}, bf16[1536,6144]{1,0:T(8,128)(2,1)}, u32[]{:S(2)}) %copy-start.6) | copy-done | bytes 18874392
  45.4 2.6 %fusion.2 = f32[256,3072]{1,0:T(8,128)S(1)} fusion(bf16[1536,6144]{1,0:T(8,128)(2,1)S(1)} %copy-done.6, bf16[128,1536]{1,0:T(8,128)(2,1)S(1)} %get-tuple-element.44, bf16[128,1536]{1,0:T(8,128)(2,1)S(1)} %collective-permute-done.1), kind=kOutput, calls=%fused_computation.2 | convolution fusion | flops 2417491968 | bytes 13369344 | tf_op jit(solution)/shard_map/dot_general | solution.py:351
  51.8 18.0 %all_gather.7 = bf16[128,3072]{1,0:T(8,128)(2,1)S(1)} all-gather(bf16[128,768]{1,0:T(8,128)(2,1)S(1)} %slice_add_fusion.2), channel_id=1, replica_groups=mesh['grp'=2,'wide'=4,'red'=2,'tok'=2] {'wide'}, dimensions={1}, use_global_device_ids=true | all-gather | bytes 983040 | tf_op jit(solution)/shard_map/all_gather | solution.py:362
  73.6 2.1 %collective-permute-done.6 = f32[2,128]{1,0:T(2,128)S(1)} collective-permute-done((f32[2,128]{1,0:T(2,128)S(1)}, f32[2,128]{1,0:T(2,128)S(1)}, u32[]{:S(2)}, u32[]{:S(2)}) %collective-permute-start.6) | collective-permute-done | bytes 1056 | tf_op jit(solution)/shard_map/ppermute | solution.py:304
  80.3 6.1 %shard_map.85 = (bf16[128,4096]{1,0:T(8,128)(2,1)S(1)}, bf16[128,4096]{1,0:T(8,128)(2,1)S(1)}) custom-call(bf16[128,1536]{1,0:T(8,128)(2,1)S(1)} %get-tuple-element.42.refs_0_, bf16[128,1536]{1,0:T(8,128)(2,1)S(1)} %collective-permute-done.7.refs_1_, bf16[1536,6144]{1,0:T(8,128)(2,1)} %refs_2_.9, bf16[256,384]{1,0:T(8,128)(2,1)S(1)} %get-tuple-element.21.refs_0_.refs_3_), custom_call_target="tpu_custom_call" | custom-call | tf_op jit(solution)/shard_map/pallas_call | solution.py:63
  87.0 2.4 %collective-permute-done.8.refs_1_ = bf16[256,384]{1,0:T(8,128)(2,1)S(1)} collective-permute-done((bf16[256,384]{1,0:T(8,128)(2,1)S(1)}, bf16[256,384]{1,0:T(8,128)(2,1)S(1)}, u32[]{:S(2)}, u32[]{:S(2)}) %collective-permute-start.8) | collective-permute-done | bytes 196640 | tf_op jit(solution)/shard_map/ppermute | solution.py:298
  90.1 3.8 %shard_map.86 = (bf16[128,2048]{1,0:T(8,128)(2,1)S(1)}, bf16[128,2048]{1,0:T(8,128)(2,1)S(1)}) custom-call(bf16[128,1536]{1,0:T(8,128)(2,1)S(1)} %get-tuple-element.42.refs_0_, bf16[128,1536]{1,0:T(8,128)(2,1)S(1)} %collective-permute-done.7.refs_1_, bf16[1536,6144]{1,0:T(8,128)(2,1)} %refs_2_.9, bf16[128,4096]{1,0:T(8,128)(2,1)S(1)} %get-tuple-element.23.refs_3_.refs_0_), custom_call_target="tpu_custom_call" | custom-call | tf_op jit(solution)/shard_map/pallas_call | solution.py:63
  94.4 5.9 %collective-permute-done.9.refs_1_ = bf16[256,384]{1,0:T(8,128)(2,1)S(1)} collective-permute-done((bf16[256,384]{1,0:T(8,128)(2,1)S(1)}, bf16[256,384]{1,0:T(8,128)(2,1)S(1)}, u32[]{:S(2)}, u32[]{:S(2)}) %collective-permute-start.9) | collective-permute-done | bytes 196640 | tf_op jit(solution)/shard_map/ppermute | solution.py:304
  105.1 5.0 %shard_map.90 = (f32[128,1536]{1,0:T(8,128)S(1)}, f32[128,1536]{1,0:T(8,128)S(1)}) custom-call(bf16[128,3072]{1,0:T(8,128)(2,1)S(1)} %shard_map.82.refs_0_, bf16[128,3072]{1,0:T(8,128)(2,1)S(1)} %collective-permute-done.11.refs_1_, bf16[6144,1536]{1,0:T(8,128)(2,1)} %refs_2_.15, bf16[80,6144]{1,0:T(8,128)(2,1)S(1)} %shard_map.89.refs_3_.refs_0_), custom_call_target="tpu_custom_call" | custom-call | tf_op jit(solution)/shard_map/pallas_call | solution.py:63
  111.2 5.1 %shard_map.93 = (bf16[128,1536]{1,0:T(8,128)(2,1)S(1)}, bf16[128,1536]{1,0:T(8,128)(2,1)S(1)}) custom-call(bf16[128,3072]{1,0:T(8,128)(2,1)S(1)} %shard_map.88.refs_4_.refs_0_, bf16[128,3072]{1,0:T(8,128)(2,1)S(1)} %collective-permute-done.10.refs_1_, bf16[6144,1536]{1,0:T(8,128)(2,1)} %refs_2_.15, f32[128,1536]{1,0:T(8,128)S(1)} %get-tuple-element.27.refs_2_.refs_3_, ...), custom_call_target="tpu_custom_call" | custom-call | tf_op jit(solution)/shard_map/pallas_call | solution.py:63
  119.3 7.2 %collective-permute-done.16.refs_1_ = bf16[80,6144]{1,0:T(8,128)(2,1)S(1)} collective-permute-done((bf16[80,6144]{1,0:T(8,128)(2,1)S(1)}, bf16[80,6144]{1,0:T(8,128)(2,1)S(1)}, u32[]{:S(2)}, u32[]{:S(2)}) %collective-permute-start.16) | collective-permute-done | bytes 983072 | tf_op jit(solution)/shard_map/ppermute | solution.py:304
  126.5 1.7 shard_map.95.refs_0_
  130.8 7.5 %shard_map.96 = (bf16[80,1536]{1,0:T(8,128)(2,1)S(1)}, bf16[80,1536]{1,0:T(8,128)(2,1)S(1)}) custom-call(bf16[80,6144]{1,0:T(8,128)(2,1)S(1)} %shard_map.95.refs_0_, bf16[80,6144]{1,0:T(8,128)(2,1)S(1)} %collective-permute-done.17.refs_1_, bf16[6144,1536]{1,0:T(8,128)(2,1)} %refs_2_.15, bf16[80,128]{1,0:T(8,128)(2,1)S(1)} %slice.113.refs_3_, ...), custom_call_target="tpu_custom_call" | custom-call | tf_op jit(solution)/shard_map/pallas_call | solution.py:63
  144.2 6.0 %shard_map.99 = (f32[48,1536]{1,0:T(8,128)S(1)}, f32[48,1536]{1,0:T(8,128)S(1)}) custom-call(bf16[48,4096]{1,0:T(8,128)(2,1)S(1)} %shard_map.97.refs_3_.refs_0_, bf16[48,4096]{1,0:T(8,128)(2,1)S(1)} %collective-permute-done.21.refs_1_, bf16[6144,1536]{1,0:T(8,128)(2,1)} %refs_2_.15, bf16[80,3072]{1,0:T(8,128)(2,1)} %shard_map.98.refs_3_), custom_call_target="tpu_custom_call" | custom-call | tf_op jit(solution)/shard_map/pallas_call | solution.py:63
  152.0 3.4 %shard_map.101 = (bf16[48,1536]{1,0:T(8,128)(2,1)S(1)}, bf16[48,1536]{1,0:T(8,128)(2,1)S(1)}) custom-call(bf16[48,2048]{1,0:T(8,128)(2,1)S(1)} %shard_map.100.refs_0_, bf16[48,2048]{1,0:T(8,128)(2,1)S(1)} %collective-permute-done.22.refs_1_, bf16[6144,1536]{1,0:T(8,128)(2,1)} %refs_2_.15, f32[48,1536]{1,0:T(8,128)S(1)} %get-tuple-element.33.refs_2_.refs_3_, ...), custom_call_target="tpu_custom_call" | custom-call | tf_op jit(solution)/shard_map/pallas_call | solution.py:63
  156.9 1.8 %collective-permute-start.24 = (bf16[48,768]{1,0:T(8,128)(2,1)S(1)}, bf16[48,768]{1,0:T(8,128)(2,1)S(1)}, u32[]{:S(2)}, u32[]{:S(2)}) collective-permute-start(bf16[48,768]{1,0:T(8,128)(2,1)S(1)} %get-tuple-element.45), channel_id=1, source_target_pairs={{0,12},{4,8},{8,4},{12,0},{1,13},{5,9},{9,5},{13,1},{2,14},{6,10},... | collective-permute-start | bytes 221192 | tf_op jit(solution)/shard_map/ppermute | solution.py:321
  158.7 2.6 %collective-permute-start.26 = (bf16[48,768]{1,0:T(8,128)(2,1)S(1)}, bf16[48,768]{1,0:T(8,128)(2,1)S(1)}, u32[]{:S(2)}, u32[]{:S(2)}) collective-permute-start(bf16[48,768]{1,0:T(8,128)(2,1)S(1)} %get-tuple-element.46), channel_id=1, source_target_pairs={{0,4},{4,0},{8,12},{12,8},{1,5},{5,1},{9,13},{13,9},{2,6},{6,2},{1... | collective-permute-start | bytes 221192 | tf_op jit(solution)/shard_map/ppermute | solution.py:321
  161.4 4.0 %collective-permute-done.24 = bf16[48,768]{1,0:T(8,128)(2,1)S(1)} collective-permute-done((bf16[48,768]{1,0:T(8,128)(2,1)S(1)}, bf16[48,768]{1,0:T(8,128)(2,1)S(1)}, u32[]{:S(2)}, u32[]{:S(2)}) %collective-permute-start.24) | collective-permute-done | bytes 73760 | tf_op jit(solution)/shard_map/ppermute | solution.py:321
  165.4 6.6 %collective-permute-done.25 = bf16[48,768]{1,0:T(8,128)(2,1)S(1)} collective-permute-done((bf16[48,768]{1,0:T(8,128)(2,1)S(1)}, bf16[48,768]{1,0:T(8,128)(2,1)S(1)}, u32[]{:S(2)}, u32[]{:S(2)}) %collective-permute-start.25) | collective-permute-done | bytes 73760 | tf_op jit(solution)/shard_map/ppermute | solution.py:321
  172.0 1.9 %reduce-scatter.5.cloned.1.call-done = bf16[80,768]{1,0:T(8,128)(2,1)} async-done(((bf16[80,3072]{1,0:T(8,128)(2,1)}), bf16[80,768]{1,0:T(8,128)(2,1)}) %reduce-scatter.5.cloned.1.call-update) | async-done | bytes 122896 | tf_op jit(solution)/shard_map/reduce_scatter | solution.py:384
  (116 shorter events, 39.3 us)
Async XLA Ops:
  6.5 135.8 %reduce-scatter.3.cloned.1.call-start = ((), (), s32[]{:S(2)}) async-start(), calls=%async_computation.2 | async-start | bytes 983040 | tf_op jit(solution)/shard_map/reduce_scatter | solution.py:384
  30.4 3.6 %collective-permute-start = (f32[2,128]{1,0:T(2,128)S(1)}, f32[2,128]{1,0:T(2,128)S(1)}, u32[]{:S(2)}, u32[]{:S(2)}) collective-permute-start(f32[2,128]{1,0:T(2,128)S(1)} %pad_maximum_fusion.7), channel_id=1, source_target_pairs={{0,2},{2,0},{1,3},{3,1},{4,6},{6,4},{5,7},{7,5},{8,10},{10,8},{9,1... | collective-permute-start | bytes 3080 | tf_op jit(solution)/shard_map/ppermute | solution.py:304
  34.4 1.8 collective-permute-start.1
  41.6 6.6 %collective-permute-start.4 = (bf16[128,3072]{1,0:T(8,128)(2,1)S(1)}, bf16[128,3072]{1,0:T(8,128)(2,1)S(1)}, u32[]{:S(2)}, u32[]{:S(2)}) collective-permute-start(bf16[128,3072]{1,0:T(8,128)(2,1)S(1)} %slice.145), channel_id=1, source_target_pairs={{0,1},{1,0},{2,3},{3,2},{4,5},{5,4},{6,7},{7,6},{8,9},{9,8},{10,11... | collective-permute-start | bytes 2359304 | tf_op jit(solution)/shard_map/ppermute | solution.py:298
  48.1 2.4 %collective-permute-start.2 = (bf16[128,3072]{1,0:T(8,128)(2,1)S(1)}, bf16[128,3072]{1,0:T(8,128)(2,1)S(1)}, u32[]{:S(2)}, u32[]{:S(2)}) collective-permute-start(bf16[128,3072]{1,0:T(8,128)(2,1)S(1)} %slice.146), channel_id=1, source_target_pairs={{0,1},{1,0},{2,3},{3,2},{4,5},{5,4},{6,7},{7,6},{8,9},{9,8},{10,11... | collective-permute-start | bytes 2359304 | tf_op jit(solution)/shard_map/ppermute | solution.py:298
  48.5 21.3 %collective-permute-start.5 = (bf16[128,3072]{1,0:T(8,128)(2,1)S(1)}, bf16[128,3072]{1,0:T(8,128)(2,1)S(1)}, u32[]{:S(2)}, u32[]{:S(2)}) collective-permute-start(bf16[128,3072]{1,0:T(8,128)(2,1)S(1)} %fusion.8.refs_0_), channel_id=1, source_target_pairs={{0,2},{2,0},{1,3},{3,1},{4,6},{6,4},{5,7},{7,5},{8,10},{10,8},{9,1... | collective-permute-start | bytes 2359304 | tf_op jit(solution)/shard_map/ppermute | solution.py:304
  72.0 3.6 %collective-permute-start.6 = (f32[2,128]{1,0:T(2,128)S(1)}, f32[2,128]{1,0:T(2,128)S(1)}, u32[]{:S(2)}, u32[]{:S(2)}) collective-permute-start(f32[2,128]{1,0:T(2,128)S(1)} %pad_maximum_fusion.8), channel_id=1, source_target_pairs={{0,2},{2,0},{1,3},{3,1},{4,6},{6,4},{5,7},{7,5},{8,10},{10,8},{9,1... | collective-permute-start | bytes 3080 | tf_op jit(solution)/shard_map/ppermute | solution.py:304
  76.2 25.0 %collective-permute-start.3 = (bf16[128,3072]{1,0:T(8,128)(2,1)S(1)}, bf16[128,3072]{1,0:T(8,128)(2,1)S(1)}, u32[]{:S(2)}, u32[]{:S(2)}) collective-permute-start(bf16[128,3072]{1,0:T(8,128)(2,1)S(1)} %fusion.9.refs_0_), channel_id=1, source_target_pairs={{0,2},{2,0},{1,3},{3,1},{4,6},{6,4},{5,7},{7,5},{8,10},{10,8},{9,1... | collective-permute-start | bytes 2359304 | tf_op jit(solution)/shard_map/ppermute | solution.py:304
  86.4 15.6 %collective-permute-start.12 = (bf16[128,4096]{1,0:T(8,128)(2,1)S(1)}, bf16[128,4096]{1,0:T(8,128)(2,1)S(1)}, u32[]{:S(2)}, u32[]{:S(2)}) collective-permute-start(bf16[128,4096]{1,0:T(8,128)(2,1)S(1)} %get-tuple-element.25), channel_id=1, source_target_pairs={{0,1},{1,0},{2,3},{3,2},{4,5},{5,4},{6,7},{7,6},{8,9},{9,8},{10,11... | collective-permute-start | bytes 3145736 | tf_op jit(solution)/shard_map/ppermute | solution.py:298
  86.7 2.8 %collective-permute-start.8 = (bf16[256,384]{1,0:T(8,128)(2,1)S(1)}, bf16[256,384]{1,0:T(8,128)(2,1)S(1)}, u32[]{:S(2)}, u32[]{:S(2)}) collective-permute-start(bf16[256,384]{1,0:T(8,128)(2,1)S(1)} %get-tuple-element.22), channel_id=1, source_target_pairs={{0,1},{1,0},{2,3},{3,2},{4,5},{5,4},{6,7},{7,6},{8,9},{9,8},{10,11... | collective-permute-start | bytes 589832 | tf_op jit(solution)/shard_map/ppermute | solution.py:298
  89.5 10.9 %collective-permute-start.9 = (bf16[256,384]{1,0:T(8,128)(2,1)S(1)}, bf16[256,384]{1,0:T(8,128)(2,1)S(1)}, u32[]{:S(2)}, u32[]{:S(2)}) collective-permute-start(bf16[256,384]{1,0:T(8,128)(2,1)S(1)} %shard_map.84.refs_0_), channel_id=1, source_target_pairs={{0,2},{2,0},{1,3},{3,1},{4,6},{6,4},{5,7},{7,5},{8,10},{10,8},{9,1... | collective-permute-start | bytes 589832 | tf_op jit(solution)/shard_map/ppermute | solution.py:304
  93.9 8.1 %collective-permute-start.13 = (bf16[128,2048]{1,0:T(8,128)(2,1)S(1)}, bf16[128,2048]{1,0:T(8,128)(2,1)S(1)}, u32[]{:S(2)}, u32[]{:S(2)}) collective-permute-start(bf16[128,2048]{1,0:T(8,128)(2,1)S(1)} %get-tuple-element.26), channel_id=1, source_target_pairs={{0,1},{1,0},{2,3},{3,2},{4,5},{5,4},{6,7},{7,6},{8,9},{9,8},{10,11... | collective-permute-start | bytes 1572872 | tf_op jit(solution)/shard_map/ppermute | solution.py:298
  94.0 11.1 %collective-permute-start.11 = (bf16[128,3072]{1,0:T(8,128)(2,1)S(1)}, bf16[128,3072]{1,0:T(8,128)(2,1)S(1)}, u32[]{:S(2)}, u32[]{:S(2)}) collective-permute-start(bf16[128,3072]{1,0:T(8,128)(2,1)S(1)} %shard_map.82.refs_0_), channel_id=1, source_target_pairs={{0,1},{1,0},{2,3},{3,2},{4,5},{5,4},{6,7},{7,6},{8,9},{9,8},{10,11... | collective-permute-start | bytes 2359304 | tf_op jit(solution)/shard_map/ppermute | solution.py:298
  101.9 8.4 %collective-permute-start.10 = (bf16[128,3072]{1,0:T(8,128)(2,1)S(1)}, bf16[128,3072]{1,0:T(8,128)(2,1)S(1)}, u32[]{:S(2)}, u32[]{:S(2)}) collective-permute-start(bf16[128,3072]{1,0:T(8,128)(2,1)S(1)} %shard_map.88.refs_4_.refs_0_), channel_id=1, source_target_pairs={{0,1},{1,0},{2,3},{3,2},{4,5},{5,4},{6,7},{7,6},{8,9},{9,8},{10,11... | collective-permute-start | bytes 2359304 | tf_op jit(solution)/shard_map/ppermute | solution.py:298
  102.2 24.2 %collective-permute-start.16 = (bf16[80,6144]{1,0:T(8,128)(2,1)S(1)}, bf16[80,6144]{1,0:T(8,128)(2,1)S(1)}, u32[]{:S(2)}, u32[]{:S(2)}) collective-permute-start(bf16[80,6144]{1,0:T(8,128)(2,1)S(1)} %shard_map.89.refs_3_.refs_0_), channel_id=1, source_target_pairs={{0,2},{2,0},{1,3},{3,1},{4,6},{6,4},{5,7},{7,5},{8,10},{10,8},{9,1... | collective-permute-start | bytes 2949128 | tf_op jit(solution)/shard_map/ppermute | solution.py:304
  119.0 54.9 %reduce-scatter.5.cloned.1.call-start = ((), (), s32[]{:S(2)}) async-start(), calls=%async_computation.3 | async-start | bytes 614400 | tf_op jit(solution)/shard_map/reduce_scatter | solution.py:384
  128.2 2.6 %collective-permute-start.17 = (bf16[80,6144]{1,0:T(8,128)(2,1)S(1)}, bf16[80,6144]{1,0:T(8,128)(2,1)S(1)}, u32[]{:S(2)}, u32[]{:S(2)}) collective-permute-start(bf16[80,6144]{1,0:T(8,128)(2,1)S(1)} %shard_map.95.refs_0_), channel_id=1, source_target_pairs={{0,1},{1,0},{2,3},{3,2},{4,5},{5,4},{6,7},{7,6},{8,9},{9,8},{10,11... | collective-permute-start | bytes 2949128 | tf_op jit(solution)/shard_map/ppermute | solution.py:298
  128.3 11.5 %collective-permute-start.19 = (bf16[48,4096]{1,0:T(8,128)(2,1)S(1)}, bf16[48,4096]{1,0:T(8,128)(2,1)S(1)}, u32[]{:S(2)}, u32[]{:S(2)}) collective-permute-start(bf16[48,4096]{1,0:T(8,128)(2,1)S(1)} %shard_map.91.refs_8_.refs_0_), channel_id=1, source_target_pairs={{0,2},{2,0},{1,3},{3,1},{4,6},{6,4},{5,7},{7,5},{8,10},{10,8},{9,1... | collective-permute-start | bytes 1179656 | tf_op jit(solution)/shard_map/ppermute | solution.py:304
  140.3 3.9 %collective-permute-start.21 = (bf16[48,4096]{1,0:T(8,128)(2,1)S(1)}, bf16[48,4096]{1,0:T(8,128)(2,1)S(1)}, u32[]{:S(2)}, u32[]{:S(2)}) collective-permute-start(bf16[48,4096]{1,0:T(8,128)(2,1)S(1)} %shard_map.97.refs_3_.refs_0_), channel_id=1, source_target_pairs={{0,1},{1,0},{2,3},{3,2},{4,5},{5,4},{6,7},{7,6},{8,9},{9,8},{10,11... | collective-permute-start | bytes 1179656 | tf_op jit(solution)/shard_map/ppermute | solution.py:298
  140.4 2.1 %collective-permute-start.18 = (bf16[80,1536]{1,0:T(8,128)(2,1)S(1)}, bf16[80,1536]{1,0:T(8,128)(2,1)S(1)}, u32[]{:S(2)}, u32[]{:S(2)}) collective-permute-start(bf16[80,1536]{1,0:T(8,128)(2,1)S(1)} %get-tuple-element.32), channel_id=1, source_target_pairs={{0,1},{1,0},{2,3},{3,2},{4,5},{5,4},{6,7},{7,6},{8,9},{9,8},{10,11... | collective-permute-start | bytes 737288 | tf_op jit(solution)/shard_map/ppermute | solution.py:298
  140.9 9.3 %collective-permute-start.20 = (bf16[48,2048]{1,0:T(8,128)(2,1)S(1)}, bf16[48,2048]{1,0:T(8,128)(2,1)S(1)}, u32[]{:S(2)}, u32[]{:S(2)}) collective-permute-start(bf16[48,2048]{1,0:T(8,128)(2,1)S(1)} %shard_map.92.refs_9_.refs_0_), channel_id=1, source_target_pairs={{0,2},{2,0},{1,3},{3,1},{4,6},{6,4},{5,7},{7,5},{8,10},{10,8},{9,1... | collective-permute-start | bytes 589832 | tf_op jit(solution)/shard_map/ppermute | solution.py:304
  156.9 8.5 %collective-permute-start.24 = (bf16[48,768]{1,0:T(8,128)(2,1)S(1)}, bf16[48,768]{1,0:T(8,128)(2,1)S(1)}, u32[]{:S(2)}, u32[]{:S(2)}) collective-permute-start(bf16[48,768]{1,0:T(8,128)(2,1)S(1)} %get-tuple-element.45), channel_id=1, source_target_pairs={{0,12},{4,8},{8,4},{12,0},{1,13},{5,9},{9,5},{13,1},{2,14},{6,10},... | collective-permute-start | bytes 221192 | tf_op jit(solution)/shard_map/ppermute | solution.py:321
  158.7 13.2 %collective-permute-start.25 = (bf16[48,768]{1,0:T(8,128)(2,1)S(1)}, bf16[48,768]{1,0:T(8,128)(2,1)S(1)}, u32[]{:S(2)}, u32[]{:S(2)}) collective-permute-start(bf16[48,768]{1,0:T(8,128)(2,1)S(1)} %get-tuple-element.47), channel_id=1, source_target_pairs={{0,8},{4,12},{8,0},{12,4},{1,9},{5,13},{9,1},{13,5},{2,10},{6,14},... | collective-permute-start | bytes 221192 | tf_op jit(solution)/shard_map/ppermute | solution.py:321
  158.7 13.2 %collective-permute-start.26 = (bf16[48,768]{1,0:T(8,128)(2,1)S(1)}, bf16[48,768]{1,0:T(8,128)(2,1)S(1)}, u32[]{:S(2)}, u32[]{:S(2)}) collective-permute-start(bf16[48,768]{1,0:T(8,128)(2,1)S(1)} %get-tuple-element.46), channel_id=1, source_target_pairs={{0,4},{4,0},{8,12},{12,8},{1,5},{5,1},{9,13},{13,9},{2,6},{6,2},{1... | collective-permute-start | bytes 221192 | tf_op jit(solution)/shard_map/ppermute | solution.py:321
  (13 other events, 53.3 us)
Sparse Core Ops, SparseCore 0:
  119.2 22.1 reduce-scatter.2
  150.9 23.0 reduce-scatter.4

commit v11 on v10

--- a/solution.py
+++ b/solution.py
@@ -389,22 +389,19 @@
         sums = chunk_sums(halves, 1, second)
         parts = all_red(sums)
         terms = output(arrived, pieces[0], (), cuts[0], [sums])
-        coming = [chunk_sums([half], 2, terms[0]) for half in halves]
-        terms = output(second, pieces[1], terms, cuts[0], coming)
-        coming = [all_red(x) for x in coming]
+        coming = chunk_sums(halves, 2, terms[0])
+        terms = output(second, pieces[1], terms, cuts[0], [coming])
+        coming = all_red(coming)
         full, got = scatter(terms[0], swap(terms[1]), [])
         scattered = [got]
 
         hidden = gelu_sum(parts, [full])
         terms = output(hidden, slice(0, units), (), cuts[1])
-        waiting = terms[0], swap(terms[1])
-
-        hidden = gelu_sum(coming[0], [terms[0]])
-        full, got = scatter(*waiting, [hidden, scattered[0]])
+        full, got = scatter(terms[0], swap(terms[1]), [scattered[0]])
         scattered.append(got)
-        terms = output(hidden, rest_pieces[0], (), cuts[2], [full])
-        hidden = gelu_sum(coming[1], [terms[0]])
-        kept, sent = output(hidden, rest_pieces[1], terms, cuts[2])
+
+        hidden = gelu_sum(coming, [full])
+        kept, sent = output(hidden, slice(0, units), (), cuts[2])
         outs = [tokens[cut].astype(F32) + got.astype(F32) for cut, got in zip(cuts, scattered)]
         outs.append(tokens[cuts[2]].astype(F32) + collect(kept, swap(sent), width))
         return jnp.concatenate(outs, axis=0)

time: 183 us -> 181 us (0.989)
  starting transfers between devices: 19.4 us -> 17.1 us
    ppermute x16 -> x15, waiting for transfers between devices: 10.7 us -> 14 us  [swap(): return lax.ppermute(x, 'tok', [(0, 1), (1, 0)])]
    ppermute x3, waiting for transfers between devices: 10.6 us -> 8.3 us  [collect(): total = total + lax.ppermute(block(chip ^ k), 'wide', pairs).astype(F32)]
    ppermute x8 -> x7, starting transfers between devices: 11.4 us -> 9.95 us  [all_red(): parts.append(lax.ppermute(x, 'red', pairs))]
    pallas_call x20 -> x17, Pallas kernels: 45 us -> 43.7 us  [call(): pl.pallas_call(body, in_specs=list(specs) + [corner_of(a) for a in earlie...]
    ppermute x8 -> x7, waiting for transfers between devices: 18.7 us -> 18.6 us  [all_red(): parts.append(lax.ppermute(x, 'red', pairs))]
  transfers between devices with their start and end apart: 29 -> 27, of which waited for: 18 -> 18; matrix products, arithmetic and copies ran while one was open for 2% -> 2% of each run, Pallas kernels for 24% -> 23%
where the time goes in v11:
time: 181 us
  waiting for transfers between devices  43.7 us (24%)
  Pallas kernels  43.7 us (24%)
  blocking collectives  39.8 us (22%)
  starting transfers between devices  17.1 us (9%)
  between operations  15.3 us (8%)
  local copies, waits for them, and re-layouts  9.41 us (5%)
  matrix products  7.91 us (4%)
  other arithmetic  3.76 us (2%)
    pallas_call x17, Pallas kernels, call(): pl.pallas_call(body, in_specs=list(specs) + [corner_of(a) for a in earlie...  43.7 us
    all_gather x1, blocking collectives, body(): lead = lax.all_gather(lead, 'wide', axis=1, tiled=True)  21.9 us
    ppermute x7, waiting for transfers between devices, all_red(): parts.append(lax.ppermute(x, 'red', pairs))  18.6 us
    all_gather x1, blocking collectives, body(): rest = lax.all_gather(rest, 'wide', axis=1, tiled=True)  18 us
    ppermute x15, waiting for transfers between devices, swap(): return lax.ppermute(x, 'tok', [(0, 1), (1, 0)])  14 us
    ppermute x7, starting transfers between devices, all_red(): parts.append(lax.ppermute(x, 'red', pairs))  9.95 us
    ppermute x3, waiting for transfers between devices, collect(): total = total + lax.ppermute(block(chip ^ k), 'wide', pairs).astype(F32)  8.3 us
    dot_general x2, matrix products, project(): part = jnp.dot(both, weight, preferred_element_type=F32)  7.91 us
  transfers between devices with their start and end apart: 27, of which 18 were waited for; matrix products, arithmetic and copies ran while one was open for 2% of the time, Pallas kernels for 23%

profile of v11, /device:TPU:0, one launch (start us, length us, event | category | flops | bytes accessed | tf_op | source)
XLA Modules:
  0.0 180.6 jit_solution(17156634511800631890)
XLA Ops:
  8.2 21.9 %all_gather.6 = bf16[136,3072]{1,0:T(8,128)(2,1)S(1)} all-gather(bf16[136,768]{1,0:T(8,128)(2,1)S(1)} %pad_maximum_fusion.6), channel_id=1, replica_groups=mesh['grp'=2,'wide'=4,'red'=2,'tok'=2] {'wide'}, dimensions={1}, use_global_device_ids=true | all-gather | bytes 1044480 | tf_op jit(solution)/shard_map/all_gather | solution.py:337
  31.9 2.1 %collective-permute-done = f32[2,128]{1,0:T(2,128)S(1)} collective-permute-done((f32[2,128]{1,0:T(2,128)S(1)}, f32[2,128]{1,0:T(2,128)S(1)}, u32[]{:S(2)}, u32[]{:S(2)}) %collective-permute-start) | collective-permute-done | bytes 1056 | tf_op jit(solution)/shard_map/ppermute | solution.py:304
  36.2 5.3 %fusion = f32[256,3072]{1,0:T(8,128)S(1)} fusion(bf16[1536,6144]{1,0:T(8,128)(2,1)} %refs_2_.8, bf16[128,1536]{1,0:T(8,128)(2,1)S(1)} %get-tuple-element.40, bf16[128,1536]{1,0:T(8,128)(2,1)S(1)} %collective-permute-done.1), kind=kOutput, calls=%fused_computation | convolution fusion | flops 2417491968 | bytes 13369344 | tf_op jit(solution)/shard_map/dot_general | solution.py:351
  41.8 3.5 %copy-done.6 = bf16[1536,6144]{1,0:T(8,128)(2,1)S(1)} copy-done((bf16[1536,6144]{1,0:T(8,128)(2,1)S(1)}, bf16[1536,6144]{1,0:T(8,128)(2,1)}, u32[]{:S(2)}) %copy-start.6) | copy-done | bytes 18874392
  45.4 2.6 %fusion.2 = f32[256,3072]{1,0:T(8,128)S(1)} fusion(bf16[1536,6144]{1,0:T(8,128)(2,1)S(1)} %copy-done.6, bf16[128,1536]{1,0:T(8,128)(2,1)S(1)} %get-tuple-element.40, bf16[128,1536]{1,0:T(8,128)(2,1)S(1)} %collective-permute-done.1), kind=kOutput, calls=%fused_computation.2 | convolution fusion | flops 2417491968 | bytes 13369344 | tf_op jit(solution)/shard_map/dot_general | solution.py:351
  51.8 18.0 %all_gather.7 = bf16[128,3072]{1,0:T(8,128)(2,1)S(1)} all-gather(bf16[128,768]{1,0:T(8,128)(2,1)S(1)} %slice_add_fusion.2), channel_id=1, replica_groups=mesh['grp'=2,'wide'=4,'red'=2,'tok'=2] {'wide'}, dimensions={1}, use_global_device_ids=true | all-gather | bytes 983040 | tf_op jit(solution)/shard_map/all_gather | solution.py:362
  73.6 2.1 %collective-permute-done.6 = f32[2,128]{1,0:T(2,128)S(1)} collective-permute-done((f32[2,128]{1,0:T(2,128)S(1)}, f32[2,128]{1,0:T(2,128)S(1)}, u32[]{:S(2)}, u32[]{:S(2)}) %collective-permute-start.6) | collective-permute-done | bytes 1056 | tf_op jit(solution)/shard_map/ppermute | solution.py:304
  80.3 6.1 %shard_map.85 = (bf16[128,4096]{1,0:T(8,128)(2,1)S(1)}, bf16[128,4096]{1,0:T(8,128)(2,1)S(1)}) custom-call(bf16[128,1536]{1,0:T(8,128)(2,1)S(1)} %get-tuple-element.38.refs_0_, bf16[128,1536]{1,0:T(8,128)(2,1)S(1)} %collective-permute-done.7.refs_1_, bf16[1536,6144]{1,0:T(8,128)(2,1)} %refs_2_.8, bf16[256,384]{1,0:T(8,128)(2,1)S(1)} %get-tuple-element.19.refs_0_.refs_3_), custom_call_target="tpu_custom_call" | custom-call | tf_op jit(solution)/shard_map/pallas_call | solution.py:63
  87.0 2.4 %collective-permute-done.8.refs_1_ = bf16[256,384]{1,0:T(8,128)(2,1)S(1)} collective-permute-done((bf16[256,384]{1,0:T(8,128)(2,1)S(1)}, bf16[256,384]{1,0:T(8,128)(2,1)S(1)}, u32[]{:S(2)}, u32[]{:S(2)}) %collective-permute-start.8) | collective-permute-done | bytes 196640 | tf_op jit(solution)/shard_map/ppermute | solution.py:298
  90.1 3.8 %shard_map.86 = (bf16[128,2048]{1,0:T(8,128)(2,1)S(1)}, bf16[128,2048]{1,0:T(8,128)(2,1)S(1)}) custom-call(bf16[128,1536]{1,0:T(8,128)(2,1)S(1)} %get-tuple-element.38.refs_0_, bf16[128,1536]{1,0:T(8,128)(2,1)S(1)} %collective-permute-done.7.refs_1_, bf16[1536,6144]{1,0:T(8,128)(2,1)} %refs_2_.8, bf16[128,4096]{1,0:T(8,128)(2,1)S(1)} %get-tuple-element.21.refs_3_.refs_0_), custom_call_target="tpu_custom_call" | custom-call | tf_op jit(solution)/shard_map/pallas_call | solution.py:63
  93.9 6.5 %collective-permute-done.9.refs_1_ = bf16[256,384]{1,0:T(8,128)(2,1)S(1)} collective-permute-done((bf16[256,384]{1,0:T(8,128)(2,1)S(1)}, bf16[256,384]{1,0:T(8,128)(2,1)S(1)}, u32[]{:S(2)}, u32[]{:S(2)}) %collective-permute-start.9) | collective-permute-done | bytes 196640 | tf_op jit(solution)/shard_map/ppermute | solution.py:304
  102.5 2.5 %collective-permute-done.13.refs_3_ = bf16[128,2048]{1,0:T(8,128)(2,1)S(1)} collective-permute-done((bf16[128,2048]{1,0:T(8,128)(2,1)S(1)}, bf16[128,2048]{1,0:T(8,128)(2,1)S(1)}, u32[]{:S(2)}, u32[]{:S(2)}) %collective-permute-start.13) | collective-permute-done | bytes 524320 | tf_op jit(solution)/shard_map/ppermute | solution.py:298
  108.1 5.0 %shard_map.90 = (f32[128,1536]{1,0:T(8,128)S(1)}, f32[128,1536]{1,0:T(8,128)S(1)}) custom-call(bf16[128,3072]{1,0:T(8,128)(2,1)S(1)} %shard_map.82.refs_0_, bf16[128,3072]{1,0:T(8,128)(2,1)S(1)} %collective-permute-done.11.refs_1_, bf16[6144,1536]{1,0:T(8,128)(2,1)} %refs_2_.13, bf16[80,6144]{1,0:T(8,128)(2,1)S(1)} %shard_map.89.refs_3_.refs_0_), custom_call_target="tpu_custom_call" | custom-call | tf_op jit(solution)/shard_map/pallas_call | solution.py:63
  114.1 5.1 %shard_map.92 = (bf16[128,1536]{1,0:T(8,128)(2,1)S(1)}, bf16[128,1536]{1,0:T(8,128)(2,1)S(1)}) custom-call(bf16[128,3072]{1,0:T(8,128)(2,1)S(1)} %shard_map.88.refs_4_.refs_0_, bf16[128,3072]{1,0:T(8,128)(2,1)S(1)} %collective-permute-done.10.refs_1_, bf16[6144,1536]{1,0:T(8,128)(2,1)} %refs_2_.13, f32[128,1536]{1,0:T(8,128)S(1)} %get-tuple-element.25.refs_4_.refs_3_, ...), custom_call_target="tpu_custom_call" | custom-call | tf_op jit(solution)/shard_map/pallas_call | solution.py:63
  122.2 6.9 %collective-permute-done.16.refs_1_ = bf16[80,6144]{1,0:T(8,128)(2,1)S(1)} collective-permute-done((bf16[80,6144]{1,0:T(8,128)(2,1)S(1)}, bf16[80,6144]{1,0:T(8,128)(2,1)S(1)}, u32[]{:S(2)}, u32[]{:S(2)}) %collective-permute-start.16) | collective-permute-done | bytes 983072 | tf_op jit(solution)/shard_map/ppermute | solution.py:304
  129.1 1.7 shard_map.94.refs_0_
  133.5 7.5 %shard_map.95 = (bf16[80,1536]{1,0:T(8,128)(2,1)S(1)}, bf16[80,1536]{1,0:T(8,128)(2,1)S(1)}) custom-call(bf16[80,6144]{1,0:T(8,128)(2,1)S(1)} %shard_map.94.refs_0_, bf16[80,6144]{1,0:T(8,128)(2,1)S(1)} %collective-permute-done.17.refs_1_, bf16[6144,1536]{1,0:T(8,128)(2,1)} %refs_2_.13, bf16[80,128]{1,0:T(8,128)(2,1)S(1)} %slice.113.refs_3_, ...), custom_call_target="tpu_custom_call" | custom-call | tf_op jit(solution)/shard_map/pallas_call | solution.py:63
  141.1 2.8 %reduce-scatter.3.cloned.1.call-done.refs_3_ = bf16[128,768]{1,0:T(8,128)(2,1)} async-done(((bf16[128,3072]{1,0:T(8,128)(2,1)}), bf16[128,768]{1,0:T(8,128)(2,1)}) %reduce-scatter.3.cloned.1.call-update) | async-done | bytes 196624 | tf_op jit(solution)/shard_map/reduce_scatter | solution.py:384
  148.4 1.8 collective-permute-done.20.refs_1_
  150.2 7.4 %shard_map.98 = (bf16[48,1536]{1,0:T(8,128)(2,1)S(1)}, bf16[48,1536]{1,0:T(8,128)(2,1)S(1)}) custom-call(bf16[48,6144]{1,0:T(8,128)(2,1)S(1)} %shard_map.97.refs_0_, bf16[48,6144]{1,0:T(8,128)(2,1)S(1)} %collective-permute-done.20.refs_1_, bf16[6144,1536]{1,0:T(8,128)(2,1)} %refs_2_.13, bf16[48,128]{1,0:T(8,128)(2,1)S(1)} %slice.115.refs_3_, ...), custom_call_target="tpu_custom_call" | custom-call | tf_op jit(solution)/shard_map/pallas_call | solution.py:63
  159.0 1.8 %collective-permute-start.22 = (bf16[48,768]{1,0:T(8,128)(2,1)S(1)}, bf16[48,768]{1,0:T(8,128)(2,1)S(1)}, u32[]{:S(2)}, u32[]{:S(2)}) collective-permute-start(bf16[48,768]{1,0:T(8,128)(2,1)S(1)} %get-tuple-element.41), channel_id=1, source_target_pairs={{0,12},{4,8},{8,4},{12,0},{1,13},{5,9},{9,5},{13,1},{2,14},{6,10},... | collective-permute-start | bytes 221192 | tf_op jit(solution)/shard_map/ppermute | solution.py:321
  160.9 2.6 %collective-permute-start.24 = (bf16[48,768]{1,0:T(8,128)(2,1)S(1)}, bf16[48,768]{1,0:T(8,128)(2,1)S(1)}, u32[]{:S(2)}, u32[]{:S(2)}) collective-permute-start(bf16[48,768]{1,0:T(8,128)(2,1)S(1)} %get-tuple-element.42), channel_id=1, source_target_pairs={{0,4},{4,0},{8,12},{12,8},{1,5},{5,1},{9,13},{13,9},{2,6},{6,2},{1... | collective-permute-start | bytes 221192 | tf_op jit(solution)/shard_map/ppermute | solution.py:321
  163.5 3.3 %collective-permute-done.22 = bf16[48,768]{1,0:T(8,128)(2,1)S(1)} collective-permute-done((bf16[48,768]{1,0:T(8,128)(2,1)S(1)}, bf16[48,768]{1,0:T(8,128)(2,1)S(1)}, u32[]{:S(2)}, u32[]{:S(2)}) %collective-permute-start.22) | collective-permute-done | bytes 73760 | tf_op jit(solution)/shard_map/ppermute | solution.py:321
  166.8 5.0 %collective-permute-done.23 = bf16[48,768]{1,0:T(8,128)(2,1)S(1)} collective-permute-done((bf16[48,768]{1,0:T(8,128)(2,1)S(1)}, bf16[48,768]{1,0:T(8,128)(2,1)S(1)}, u32[]{:S(2)}, u32[]{:S(2)}) %collective-permute-start.23) | collective-permute-done | bytes 73760 | tf_op jit(solution)/shard_map/ppermute | solution.py:321
  (109 shorter events, 37.7 us)
Async XLA Ops:
  6.5 137.4 %reduce-scatter.3.cloned.1.call-start = ((), (), s32[]{:S(2)}) async-start(), calls=%async_computation.2 | async-start | bytes 983040 | tf_op jit(solution)/shard_map/reduce_scatter | solution.py:384
  30.4 3.6 %collective-permute-start = (f32[2,128]{1,0:T(2,128)S(1)}, f32[2,128]{1,0:T(2,128)S(1)}, u32[]{:S(2)}, u32[]{:S(2)}) collective-permute-start(f32[2,128]{1,0:T(2,128)S(1)} %pad_maximum_fusion.7), channel_id=1, source_target_pairs={{0,2},{2,0},{1,3},{3,1},{4,6},{6,4},{5,7},{7,5},{8,10},{10,8},{9,1... | collective-permute-start | bytes 3080 | tf_op jit(solution)/shard_map/ppermute | solution.py:304
  34.4 1.8 collective-permute-start.1
  41.6 6.6 %collective-permute-start.4 = (bf16[128,3072]{1,0:T(8,128)(2,1)S(1)}, bf16[128,3072]{1,0:T(8,128)(2,1)S(1)}, u32[]{:S(2)}, u32[]{:S(2)}) collective-permute-start(bf16[128,3072]{1,0:T(8,128)(2,1)S(1)} %slice.145), channel_id=1, source_target_pairs={{0,1},{1,0},{2,3},{3,2},{4,5},{5,4},{6,7},{7,6},{8,9},{9,8},{10,11... | collective-permute-start | bytes 2359304 | tf_op jit(solution)/shard_map/ppermute | solution.py:298
  48.1 2.4 %collective-permute-start.2 = (bf16[128,3072]{1,0:T(8,128)(2,1)S(1)}, bf16[128,3072]{1,0:T(8,128)(2,1)S(1)}, u32[]{:S(2)}, u32[]{:S(2)}) collective-permute-start(bf16[128,3072]{1,0:T(8,128)(2,1)S(1)} %slice.146), channel_id=1, source_target_pairs={{0,1},{1,0},{2,3},{3,2},{4,5},{5,4},{6,7},{7,6},{8,9},{9,8},{10,11... | collective-permute-start | bytes 2359304 | tf_op jit(solution)/shard_map/ppermute | solution.py:298
  48.5 21.3 %collective-permute-start.5 = (bf16[128,3072]{1,0:T(8,128)(2,1)S(1)}, bf16[128,3072]{1,0:T(8,128)(2,1)S(1)}, u32[]{:S(2)}, u32[]{:S(2)}) collective-permute-start(bf16[128,3072]{1,0:T(8,128)(2,1)S(1)} %fusion.8.refs_0_), channel_id=1, source_target_pairs={{0,2},{2,0},{1,3},{3,1},{4,6},{6,4},{5,7},{7,5},{8,10},{10,8},{9,1... | collective-permute-start | bytes 2359304 | tf_op jit(solution)/shard_map/ppermute | solution.py:304
  72.0 3.6 %collective-permute-start.6 = (f32[2,128]{1,0:T(2,128)S(1)}, f32[2,128]{1,0:T(2,128)S(1)}, u32[]{:S(2)}, u32[]{:S(2)}) collective-permute-start(f32[2,128]{1,0:T(2,128)S(1)} %pad_maximum_fusion.8), channel_id=1, source_target_pairs={{0,2},{2,0},{1,3},{3,1},{4,6},{6,4},{5,7},{7,5},{8,10},{10,8},{9,1... | collective-permute-start | bytes 3080 | tf_op jit(solution)/shard_map/ppermute | solution.py:304
  76.2 25.0 %collective-permute-start.3 = (bf16[128,3072]{1,0:T(8,128)(2,1)S(1)}, bf16[128,3072]{1,0:T(8,128)(2,1)S(1)}, u32[]{:S(2)}, u32[]{:S(2)}) collective-permute-start(bf16[128,3072]{1,0:T(8,128)(2,1)S(1)} %fusion.9.refs_0_), channel_id=1, source_target_pairs={{0,2},{2,0},{1,3},{3,1},{4,6},{6,4},{5,7},{7,5},{8,10},{10,8},{9,1... | collective-permute-start | bytes 2359304 | tf_op jit(solution)/shard_map/ppermute | solution.py:304
  86.4 18.6 %collective-permute-start.12 = (bf16[128,4096]{1,0:T(8,128)(2,1)S(1)}, bf16[128,4096]{1,0:T(8,128)(2,1)S(1)}, u32[]{:S(2)}, u32[]{:S(2)}) collective-permute-start(bf16[128,4096]{1,0:T(8,128)(2,1)S(1)} %get-tuple-element.23), channel_id=1, source_target_pairs={{0,1},{1,0},{2,3},{3,2},{4,5},{5,4},{6,7},{7,6},{8,9},{9,8},{10,11... | collective-permute-start | bytes 3145736 | tf_op jit(solution)/shard_map/ppermute | solution.py:298
  86.7 2.8 %collective-permute-start.8 = (bf16[256,384]{1,0:T(8,128)(2,1)S(1)}, bf16[256,384]{1,0:T(8,128)(2,1)S(1)}, u32[]{:S(2)}, u32[]{:S(2)}) collective-permute-start(bf16[256,384]{1,0:T(8,128)(2,1)S(1)} %get-tuple-element.20), channel_id=1, source_target_pairs={{0,1},{1,0},{2,3},{3,2},{4,5},{5,4},{6,7},{7,6},{8,9},{9,8},{10,11... | collective-permute-start | bytes 589832 | tf_op jit(solution)/shard_map/ppermute | solution.py:298
  89.5 10.9 %collective-permute-start.9 = (bf16[256,384]{1,0:T(8,128)(2,1)S(1)}, bf16[256,384]{1,0:T(8,128)(2,1)S(1)}, u32[]{:S(2)}, u32[]{:S(2)}) collective-permute-start(bf16[256,384]{1,0:T(8,128)(2,1)S(1)} %shard_map.84.refs_0_), channel_id=1, source_target_pairs={{0,2},{2,0},{1,3},{3,1},{4,6},{6,4},{5,7},{7,5},{8,10},{10,8},{9,1... | collective-permute-start | bytes 589832 | tf_op jit(solution)/shard_map/ppermute | solution.py:304
  90.1 18.0 %collective-permute-start.11 = (bf16[128,3072]{1,0:T(8,128)(2,1)S(1)}, bf16[128,3072]{1,0:T(8,128)(2,1)S(1)}, u32[]{:S(2)}, u32[]{:S(2)}) collective-permute-start(bf16[128,3072]{1,0:T(8,128)(2,1)S(1)} %shard_map.82.refs_0_), channel_id=1, source_target_pairs={{0,1},{1,0},{2,3},{3,2},{4,5},{5,4},{6,7},{7,6},{8,9},{9,8},{10,11... | collective-permute-start | bytes 2359304 | tf_op jit(solution)/shard_map/ppermute | solution.py:298
  101.9 11.4 %collective-permute-start.10 = (bf16[128,3072]{1,0:T(8,128)(2,1)S(1)}, bf16[128,3072]{1,0:T(8,128)(2,1)S(1)}, u32[]{:S(2)}, u32[]{:S(2)}) collective-permute-start(bf16[128,3072]{1,0:T(8,128)(2,1)S(1)} %shard_map.88.refs_4_.refs_0_), channel_id=1, source_target_pairs={{0,1},{1,0},{2,3},{3,2},{4,5},{5,4},{6,7},{7,6},{8,9},{9,8},{10,11... | collective-permute-start | bytes 2359304 | tf_op jit(solution)/shard_map/ppermute | solution.py:298
  102.0 3.0 %collective-permute-start.13 = (bf16[128,2048]{1,0:T(8,128)(2,1)S(1)}, bf16[128,2048]{1,0:T(8,128)(2,1)S(1)}, u32[]{:S(2)}, u32[]{:S(2)}) collective-permute-start(bf16[128,2048]{1,0:T(8,128)(2,1)S(1)} %get-tuple-element.24), channel_id=1, source_target_pairs={{0,1},{1,0},{2,3},{3,2},{4,5},{5,4},{6,7},{7,6},{8,9},{9,8},{10,11... | collective-permute-start | bytes 1572872 | tf_op jit(solution)/shard_map/ppermute | solution.py:298
  105.2 23.9 %collective-permute-start.16 = (bf16[80,6144]{1,0:T(8,128)(2,1)S(1)}, bf16[80,6144]{1,0:T(8,128)(2,1)S(1)}, u32[]{:S(2)}, u32[]{:S(2)}) collective-permute-start(bf16[80,6144]{1,0:T(8,128)(2,1)S(1)} %shard_map.89.refs_3_.refs_0_), channel_id=1, source_target_pairs={{0,2},{2,0},{1,3},{3,1},{4,6},{6,4},{5,7},{7,5},{8,10},{10,8},{9,1... | collective-permute-start | bytes 2949128 | tf_op jit(solution)/shard_map/ppermute | solution.py:304
  119.2 1.8 collective-permute-start.15
  121.9 50.0 %reduce-scatter.5.cloned.1.call-start = ((), (), s32[]{:S(2)}) async-start(), calls=%async_computation.3 | async-start | bytes 614400 | tf_op jit(solution)/shard_map/reduce_scatter | solution.py:384
  130.8 2.6 %collective-permute-start.17 = (bf16[80,6144]{1,0:T(8,128)(2,1)S(1)}, bf16[80,6144]{1,0:T(8,128)(2,1)S(1)}, u32[]{:S(2)}, u32[]{:S(2)}) collective-permute-start(bf16[80,6144]{1,0:T(8,128)(2,1)S(1)} %shard_map.94.refs_0_), channel_id=1, source_target_pairs={{0,1},{1,0},{2,3},{3,2},{4,5},{5,4},{6,7},{7,6},{8,9},{9,8},{10,11... | collective-permute-start | bytes 2949128 | tf_op jit(solution)/shard_map/ppermute | solution.py:298
  130.9 15.7 %collective-permute-start.19 = (bf16[48,6144]{1,0:T(8,128)(2,1)S(1)}, bf16[48,6144]{1,0:T(8,128)(2,1)S(1)}, u32[]{:S(2)}, u32[]{:S(2)}) collective-permute-start(bf16[48,6144]{1,0:T(8,128)(2,1)S(1)} %shard_map.91.refs_8_.refs_0_), channel_id=1, source_target_pairs={{0,2},{2,0},{1,3},{3,1},{4,6},{6,4},{5,7},{7,5},{8,10},{10,8},{9,1... | collective-permute-start | bytes 1769480 | tf_op jit(solution)/shard_map/ppermute | solution.py:304
  140.9 3.0 %collective-permute-start.18 = (bf16[80,1536]{1,0:T(8,128)(2,1)S(1)}, bf16[80,1536]{1,0:T(8,128)(2,1)S(1)}, u32[]{:S(2)}, u32[]{:S(2)}) collective-permute-start(bf16[80,1536]{1,0:T(8,128)(2,1)S(1)} %get-tuple-element.30), channel_id=1, source_target_pairs={{0,1},{1,0},{2,3},{3,2},{4,5},{5,4},{6,7},{7,6},{8,9},{9,8},{10,11... | collective-permute-start | bytes 737288 | tf_op jit(solution)/shard_map/ppermute | solution.py:298
  148.1 2.1 %collective-permute-start.20 = (bf16[48,6144]{1,0:T(8,128)(2,1)S(1)}, bf16[48,6144]{1,0:T(8,128)(2,1)S(1)}, u32[]{:S(2)}, u32[]{:S(2)}) collective-permute-start(bf16[48,6144]{1,0:T(8,128)(2,1)S(1)} %shard_map.97.refs_0_), channel_id=1, source_target_pairs={{0,1},{1,0},{2,3},{3,2},{4,5},{5,4},{6,7},{7,6},{8,9},{9,8},{10,11... | collective-permute-start | bytes 1769480 | tf_op jit(solution)/shard_map/ppermute | solution.py:298
  159.0 7.8 %collective-permute-start.22 = (bf16[48,768]{1,0:T(8,128)(2,1)S(1)}, bf16[48,768]{1,0:T(8,128)(2,1)S(1)}, u32[]{:S(2)}, u32[]{:S(2)}) collective-permute-start(bf16[48,768]{1,0:T(8,128)(2,1)S(1)} %get-tuple-element.41), channel_id=1, source_target_pairs={{0,12},{4,8},{8,4},{12,0},{1,13},{5,9},{9,5},{13,1},{2,14},{6,10},... | collective-permute-start | bytes 221192 | tf_op jit(solution)/shard_map/ppermute | solution.py:321
  160.9 11.0 %collective-permute-start.23 = (bf16[48,768]{1,0:T(8,128)(2,1)S(1)}, bf16[48,768]{1,0:T(8,128)(2,1)S(1)}, u32[]{:S(2)}, u32[]{:S(2)}) collective-permute-start(bf16[48,768]{1,0:T(8,128)(2,1)S(1)} %get-tuple-element.43), channel_id=1, source_target_pairs={{0,8},{4,12},{8,0},{12,4},{1,9},{5,13},{9,1},{13,5},{2,10},{6,14},... | collective-permute-start | bytes 221192 | tf_op jit(solution)/shard_map/ppermute | solution.py:321
  160.9 11.0 %collective-permute-start.24 = (bf16[48,768]{1,0:T(8,128)(2,1)S(1)}, bf16[48,768]{1,0:T(8,128)(2,1)S(1)}, u32[]{:S(2)}, u32[]{:S(2)}) collective-permute-start(bf16[48,768]{1,0:T(8,128)(2,1)S(1)} %get-tuple-element.42), channel_id=1, source_target_pairs={{0,4},{4,0},{8,12},{12,8},{1,5},{5,1},{9,13},{13,9},{2,6},{6,2},{1... | collective-permute-start | bytes 221192 | tf_op jit(solution)/shard_map/ppermute | solution.py:321
  (11 other events, 55.8 us)
Sparse Core Ops, SparseCore 0:
  122.1 21.7 reduce-scatter.2
  148.5 23.1 reduce-scatter.4

commit v12 on v11

--- a/solution.py
+++ b/solution.py
@@ -354,15 +354,20 @@
 
         weights = [w_up[:, piece] for piece in pieces]
         lead_pair = normed(lead[GAIN_ROWS:].astype(F32))
-        leads = [project(lead_pair, weight) for weight in weights]
-        lead_parts = [all_red(x) for x in leads]
+        leads = [project(lead_pair, weights[0])]
+        lead_parts = [all_red(leads[0])]
         arrived = gelu_sum(lead_parts[0])
 
         rest = tokens[first:] + nothing(leads[-1]).astype(BF16)
         rest = lax.all_gather(rest, "wide", axis=1, tiled=True)
+        later_pair = [a + nothing(rest).astype(BF16) for a in lead_pair]
+        leads.append(project(later_pair, weights[1]))
+        lead_parts.append(all_red(leads[1]))
         rest_pair = normed(rest.astype(F32) + nothing(arrived))
         pair = [jnp.concatenate(p, axis=0) for p in zip(lead_pair, rest_pair)]
-        near, far = project_rows(*pair, qkv_rows, slice(0, qkv_rows.shape[1]))
+        arrived_other = swap(arrived)
+        every = slice(0, qkv_rows.shape[1])
+        near, far = project_rows(*pair, qkv_rows, every, [arrived_other, leads[1]])
         halves, before = [], [near]
         qkv = sum_rows([(near, swap(far))], slice(0, tokens.shape[0]))
         for piece in rest_pieces:
@@ -370,10 +375,10 @@
             halves.append((near, swap(far)))
             before = [near]
 
-        def output(have, piece, terms, cut, earlier=()):
+        def output(have, other, piece, terms, cut, earlier=()):
             last = piece.stop == units
             attention = (attended[cut], attended_other[cut], attn_rows) if last else ()
-            return project_hidden(have, swap(have), w_down, piece, terms, attention, last, earlier)
+            return project_hidden(have, other, w_down, piece, terms, attention, last, earlier)
 
         def chunk_sums(pairs, c, earlier):
             part = slice(cuts[c].start - first, cuts[c].stop - first)
@@ -383,25 +388,26 @@
             full = side_by_side(kept, got, core, earlier)
             return full, lax.psum_scatter(full, "wide", scatter_dimension=1, tiled=True)
 
-        attended = attend(all_red(qkv), q_gain, k_gain, [halves[-1][0]])
+        terms = output(arrived, arrived_other, pieces[0], (), cuts[0], [halves[-1][0]])
+        earlier = [terms[0], halves[-1][1]]
+        attended = attend(all_red(qkv), q_gain, k_gain, earlier)
         attended_other = swap(attended)
         second = gelu_sum(lead_parts[1], [attended])
         sums = chunk_sums(halves, 1, second)
         parts = all_red(sums)
-        terms = output(arrived, pieces[0], (), cuts[0], [sums])
-        coming = chunk_sums(halves, 2, terms[0])
-        terms = output(second, pieces[1], terms, cuts[0], [coming])
+        coming = chunk_sums(halves, 2, sums)
+        terms = output(second, swap(second), pieces[1], terms, cuts[0], [coming])
         coming = all_red(coming)
         full, got = scatter(terms[0], swap(terms[1]), [])
         scattered = [got]
 
         hidden = gelu_sum(parts, [full])
-        terms = output(hidden, slice(0, units), (), cuts[1])
+        terms = output(hidden, swap(hidden), slice(0, units), (), cuts[1])
         full, got = scatter(terms[0], swap(terms[1]), [scattered[0]])
         scattered.append(got)
 
         hidden = gelu_sum(coming, [full])
-        kept, sent = output(hidden, slice(0, units), (), cuts[2])
+        kept, sent = output(hidden, swap(hidden), slice(0, units), (), cuts[2])
         outs = [tokens[cut].astype(F32) + got.astype(F32) for cut, got in zip(cuts, scattered)]
         outs.append(tokens[cuts[2]].astype(F32) + collect(kept, swap(sent), width))
         return jnp.concatenate(outs, axis=0)

time: 181 us -> 176 us (0.972)
  local copies, waits for them, and re-layouts: 9.41 us -> 6.48 us
  starting transfers between devices: 17.1 us -> 14.4 us
    unnamed x17, local copies, waits for them, and re-layouts: 6.38 us -> 2.94 us
    ppermute x15, waiting for transfers between devices: 14 us -> 17.4 us  [swap(): return lax.ppermute(x, 'tok', [(0, 1), (1, 0)])]
    ppermute x7, starting transfers between devices: 9.95 us -> 7.02 us  [all_red(): parts.append(lax.ppermute(x, 'red', pairs))]
    reduce_scatter x2, waiting for transfers between devices: 2.8 us -> 0.02 us  [scatter(): lax.psum_scatter(full, 'wide', scatter_dimension=1, tiled=True)]
  transfers between devices with their start and end apart: 27 -> 27, of which waited for: 18 -> 16; matrix products, arithmetic and copies ran while one was open for 2% -> 2% of each run, Pallas kernels for 23% -> 24%
where the time goes in v12:
time: 176 us
  waiting for transfers between devices  43.7 us (25%)
  Pallas kernels  43.6 us (25%)
  blocking collectives  39.9 us (23%)
  between operations  16 us (9%)
  starting transfers between devices  14.4 us (8%)
  matrix products  7.91 us (4%)
  local copies, waits for them, and re-layouts  6.48 us (4%)
  other arithmetic  3.85 us (2%)
    pallas_call x17, Pallas kernels, call(): pl.pallas_call(body, in_specs=list(specs) + [corner_of(a) for a in earlie...  43.6 us
    all_gather x1, blocking collectives, body(): lead = lax.all_gather(lead, 'wide', axis=1, tiled=True)  21.9 us
    ppermute x7, waiting for transfers between devices, all_red(): parts.append(lax.ppermute(x, 'red', pairs))  18.9 us
    all_gather x1, blocking collectives, body(): rest = lax.all_gather(rest, 'wide', axis=1, tiled=True)  18 us
    ppermute x15, waiting for transfers between devices, swap(): return lax.ppermute(x, 'tok', [(0, 1), (1, 0)])  17.4 us
    dot_general x2, matrix products, project(): part = jnp.dot(both, weight, preferred_element_type=F32)  7.91 us
    ppermute x3, waiting for transfers between devices, collect(): total = total + lax.ppermute(block(chip ^ k), 'wide', pairs).astype(F32)  7.43 us
    ppermute x7, starting transfers between devices, all_red(): parts.append(lax.ppermute(x, 'red', pairs))  7.02 us
  transfers between devices with their start and end apart: 27, of which 16 were waited for; matrix products, arithmetic and copies ran while one was open for 2% of the time, Pallas kernels for 24%

profile of v12, /device:TPU:0, one launch (start us, length us, event | category | flops | bytes accessed | tf_op | source)
XLA Modules:
  0.0 175.8 jit_solution(7455083063066349231)
XLA Ops:
  8.2 21.9 %all_gather.6 = bf16[136,3072]{1,0:T(8,128)(2,1)S(1)} all-gather(bf16[136,768]{1,0:T(8,128)(2,1)S(1)} %pad_maximum_fusion.5), channel_id=1, replica_groups=mesh['grp'=2,'wide'=4,'red'=2,'tok'=2] {'wide'}, dimensions={1}, use_global_device_ids=true | all-gather | bytes 1044480 | tf_op jit(solution)/shard_map/all_gather | solution.py:337
  31.9 2.1 %collective-permute-done = f32[2,128]{1,0:T(2,128)S(1)} collective-permute-done((f32[2,128]{1,0:T(2,128)S(1)}, f32[2,128]{1,0:T(2,128)S(1)}, u32[]{:S(2)}, u32[]{:S(2)}) %collective-permute-start) | collective-permute-done | bytes 1056 | tf_op jit(solution)/shard_map/ppermute | solution.py:304
  34.5 1.7 collective-permute-done.1
  36.2 5.3 %fusion.2 = f32[256,3072]{1,0:T(8,128)S(1)} fusion(bf16[1536,6144]{1,0:T(8,128)(2,1)} %refs_2_.8, bf16[128,1536]{1,0:T(8,128)(2,1)S(1)} %get-tuple-element.40, bf16[128,1536]{1,0:T(8,128)(2,1)S(1)} %collective-permute-done.1), kind=kOutput, calls=%fused_computation.2 | convolution fusion | flops 2417491968 | bytes 13369344 | tf_op jit(solution)/shard_map/dot_general | solution.py:351
  41.9 2.1 %collective-permute-done.2 = bf16[128,3072]{1,0:T(8,128)(2,1)S(1)} collective-permute-done((bf16[128,3072]{1,0:T(8,128)(2,1)S(1)}, bf16[128,3072]{1,0:T(8,128)(2,1)S(1)}, u32[]{:S(2)}, u32[]{:S(2)}) %collective-permute-start.2) | collective-permute-done | bytes 786464 | tf_op jit(solution)/shard_map/ppermute | solution.py:298
  46.9 18.0 %all_gather.7 = bf16[128,3072]{1,0:T(8,128)(2,1)S(1)} all-gather(bf16[128,768]{1,0:T(8,128)(2,1)S(1)} %slice_add_fusion.2), channel_id=1, replica_groups=mesh['grp'=2,'wide'=4,'red'=2,'tok'=2] {'wide'}, dimensions={1}, use_global_device_ids=true | all-gather | bytes 983040 | tf_op jit(solution)/shard_map/all_gather | solution.py:362
  69.0 2.6 %fusion = f32[256,3072]{1,0:T(8,128)S(1)} fusion(bf16[1536,6144]{1,0:T(8,128)(2,1)S(1)} %copy-done.6, bf16[128,1536]{1,0:T(8,128)(2,1)S(1)} %get-tuple-element.44, bf16[128,1536]{1,0:T(8,128)(2,1)S(1)} %get-tuple-element.45), kind=kOutput, calls=%fused_computation | convolution fusion | flops 2417491968 | bytes 13369344 | tf_op jit(solution)/shard_map/dot_general | solution.py:351
  78.4 6.1 %shard_map.85 = (bf16[128,4096]{1,0:T(8,128)(2,1)S(1)}, bf16[128,4096]{1,0:T(8,128)(2,1)S(1)}) custom-call(bf16[128,1536]{1,0:T(8,128)(2,1)S(1)} %get-tuple-element.38.refs_0_, bf16[128,1536]{1,0:T(8,128)(2,1)S(1)} %collective-permute-done.7.refs_1_, bf16[1536,6144]{1,0:T(8,128)(2,1)} %refs_2_.8, bf16[256,384]{1,0:T(8,128)(2,1)S(1)} %get-tuple-element.19.refs_0_.refs_3_), custom_call_target="tpu_custom_call" | custom-call | tf_op jit(solution)/shard_map/pallas_call | solution.py:63
  84.5 3.7 %shard_map.86 = (bf16[128,2048]{1,0:T(8,128)(2,1)S(1)}, bf16[128,2048]{1,0:T(8,128)(2,1)S(1)}) custom-call(bf16[128,1536]{1,0:T(8,128)(2,1)S(1)} %get-tuple-element.38.refs_0_, bf16[128,1536]{1,0:T(8,128)(2,1)S(1)} %collective-permute-done.7.refs_1_, bf16[1536,6144]{1,0:T(8,128)(2,1)} %refs_2_.8, bf16[128,4096]{1,0:T(8,128)(2,1)S(1)} %get-tuple-element.21.refs_3_.refs_0_), custom_call_target="tpu_custom_call" | custom-call | tf_op jit(solution)/shard_map/pallas_call | solution.py:63
  88.9 3.1 %collective-permute-done.9.refs_1_ = bf16[256,384]{1,0:T(8,128)(2,1)S(1)} collective-permute-done((bf16[256,384]{1,0:T(8,128)(2,1)S(1)}, bf16[256,384]{1,0:T(8,128)(2,1)S(1)}, u32[]{:S(2)}, u32[]{:S(2)}) %collective-permute-start.9) | collective-permute-done | bytes 196640 | tf_op jit(solution)/shard_map/ppermute | solution.py:298
  92.7 5.1 %shard_map.87 = (f32[128,1536]{1,0:T(8,128)S(1)}, f32[128,1536]{1,0:T(8,128)S(1)}) custom-call(bf16[128,3072]{1,0:T(8,128)(2,1)S(1)} %shard_map.82.refs_0_, bf16[128,3072]{1,0:T(8,128)(2,1)S(1)} %collective-permute-done.8.refs_3_.refs_1_, bf16[6144,1536]{1,0:T(8,128)(2,1)} %refs_2_.13, bf16[128,2048]{1,0:T(8,128)(2,1)S(1)} %get-tuple-element.22.refs_3_.refs_2_), custom_call_target="tpu_custom_call" | custom-call | tf_op jit(solution)/shard_map/pallas_call | solution.py:63
  104.0 5.1 %shard_map.92 = (bf16[128,1536]{1,0:T(8,128)(2,1)S(1)}, bf16[128,1536]{1,0:T(8,128)(2,1)S(1)}) custom-call(bf16[128,3072]{1,0:T(8,128)(2,1)S(1)} %shard_map.89.refs_4_.refs_0_, bf16[128,3072]{1,0:T(8,128)(2,1)S(1)} %collective-permute-done.12.refs_1_, bf16[6144,1536]{1,0:T(8,128)(2,1)} %refs_2_.13, f32[128,1536]{1,0:T(8,128)S(1)} %get-tuple-element.23.refs_4_.refs_3_, ...), custom_call_target="tpu_custom_call" | custom-call | tf_op jit(solution)/shard_map/pallas_call | solution.py:63
  109.3 1.6 collective-permute-done.15.refs_1_
  112.1 13.0 %collective-permute-done.16.refs_1_ = bf16[80,6144]{1,0:T(8,128)(2,1)S(1)} collective-permute-done((bf16[80,6144]{1,0:T(8,128)(2,1)S(1)}, bf16[80,6144]{1,0:T(8,128)(2,1)S(1)}, u32[]{:S(2)}, u32[]{:S(2)}) %collective-permute-start.16) | collective-permute-done | bytes 983072 | tf_op jit(solution)/shard_map/ppermute | solution.py:304
  125.1 1.7 shard_map.94.refs_0_
  127.6 1.9 %collective-permute-done.17.refs_1_ = bf16[80,6144]{1,0:T(8,128)(2,1)S(1)} collective-permute-done((bf16[80,6144]{1,0:T(8,128)(2,1)S(1)}, bf16[80,6144]{1,0:T(8,128)(2,1)S(1)}, u32[]{:S(2)}, u32[]{:S(2)}) %collective-permute-start.17) | collective-permute-done | bytes 983072 | tf_op jit(solution)/shard_map/ppermute | solution.py:298
  129.5 7.4 %shard_map.95 = (bf16[80,1536]{1,0:T(8,128)(2,1)S(1)}, bf16[80,1536]{1,0:T(8,128)(2,1)S(1)}) custom-call(bf16[80,6144]{1,0:T(8,128)(2,1)S(1)} %shard_map.94.refs_0_, bf16[80,6144]{1,0:T(8,128)(2,1)S(1)} %collective-permute-done.17.refs_1_, bf16[6144,1536]{1,0:T(8,128)(2,1)} %refs_2_.13, bf16[80,128]{1,0:T(8,128)(2,1)S(1)} %slice.119.refs_3_, ...), custom_call_target="tpu_custom_call" | custom-call | tf_op jit(solution)/shard_map/pallas_call | solution.py:63
  140.2 2.4 %collective-permute-done.19.refs_1_ = bf16[48,6144]{1,0:T(8,128)(2,1)S(1)} collective-permute-done((bf16[48,6144]{1,0:T(8,128)(2,1)S(1)}, bf16[48,6144]{1,0:T(8,128)(2,1)S(1)}, u32[]{:S(2)}, u32[]{:S(2)}) %collective-permute-start.19) | collective-permute-done | bytes 589856 | tf_op jit(solution)/shard_map/ppermute | solution.py:304
  144.4 1.8 %collective-permute-done.20.refs_1_ = bf16[48,6144]{1,0:T(8,128)(2,1)S(1)} collective-permute-done((bf16[48,6144]{1,0:T(8,128)(2,1)S(1)}, bf16[48,6144]{1,0:T(8,128)(2,1)S(1)}, u32[]{:S(2)}, u32[]{:S(2)}) %collective-permute-start.20) | collective-permute-done | bytes 589856 | tf_op jit(solution)/shard_map/ppermute | solution.py:298
  146.2 7.4 %shard_map.98 = (bf16[48,1536]{1,0:T(8,128)(2,1)S(1)}, bf16[48,1536]{1,0:T(8,128)(2,1)S(1)}) custom-call(bf16[48,6144]{1,0:T(8,128)(2,1)S(1)} %shard_map.97.refs_0_, bf16[48,6144]{1,0:T(8,128)(2,1)S(1)} %collective-permute-done.20.refs_1_, bf16[6144,1536]{1,0:T(8,128)(2,1)} %refs_2_.13, bf16[48,128]{1,0:T(8,128)(2,1)S(1)} %slice.121.refs_3_, ...), custom_call_target="tpu_custom_call" | custom-call | tf_op jit(solution)/shard_map/pallas_call | solution.py:63
  155.1 1.9 %collective-permute-start.22 = (bf16[48,768]{1,0:T(8,128)(2,1)S(1)}, bf16[48,768]{1,0:T(8,128)(2,1)S(1)}, u32[]{:S(2)}, u32[]{:S(2)}) collective-permute-start(bf16[48,768]{1,0:T(8,128)(2,1)S(1)} %get-tuple-element.41), channel_id=1, source_target_pairs={{0,12},{4,8},{8,4},{12,0},{1,13},{5,9},{9,5},{13,1},{2,14},{6,10},... | collective-permute-start | bytes 221192 | tf_op jit(solution)/shard_map/ppermute | solution.py:321
  156.9 2.6 %collective-permute-start.24 = (bf16[48,768]{1,0:T(8,128)(2,1)S(1)}, bf16[48,768]{1,0:T(8,128)(2,1)S(1)}, u32[]{:S(2)}, u32[]{:S(2)}) collective-permute-start(bf16[48,768]{1,0:T(8,128)(2,1)S(1)} %get-tuple-element.42), channel_id=1, source_target_pairs={{0,4},{4,0},{8,12},{12,8},{1,5},{5,1},{9,13},{13,9},{2,6},{6,2},{1... | collective-permute-start | bytes 221192 | tf_op jit(solution)/shard_map/ppermute | solution.py:321
  159.6 3.6 %collective-permute-done.22 = bf16[48,768]{1,0:T(8,128)(2,1)S(1)} collective-permute-done((bf16[48,768]{1,0:T(8,128)(2,1)S(1)}, bf16[48,768]{1,0:T(8,128)(2,1)S(1)}, u32[]{:S(2)}, u32[]{:S(2)}) %collective-permute-start.22) | collective-permute-done | bytes 73760 | tf_op jit(solution)/shard_map/ppermute | solution.py:321
  163.1 3.9 %collective-permute-done.23 = bf16[48,768]{1,0:T(8,128)(2,1)S(1)} collective-permute-done((bf16[48,768]{1,0:T(8,128)(2,1)S(1)}, bf16[48,768]{1,0:T(8,128)(2,1)S(1)}, u32[]{:S(2)}, u32[]{:S(2)}) %collective-permute-start.23) | collective-permute-done | bytes 73760 | tf_op jit(solution)/shard_map/ppermute | solution.py:321
  (111 shorter events, 33.9 us)
Async XLA Ops:
  6.5 132.0 %reduce-scatter.3.cloned.1.call-start = ((), (), s32[]{:S(2)}) async-start(), calls=%async_computation.2 | async-start | bytes 983040 | tf_op jit(solution)/shard_map/reduce_scatter | solution.py:389
  30.4 3.6 %collective-permute-start = (f32[2,128]{1,0:T(2,128)S(1)}, f32[2,128]{1,0:T(2,128)S(1)}, u32[]{:S(2)}, u32[]{:S(2)}) collective-permute-start(f32[2,128]{1,0:T(2,128)S(1)} %pad_maximum_fusion.6), channel_id=1, source_target_pairs={{0,2},{2,0},{1,3},{3,1},{4,6},{6,4},{5,7},{7,5},{8,10},{10,8},{9,1... | collective-permute-start | bytes 3080 | tf_op jit(solution)/shard_map/ppermute | solution.py:304
  34.4 1.8 %collective-permute-start.1 = (bf16[128,1536]{1,0:T(8,128)(2,1)S(1)}, bf16[128,1536]{1,0:T(8,128)(2,1)S(1)}, u32[]{:S(2)}, u32[]{:S(2)}) collective-permute-start(bf16[128,1536]{1,0:T(8,128)(2,1)S(1)} %get-tuple-element.39), channel_id=1, source_target_pairs={{0,1},{1,0},{2,3},{3,2},{4,5},{5,4},{6,7},{7,6},{8,9},{9,8},{10,11... | collective-permute-start | bytes 1179656 | tf_op jit(solution)/shard_map/ppermute | solution.py:298
  41.7 2.4 %collective-permute-start.2 = (bf16[128,3072]{1,0:T(8,128)(2,1)S(1)}, bf16[128,3072]{1,0:T(8,128)(2,1)S(1)}, u32[]{:S(2)}, u32[]{:S(2)}) collective-permute-start(bf16[128,3072]{1,0:T(8,128)(2,1)S(1)} %slice.152), channel_id=1, source_target_pairs={{0,1},{1,0},{2,3},{3,2},{4,5},{5,4},{6,7},{7,6},{8,9},{9,8},{10,11... | collective-permute-start | bytes 2359304 | tf_op jit(solution)/shard_map/ppermute | solution.py:298
  44.7 21.4 %collective-permute-start.5 = (bf16[128,3072]{1,0:T(8,128)(2,1)S(1)}, bf16[128,3072]{1,0:T(8,128)(2,1)S(1)}, u32[]{:S(2)}, u32[]{:S(2)}) collective-permute-start(bf16[128,3072]{1,0:T(8,128)(2,1)S(1)} %fusion.9.refs_0_), channel_id=1, source_target_pairs={{0,2},{2,0},{1,3},{3,1},{4,6},{6,4},{5,7},{7,5},{8,10},{10,8},{9,1... | collective-permute-start | bytes 2359304 | tf_op jit(solution)/shard_map/ppermute | solution.py:304
  68.4 3.9 %collective-permute-start.6 = (f32[2,128]{1,0:T(2,128)S(1)}, f32[2,128]{1,0:T(2,128)S(1)}, u32[]{:S(2)}, u32[]{:S(2)}) collective-permute-start(f32[2,128]{1,0:T(2,128)S(1)} %pad_maximum_fusion.7), channel_id=1, source_target_pairs={{0,2},{2,0},{1,3},{3,1},{4,6},{6,4},{5,7},{7,5},{8,10},{10,8},{9,1... | collective-permute-start | bytes 3080 | tf_op jit(solution)/shard_map/ppermute | solution.py:304
  71.7 2.4 %collective-permute-start.3 = (bf16[128,3072]{1,0:T(8,128)(2,1)S(1)}, bf16[128,3072]{1,0:T(8,128)(2,1)S(1)}, u32[]{:S(2)}, u32[]{:S(2)}) collective-permute-start(bf16[128,3072]{1,0:T(8,128)(2,1)S(1)} %slice.151), channel_id=1, source_target_pairs={{0,1},{1,0},{2,3},{3,2},{4,5},{5,4},{6,7},{7,6},{8,9},{9,8},{10,11... | collective-permute-start | bytes 2359304 | tf_op jit(solution)/shard_map/ppermute | solution.py:298
  71.8 4.1 %collective-permute-start.8 = (bf16[128,3072]{1,0:T(8,128)(2,1)S(1)}, bf16[128,3072]{1,0:T(8,128)(2,1)S(1)}, u32[]{:S(2)}, u32[]{:S(2)}) collective-permute-start(bf16[128,3072]{1,0:T(8,128)(2,1)S(1)} %shard_map.82.refs_0_), channel_id=1, source_target_pairs={{0,1},{1,0},{2,3},{3,2},{4,5},{5,4},{6,7},{7,6},{8,9},{9,8},{10,11... | collective-permute-start | bytes 2359304 | tf_op jit(solution)/shard_map/ppermute | solution.py:298
  72.8 3.1 %collective-permute-start.7 = (bf16[128,1536]{1,0:T(8,128)(2,1)S(1)}, bf16[128,1536]{1,0:T(8,128)(2,1)S(1)}, u32[]{:S(2)}, u32[]{:S(2)}) collective-permute-start(bf16[128,1536]{1,0:T(8,128)(2,1)S(1)} %get-tuple-element.37), channel_id=1, source_target_pairs={{0,1},{1,0},{2,3},{3,2},{4,5},{5,4},{6,7},{7,6},{8,9},{9,8},{10,11... | collective-permute-start | bytes 1179656 | tf_op jit(solution)/shard_map/ppermute | solution.py:298
  74.2 25.6 %collective-permute-start.4 = (bf16[128,3072]{1,0:T(8,128)(2,1)S(1)}, bf16[128,3072]{1,0:T(8,128)(2,1)S(1)}, u32[]{:S(2)}, u32[]{:S(2)}) collective-permute-start(bf16[128,3072]{1,0:T(8,128)(2,1)S(1)} %fusion.8.refs_4_.refs_0_), channel_id=1, source_target_pairs={{0,2},{2,0},{1,3},{3,1},{4,6},{6,4},{5,7},{7,5},{8,10},{10,8},{9,1... | collective-permute-start | bytes 2359304 | tf_op jit(solution)/shard_map/ppermute | solution.py:304
  88.2 10.8 %collective-permute-start.11 = (bf16[128,2048]{1,0:T(8,128)(2,1)S(1)}, bf16[128,2048]{1,0:T(8,128)(2,1)S(1)}, u32[]{:S(2)}, u32[]{:S(2)}) collective-permute-start(bf16[128,2048]{1,0:T(8,128)(2,1)S(1)} %get-tuple-element.24), channel_id=1, source_target_pairs={{0,1},{1,0},{2,3},{3,2},{4,5},{5,4},{6,7},{7,6},{8,9},{9,8},{10,11... | collective-permute-start | bytes 1572872 | tf_op jit(solution)/shard_map/ppermute | solution.py:298
  88.3 12.4 %collective-permute-start.14 = (bf16[128,4096]{1,0:T(8,128)(2,1)S(1)}, bf16[128,4096]{1,0:T(8,128)(2,1)S(1)}, u32[]{:S(2)}, u32[]{:S(2)}) collective-permute-start(bf16[128,4096]{1,0:T(8,128)(2,1)S(1)} %get-tuple-element.26), channel_id=1, source_target_pairs={{0,1},{1,0},{2,3},{3,2},{4,5},{5,4},{6,7},{7,6},{8,9},{9,8},{10,11... | collective-permute-start | bytes 3145736 | tf_op jit(solution)/shard_map/ppermute | solution.py:298
  88.8 3.2 %collective-permute-start.9 = (bf16[256,384]{1,0:T(8,128)(2,1)S(1)}, bf16[256,384]{1,0:T(8,128)(2,1)S(1)}, u32[]{:S(2)}, u32[]{:S(2)}) collective-permute-start(bf16[256,384]{1,0:T(8,128)(2,1)S(1)} %get-tuple-element.20), channel_id=1, source_target_pairs={{0,1},{1,0},{2,3},{3,2},{4,5},{5,4},{6,7},{7,6},{8,9},{9,8},{10,11... | collective-permute-start | bytes 589832 | tf_op jit(solution)/shard_map/ppermute | solution.py:298
  92.0 7.0 %collective-permute-start.10 = (bf16[256,384]{1,0:T(8,128)(2,1)S(1)}, bf16[256,384]{1,0:T(8,128)(2,1)S(1)}, u32[]{:S(2)}, u32[]{:S(2)}) collective-permute-start(bf16[256,384]{1,0:T(8,128)(2,1)S(1)} %shard_map.84.refs_0_), channel_id=1, source_target_pairs={{0,2},{2,0},{1,3},{3,1},{4,6},{6,4},{5,7},{7,5},{8,10},{10,8},{9,1... | collective-permute-start | bytes 589832 | tf_op jit(solution)/shard_map/ppermute | solution.py:304
  100.6 2.6 %collective-permute-start.12 = (bf16[128,3072]{1,0:T(8,128)(2,1)S(1)}, bf16[128,3072]{1,0:T(8,128)(2,1)S(1)}, u32[]{:S(2)}, u32[]{:S(2)}) collective-permute-start(bf16[128,3072]{1,0:T(8,128)(2,1)S(1)} %shard_map.89.refs_4_.refs_0_), channel_id=1, source_target_pairs={{0,1},{1,0},{2,3},{3,2},{4,5},{5,4},{6,7},{7,6},{8,9},{9,8},{10,11... | collective-permute-start | bytes 2359304 | tf_op jit(solution)/shard_map/ppermute | solution.py:298
  100.9 24.2 %collective-permute-start.16 = (bf16[80,6144]{1,0:T(8,128)(2,1)S(1)}, bf16[80,6144]{1,0:T(8,128)(2,1)S(1)}, u32[]{:S(2)}, u32[]{:S(2)}) collective-permute-start(bf16[80,6144]{1,0:T(8,128)(2,1)S(1)} %shard_map.90.refs_4_.refs_0_), channel_id=1, source_target_pairs={{0,2},{2,0},{1,3},{3,1},{4,6},{6,4},{5,7},{7,5},{8,10},{10,8},{9,1... | collective-permute-start | bytes 2949128 | tf_op jit(solution)/shard_map/ppermute | solution.py:304
  109.1 1.8 %collective-permute-start.15 = (bf16[128,1536]{1,0:T(8,128)(2,1)S(1)}, bf16[128,1536]{1,0:T(8,128)(2,1)S(1)}, u32[]{:S(2)}, u32[]{:S(2)}) collective-permute-start(bf16[128,1536]{1,0:T(8,128)(2,1)S(1)} %get-tuple-element.28), channel_id=1, source_target_pairs={{0,1},{1,0},{2,3},{3,2},{4,5},{5,4},{6,7},{7,6},{8,9},{9,8},{10,11... | collective-permute-start | bytes 1179656 | tf_op jit(solution)/shard_map/ppermute | solution.py:298
  111.9 55.2 %reduce-scatter.5.cloned.1.call-start = ((), (), s32[]{:S(2)}) async-start(), calls=%async_computation.3 | async-start | bytes 614400 | tf_op jit(solution)/shard_map/reduce_scatter | solution.py:389
  126.9 2.6 %collective-permute-start.17 = (bf16[80,6144]{1,0:T(8,128)(2,1)S(1)}, bf16[80,6144]{1,0:T(8,128)(2,1)S(1)}, u32[]{:S(2)}, u32[]{:S(2)}) collective-permute-start(bf16[80,6144]{1,0:T(8,128)(2,1)S(1)} %shard_map.94.refs_0_), channel_id=1, source_target_pairs={{0,1},{1,0},{2,3},{3,2},{4,5},{5,4},{6,7},{7,6},{8,9},{9,8},{10,11... | collective-permute-start | bytes 2949128 | tf_op jit(solution)/shard_map/ppermute | solution.py:298
  126.9 15.7 %collective-permute-start.19 = (bf16[48,6144]{1,0:T(8,128)(2,1)S(1)}, bf16[48,6144]{1,0:T(8,128)(2,1)S(1)}, u32[]{:S(2)}, u32[]{:S(2)}) collective-permute-start(bf16[48,6144]{1,0:T(8,128)(2,1)S(1)} %shard_map.91.refs_8_.refs_0_), channel_id=1, source_target_pairs={{0,2},{2,0},{1,3},{3,1},{4,6},{6,4},{5,7},{7,5},{8,10},{10,8},{9,1... | collective-permute-start | bytes 1769480 | tf_op jit(solution)/shard_map/ppermute | solution.py:304
  144.1 2.1 %collective-permute-start.20 = (bf16[48,6144]{1,0:T(8,128)(2,1)S(1)}, bf16[48,6144]{1,0:T(8,128)(2,1)S(1)}, u32[]{:S(2)}, u32[]{:S(2)}) collective-permute-start(bf16[48,6144]{1,0:T(8,128)(2,1)S(1)} %shard_map.97.refs_0_), channel_id=1, source_target_pairs={{0,1},{1,0},{2,3},{3,2},{4,5},{5,4},{6,7},{7,6},{8,9},{9,8},{10,11... | collective-permute-start | bytes 1769480 | tf_op jit(solution)/shard_map/ppermute | solution.py:298
  155.1 8.1 %collective-permute-start.22 = (bf16[48,768]{1,0:T(8,128)(2,1)S(1)}, bf16[48,768]{1,0:T(8,128)(2,1)S(1)}, u32[]{:S(2)}, u32[]{:S(2)}) collective-permute-start(bf16[48,768]{1,0:T(8,128)(2,1)S(1)} %get-tuple-element.41), channel_id=1, source_target_pairs={{0,12},{4,8},{8,4},{12,0},{1,13},{5,9},{9,5},{13,1},{2,14},{6,10},... | collective-permute-start | bytes 221192 | tf_op jit(solution)/shard_map/ppermute | solution.py:321
  156.9 10.1 %collective-permute-start.23 = (bf16[48,768]{1,0:T(8,128)(2,1)S(1)}, bf16[48,768]{1,0:T(8,128)(2,1)S(1)}, u32[]{:S(2)}, u32[]{:S(2)}) collective-permute-start(bf16[48,768]{1,0:T(8,128)(2,1)S(1)} %get-tuple-element.43), channel_id=1, source_target_pairs={{0,8},{4,12},{8,0},{12,4},{1,9},{5,13},{9,1},{13,5},{2,10},{6,14},... | collective-permute-start | bytes 221192 | tf_op jit(solution)/shard_map/ppermute | solution.py:321
  156.9 10.1 %collective-permute-start.24 = (bf16[48,768]{1,0:T(8,128)(2,1)S(1)}, bf16[48,768]{1,0:T(8,128)(2,1)S(1)}, u32[]{:S(2)}, u32[]{:S(2)}) collective-permute-start(bf16[48,768]{1,0:T(8,128)(2,1)S(1)} %get-tuple-element.42), channel_id=1, source_target_pairs={{0,4},{4,0},{8,12},{12,8},{1,5},{5,1},{9,13},{13,9},{2,6},{6,2},{1... | collective-permute-start | bytes 221192 | tf_op jit(solution)/shard_map/ppermute | solution.py:321
  (11 other events, 73.7 us)
Sparse Core Ops, SparseCore 0:
  112.0 22.4 reduce-scatter.2
  144.5 21.5 reduce-scatter.4

commit v13 on v12

--- a/solution.py
+++ b/solution.py
@@ -337,9 +337,9 @@
         lead = lax.all_gather(lead, "wide", axis=1, tiled=True)
         gain = lead[:1]
 
-        def normed(floats):
+        def normed(floats, start=0.0):
             sums = jnp.stack([jnp.sum(floats, axis=1), jnp.sum(floats * floats, axis=1)])
-            sums = sum_red(sums)[:, :, None] / D
+            sums = sum_red(sums)[:, :, None] / D + start
             values = normalize(floats, sums[0], sums[1], gain).astype(BF16)
             mine = lax.dynamic_slice_in_dim(values, core * depth, depth, axis=1)
             theirs = lax.dynamic_slice_in_dim(values, (1 - core) * depth, depth, axis=1)
@@ -349,21 +349,22 @@
             both = jnp.concatenate(pair, axis=0)
             half = both.shape[0] // 2
             part = jnp.dot(both, weight, preferred_element_type=F32)
-            far = swap(part[half:].astype(BF16)).astype(F32)
-            return (part[:half] + far).astype(BF16)
+            sent = part[half:].astype(BF16)
+            return (part[:half] + swap(sent).astype(F32)).astype(BF16), sent
 
         weights = [w_up[:, piece] for piece in pieces]
         lead_pair = normed(lead[GAIN_ROWS:].astype(F32))
-        leads = [project(lead_pair, weights[0])]
+        leads = [project(lead_pair, weights[0])[0]]
         lead_parts = [all_red(leads[0])]
-        arrived = gelu_sum(lead_parts[0])
 
         rest = tokens[first:] + nothing(leads[-1]).astype(BF16)
         rest = lax.all_gather(rest, "wide", axis=1, tiled=True)
         later_pair = [a + nothing(rest).astype(BF16) for a in lead_pair]
-        leads.append(project(later_pair, weights[1]))
-        lead_parts.append(all_red(leads[1]))
-        rest_pair = normed(rest.astype(F32) + nothing(arrived))
+        lead, sent = project(later_pair, weights[1])
+        leads.append(lead)
+        lead_parts.append(all_red(lead))
+        arrived = gelu_sum(lead_parts[0], [sent])
+        rest_pair = normed(rest.astype(F32) + nothing(arrived), nothing(leads[1]))
         pair = [jnp.concatenate(p, axis=0) for p in zip(lead_pair, rest_pair)]
         arrived_other = swap(arrived)
         every = slice(0, qkv_rows.shape[1])
@@ -373,7 +374,7 @@
         for piece in rest_pieces:
             near, far = project_rows(*rest_pair, w_up, piece, before)
             halves.append((near, swap(far)))
-            before = [near]
+            before = [near, qkv]
 
         def output(have, other, piece, terms, cut, earlier=()):
             last = piece.stop == units

time: 176 us -> 177 us (level)
    ppermute x7, waiting for transfers between devices: 18.9 us -> 22.9 us  [all_red(): parts.append(lax.ppermute(x, 'red', pairs))]
    ppermute x15, waiting for transfers between devices: 17.4 us -> 14.2 us  [swap(): return lax.ppermute(x, 'tok', [(0, 1), (1, 0)])]
  transfers between devices with their start and end apart: 27 -> 27, of which waited for: 16 -> 16; matrix products, arithmetic and copies ran while one was open for 2% -> 3% of each run, Pallas kernels for 24% -> 24%
where the time goes in v13:
time: 177 us
  waiting for transfers between devices  44.6 us (25%)
  Pallas kernels  43.7 us (25%)
  blocking collectives  39.9 us (23%)
  between operations  16.6 us (9%)
  starting transfers between devices  14.3 us (8%)
  matrix products  7.91 us (4%)
  local copies, waits for them, and re-layouts  5.99 us (3%)
  other arithmetic  3.85 us (2%)
    pallas_call x17, Pallas kernels, call(): pl.pallas_call(body, in_specs=list(specs) + [corner_of(a) for a in earlie...  43.7 us
    ppermute x7, waiting for transfers between devices, all_red(): parts.append(lax.ppermute(x, 'red', pairs))  22.9 us
    all_gather x1, blocking collectives, body(): lead = lax.all_gather(lead, 'wide', axis=1, tiled=True)  21.9 us
    all_gather x1, blocking collectives, body(): rest = lax.all_gather(rest, 'wide', axis=1, tiled=True)  18 us
    ppermute x15, waiting for transfers between devices, swap(): return lax.ppermute(x, 'tok', [(0, 1), (1, 0)])  14.2 us
    dot_general x2, matrix products, project(): part = jnp.dot(both, weight, preferred_element_type=F32)  7.91 us
    ppermute x3, waiting for transfers between devices, collect(): total = total + lax.ppermute(block(chip ^ k), 'wide', pairs).astype(F32)  7.43 us
    ppermute x7, starting transfers between devices, all_red(): parts.append(lax.ppermute(x, 'red', pairs))  6.94 us
  transfers between devices with their start and end apart: 27, of which 16 were waited for; matrix products, arithmetic and copies ran while one was open for 3% of the time, Pallas kernels for 24%

profile of v13, /device:TPU:0, one launch (start us, length us, event | category | flops | bytes accessed | tf_op | source)
XLA Modules:
  0.0 176.8 jit_solution(17522628213814154415)
XLA Ops:
  8.2 21.9 %all_gather.6 = bf16[136,3072]{1,0:T(8,128)(2,1)S(1)} all-gather(bf16[136,768]{1,0:T(8,128)(2,1)S(1)} %pad_maximum_fusion.5), channel_id=1, replica_groups=mesh['grp'=2,'wide'=4,'red'=2,'tok'=2] {'wide'}, dimensions={1}, use_global_device_ids=true | all-gather | bytes 1044480 | tf_op jit(solution)/shard_map/all_gather | solution.py:337
  31.9 2.1 %collective-permute-done = f32[2,128]{1,0:T(2,128)S(1)} collective-permute-done((f32[2,128]{1,0:T(2,128)S(1)}, f32[2,128]{1,0:T(2,128)S(1)}, u32[]{:S(2)}, u32[]{:S(2)}) %collective-permute-start) | collective-permute-done | bytes 1056 | tf_op jit(solution)/shard_map/ppermute | solution.py:304
  34.5 1.7 collective-permute-done.1
  36.2 5.3 %fusion.2 = f32[256,3072]{1,0:T(8,128)S(1)} fusion(bf16[1536,6144]{1,0:T(8,128)(2,1)} %refs_2_.8, bf16[128,1536]{1,0:T(8,128)(2,1)S(1)} %get-tuple-element.40, bf16[128,1536]{1,0:T(8,128)(2,1)S(1)} %collective-permute-done.1), kind=kOutput, calls=%fused_computation.2 | convolution fusion | flops 2417491968 | bytes 13369344 | tf_op jit(solution)/shard_map/dot_general | solution.py:351
  41.9 2.1 %collective-permute-done.2 = bf16[128,3072]{1,0:T(8,128)(2,1)S(1)} collective-permute-done((bf16[128,3072]{1,0:T(8,128)(2,1)S(1)}, bf16[128,3072]{1,0:T(8,128)(2,1)S(1)}, u32[]{:S(2)}, u32[]{:S(2)}) %collective-permute-start.2) | collective-permute-done | bytes 786464 | tf_op jit(solution)/shard_map/ppermute | solution.py:298
  46.9 18.0 %all_gather.7 = bf16[128,3072]{1,0:T(8,128)(2,1)S(1)} all-gather(bf16[128,768]{1,0:T(8,128)(2,1)S(1)} %slice_add_fusion.2), channel_id=1, replica_groups=mesh['grp'=2,'wide'=4,'red'=2,'tok'=2] {'wide'}, dimensions={1}, use_global_device_ids=true | all-gather | bytes 983040 | tf_op jit(solution)/shard_map/all_gather | solution.py:361
  66.2 2.6 %fusion = f32[256,3072]{1,0:T(8,128)S(1)} fusion(bf16[1536,6144]{1,0:T(8,128)(2,1)S(1)} %copy-done.6, bf16[128,1536]{1,0:T(8,128)(2,1)S(1)} %get-tuple-element.44, bf16[128,1536]{1,0:T(8,128)(2,1)S(1)} %get-tuple-element.45), kind=kOutput, calls=%fused_computation | convolution fusion | flops 2417491968 | bytes 13369344 | tf_op jit(solution)/shard_map/dot_general | solution.py:351
  73.6 1.7 collective-permute-done.6
  79.3 6.1 %shard_map.85 = (bf16[128,4096]{1,0:T(8,128)(2,1)S(1)}, bf16[128,4096]{1,0:T(8,128)(2,1)S(1)}) custom-call(bf16[128,1536]{1,0:T(8,128)(2,1)S(1)} %get-tuple-element.38.refs_0_, bf16[128,1536]{1,0:T(8,128)(2,1)S(1)} %collective-permute-done.7.refs_1_, bf16[1536,6144]{1,0:T(8,128)(2,1)} %refs_2_.8, bf16[256,384]{1,0:T(8,128)(2,1)S(1)} %get-tuple-element.19.refs_0_.refs_3_), custom_call_target="tpu_custom_call" | custom-call | tf_op jit(solution)/shard_map/pallas_call | solution.py:63
  85.4 3.7 %shard_map.86 = (bf16[128,2048]{1,0:T(8,128)(2,1)S(1)}, bf16[128,2048]{1,0:T(8,128)(2,1)S(1)}) custom-call(bf16[128,1536]{1,0:T(8,128)(2,1)S(1)} %get-tuple-element.38.refs_0_, bf16[128,1536]{1,0:T(8,128)(2,1)S(1)} %collective-permute-done.7.refs_1_, bf16[1536,6144]{1,0:T(8,128)(2,1)} %refs_2_.8, bf16[128,4096]{1,0:T(8,128)(2,1)S(1)} %get-tuple-element.21.refs_3_.refs_0_, ...), custom_call_target="tpu_custom_call" | custom-call | tf_op jit(solution)/shard_map/pallas_call | solution.py:63
  91.3 5.1 %shard_map.87 = (f32[128,1536]{1,0:T(8,128)S(1)}, f32[128,1536]{1,0:T(8,128)S(1)}) custom-call(bf16[128,3072]{1,0:T(8,128)(2,1)S(1)} %shard_map.82.refs_0_, bf16[128,3072]{1,0:T(8,128)(2,1)S(1)} %collective-permute-done.8.refs_3_.refs_1_, bf16[6144,1536]{1,0:T(8,128)(2,1)} %refs_2_.13, bf16[128,2048]{1,0:T(8,128)(2,1)S(1)} %get-tuple-element.22.refs_3_.refs_2_), custom_call_target="tpu_custom_call" | custom-call | tf_op jit(solution)/shard_map/pallas_call | solution.py:63
  96.4 3.7 %collective-permute-done.10.refs_1_ = bf16[256,384]{1,0:T(8,128)(2,1)S(1)} collective-permute-done((bf16[256,384]{1,0:T(8,128)(2,1)S(1)}, bf16[256,384]{1,0:T(8,128)(2,1)S(1)}, u32[]{:S(2)}, u32[]{:S(2)}) %collective-permute-start.10) | collective-permute-done | bytes 196640 | tf_op jit(solution)/shard_map/ppermute | solution.py:304
  105.0 5.1 %shard_map.92 = (bf16[128,1536]{1,0:T(8,128)(2,1)S(1)}, bf16[128,1536]{1,0:T(8,128)(2,1)S(1)}) custom-call(bf16[128,3072]{1,0:T(8,128)(2,1)S(1)} %shard_map.89.refs_4_.refs_0_, bf16[128,3072]{1,0:T(8,128)(2,1)S(1)} %collective-permute-done.12.refs_1_, bf16[6144,1536]{1,0:T(8,128)(2,1)} %refs_2_.13, f32[128,1536]{1,0:T(8,128)S(1)} %get-tuple-element.23.refs_4_.refs_3_, ...), custom_call_target="tpu_custom_call" | custom-call | tf_op jit(solution)/shard_map/pallas_call | solution.py:63
  113.1 13.0 %collective-permute-done.16.refs_1_ = bf16[80,6144]{1,0:T(8,128)(2,1)S(1)} collective-permute-done((bf16[80,6144]{1,0:T(8,128)(2,1)S(1)}, bf16[80,6144]{1,0:T(8,128)(2,1)S(1)}, u32[]{:S(2)}, u32[]{:S(2)}) %collective-permute-start.16) | collective-permute-done | bytes 983072 | tf_op jit(solution)/shard_map/ppermute | solution.py:304
  126.1 1.7 shard_map.94.refs_0_
  128.5 1.9 %collective-permute-done.17.refs_1_ = bf16[80,6144]{1,0:T(8,128)(2,1)S(1)} collective-permute-done((bf16[80,6144]{1,0:T(8,128)(2,1)S(1)}, bf16[80,6144]{1,0:T(8,128)(2,1)S(1)}, u32[]{:S(2)}, u32[]{:S(2)}) %collective-permute-start.17) | collective-permute-done | bytes 983072 | tf_op jit(solution)/shard_map/ppermute | solution.py:298
  130.5 7.4 %shard_map.95 = (bf16[80,1536]{1,0:T(8,128)(2,1)S(1)}, bf16[80,1536]{1,0:T(8,128)(2,1)S(1)}) custom-call(bf16[80,6144]{1,0:T(8,128)(2,1)S(1)} %shard_map.94.refs_0_, bf16[80,6144]{1,0:T(8,128)(2,1)S(1)} %collective-permute-done.17.refs_1_, bf16[6144,1536]{1,0:T(8,128)(2,1)} %refs_2_.13, bf16[80,128]{1,0:T(8,128)(2,1)S(1)} %slice.124.refs_3_, ...), custom_call_target="tpu_custom_call" | custom-call | tf_op jit(solution)/shard_map/pallas_call | solution.py:63
  141.2 2.4 %collective-permute-done.19.refs_1_ = bf16[48,6144]{1,0:T(8,128)(2,1)S(1)} collective-permute-done((bf16[48,6144]{1,0:T(8,128)(2,1)S(1)}, bf16[48,6144]{1,0:T(8,128)(2,1)S(1)}, u32[]{:S(2)}, u32[]{:S(2)}) %collective-permute-start.19) | collective-permute-done | bytes 589856 | tf_op jit(solution)/shard_map/ppermute | solution.py:304
  145.4 1.8 %collective-permute-done.20.refs_1_ = bf16[48,6144]{1,0:T(8,128)(2,1)S(1)} collective-permute-done((bf16[48,6144]{1,0:T(8,128)(2,1)S(1)}, bf16[48,6144]{1,0:T(8,128)(2,1)S(1)}, u32[]{:S(2)}, u32[]{:S(2)}) %collective-permute-start.20) | collective-permute-done | bytes 589856 | tf_op jit(solution)/shard_map/ppermute | solution.py:298
  147.2 7.4 %shard_map.98 = (bf16[48,1536]{1,0:T(8,128)(2,1)S(1)}, bf16[48,1536]{1,0:T(8,128)(2,1)S(1)}) custom-call(bf16[48,6144]{1,0:T(8,128)(2,1)S(1)} %shard_map.97.refs_0_, bf16[48,6144]{1,0:T(8,128)(2,1)S(1)} %collective-permute-done.20.refs_1_, bf16[6144,1536]{1,0:T(8,128)(2,1)} %refs_2_.13, bf16[48,128]{1,0:T(8,128)(2,1)S(1)} %slice.126.refs_3_, ...), custom_call_target="tpu_custom_call" | custom-call | tf_op jit(solution)/shard_map/pallas_call | solution.py:63
  156.1 1.9 %collective-permute-start.22 = (bf16[48,768]{1,0:T(8,128)(2,1)S(1)}, bf16[48,768]{1,0:T(8,128)(2,1)S(1)}, u32[]{:S(2)}, u32[]{:S(2)}) collective-permute-start(bf16[48,768]{1,0:T(8,128)(2,1)S(1)} %get-tuple-element.41), channel_id=1, source_target_pairs={{0,12},{4,8},{8,4},{12,0},{1,13},{5,9},{9,5},{13,1},{2,14},{6,10},... | collective-permute-start | bytes 221192 | tf_op jit(solution)/shard_map/ppermute | solution.py:321
  157.9 2.6 %collective-permute-start.24 = (bf16[48,768]{1,0:T(8,128)(2,1)S(1)}, bf16[48,768]{1,0:T(8,128)(2,1)S(1)}, u32[]{:S(2)}, u32[]{:S(2)}) collective-permute-start(bf16[48,768]{1,0:T(8,128)(2,1)S(1)} %get-tuple-element.42), channel_id=1, source_target_pairs={{0,4},{4,0},{8,12},{12,8},{1,5},{5,1},{9,13},{13,9},{2,6},{6,2},{1... | collective-permute-start | bytes 221192 | tf_op jit(solution)/shard_map/ppermute | solution.py:321
  160.6 3.6 %collective-permute-done.22 = bf16[48,768]{1,0:T(8,128)(2,1)S(1)} collective-permute-done((bf16[48,768]{1,0:T(8,128)(2,1)S(1)}, bf16[48,768]{1,0:T(8,128)(2,1)S(1)}, u32[]{:S(2)}, u32[]{:S(2)}) %collective-permute-start.22) | collective-permute-done | bytes 73760 | tf_op jit(solution)/shard_map/ppermute | solution.py:321
  164.1 3.9 %collective-permute-done.23 = bf16[48,768]{1,0:T(8,128)(2,1)S(1)} collective-permute-done((bf16[48,768]{1,0:T(8,128)(2,1)S(1)}, bf16[48,768]{1,0:T(8,128)(2,1)S(1)}, u32[]{:S(2)}, u32[]{:S(2)}) %collective-permute-start.23) | collective-permute-done | bytes 73760 | tf_op jit(solution)/shard_map/ppermute | solution.py:321
  (112 shorter events, 33.5 us)
Async XLA Ops:
  6.5 132.9 %reduce-scatter.3.cloned.1.call-start = ((), (), s32[]{:S(2)}) async-start(), calls=%async_computation.2 | async-start | bytes 983040 | tf_op jit(solution)/shard_map/reduce_scatter | solution.py:390
  30.4 3.6 %collective-permute-start = (f32[2,128]{1,0:T(2,128)S(1)}, f32[2,128]{1,0:T(2,128)S(1)}, u32[]{:S(2)}, u32[]{:S(2)}) collective-permute-start(f32[2,128]{1,0:T(2,128)S(1)} %pad_maximum_fusion.6), channel_id=1, source_target_pairs={{0,2},{2,0},{1,3},{3,1},{4,6},{6,4},{5,7},{7,5},{8,10},{10,8},{9,1... | collective-permute-start | bytes 3080 | tf_op jit(solution)/shard_map/ppermute | solution.py:304
  34.4 1.8 %collective-permute-start.1 = (bf16[128,1536]{1,0:T(8,128)(2,1)S(1)}, bf16[128,1536]{1,0:T(8,128)(2,1)S(1)}, u32[]{:S(2)}, u32[]{:S(2)}) collective-permute-start(bf16[128,1536]{1,0:T(8,128)(2,1)S(1)} %get-tuple-element.39), channel_id=1, source_target_pairs={{0,1},{1,0},{2,3},{3,2},{4,5},{5,4},{6,7},{7,6},{8,9},{9,8},{10,11... | collective-permute-start | bytes 1179656 | tf_op jit(solution)/shard_map/ppermute | solution.py:298
  41.7 2.4 %collective-permute-start.2 = (bf16[128,3072]{1,0:T(8,128)(2,1)S(1)}, bf16[128,3072]{1,0:T(8,128)(2,1)S(1)}, u32[]{:S(2)}, u32[]{:S(2)}) collective-permute-start(bf16[128,3072]{1,0:T(8,128)(2,1)S(1)} %slice.157), channel_id=1, source_target_pairs={{0,1},{1,0},{2,3},{3,2},{4,5},{5,4},{6,7},{7,6},{8,9},{9,8},{10,11... | collective-permute-start | bytes 2359304 | tf_op jit(solution)/shard_map/ppermute | solution.py:298
  44.7 24.2 %collective-permute-start.5 = (bf16[128,3072]{1,0:T(8,128)(2,1)S(1)}, bf16[128,3072]{1,0:T(8,128)(2,1)S(1)}, u32[]{:S(2)}, u32[]{:S(2)}) collective-permute-start(bf16[128,3072]{1,0:T(8,128)(2,1)S(1)} %fusion.9.refs_0_), channel_id=1, source_target_pairs={{0,2},{2,0},{1,3},{3,1},{4,6},{6,4},{5,7},{7,5},{8,10},{10,8},{9,1... | collective-permute-start | bytes 2359304 | tf_op jit(solution)/shard_map/ppermute | solution.py:304
  68.9 3.5 %collective-permute-start.3 = (bf16[128,3072]{1,0:T(8,128)(2,1)S(1)}, bf16[128,3072]{1,0:T(8,128)(2,1)S(1)}, u32[]{:S(2)}, u32[]{:S(2)}) collective-permute-start(bf16[128,3072]{1,0:T(8,128)(2,1)S(1)} %slice.156.refs_2_), channel_id=1, source_target_pairs={{0,1},{1,0},{2,3},{3,2},{4,5},{5,4},{6,7},{7,6},{8,9},{9,8},{10,11... | collective-permute-start | bytes 2359304 | tf_op jit(solution)/shard_map/ppermute | solution.py:298
  70.2 7.4 %collective-permute-start.8 = (bf16[128,3072]{1,0:T(8,128)(2,1)S(1)}, bf16[128,3072]{1,0:T(8,128)(2,1)S(1)}, u32[]{:S(2)}, u32[]{:S(2)}) collective-permute-start(bf16[128,3072]{1,0:T(8,128)(2,1)S(1)} %shard_map.82.refs_0_), channel_id=1, source_target_pairs={{0,1},{1,0},{2,3},{3,2},{4,5},{5,4},{6,7},{7,6},{8,9},{9,8},{10,11... | collective-permute-start | bytes 2359304 | tf_op jit(solution)/shard_map/ppermute | solution.py:298
  71.7 3.6 %collective-permute-start.6 = (f32[2,128]{1,0:T(2,128)S(1)}, f32[2,128]{1,0:T(2,128)S(1)}, u32[]{:S(2)}, u32[]{:S(2)}) collective-permute-start(f32[2,128]{1,0:T(2,128)S(1)} %pad_maximum_fusion.7), channel_id=1, source_target_pairs={{0,2},{2,0},{1,3},{3,1},{4,6},{6,4},{5,7},{7,5},{8,10},{10,8},{9,1... | collective-permute-start | bytes 3080 | tf_op jit(solution)/shard_map/ppermute | solution.py:304
  75.8 1.8 %collective-permute-start.7 = (bf16[128,1536]{1,0:T(8,128)(2,1)S(1)}, bf16[128,1536]{1,0:T(8,128)(2,1)S(1)}, u32[]{:S(2)}, u32[]{:S(2)}) collective-permute-start(bf16[128,1536]{1,0:T(8,128)(2,1)S(1)} %get-tuple-element.37), channel_id=1, source_target_pairs={{0,1},{1,0},{2,3},{3,2},{4,5},{5,4},{6,7},{7,6},{8,9},{9,8},{10,11... | collective-permute-start | bytes 1179656 | tf_op jit(solution)/shard_map/ppermute | solution.py:298
  75.9 25.0 %collective-permute-start.4 = (bf16[128,3072]{1,0:T(8,128)(2,1)S(1)}, bf16[128,3072]{1,0:T(8,128)(2,1)S(1)}, u32[]{:S(2)}, u32[]{:S(2)}) collective-permute-start(bf16[128,3072]{1,0:T(8,128)(2,1)S(1)} %fusion.8.refs_4_.refs_0_), channel_id=1, source_target_pairs={{0,2},{2,0},{1,3},{3,1},{4,6},{6,4},{5,7},{7,5},{8,10},{10,8},{9,1... | collective-permute-start | bytes 2359304 | tf_op jit(solution)/shard_map/ppermute | solution.py:304
  79.1 6.3 %collective-permute-start.9 = (bf16[256,384]{1,0:T(8,128)(2,1)S(1)}, bf16[256,384]{1,0:T(8,128)(2,1)S(1)}, u32[]{:S(2)}, u32[]{:S(2)}) collective-permute-start(bf16[256,384]{1,0:T(8,128)(2,1)S(1)} %get-tuple-element.20), channel_id=1, source_target_pairs={{0,1},{1,0},{2,3},{3,2},{4,5},{5,4},{6,7},{7,6},{8,9},{9,8},{10,11... | collective-permute-start | bytes 589832 | tf_op jit(solution)/shard_map/ppermute | solution.py:298
  89.2 10.8 %collective-permute-start.11 = (bf16[128,2048]{1,0:T(8,128)(2,1)S(1)}, bf16[128,2048]{1,0:T(8,128)(2,1)S(1)}, u32[]{:S(2)}, u32[]{:S(2)}) collective-permute-start(bf16[128,2048]{1,0:T(8,128)(2,1)S(1)} %get-tuple-element.24), channel_id=1, source_target_pairs={{0,1},{1,0},{2,3},{3,2},{4,5},{5,4},{6,7},{7,6},{8,9},{9,8},{10,11... | collective-permute-start | bytes 1572872 | tf_op jit(solution)/shard_map/ppermute | solution.py:298
  89.6 12.1 %collective-permute-start.14 = (bf16[128,4096]{1,0:T(8,128)(2,1)S(1)}, bf16[128,4096]{1,0:T(8,128)(2,1)S(1)}, u32[]{:S(2)}, u32[]{:S(2)}) collective-permute-start(bf16[128,4096]{1,0:T(8,128)(2,1)S(1)} %get-tuple-element.26), channel_id=1, source_target_pairs={{0,1},{1,0},{2,3},{3,2},{4,5},{5,4},{6,7},{7,6},{8,9},{9,8},{10,11... | collective-permute-start | bytes 3145736 | tf_op jit(solution)/shard_map/ppermute | solution.py:298
  89.8 10.3 %collective-permute-start.10 = (bf16[256,384]{1,0:T(8,128)(2,1)S(1)}, bf16[256,384]{1,0:T(8,128)(2,1)S(1)}, u32[]{:S(2)}, u32[]{:S(2)}) collective-permute-start(bf16[256,384]{1,0:T(8,128)(2,1)S(1)} %shard_map.84.refs_4_.refs_0_), channel_id=1, source_target_pairs={{0,2},{2,0},{1,3},{3,1},{4,6},{6,4},{5,7},{7,5},{8,10},{10,8},{9,1... | collective-permute-start | bytes 589832 | tf_op jit(solution)/shard_map/ppermute | solution.py:304
  101.6 2.6 %collective-permute-start.12 = (bf16[128,3072]{1,0:T(8,128)(2,1)S(1)}, bf16[128,3072]{1,0:T(8,128)(2,1)S(1)}, u32[]{:S(2)}, u32[]{:S(2)}) collective-permute-start(bf16[128,3072]{1,0:T(8,128)(2,1)S(1)} %shard_map.89.refs_4_.refs_0_), channel_id=1, source_target_pairs={{0,1},{1,0},{2,3},{3,2},{4,5},{5,4},{6,7},{7,6},{8,9},{9,8},{10,11... | collective-permute-start | bytes 2359304 | tf_op jit(solution)/shard_map/ppermute | solution.py:298
  101.9 24.2 %collective-permute-start.16 = (bf16[80,6144]{1,0:T(8,128)(2,1)S(1)}, bf16[80,6144]{1,0:T(8,128)(2,1)S(1)}, u32[]{:S(2)}, u32[]{:S(2)}) collective-permute-start(bf16[80,6144]{1,0:T(8,128)(2,1)S(1)} %shard_map.90.refs_4_.refs_0_), channel_id=1, source_target_pairs={{0,2},{2,0},{1,3},{3,1},{4,6},{6,4},{5,7},{7,5},{8,10},{10,8},{9,1... | collective-permute-start | bytes 2949128 | tf_op jit(solution)/shard_map/ppermute | solution.py:304
  110.1 1.8 %collective-permute-start.15 = (bf16[128,1536]{1,0:T(8,128)(2,1)S(1)}, bf16[128,1536]{1,0:T(8,128)(2,1)S(1)}, u32[]{:S(2)}, u32[]{:S(2)}) collective-permute-start(bf16[128,1536]{1,0:T(8,128)(2,1)S(1)} %get-tuple-element.28), channel_id=1, source_target_pairs={{0,1},{1,0},{2,3},{3,2},{4,5},{5,4},{6,7},{7,6},{8,9},{9,8},{10,11... | collective-permute-start | bytes 1179656 | tf_op jit(solution)/shard_map/ppermute | solution.py:298
  112.9 55.2 %reduce-scatter.5.cloned.1.call-start = ((), (), s32[]{:S(2)}) async-start(), calls=%async_computation.3 | async-start | bytes 614400 | tf_op jit(solution)/shard_map/reduce_scatter | solution.py:390
  127.8 2.6 %collective-permute-start.17 = (bf16[80,6144]{1,0:T(8,128)(2,1)S(1)}, bf16[80,6144]{1,0:T(8,128)(2,1)S(1)}, u32[]{:S(2)}, u32[]{:S(2)}) collective-permute-start(bf16[80,6144]{1,0:T(8,128)(2,1)S(1)} %shard_map.94.refs_0_), channel_id=1, source_target_pairs={{0,1},{1,0},{2,3},{3,2},{4,5},{5,4},{6,7},{7,6},{8,9},{9,8},{10,11... | collective-permute-start | bytes 2949128 | tf_op jit(solution)/shard_map/ppermute | solution.py:298
  127.9 15.7 %collective-permute-start.19 = (bf16[48,6144]{1,0:T(8,128)(2,1)S(1)}, bf16[48,6144]{1,0:T(8,128)(2,1)S(1)}, u32[]{:S(2)}, u32[]{:S(2)}) collective-permute-start(bf16[48,6144]{1,0:T(8,128)(2,1)S(1)} %shard_map.91.refs_8_.refs_0_), channel_id=1, source_target_pairs={{0,2},{2,0},{1,3},{3,1},{4,6},{6,4},{5,7},{7,5},{8,10},{10,8},{9,1... | collective-permute-start | bytes 1769480 | tf_op jit(solution)/shard_map/ppermute | solution.py:304
  145.1 2.1 %collective-permute-start.20 = (bf16[48,6144]{1,0:T(8,128)(2,1)S(1)}, bf16[48,6144]{1,0:T(8,128)(2,1)S(1)}, u32[]{:S(2)}, u32[]{:S(2)}) collective-permute-start(bf16[48,6144]{1,0:T(8,128)(2,1)S(1)} %shard_map.97.refs_0_), channel_id=1, source_target_pairs={{0,1},{1,0},{2,3},{3,2},{4,5},{5,4},{6,7},{7,6},{8,9},{9,8},{10,11... | collective-permute-start | bytes 1769480 | tf_op jit(solution)/shard_map/ppermute | solution.py:298
  156.1 8.1 %collective-permute-start.22 = (bf16[48,768]{1,0:T(8,128)(2,1)S(1)}, bf16[48,768]{1,0:T(8,128)(2,1)S(1)}, u32[]{:S(2)}, u32[]{:S(2)}) collective-permute-start(bf16[48,768]{1,0:T(8,128)(2,1)S(1)} %get-tuple-element.41), channel_id=1, source_target_pairs={{0,12},{4,8},{8,4},{12,0},{1,13},{5,9},{9,5},{13,1},{2,14},{6,10},... | collective-permute-start | bytes 221192 | tf_op jit(solution)/shard_map/ppermute | solution.py:321
  157.9 10.1 %collective-permute-start.23 = (bf16[48,768]{1,0:T(8,128)(2,1)S(1)}, bf16[48,768]{1,0:T(8,128)(2,1)S(1)}, u32[]{:S(2)}, u32[]{:S(2)}) collective-permute-start(bf16[48,768]{1,0:T(8,128)(2,1)S(1)} %get-tuple-element.43), channel_id=1, source_target_pairs={{0,8},{4,12},{8,0},{12,4},{1,9},{5,13},{9,1},{13,5},{2,10},{6,14},... | collective-permute-start | bytes 221192 | tf_op jit(solution)/shard_map/ppermute | solution.py:321
  157.9 10.1 %collective-permute-start.24 = (bf16[48,768]{1,0:T(8,128)(2,1)S(1)}, bf16[48,768]{1,0:T(8,128)(2,1)S(1)}, u32[]{:S(2)}, u32[]{:S(2)}) collective-permute-start(bf16[48,768]{1,0:T(8,128)(2,1)S(1)} %get-tuple-element.42), channel_id=1, source_target_pairs={{0,4},{4,0},{8,12},{12,8},{1,5},{5,1},{9,13},{13,9},{2,6},{6,2},{1... | collective-permute-start | bytes 221192 | tf_op jit(solution)/shard_map/ppermute | solution.py:321
  (11 other events, 75.6 us)
Sparse Core Ops, SparseCore 0:
  113.0 22.4 reduce-scatter.2
  145.5 21.5 reduce-scatter.4

commit v14 on v12

--- a/solution.py
+++ b/solution.py
@@ -337,10 +337,13 @@
         lead = lax.all_gather(lead, "wide", axis=1, tiled=True)
         gain = lead[:1]
 
-        def normed(floats):
-            sums = jnp.stack([jnp.sum(floats, axis=1), jnp.sum(floats * floats, axis=1)])
-            sums = sum_red(sums)[:, :, None] / D
-            values = normalize(floats, sums[0], sums[1], gain).astype(BF16)
+        def row_sums(raw):
+            floats = raw.astype(F32)
+            return jnp.stack([jnp.sum(floats, axis=1), jnp.sum(floats * floats, axis=1)])
+
+        def normed(raw, sums, start=0.0):
+            sums = sum_red(sums)[:, :, None] / D + start
+            values = normalize(raw.astype(F32), sums[0], sums[1], gain).astype(BF16)
             mine = lax.dynamic_slice_in_dim(values, core * depth, depth, axis=1)
             theirs = lax.dynamic_slice_in_dim(values, (1 - core) * depth, depth, axis=1)
             return mine, swap(theirs)
@@ -353,17 +356,18 @@
             return (part[:half] + far).astype(BF16)
 
         weights = [w_up[:, piece] for piece in pieces]
-        lead_pair = normed(lead[GAIN_ROWS:].astype(F32))
+        lead_pair = normed(lead[GAIN_ROWS:], row_sums(lead[GAIN_ROWS:]))
         leads = [project(lead_pair, weights[0])]
         lead_parts = [all_red(leads[0])]
         arrived = gelu_sum(lead_parts[0])
 
         rest = tokens[first:] + nothing(leads[-1]).astype(BF16)
         rest = lax.all_gather(rest, "wide", axis=1, tiled=True)
-        later_pair = [a + nothing(rest).astype(BF16) for a in lead_pair]
+        sums = row_sums(rest)
+        later_pair = [a + nothing(sums).astype(BF16) for a in lead_pair]
         leads.append(project(later_pair, weights[1]))
         lead_parts.append(all_red(leads[1]))
-        rest_pair = normed(rest.astype(F32) + nothing(arrived))
+        rest_pair = normed(rest, sums, nothing(arrived))
         pair = [jnp.concatenate(p, axis=0) for p in zip(lead_pair, rest_pair)]
         arrived_other = swap(arrived)
         every = slice(0, qkv_rows.shape[1])

time: 176 us -> 174 us (0.989)
  transfers between devices with their start and end apart: 27 -> 27, of which waited for: 16 -> 16; matrix products, arithmetic and copies ran while one was open for 2% -> 3% of each run, Pallas kernels for 24% -> 24%
where the time goes in v14:
time: 174 us
  Pallas kernels  43.6 us (25%)
  waiting for transfers between devices  42.3 us (24%)
  blocking collectives  39.9 us (23%)
  between operations  15.4 us (9%)
  starting transfers between devices  15.2 us (9%)
  matrix products  7.91 us (5%)
  local copies, waits for them, and re-layouts  5.78 us (3%)
  other arithmetic  3.78 us (2%)
    pallas_call x17, Pallas kernels, call(): pl.pallas_call(body, in_specs=list(specs) + [corner_of(a) for a in earlie...  43.6 us
    all_gather x1, blocking collectives, body(): lead = lax.all_gather(lead, 'wide', axis=1, tiled=True)  21.9 us
    ppermute x7, waiting for transfers between devices, all_red(): parts.append(lax.ppermute(x, 'red', pairs))  18.9 us
    all_gather x1, blocking collectives, body(): rest = lax.all_gather(rest, 'wide', axis=1, tiled=True)  18 us
    ppermute x15, waiting for transfers between devices, swap(): return lax.ppermute(x, 'tok', [(0, 1), (1, 0)])  15.7 us
    dot_general x2, matrix products, project(): part = jnp.dot(both, weight, preferred_element_type=F32)  7.91 us
    ppermute x3, waiting for transfers between devices, collect(): total = total + lax.ppermute(block(chip ^ k), 'wide', pairs).astype(F32)  7.71 us
    ppermute x7, starting transfers between devices, all_red(): parts.append(lax.ppermute(x, 'red', pairs))  7.65 us
  transfers between devices with their start and end apart: 27, of which 16 were waited for; matrix products, arithmetic and copies ran while one was open for 3% of the time, Pallas kernels for 24%

profile of v14, /device:TPU:0, one launch (start us, length us, event | category | flops | bytes accessed | tf_op | source)
XLA Modules:
  0.0 173.8 jit_solution(3616087346169753198)
XLA Ops:
  8.2 21.9 %all_gather.6 = bf16[136,3072]{1,0:T(8,128)(2,1)S(1)} all-gather(bf16[136,768]{1,0:T(8,128)(2,1)S(1)} %pad_maximum_fusion.5), channel_id=1, replica_groups=mesh['grp'=2,'wide'=4,'red'=2,'tok'=2] {'wide'}, dimensions={1}, use_global_device_ids=true | all-gather | bytes 1044480 | tf_op jit(solution)/shard_map/all_gather | solution.py:337
  31.9 2.1 %collective-permute-done = f32[2,128]{1,0:T(2,128)S(1)} collective-permute-done((f32[2,128]{1,0:T(2,128)S(1)}, f32[2,128]{1,0:T(2,128)S(1)}, u32[]{:S(2)}, u32[]{:S(2)}) %collective-permute-start) | collective-permute-done | bytes 1056 | tf_op jit(solution)/shard_map/ppermute | solution.py:304
  34.5 1.7 collective-permute-done.1
  36.2 5.3 %fusion.2 = f32[256,3072]{1,0:T(8,128)S(1)} fusion(bf16[1536,6144]{1,0:T(8,128)(2,1)} %refs_2_.8, bf16[128,1536]{1,0:T(8,128)(2,1)S(1)} %get-tuple-element.40, bf16[128,1536]{1,0:T(8,128)(2,1)S(1)} %collective-permute-done.1), kind=kOutput, calls=%fused_computation.2 | convolution fusion | flops 2417491968 | bytes 13369344 | tf_op jit(solution)/shard_map/dot_general | solution.py:354
  41.9 2.1 %collective-permute-done.2 = bf16[128,3072]{1,0:T(8,128)(2,1)S(1)} collective-permute-done((bf16[128,3072]{1,0:T(8,128)(2,1)S(1)}, bf16[128,3072]{1,0:T(8,128)(2,1)S(1)}, u32[]{:S(2)}, u32[]{:S(2)}) %collective-permute-start.2) | collective-permute-done | bytes 786464 | tf_op jit(solution)/shard_map/ppermute | solution.py:298
  46.9 18.0 %all_gather.7 = bf16[128,3072]{1,0:T(8,128)(2,1)S(1)} all-gather(bf16[128,768]{1,0:T(8,128)(2,1)S(1)} %slice_add_fusion.2), channel_id=1, replica_groups=mesh['grp'=2,'wide'=4,'red'=2,'tok'=2] {'wide'}, dimensions={1}, use_global_device_ids=true | all-gather | bytes 983040 | tf_op jit(solution)/shard_map/all_gather | solution.py:365
  65.9 2.6 %fusion = f32[256,3072]{1,0:T(8,128)S(1)} fusion(bf16[1536,6144]{1,0:T(8,128)(2,1)S(1)} %copy-done.6, bf16[128,1536]{1,0:T(8,128)(2,1)S(1)} %get-tuple-element.44, bf16[128,1536]{1,0:T(8,128)(2,1)S(1)} %get-tuple-element.45), kind=kOutput, calls=%fused_computation | convolution fusion | flops 2417491968 | bytes 13369344 | tf_op jit(solution)/shard_map/dot_general | solution.py:354
  71.9 1.6 collective-permute-start.4
  76.1 6.1 %shard_map.85 = (bf16[128,4096]{1,0:T(8,128)(2,1)S(1)}, bf16[128,4096]{1,0:T(8,128)(2,1)S(1)}) custom-call(bf16[128,1536]{1,0:T(8,128)(2,1)S(1)} %get-tuple-element.38.refs_0_, bf16[128,1536]{1,0:T(8,128)(2,1)S(1)} %collective-permute-done.7.refs_1_, bf16[1536,6144]{1,0:T(8,128)(2,1)} %refs_2_.8, bf16[256,384]{1,0:T(8,128)(2,1)S(1)} %get-tuple-element.19.refs_0_.refs_3_), custom_call_target="tpu_custom_call" | custom-call | tf_op jit(solution)/shard_map/pallas_call | solution.py:63
  82.1 3.7 %shard_map.86 = (bf16[128,2048]{1,0:T(8,128)(2,1)S(1)}, bf16[128,2048]{1,0:T(8,128)(2,1)S(1)}) custom-call(bf16[128,1536]{1,0:T(8,128)(2,1)S(1)} %get-tuple-element.38.refs_0_, bf16[128,1536]{1,0:T(8,128)(2,1)S(1)} %collective-permute-done.7.refs_1_, bf16[1536,6144]{1,0:T(8,128)(2,1)} %refs_2_.8, bf16[128,4096]{1,0:T(8,128)(2,1)S(1)} %get-tuple-element.21.refs_3_.refs_0_), custom_call_target="tpu_custom_call" | custom-call | tf_op jit(solution)/shard_map/pallas_call | solution.py:63
  86.7 3.0 %collective-permute-done.9.refs_1_ = bf16[256,384]{1,0:T(8,128)(2,1)S(1)} collective-permute-done((bf16[256,384]{1,0:T(8,128)(2,1)S(1)}, bf16[256,384]{1,0:T(8,128)(2,1)S(1)}, u32[]{:S(2)}, u32[]{:S(2)}) %collective-permute-start.9) | collective-permute-done | bytes 196640 | tf_op jit(solution)/shard_map/ppermute | solution.py:298
  90.3 5.1 %shard_map.87 = (f32[128,1536]{1,0:T(8,128)S(1)}, f32[128,1536]{1,0:T(8,128)S(1)}) custom-call(bf16[128,3072]{1,0:T(8,128)(2,1)S(1)} %shard_map.82.refs_0_, bf16[128,3072]{1,0:T(8,128)(2,1)S(1)} %collective-permute-done.8.refs_3_.refs_1_, bf16[6144,1536]{1,0:T(8,128)(2,1)} %refs_2_.13, bf16[128,2048]{1,0:T(8,128)(2,1)S(1)} %get-tuple-element.22.refs_3_.refs_2_), custom_call_target="tpu_custom_call" | custom-call | tf_op jit(solution)/shard_map/pallas_call | solution.py:63
  101.8 5.1 %shard_map.92 = (bf16[128,1536]{1,0:T(8,128)(2,1)S(1)}, bf16[128,1536]{1,0:T(8,128)(2,1)S(1)}) custom-call(bf16[128,3072]{1,0:T(8,128)(2,1)S(1)} %shard_map.89.refs_4_.refs_0_, bf16[128,3072]{1,0:T(8,128)(2,1)S(1)} %collective-permute-done.12.refs_1_, bf16[6144,1536]{1,0:T(8,128)(2,1)} %refs_2_.13, f32[128,1536]{1,0:T(8,128)S(1)} %get-tuple-element.23.refs_4_.refs_3_, ...), custom_call_target="tpu_custom_call" | custom-call | tf_op jit(solution)/shard_map/pallas_call | solution.py:63
  109.9 13.0 %collective-permute-done.16.refs_1_ = bf16[80,6144]{1,0:T(8,128)(2,1)S(1)} collective-permute-done((bf16[80,6144]{1,0:T(8,128)(2,1)S(1)}, bf16[80,6144]{1,0:T(8,128)(2,1)S(1)}, u32[]{:S(2)}, u32[]{:S(2)}) %collective-permute-start.16) | collective-permute-done | bytes 983072 | tf_op jit(solution)/shard_map/ppermute | solution.py:304
  122.9 1.7 shard_map.94.refs_0_
  125.6 1.6 collective-permute-done.17.refs_1_
  127.2 7.4 %shard_map.95 = (bf16[80,1536]{1,0:T(8,128)(2,1)S(1)}, bf16[80,1536]{1,0:T(8,128)(2,1)S(1)}) custom-call(bf16[80,6144]{1,0:T(8,128)(2,1)S(1)} %shard_map.94.refs_0_, bf16[80,6144]{1,0:T(8,128)(2,1)S(1)} %collective-permute-done.17.refs_1_, bf16[6144,1536]{1,0:T(8,128)(2,1)} %refs_2_.13, bf16[80,128]{1,0:T(8,128)(2,1)S(1)} %slice.119.refs_3_, ...), custom_call_target="tpu_custom_call" | custom-call | tf_op jit(solution)/shard_map/pallas_call | solution.py:63
  138.0 2.4 %collective-permute-done.19.refs_1_ = bf16[48,6144]{1,0:T(8,128)(2,1)S(1)} collective-permute-done((bf16[48,6144]{1,0:T(8,128)(2,1)S(1)}, bf16[48,6144]{1,0:T(8,128)(2,1)S(1)}, u32[]{:S(2)}, u32[]{:S(2)}) %collective-permute-start.19) | collective-permute-done | bytes 589856 | tf_op jit(solution)/shard_map/ppermute | solution.py:304
  142.1 1.8 %collective-permute-done.20.refs_1_ = bf16[48,6144]{1,0:T(8,128)(2,1)S(1)} collective-permute-done((bf16[48,6144]{1,0:T(8,128)(2,1)S(1)}, bf16[48,6144]{1,0:T(8,128)(2,1)S(1)}, u32[]{:S(2)}, u32[]{:S(2)}) %collective-permute-start.20) | collective-permute-done | bytes 589856 | tf_op jit(solution)/shard_map/ppermute | solution.py:298
  143.9 7.4 %shard_map.98 = (bf16[48,1536]{1,0:T(8,128)(2,1)S(1)}, bf16[48,1536]{1,0:T(8,128)(2,1)S(1)}) custom-call(bf16[48,6144]{1,0:T(8,128)(2,1)S(1)} %shard_map.97.refs_0_, bf16[48,6144]{1,0:T(8,128)(2,1)S(1)} %collective-permute-done.20.refs_1_, bf16[6144,1536]{1,0:T(8,128)(2,1)} %refs_2_.13, bf16[48,128]{1,0:T(8,128)(2,1)S(1)} %slice.121.refs_3_, ...), custom_call_target="tpu_custom_call" | custom-call | tf_op jit(solution)/shard_map/pallas_call | solution.py:63
  152.8 1.9 %collective-permute-start.22 = (bf16[48,768]{1,0:T(8,128)(2,1)S(1)}, bf16[48,768]{1,0:T(8,128)(2,1)S(1)}, u32[]{:S(2)}, u32[]{:S(2)}) collective-permute-start(bf16[48,768]{1,0:T(8,128)(2,1)S(1)} %get-tuple-element.41), channel_id=1, source_target_pairs={{0,12},{4,8},{8,4},{12,0},{1,13},{5,9},{9,5},{13,1},{2,14},{6,10},... | collective-permute-start | bytes 221192 | tf_op jit(solution)/shard_map/ppermute | solution.py:321
  154.7 2.6 %collective-permute-start.24 = (bf16[48,768]{1,0:T(8,128)(2,1)S(1)}, bf16[48,768]{1,0:T(8,128)(2,1)S(1)}, u32[]{:S(2)}, u32[]{:S(2)}) collective-permute-start(bf16[48,768]{1,0:T(8,128)(2,1)S(1)} %get-tuple-element.42), channel_id=1, source_target_pairs={{0,4},{4,0},{8,12},{12,8},{1,5},{5,1},{9,13},{13,9},{2,6},{6,2},{1... | collective-permute-start | bytes 221192 | tf_op jit(solution)/shard_map/ppermute | solution.py:321
  157.3 3.3 %collective-permute-done.22 = bf16[48,768]{1,0:T(8,128)(2,1)S(1)} collective-permute-done((bf16[48,768]{1,0:T(8,128)(2,1)S(1)}, bf16[48,768]{1,0:T(8,128)(2,1)S(1)}, u32[]{:S(2)}, u32[]{:S(2)}) %collective-permute-start.22) | collective-permute-done | bytes 73760 | tf_op jit(solution)/shard_map/ppermute | solution.py:321
  160.6 4.4 %collective-permute-done.23 = bf16[48,768]{1,0:T(8,128)(2,1)S(1)} collective-permute-done((bf16[48,768]{1,0:T(8,128)(2,1)S(1)}, bf16[48,768]{1,0:T(8,128)(2,1)S(1)}, u32[]{:S(2)}, u32[]{:S(2)}) %collective-permute-start.23) | collective-permute-done | bytes 73760 | tf_op jit(solution)/shard_map/ppermute | solution.py:321
  (110 shorter events, 32.7 us)
Async XLA Ops:
  6.5 129.7 %reduce-scatter.3.cloned.1.call-start = ((), (), s32[]{:S(2)}) async-start(), calls=%async_computation.2 | async-start | bytes 983040 | tf_op jit(solution)/shard_map/reduce_scatter | solution.py:393
  30.4 3.6 %collective-permute-start = (f32[2,128]{1,0:T(2,128)S(1)}, f32[2,128]{1,0:T(2,128)S(1)}, u32[]{:S(2)}, u32[]{:S(2)}) collective-permute-start(f32[2,128]{1,0:T(2,128)S(1)} %pad_maximum_fusion.6), channel_id=1, source_target_pairs={{0,2},{2,0},{1,3},{3,1},{4,6},{6,4},{5,7},{7,5},{8,10},{10,8},{9,1... | collective-permute-start | bytes 3080 | tf_op jit(solution)/shard_map/ppermute | solution.py:304
  34.4 1.8 %collective-permute-start.1 = (bf16[128,1536]{1,0:T(8,128)(2,1)S(1)}, bf16[128,1536]{1,0:T(8,128)(2,1)S(1)}, u32[]{:S(2)}, u32[]{:S(2)}) collective-permute-start(bf16[128,1536]{1,0:T(8,128)(2,1)S(1)} %get-tuple-element.39), channel_id=1, source_target_pairs={{0,1},{1,0},{2,3},{3,2},{4,5},{5,4},{6,7},{7,6},{8,9},{9,8},{10,11... | collective-permute-start | bytes 1179656 | tf_op jit(solution)/shard_map/ppermute | solution.py:298
  41.7 2.4 %collective-permute-start.2 = (bf16[128,3072]{1,0:T(8,128)(2,1)S(1)}, bf16[128,3072]{1,0:T(8,128)(2,1)S(1)}, u32[]{:S(2)}, u32[]{:S(2)}) collective-permute-start(bf16[128,3072]{1,0:T(8,128)(2,1)S(1)} %slice.152), channel_id=1, source_target_pairs={{0,1},{1,0},{2,3},{3,2},{4,5},{5,4},{6,7},{7,6},{8,9},{9,8},{10,11... | collective-permute-start | bytes 2359304 | tf_op jit(solution)/shard_map/ppermute | solution.py:298
  44.7 24.0 %collective-permute-start.6 = (bf16[128,3072]{1,0:T(8,128)(2,1)S(1)}, bf16[128,3072]{1,0:T(8,128)(2,1)S(1)}, u32[]{:S(2)}, u32[]{:S(2)}) collective-permute-start(bf16[128,3072]{1,0:T(8,128)(2,1)S(1)} %fusion.13.refs_0_), channel_id=1, source_target_pairs={{0,2},{2,0},{1,3},{3,1},{4,6},{6,4},{5,7},{7,5},{8,10},{10,8},{9,1... | collective-permute-start | bytes 2359304 | tf_op jit(solution)/shard_map/ppermute | solution.py:304
  65.3 5.4 %collective-permute-start.5 = (f32[2,128]{1,0:T(2,128)S(1)}, f32[2,128]{1,0:T(2,128)S(1)}, u32[]{:S(2)}, u32[]{:S(2)}) collective-permute-start(f32[2,128]{1,0:T(2,128)S(1)} %pad_maximum_fusion.7), channel_id=1, source_target_pairs={{0,2},{2,0},{1,3},{3,1},{4,6},{6,4},{5,7},{7,5},{8,10},{10,8},{9,1... | collective-permute-start | bytes 3080 | tf_op jit(solution)/shard_map/ppermute | solution.py:304
  68.6 3.1 %collective-permute-start.3 = (bf16[128,3072]{1,0:T(8,128)(2,1)S(1)}, bf16[128,3072]{1,0:T(8,128)(2,1)S(1)}, u32[]{:S(2)}, u32[]{:S(2)}) collective-permute-start(bf16[128,3072]{1,0:T(8,128)(2,1)S(1)} %slice.151), channel_id=1, source_target_pairs={{0,1},{1,0},{2,3},{3,2},{4,5},{5,4},{6,7},{7,6},{8,9},{9,8},{10,11... | collective-permute-start | bytes 2359304 | tf_op jit(solution)/shard_map/ppermute | solution.py:298
  70.7 3.1 %collective-permute-start.8 = (bf16[128,3072]{1,0:T(8,128)(2,1)S(1)}, bf16[128,3072]{1,0:T(8,128)(2,1)S(1)}, u32[]{:S(2)}, u32[]{:S(2)}) collective-permute-start(bf16[128,3072]{1,0:T(8,128)(2,1)S(1)} %shard_map.82.refs_0_), channel_id=1, source_target_pairs={{0,1},{1,0},{2,3},{3,2},{4,5},{5,4},{6,7},{7,6},{8,9},{9,8},{10,11... | collective-permute-start | bytes 2359304 | tf_op jit(solution)/shard_map/ppermute | solution.py:298
  71.6 2.1 %collective-permute-start.7 = (bf16[128,1536]{1,0:T(8,128)(2,1)S(1)}, bf16[128,1536]{1,0:T(8,128)(2,1)S(1)}, u32[]{:S(2)}, u32[]{:S(2)}) collective-permute-start(bf16[128,1536]{1,0:T(8,128)(2,1)S(1)} %get-tuple-element.37), channel_id=1, source_target_pairs={{0,1},{1,0},{2,3},{3,2},{4,5},{5,4},{6,7},{7,6},{8,9},{9,8},{10,11... | collective-permute-start | bytes 1179656 | tf_op jit(solution)/shard_map/ppermute | solution.py:298
  71.9 25.7 %collective-permute-start.4 = (bf16[128,3072]{1,0:T(8,128)(2,1)S(1)}, bf16[128,3072]{1,0:T(8,128)(2,1)S(1)}, u32[]{:S(2)}, u32[]{:S(2)}) collective-permute-start(bf16[128,3072]{1,0:T(8,128)(2,1)S(1)} %fusion.12.refs_4_.refs_0_), channel_id=1, source_target_pairs={{0,2},{2,0},{1,3},{3,1},{4,6},{6,4},{5,7},{7,5},{8,10},{10,8},{9,1... | collective-permute-start | bytes 2359304 | tf_op jit(solution)/shard_map/ppermute | solution.py:304
  85.9 10.9 %collective-permute-start.11 = (bf16[128,2048]{1,0:T(8,128)(2,1)S(1)}, bf16[128,2048]{1,0:T(8,128)(2,1)S(1)}, u32[]{:S(2)}, u32[]{:S(2)}) collective-permute-start(bf16[128,2048]{1,0:T(8,128)(2,1)S(1)} %get-tuple-element.24), channel_id=1, source_target_pairs={{0,1},{1,0},{2,3},{3,2},{4,5},{5,4},{6,7},{7,6},{8,9},{9,8},{10,11... | collective-permute-start | bytes 1572872 | tf_op jit(solution)/shard_map/ppermute | solution.py:298
  86.2 12.2 %collective-permute-start.14 = (bf16[128,4096]{1,0:T(8,128)(2,1)S(1)}, bf16[128,4096]{1,0:T(8,128)(2,1)S(1)}, u32[]{:S(2)}, u32[]{:S(2)}) collective-permute-start(bf16[128,4096]{1,0:T(8,128)(2,1)S(1)} %get-tuple-element.26), channel_id=1, source_target_pairs={{0,1},{1,0},{2,3},{3,2},{4,5},{5,4},{6,7},{7,6},{8,9},{9,8},{10,11... | collective-permute-start | bytes 3145736 | tf_op jit(solution)/shard_map/ppermute | solution.py:298
  86.5 3.2 %collective-permute-start.9 = (bf16[256,384]{1,0:T(8,128)(2,1)S(1)}, bf16[256,384]{1,0:T(8,128)(2,1)S(1)}, u32[]{:S(2)}, u32[]{:S(2)}) collective-permute-start(bf16[256,384]{1,0:T(8,128)(2,1)S(1)} %get-tuple-element.20), channel_id=1, source_target_pairs={{0,1},{1,0},{2,3},{3,2},{4,5},{5,4},{6,7},{7,6},{8,9},{9,8},{10,11... | collective-permute-start | bytes 589832 | tf_op jit(solution)/shard_map/ppermute | solution.py:298
  89.7 7.1 %collective-permute-start.10 = (bf16[256,384]{1,0:T(8,128)(2,1)S(1)}, bf16[256,384]{1,0:T(8,128)(2,1)S(1)}, u32[]{:S(2)}, u32[]{:S(2)}) collective-permute-start(bf16[256,384]{1,0:T(8,128)(2,1)S(1)} %shard_map.84.refs_0_), channel_id=1, source_target_pairs={{0,2},{2,0},{1,3},{3,1},{4,6},{6,4},{5,7},{7,5},{8,10},{10,8},{9,1... | collective-permute-start | bytes 589832 | tf_op jit(solution)/shard_map/ppermute | solution.py:304
  98.3 2.6 %collective-permute-start.12 = (bf16[128,3072]{1,0:T(8,128)(2,1)S(1)}, bf16[128,3072]{1,0:T(8,128)(2,1)S(1)}, u32[]{:S(2)}, u32[]{:S(2)}) collective-permute-start(bf16[128,3072]{1,0:T(8,128)(2,1)S(1)} %shard_map.89.refs_4_.refs_0_), channel_id=1, source_target_pairs={{0,1},{1,0},{2,3},{3,2},{4,5},{5,4},{6,7},{7,6},{8,9},{9,8},{10,11... | collective-permute-start | bytes 2359304 | tf_op jit(solution)/shard_map/ppermute | solution.py:298
  98.6 24.2 %collective-permute-start.16 = (bf16[80,6144]{1,0:T(8,128)(2,1)S(1)}, bf16[80,6144]{1,0:T(8,128)(2,1)S(1)}, u32[]{:S(2)}, u32[]{:S(2)}) collective-permute-start(bf16[80,6144]{1,0:T(8,128)(2,1)S(1)} %shard_map.90.refs_4_.refs_0_), channel_id=1, source_target_pairs={{0,2},{2,0},{1,3},{3,1},{4,6},{6,4},{5,7},{7,5},{8,10},{10,8},{9,1... | collective-permute-start | bytes 2949128 | tf_op jit(solution)/shard_map/ppermute | solution.py:304
  106.9 1.8 %collective-permute-start.15 = (bf16[128,1536]{1,0:T(8,128)(2,1)S(1)}, bf16[128,1536]{1,0:T(8,128)(2,1)S(1)}, u32[]{:S(2)}, u32[]{:S(2)}) collective-permute-start(bf16[128,1536]{1,0:T(8,128)(2,1)S(1)} %get-tuple-element.28), channel_id=1, source_target_pairs={{0,1},{1,0},{2,3},{3,2},{4,5},{5,4},{6,7},{7,6},{8,9},{9,8},{10,11... | collective-permute-start | bytes 1179656 | tf_op jit(solution)/shard_map/ppermute | solution.py:298
  109.6 55.5 %reduce-scatter.5.cloned.1.call-start = ((), (), s32[]{:S(2)}) async-start(), calls=%async_computation.3 | async-start | bytes 614400 | tf_op jit(solution)/shard_map/reduce_scatter | solution.py:393
  124.6 2.6 %collective-permute-start.17 = (bf16[80,6144]{1,0:T(8,128)(2,1)S(1)}, bf16[80,6144]{1,0:T(8,128)(2,1)S(1)}, u32[]{:S(2)}, u32[]{:S(2)}) collective-permute-start(bf16[80,6144]{1,0:T(8,128)(2,1)S(1)} %shard_map.94.refs_0_), channel_id=1, source_target_pairs={{0,1},{1,0},{2,3},{3,2},{4,5},{5,4},{6,7},{7,6},{8,9},{9,8},{10,11... | collective-permute-start | bytes 2949128 | tf_op jit(solution)/shard_map/ppermute | solution.py:298
  124.7 15.7 %collective-permute-start.19 = (bf16[48,6144]{1,0:T(8,128)(2,1)S(1)}, bf16[48,6144]{1,0:T(8,128)(2,1)S(1)}, u32[]{:S(2)}, u32[]{:S(2)}) collective-permute-start(bf16[48,6144]{1,0:T(8,128)(2,1)S(1)} %shard_map.91.refs_8_.refs_0_), channel_id=1, source_target_pairs={{0,2},{2,0},{1,3},{3,1},{4,6},{6,4},{5,7},{7,5},{8,10},{10,8},{9,1... | collective-permute-start | bytes 1769480 | tf_op jit(solution)/shard_map/ppermute | solution.py:304
  141.9 2.1 %collective-permute-start.20 = (bf16[48,6144]{1,0:T(8,128)(2,1)S(1)}, bf16[48,6144]{1,0:T(8,128)(2,1)S(1)}, u32[]{:S(2)}, u32[]{:S(2)}) collective-permute-start(bf16[48,6144]{1,0:T(8,128)(2,1)S(1)} %shard_map.97.refs_0_), channel_id=1, source_target_pairs={{0,1},{1,0},{2,3},{3,2},{4,5},{5,4},{6,7},{7,6},{8,9},{9,8},{10,11... | collective-permute-start | bytes 1769480 | tf_op jit(solution)/shard_map/ppermute | solution.py:298
  152.8 7.8 %collective-permute-start.22 = (bf16[48,768]{1,0:T(8,128)(2,1)S(1)}, bf16[48,768]{1,0:T(8,128)(2,1)S(1)}, u32[]{:S(2)}, u32[]{:S(2)}) collective-permute-start(bf16[48,768]{1,0:T(8,128)(2,1)S(1)} %get-tuple-element.41), channel_id=1, source_target_pairs={{0,12},{4,8},{8,4},{12,0},{1,13},{5,9},{9,5},{13,1},{2,14},{6,10},... | collective-permute-start | bytes 221192 | tf_op jit(solution)/shard_map/ppermute | solution.py:321
  154.7 10.4 %collective-permute-start.23 = (bf16[48,768]{1,0:T(8,128)(2,1)S(1)}, bf16[48,768]{1,0:T(8,128)(2,1)S(1)}, u32[]{:S(2)}, u32[]{:S(2)}) collective-permute-start(bf16[48,768]{1,0:T(8,128)(2,1)S(1)} %get-tuple-element.43), channel_id=1, source_target_pairs={{0,8},{4,12},{8,0},{12,4},{1,9},{5,13},{9,1},{13,5},{2,10},{6,14},... | collective-permute-start | bytes 221192 | tf_op jit(solution)/shard_map/ppermute | solution.py:321
  154.7 10.4 %collective-permute-start.24 = (bf16[48,768]{1,0:T(8,128)(2,1)S(1)}, bf16[48,768]{1,0:T(8,128)(2,1)S(1)}, u32[]{:S(2)}, u32[]{:S(2)}) collective-permute-start(bf16[48,768]{1,0:T(8,128)(2,1)S(1)} %get-tuple-element.42), channel_id=1, source_target_pairs={{0,4},{4,0},{8,12},{12,8},{1,5},{5,1},{9,13},{13,9},{2,6},{6,2},{1... | collective-permute-start | bytes 221192 | tf_op jit(solution)/shard_map/ppermute | solution.py:321
  (11 other events, 70.4 us)
Sparse Core Ops, SparseCore 0:
  109.8 22.4 reduce-scatter.2
  142.2 21.8 reduce-scatter.4

commit v15 on v14

--- a/solution.py
+++ b/solution.py
@@ -11,7 +11,7 @@
 D = 6144
 PATCHES = 256
 EPS = 1e-06
-SHARES = (8, 5, 3)
+SHARES = (8, 3, 5)
 LEAD_PIECES = (1, 1)
 REST_PIECES = (2, 1)
 AHEAD = 4

time: 174 us -> 182 us (1.046)
  waiting for transfers between devices: 42.3 us -> 49.3 us
    ppermute x7, waiting for transfers between devices: 18.9 us -> 24.7 us  [all_red(): parts.append(lax.ppermute(x, 'red', pairs))]
    reduce_scatter x2, waiting for transfers between devices: 0.02 us -> 4.75 us  [scatter(): lax.psum_scatter(full, 'wide', scatter_dimension=1, tiled=True)]
    ppermute x3, waiting for transfers between devices: 7.71 us -> 3.91 us  [collect(): total = total + lax.ppermute(block(chip ^ k), 'wide', pairs).astype(F32)]
  transfers between devices with their start and end apart: 27 -> 27, of which waited for: 16 -> 16; matrix products, arithmetic and copies ran while one was open for 3% -> 3% of each run, Pallas kernels for 24% -> 20%
where the time goes in v15:
time: 182 us; the launch traced here: 181 us
  waiting for transfers between devices  49.3 us (27%)
  Pallas kernels  43.5 us (24%)
  blocking collectives  39.9 us (22%)
  starting transfers between devices  15.6 us (9%)
  between operations  15.4 us (8%)
  matrix products  7.91 us (4%)
  local copies, waits for them, and re-layouts  5.75 us (3%)
  other arithmetic  3.83 us (2%)
    pallas_call x17, Pallas kernels, call(): pl.pallas_call(body, in_specs=list(specs) + [corner_of(a) for a in earlie...  43.5 us
    ppermute x7, waiting for transfers between devices, all_red(): parts.append(lax.ppermute(x, 'red', pairs))  24.7 us
    all_gather x1, blocking collectives, body(): lead = lax.all_gather(lead, 'wide', axis=1, tiled=True)  21.9 us
    all_gather x1, blocking collectives, body(): rest = lax.all_gather(rest, 'wide', axis=1, tiled=True)  18 us
    ppermute x15, waiting for transfers between devices, swap(): return lax.ppermute(x, 'tok', [(0, 1), (1, 0)])  15.9 us
    dot_general x2, matrix products, project(): part = jnp.dot(both, weight, preferred_element_type=F32)  7.91 us
    ppermute x7, starting transfers between devices, all_red(): parts.append(lax.ppermute(x, 'red', pairs))  7.91 us
    reduce_scatter x2, waiting for transfers between devices, scatter(): lax.psum_scatter(full, 'wide', scatter_dimension=1, tiled=True)  4.75 us
  transfers between devices with their start and end apart: 27, of which 16 were waited for; matrix products, arithmetic and copies ran while one was open for 3% of the time, Pallas kernels for 20%

profile of v15, /device:TPU:0, one launch (start us, length us, event | category | flops | bytes accessed | tf_op | source)
XLA Modules:
  0.0 181.1 jit_solution(3307882071655812669)
XLA Ops:
  8.2 21.9 %all_gather.6 = bf16[136,3072]{1,0:T(8,128)(2,1)S(1)} all-gather(bf16[136,768]{1,0:T(8,128)(2,1)S(1)} %pad_maximum_fusion.5), channel_id=1, replica_groups=mesh['grp'=2,'wide'=4,'red'=2,'tok'=2] {'wide'}, dimensions={1}, use_global_device_ids=true | all-gather | bytes 1044480 | tf_op jit(solution)/shard_map/all_gather | solution.py:337
  31.9 2.1 %collective-permute-done = f32[2,128]{1,0:T(2,128)S(1)} collective-permute-done((f32[2,128]{1,0:T(2,128)S(1)}, f32[2,128]{1,0:T(2,128)S(1)}, u32[]{:S(2)}, u32[]{:S(2)}) %collective-permute-start) | collective-permute-done | bytes 1056 | tf_op jit(solution)/shard_map/ppermute | solution.py:304
  34.5 1.7 collective-permute-done.1
  36.2 5.3 %fusion.2 = f32[256,3072]{1,0:T(8,128)S(1)} fusion(bf16[1536,6144]{1,0:T(8,128)(2,1)} %refs_2_.8, bf16[128,1536]{1,0:T(8,128)(2,1)S(1)} %get-tuple-element.40, bf16[128,1536]{1,0:T(8,128)(2,1)S(1)} %collective-permute-done.1), kind=kOutput, calls=%fused_computation.2 | convolution fusion | flops 2417491968 | bytes 13369344 | tf_op jit(solution)/shard_map/dot_general | solution.py:354
  41.9 2.1 %collective-permute-done.2 = bf16[128,3072]{1,0:T(8,128)(2,1)S(1)} collective-permute-done((bf16[128,3072]{1,0:T(8,128)(2,1)S(1)}, bf16[128,3072]{1,0:T(8,128)(2,1)S(1)}, u32[]{:S(2)}, u32[]{:S(2)}) %collective-permute-start.2) | collective-permute-done | bytes 786464 | tf_op jit(solution)/shard_map/ppermute | solution.py:298
  46.9 18.0 %all_gather.7 = bf16[128,3072]{1,0:T(8,128)(2,1)S(1)} all-gather(bf16[128,768]{1,0:T(8,128)(2,1)S(1)} %slice_add_fusion.2), channel_id=1, replica_groups=mesh['grp'=2,'wide'=4,'red'=2,'tok'=2] {'wide'}, dimensions={1}, use_global_device_ids=true | all-gather | bytes 983040 | tf_op jit(solution)/shard_map/all_gather | solution.py:365
  65.9 2.6 %fusion = f32[256,3072]{1,0:T(8,128)S(1)} fusion(bf16[1536,6144]{1,0:T(8,128)(2,1)S(1)} %copy-done.6, bf16[128,1536]{1,0:T(8,128)(2,1)S(1)} %get-tuple-element.44, bf16[128,1536]{1,0:T(8,128)(2,1)S(1)} %get-tuple-element.45), kind=kOutput, calls=%fused_computation | convolution fusion | flops 2417491968 | bytes 13369344 | tf_op jit(solution)/shard_map/dot_general | solution.py:354
  76.1 6.1 %shard_map.85 = (bf16[128,4096]{1,0:T(8,128)(2,1)S(1)}, bf16[128,4096]{1,0:T(8,128)(2,1)S(1)}) custom-call(bf16[128,1536]{1,0:T(8,128)(2,1)S(1)} %get-tuple-element.38.refs_0_, bf16[128,1536]{1,0:T(8,128)(2,1)S(1)} %collective-permute-done.7.refs_1_, bf16[1536,6144]{1,0:T(8,128)(2,1)} %refs_2_.8, bf16[256,384]{1,0:T(8,128)(2,1)S(1)} %get-tuple-element.19.refs_0_.refs_3_), custom_call_target="tpu_custom_call" | custom-call | tf_op jit(solution)/shard_map/pallas_call | solution.py:63
  82.2 3.7 %shard_map.86 = (bf16[128,2048]{1,0:T(8,128)(2,1)S(1)}, bf16[128,2048]{1,0:T(8,128)(2,1)S(1)}) custom-call(bf16[128,1536]{1,0:T(8,128)(2,1)S(1)} %get-tuple-element.38.refs_0_, bf16[128,1536]{1,0:T(8,128)(2,1)S(1)} %collective-permute-done.7.refs_1_, bf16[1536,6144]{1,0:T(8,128)(2,1)} %refs_2_.8, bf16[128,4096]{1,0:T(8,128)(2,1)S(1)} %get-tuple-element.21.refs_3_.refs_0_), custom_call_target="tpu_custom_call" | custom-call | tf_op jit(solution)/shard_map/pallas_call | solution.py:63
  88.9 5.1 %shard_map.87 = (f32[128,1536]{1,0:T(8,128)S(1)}, f32[128,1536]{1,0:T(8,128)S(1)}) custom-call(bf16[128,3072]{1,0:T(8,128)(2,1)S(1)} %shard_map.82.refs_0_, bf16[128,3072]{1,0:T(8,128)(2,1)S(1)} %collective-permute-done.8.refs_3_.refs_1_, bf16[6144,1536]{1,0:T(8,128)(2,1)} %refs_2_.13, bf16[128,2048]{1,0:T(8,128)(2,1)S(1)} %get-tuple-element.22.refs_3_.refs_2_), custom_call_target="tpu_custom_call" | custom-call | tf_op jit(solution)/shard_map/pallas_call | solution.py:63
  93.9 2.2 %collective-permute-done.10.refs_1_ = bf16[256,384]{1,0:T(8,128)(2,1)S(1)} collective-permute-done((bf16[256,384]{1,0:T(8,128)(2,1)S(1)}, bf16[256,384]{1,0:T(8,128)(2,1)S(1)}, u32[]{:S(2)}, u32[]{:S(2)}) %collective-permute-start.10) | collective-permute-done | bytes 196640 | tf_op jit(solution)/shard_map/ppermute | solution.py:304
  98.3 1.9 %collective-permute-done.13 = bf16[256,128]{1,0:T(8,128)(2,1)S(1)} collective-permute-done((bf16[256,128]{1,0:T(8,128)(2,1)S(1)}, bf16[256,128]{1,0:T(8,128)(2,1)S(1)}, u32[]{:S(2)}, u32[]{:S(2)}) %collective-permute-start.13) | collective-permute-done | bytes 65568 | tf_op jit(solution)/shard_map/ppermute | solution.py:298
  101.3 5.1 %shard_map.92 = (bf16[128,1536]{1,0:T(8,128)(2,1)S(1)}, bf16[128,1536]{1,0:T(8,128)(2,1)S(1)}) custom-call(bf16[128,3072]{1,0:T(8,128)(2,1)S(1)} %shard_map.89.refs_4_.refs_0_, bf16[128,3072]{1,0:T(8,128)(2,1)S(1)} %collective-permute-done.12.refs_1_, bf16[6144,1536]{1,0:T(8,128)(2,1)} %refs_2_.13, f32[128,1536]{1,0:T(8,128)S(1)} %get-tuple-element.23.refs_4_.refs_3_, ...), custom_call_target="tpu_custom_call" | custom-call | tf_op jit(solution)/shard_map/pallas_call | solution.py:63
  111.4 14.1 %collective-permute-done.16.refs_1_ = bf16[48,6144]{1,0:T(8,128)(2,1)S(1)} collective-permute-done((bf16[48,6144]{1,0:T(8,128)(2,1)S(1)}, bf16[48,6144]{1,0:T(8,128)(2,1)S(1)}, u32[]{:S(2)}, u32[]{:S(2)}) %collective-permute-start.16) | collective-permute-done | bytes 589856 | tf_op jit(solution)/shard_map/ppermute | solution.py:304
  127.1 2.0 %collective-permute-done.17.refs_1_ = bf16[48,6144]{1,0:T(8,128)(2,1)S(1)} collective-permute-done((bf16[48,6144]{1,0:T(8,128)(2,1)S(1)}, bf16[48,6144]{1,0:T(8,128)(2,1)S(1)}, u32[]{:S(2)}, u32[]{:S(2)}) %collective-permute-start.17) | collective-permute-done | bytes 589856 | tf_op jit(solution)/shard_map/ppermute | solution.py:298
  129.1 7.3 %shard_map.95 = (bf16[48,1536]{1,0:T(8,128)(2,1)S(1)}, bf16[48,1536]{1,0:T(8,128)(2,1)S(1)}) custom-call(bf16[48,6144]{1,0:T(8,128)(2,1)S(1)} %shard_map.94.refs_0_, bf16[48,6144]{1,0:T(8,128)(2,1)S(1)} %collective-permute-done.17.refs_1_, bf16[6144,1536]{1,0:T(8,128)(2,1)} %refs_2_.13, bf16[48,128]{1,0:T(8,128)(2,1)S(1)} %slice.119.refs_3_, ...), custom_call_target="tpu_custom_call" | custom-call | tf_op jit(solution)/shard_map/pallas_call | solution.py:63
  139.5 6.3 %collective-permute-done.19.refs_1_ = bf16[80,6144]{1,0:T(8,128)(2,1)S(1)} collective-permute-done((bf16[80,6144]{1,0:T(8,128)(2,1)S(1)}, bf16[80,6144]{1,0:T(8,128)(2,1)S(1)}, u32[]{:S(2)}, u32[]{:S(2)}) %collective-permute-start.19) | collective-permute-done | bytes 983072 | tf_op jit(solution)/shard_map/ppermute | solution.py:304
  145.8 1.7 shard_map.97.refs_0_
  147.8 2.4 %collective-permute-done.20.refs_1_ = bf16[80,6144]{1,0:T(8,128)(2,1)S(1)} collective-permute-done((bf16[80,6144]{1,0:T(8,128)(2,1)S(1)}, bf16[80,6144]{1,0:T(8,128)(2,1)S(1)}, u32[]{:S(2)}, u32[]{:S(2)}) %collective-permute-start.20) | collective-permute-done | bytes 983072 | tf_op jit(solution)/shard_map/ppermute | solution.py:298
  150.2 7.4 %shard_map.98 = (bf16[80,1536]{1,0:T(8,128)(2,1)S(1)}, bf16[80,1536]{1,0:T(8,128)(2,1)S(1)}) custom-call(bf16[80,6144]{1,0:T(8,128)(2,1)S(1)} %shard_map.97.refs_0_, bf16[80,6144]{1,0:T(8,128)(2,1)S(1)} %collective-permute-done.20.refs_1_, bf16[6144,1536]{1,0:T(8,128)(2,1)} %refs_2_.13, bf16[80,128]{1,0:T(8,128)(2,1)S(1)} %slice.121.refs_3_, ...), custom_call_target="tpu_custom_call" | custom-call | tf_op jit(solution)/shard_map/pallas_call | solution.py:63
  159.2 1.9 %collective-permute-start.22 = (bf16[80,768]{1,0:T(8,128)(2,1)S(1)}, bf16[80,768]{1,0:T(8,128)(2,1)S(1)}, u32[]{:S(2)}, u32[]{:S(2)}) collective-permute-start(bf16[80,768]{1,0:T(8,128)(2,1)S(1)} %get-tuple-element.41), channel_id=1, source_target_pairs={{0,12},{4,8},{8,4},{12,0},{1,13},{5,9},{9,5},{13,1},{2,14},{6,10},... | collective-permute-start | bytes 368648 | tf_op jit(solution)/shard_map/ppermute | solution.py:321
  161.1 2.6 %collective-permute-start.24 = (bf16[80,768]{1,0:T(8,128)(2,1)S(1)}, bf16[80,768]{1,0:T(8,128)(2,1)S(1)}, u32[]{:S(2)}, u32[]{:S(2)}) collective-permute-start(bf16[80,768]{1,0:T(8,128)(2,1)S(1)} %get-tuple-element.42), channel_id=1, source_target_pairs={{0,4},{4,0},{8,12},{12,8},{1,5},{5,1},{9,13},{13,9},{2,6},{6,2},{1... | collective-permute-start | bytes 368648 | tf_op jit(solution)/shard_map/ppermute | solution.py:321
  163.7 4.8 %reduce-scatter.5.cloned.1.call-done = bf16[48,768]{1,0:T(8,128)(2,1)} async-done(((bf16[48,3072]{1,0:T(8,128)(2,1)}), bf16[48,768]{1,0:T(8,128)(2,1)}) %reduce-scatter.5.cloned.1.call-update) | async-done | bytes 73744 | tf_op jit(solution)/shard_map/reduce_scatter | solution.py:393
  169.4 3.9 %collective-permute-done.23 = bf16[80,768]{1,0:T(8,128)(2,1)S(1)} collective-permute-done((bf16[80,768]{1,0:T(8,128)(2,1)S(1)}, bf16[80,768]{1,0:T(8,128)(2,1)S(1)}, u32[]{:S(2)}, u32[]{:S(2)}) %collective-permute-start.23) | collective-permute-done | bytes 122912 | tf_op jit(solution)/shard_map/ppermute | solution.py:321
  (112 shorter events, 33.7 us)
Async XLA Ops:
  6.5 131.3 %reduce-scatter.3.cloned.1.call-start = ((), (), s32[]{:S(2)}) async-start(), calls=%async_computation.2 | async-start | bytes 983040 | tf_op jit(solution)/shard_map/reduce_scatter | solution.py:393
  30.4 3.6 %collective-permute-start = (f32[2,128]{1,0:T(2,128)S(1)}, f32[2,128]{1,0:T(2,128)S(1)}, u32[]{:S(2)}, u32[]{:S(2)}) collective-permute-start(f32[2,128]{1,0:T(2,128)S(1)} %pad_maximum_fusion.6), channel_id=1, source_target_pairs={{0,2},{2,0},{1,3},{3,1},{4,6},{6,4},{5,7},{7,5},{8,10},{10,8},{9,1... | collective-permute-start | bytes 3080 | tf_op jit(solution)/shard_map/ppermute | solution.py:304
  34.4 1.8 collective-permute-start.1
  41.7 2.4 %collective-permute-start.2 = (bf16[128,3072]{1,0:T(8,128)(2,1)S(1)}, bf16[128,3072]{1,0:T(8,128)(2,1)S(1)}, u32[]{:S(2)}, u32[]{:S(2)}) collective-permute-start(bf16[128,3072]{1,0:T(8,128)(2,1)S(1)} %slice.152), channel_id=1, source_target_pairs={{0,1},{1,0},{2,3},{3,2},{4,5},{5,4},{6,7},{7,6},{8,9},{9,8},{10,11... | collective-permute-start | bytes 2359304 | tf_op jit(solution)/shard_map/ppermute | solution.py:298
  44.7 24.0 %collective-permute-start.6 = (bf16[128,3072]{1,0:T(8,128)(2,1)S(1)}, bf16[128,3072]{1,0:T(8,128)(2,1)S(1)}, u32[]{:S(2)}, u32[]{:S(2)}) collective-permute-start(bf16[128,3072]{1,0:T(8,128)(2,1)S(1)} %fusion.13.refs_0_), channel_id=1, source_target_pairs={{0,2},{2,0},{1,3},{3,1},{4,6},{6,4},{5,7},{7,5},{8,10},{10,8},{9,1... | collective-permute-start | bytes 2359304 | tf_op jit(solution)/shard_map/ppermute | solution.py:304
  65.3 5.4 %collective-permute-start.5 = (f32[2,128]{1,0:T(2,128)S(1)}, f32[2,128]{1,0:T(2,128)S(1)}, u32[]{:S(2)}, u32[]{:S(2)}) collective-permute-start(f32[2,128]{1,0:T(2,128)S(1)} %pad_maximum_fusion.7), channel_id=1, source_target_pairs={{0,2},{2,0},{1,3},{3,1},{4,6},{6,4},{5,7},{7,5},{8,10},{10,8},{9,1... | collective-permute-start | bytes 3080 | tf_op jit(solution)/shard_map/ppermute | solution.py:304
  68.6 3.1 %collective-permute-start.3 = (bf16[128,3072]{1,0:T(8,128)(2,1)S(1)}, bf16[128,3072]{1,0:T(8,128)(2,1)S(1)}, u32[]{:S(2)}, u32[]{:S(2)}) collective-permute-start(bf16[128,3072]{1,0:T(8,128)(2,1)S(1)} %slice.151), channel_id=1, source_target_pairs={{0,1},{1,0},{2,3},{3,2},{4,5},{5,4},{6,7},{7,6},{8,9},{9,8},{10,11... | collective-permute-start | bytes 2359304 | tf_op jit(solution)/shard_map/ppermute | solution.py:298
  70.7 3.1 %collective-permute-start.8 = (bf16[128,3072]{1,0:T(8,128)(2,1)S(1)}, bf16[128,3072]{1,0:T(8,128)(2,1)S(1)}, u32[]{:S(2)}, u32[]{:S(2)}) collective-permute-start(bf16[128,3072]{1,0:T(8,128)(2,1)S(1)} %shard_map.82.refs_0_), channel_id=1, source_target_pairs={{0,1},{1,0},{2,3},{3,2},{4,5},{5,4},{6,7},{7,6},{8,9},{9,8},{10,11... | collective-permute-start | bytes 2359304 | tf_op jit(solution)/shard_map/ppermute | solution.py:298
  71.6 2.1 %collective-permute-start.7 = (bf16[128,1536]{1,0:T(8,128)(2,1)S(1)}, bf16[128,1536]{1,0:T(8,128)(2,1)S(1)}, u32[]{:S(2)}, u32[]{:S(2)}) collective-permute-start(bf16[128,1536]{1,0:T(8,128)(2,1)S(1)} %get-tuple-element.37), channel_id=1, source_target_pairs={{0,1},{1,0},{2,3},{3,2},{4,5},{5,4},{6,7},{7,6},{8,9},{9,8},{10,11... | collective-permute-start | bytes 1179656 | tf_op jit(solution)/shard_map/ppermute | solution.py:298
  71.9 25.0 %collective-permute-start.4 = (bf16[128,3072]{1,0:T(8,128)(2,1)S(1)}, bf16[128,3072]{1,0:T(8,128)(2,1)S(1)}, u32[]{:S(2)}, u32[]{:S(2)}) collective-permute-start(bf16[128,3072]{1,0:T(8,128)(2,1)S(1)} %fusion.12.refs_4_.refs_0_), channel_id=1, source_target_pairs={{0,2},{2,0},{1,3},{3,1},{4,6},{6,4},{5,7},{7,5},{8,10},{10,8},{9,1... | collective-permute-start | bytes 2359304 | tf_op jit(solution)/shard_map/ppermute | solution.py:304
  85.9 10.2 %collective-permute-start.11 = (bf16[128,2048]{1,0:T(8,128)(2,1)S(1)}, bf16[128,2048]{1,0:T(8,128)(2,1)S(1)}, u32[]{:S(2)}, u32[]{:S(2)}) collective-permute-start(bf16[128,2048]{1,0:T(8,128)(2,1)S(1)} %get-tuple-element.24), channel_id=1, source_target_pairs={{0,1},{1,0},{2,3},{3,2},{4,5},{5,4},{6,7},{7,6},{8,9},{9,8},{10,11... | collective-permute-start | bytes 1572872 | tf_op jit(solution)/shard_map/ppermute | solution.py:298
  86.2 2.0 %collective-permute-start.9 = (bf16[256,384]{1,0:T(8,128)(2,1)S(1)}, bf16[256,384]{1,0:T(8,128)(2,1)S(1)}, u32[]{:S(2)}, u32[]{:S(2)}) collective-permute-start(bf16[256,384]{1,0:T(8,128)(2,1)S(1)} %get-tuple-element.20), channel_id=1, source_target_pairs={{0,1},{1,0},{2,3},{3,2},{4,5},{5,4},{6,7},{7,6},{8,9},{9,8},{10,11... | collective-permute-start | bytes 589832 | tf_op jit(solution)/shard_map/ppermute | solution.py:298
  86.5 13.6 %collective-permute-start.14 = (bf16[128,4096]{1,0:T(8,128)(2,1)S(1)}, bf16[128,4096]{1,0:T(8,128)(2,1)S(1)}, u32[]{:S(2)}, u32[]{:S(2)}) collective-permute-start(bf16[128,4096]{1,0:T(8,128)(2,1)S(1)} %get-tuple-element.26), channel_id=1, source_target_pairs={{0,1},{1,0},{2,3},{3,2},{4,5},{5,4},{6,7},{7,6},{8,9},{9,8},{10,11... | collective-permute-start | bytes 3145736 | tf_op jit(solution)/shard_map/ppermute | solution.py:298
  88.2 7.9 %collective-permute-start.10 = (bf16[256,384]{1,0:T(8,128)(2,1)S(1)}, bf16[256,384]{1,0:T(8,128)(2,1)S(1)}, u32[]{:S(2)}, u32[]{:S(2)}) collective-permute-start(bf16[256,384]{1,0:T(8,128)(2,1)S(1)} %shard_map.84.refs_0_), channel_id=1, source_target_pairs={{0,2},{2,0},{1,3},{3,1},{4,6},{6,4},{5,7},{7,5},{8,10},{10,8},{9,1... | collective-permute-start | bytes 589832 | tf_op jit(solution)/shard_map/ppermute | solution.py:304
  97.7 2.8 %collective-permute-start.12 = (bf16[128,3072]{1,0:T(8,128)(2,1)S(1)}, bf16[128,3072]{1,0:T(8,128)(2,1)S(1)}, u32[]{:S(2)}, u32[]{:S(2)}) collective-permute-start(bf16[128,3072]{1,0:T(8,128)(2,1)S(1)} %shard_map.89.refs_4_.refs_0_), channel_id=1, source_target_pairs={{0,1},{1,0},{2,3},{3,2},{4,5},{5,4},{6,7},{7,6},{8,9},{9,8},{10,11... | collective-permute-start | bytes 2359304 | tf_op jit(solution)/shard_map/ppermute | solution.py:298
  97.8 2.4 %collective-permute-start.13 = (bf16[256,128]{1,0:T(8,128)(2,1)S(1)}, bf16[256,128]{1,0:T(8,128)(2,1)S(1)}, u32[]{:S(2)}, u32[]{:S(2)}) collective-permute-start(bf16[256,128]{1,0:T(8,128)(2,1)S(1)} %shard_map.88.refs_2_), channel_id=1, source_target_pairs={{0,1},{1,0},{2,3},{3,2},{4,5},{5,4},{6,7},{7,6},{8,9},{9,8},{10,11... | collective-permute-start | bytes 196616 | tf_op jit(solution)/shard_map/ppermute | solution.py:298
  109.1 59.3 %reduce-scatter.5.cloned.1.call-start = ((), (), s32[]{:S(2)}) async-start(), calls=%async_computation.3 | async-start | bytes 368640 | tf_op jit(solution)/shard_map/reduce_scatter | solution.py:393
  109.3 16.2 %collective-permute-start.16 = (bf16[48,6144]{1,0:T(8,128)(2,1)S(1)}, bf16[48,6144]{1,0:T(8,128)(2,1)S(1)}, u32[]{:S(2)}, u32[]{:S(2)}) collective-permute-start(bf16[48,6144]{1,0:T(8,128)(2,1)S(1)} %shard_map.90.refs_4_.refs_0_), channel_id=1, source_target_pairs={{0,2},{2,0},{1,3},{3,1},{4,6},{6,4},{5,7},{7,5},{8,10},{10,8},{9,1... | collective-permute-start | bytes 1769480 | tf_op jit(solution)/shard_map/ppermute | solution.py:304
  110.9 34.9 %collective-permute-start.19 = (bf16[80,6144]{1,0:T(8,128)(2,1)S(1)}, bf16[80,6144]{1,0:T(8,128)(2,1)S(1)}, u32[]{:S(2)}, u32[]{:S(2)}) collective-permute-start(bf16[80,6144]{1,0:T(8,128)(2,1)S(1)} %shard_map.91.refs_8_.refs_0_), channel_id=1, source_target_pairs={{0,2},{2,0},{1,3},{3,1},{4,6},{6,4},{5,7},{7,5},{8,10},{10,8},{9,1... | collective-permute-start | bytes 2949128 | tf_op jit(solution)/shard_map/ppermute | solution.py:304
  127.0 2.1 %collective-permute-start.17 = (bf16[48,6144]{1,0:T(8,128)(2,1)S(1)}, bf16[48,6144]{1,0:T(8,128)(2,1)S(1)}, u32[]{:S(2)}, u32[]{:S(2)}) collective-permute-start(bf16[48,6144]{1,0:T(8,128)(2,1)S(1)} %shard_map.94.refs_0_), channel_id=1, source_target_pairs={{0,1},{1,0},{2,3},{3,2},{4,5},{5,4},{6,7},{7,6},{8,9},{9,8},{10,11... | collective-permute-start | bytes 1769480 | tf_op jit(solution)/shard_map/ppermute | solution.py:298
  147.6 2.6 %collective-permute-start.20 = (bf16[80,6144]{1,0:T(8,128)(2,1)S(1)}, bf16[80,6144]{1,0:T(8,128)(2,1)S(1)}, u32[]{:S(2)}, u32[]{:S(2)}) collective-permute-start(bf16[80,6144]{1,0:T(8,128)(2,1)S(1)} %shard_map.97.refs_0_), channel_id=1, source_target_pairs={{0,1},{1,0},{2,3},{3,2},{4,5},{5,4},{6,7},{7,6},{8,9},{9,8},{10,11... | collective-permute-start | bytes 2949128 | tf_op jit(solution)/shard_map/ppermute | solution.py:298
  159.2 10.1 %collective-permute-start.22 = (bf16[80,768]{1,0:T(8,128)(2,1)S(1)}, bf16[80,768]{1,0:T(8,128)(2,1)S(1)}, u32[]{:S(2)}, u32[]{:S(2)}) collective-permute-start(bf16[80,768]{1,0:T(8,128)(2,1)S(1)} %get-tuple-element.41), channel_id=1, source_target_pairs={{0,12},{4,8},{8,4},{12,0},{1,13},{5,9},{9,5},{13,1},{2,14},{6,10},... | collective-permute-start | bytes 368648 | tf_op jit(solution)/shard_map/ppermute | solution.py:321
  161.1 12.2 %collective-permute-start.23 = (bf16[80,768]{1,0:T(8,128)(2,1)S(1)}, bf16[80,768]{1,0:T(8,128)(2,1)S(1)}, u32[]{:S(2)}, u32[]{:S(2)}) collective-permute-start(bf16[80,768]{1,0:T(8,128)(2,1)S(1)} %get-tuple-element.43), channel_id=1, source_target_pairs={{0,8},{4,12},{8,0},{12,4},{1,9},{5,13},{9,1},{13,5},{2,10},{6,14},... | collective-permute-start | bytes 368648 | tf_op jit(solution)/shard_map/ppermute | solution.py:321
  161.1 12.2 %collective-permute-start.24 = (bf16[80,768]{1,0:T(8,128)(2,1)S(1)}, bf16[80,768]{1,0:T(8,128)(2,1)S(1)}, u32[]{:S(2)}, u32[]{:S(2)}) collective-permute-start(bf16[80,768]{1,0:T(8,128)(2,1)S(1)} %get-tuple-element.42), channel_id=1, source_target_pairs={{0,4},{4,0},{8,12},{12,8},{1,5},{5,1},{9,13},{13,9},{2,6},{6,2},{1... | collective-permute-start | bytes 368648 | tf_op jit(solution)/shard_map/ppermute | solution.py:321
  (12 other events, 77.5 us)
Sparse Core Ops, SparseCore 0:
  109.2 22.7 reduce-scatter.2
  147.9 20.4 reduce-scatter.4

commit v16 on v15

--- a/solution.py
+++ b/solution.py
@@ -11,7 +11,7 @@
 D = 6144
 PATCHES = 256
 EPS = 1e-06
-SHARES = (8, 3, 5)
+SHARES = (9, 5, 2)
 LEAD_PIECES = (1, 1)
 REST_PIECES = (2, 1)
 AHEAD = 4

time: 182 us -> 176 us (0.967)
  waiting for transfers between devices: 49.3 us -> 43.3 us
  starting transfers between devices: 15.6 us -> 17.5 us
    ppermute x7, waiting for transfers between devices: 24.7 us -> 20.3 us  [all_red(): parts.append(lax.ppermute(x, 'red', pairs))]
    reduce_scatter x2, waiting for transfers between devices: 4.75 us -> 1.25 us  [scatter(): lax.psum_scatter(full, 'wide', scatter_dimension=1, tiled=True)]
    ppermute x3, waiting for transfers between devices: 3.91 us -> 6.88 us  [collect(): total = total + lax.ppermute(block(chip ^ k), 'wide', pairs).astype(F32)]
    ppermute x7, starting transfers between devices: 7.91 us -> 9.85 us  [all_red(): parts.append(lax.ppermute(x, 'red', pairs))]
  transfers between devices with their start and end apart: 27 -> 27, of which waited for: 16 -> 16; matrix products, arithmetic and copies ran while one was open for 3% -> 3% of each run, Pallas kernels for 20% -> 24%
where the time goes in v16:
time: 176 us
  Pallas kernels  43.7 us (25%)
  waiting for transfers between devices  43.3 us (25%)
  blocking collectives  39.8 us (23%)
  starting transfers between devices  17.5 us (10%)
  between operations  15.3 us (9%)
  matrix products  8.49 us (5%)
  local copies, waits for them, and re-layouts  4.05 us (2%)
  other arithmetic  3.86 us (2%)
    pallas_call x17, Pallas kernels, call(): pl.pallas_call(body, in_specs=list(specs) + [corner_of(a) for a in earlie...  43.7 us
    all_gather x1, blocking collectives, body(): lead = lax.all_gather(lead, 'wide', axis=1, tiled=True)  23 us
    ppermute x7, waiting for transfers between devices, all_red(): parts.append(lax.ppermute(x, 'red', pairs))  20.3 us
    all_gather x1, blocking collectives, body(): rest = lax.all_gather(rest, 'wide', axis=1, tiled=True)  16.8 us
    ppermute x15, waiting for transfers between devices, swap(): return lax.ppermute(x, 'tok', [(0, 1), (1, 0)])  14.8 us
    ppermute x7, starting transfers between devices, all_red(): parts.append(lax.ppermute(x, 'red', pairs))  9.85 us
    dot_general x2, matrix products, project(): part = jnp.dot(both, weight, preferred_element_type=F32)  8.49 us
    ppermute x3, waiting for transfers between devices, collect(): total = total + lax.ppermute(block(chip ^ k), 'wide', pairs).astype(F32)  6.88 us
  transfers between devices with their start and end apart: 27, of which 16 were waited for; matrix products, arithmetic and copies ran while one was open for 3% of the time, Pallas kernels for 24%

profile of v16, /device:TPU:0, one launch (start us, length us, event | category | flops | bytes accessed | tf_op | source)
XLA Modules:
  0.0 175.9 jit_solution(12403246125011278991)
XLA Ops:
  8.2 23.0 %all_gather.6 = bf16[152,3072]{1,0:T(8,128)(2,1)S(1)} all-gather(bf16[152,768]{1,0:T(8,128)(2,1)S(1)} %pad_maximum_fusion.3), channel_id=1, replica_groups=mesh['grp'=2,'wide'=4,'red'=2,'tok'=2] {'wide'}, dimensions={1}, use_global_device_ids=true | all-gather | bytes 1167360 | tf_op jit(solution)/shard_map/all_gather | solution.py:337
  33.1 2.1 %collective-permute-done = f32[2,144]{1,0:T(2,128)S(1)} collective-permute-done((f32[2,144]{1,0:T(2,128)S(1)}, f32[2,144]{1,0:T(2,128)S(1)}, u32[]{:S(2)}, u32[]{:S(2)}) %collective-permute-start) | collective-permute-done | bytes 1184 | tf_op jit(solution)/shard_map/ppermute | solution.py:304
  35.8 1.8 %collective-permute-done.1 = bf16[144,1536]{1,0:T(8,128)(2,1)S(1)} collective-permute-done((bf16[144,1536]{1,0:T(8,128)(2,1)S(1)}, bf16[144,1536]{1,0:T(8,128)(2,1)S(1)}, u32[]{:S(2)}, u32[]{:S(2)}) %collective-permute-start.1) | collective-permute-done | bytes 442400 | tf_op jit(solution)/shard_map/ppermute | solution.py:298
  37.6 5.6 %fusion.2 = f32[288,3072]{1,0:T(8,128)S(1)} fusion(bf16[1536,6144]{1,0:T(8,128)(2,1)} %refs_2_.8, bf16[144,1536]{1,0:T(8,128)(2,1)S(1)} %collective-permute-done.1, bf16[144,1536]{1,0:T(8,128)(2,1)S(1)} %get-tuple-element.37), kind=kOutput, calls=%fused_computation.2 | convolution fusion | flops 2719678464 | bytes 13860864 | tf_op jit(solution)/shard_map/dot_general | solution.py:354
  43.5 2.3 %collective-permute-done.2 = bf16[144,3072]{1,0:T(8,128)(2,1)S(1)} collective-permute-done((bf16[144,3072]{1,0:T(8,128)(2,1)S(1)}, bf16[144,3072]{1,0:T(8,128)(2,1)S(1)}, u32[]{:S(2)}, u32[]{:S(2)}) %collective-permute-start.2) | collective-permute-done | bytes 884768 | tf_op jit(solution)/shard_map/ppermute | solution.py:298
  48.7 16.8 %all_gather.7 = bf16[112,3072]{1,0:T(8,128)(2,1)S(1)} all-gather(bf16[112,768]{1,0:T(8,128)(2,1)S(1)} %slice_add_fusion.2), channel_id=1, replica_groups=mesh['grp'=2,'wide'=4,'red'=2,'tok'=2] {'wide'}, dimensions={1}, use_global_device_ids=true | all-gather | bytes 860160 | tf_op jit(solution)/shard_map/all_gather | solution.py:365
  66.6 2.9 %fusion = f32[288,3072]{1,0:T(8,128)S(1)} fusion(bf16[1536,6144]{1,0:T(8,128)(2,1)S(1)} %bitcast.29, bf16[144,1536]{1,0:T(8,128)(2,1)S(1)} %get-tuple-element.46, bf16[144,1536]{1,0:T(8,128)(2,1)S(1)} %get-tuple-element.47), kind=kOutput, calls=%fused_computation | convolution fusion | flops 2719678464 | bytes 13860864 | tf_op jit(solution)/shard_map/dot_general | solution.py:354
  76.2 5.7 %shard_map.85 = (bf16[112,4096]{1,0:T(8,128)(2,1)S(1)}, bf16[112,4096]{1,0:T(8,128)(2,1)S(1)}) custom-call(bf16[112,1536]{1,0:T(8,128)(2,1)S(1)} %get-tuple-element.40.refs_0_, bf16[112,1536]{1,0:T(8,128)(2,1)S(1)} %collective-permute-done.7.refs_1_, bf16[1536,6144]{1,0:T(8,128)(2,1)} %refs_2_.8, bf16[256,384]{1,0:T(8,128)(2,1)S(1)} %get-tuple-element.19.refs_0_.refs_3_), custom_call_target="tpu_custom_call" | custom-call | tf_op jit(solution)/shard_map/pallas_call | solution.py:63
  82.0 3.5 %shard_map.86 = (bf16[112,2048]{1,0:T(8,128)(2,1)S(1)}, bf16[112,2048]{1,0:T(8,128)(2,1)S(1)}) custom-call(bf16[112,1536]{1,0:T(8,128)(2,1)S(1)} %get-tuple-element.40.refs_0_, bf16[112,1536]{1,0:T(8,128)(2,1)S(1)} %collective-permute-done.7.refs_1_, bf16[1536,6144]{1,0:T(8,128)(2,1)} %refs_2_.8, bf16[112,4096]{1,0:T(8,128)(2,1)S(1)} %get-tuple-element.21.refs_3_.refs_0_), custom_call_target="tpu_custom_call" | custom-call | tf_op jit(solution)/shard_map/pallas_call | solution.py:63
  86.1 1.6 collective-permute-done.9.refs_1_
  87.8 1.6 collective-permute-start.10
  89.4 5.4 %shard_map.87 = (f32[144,1536]{1,0:T(8,128)S(1)}, f32[144,1536]{1,0:T(8,128)S(1)}) custom-call(bf16[144,3072]{1,0:T(8,128)(2,1)S(1)} %shard_map.82.refs_0_, bf16[144,3072]{1,0:T(8,128)(2,1)S(1)} %collective-permute-done.8.refs_3_.refs_1_, bf16[6144,1536]{1,0:T(8,128)(2,1)} %refs_2_.13, bf16[112,2048]{1,0:T(8,128)(2,1)S(1)} %get-tuple-element.22.refs_3_.refs_2_), custom_call_target="tpu_custom_call" | custom-call | tf_op jit(solution)/shard_map/pallas_call | solution.py:63
  94.8 4.4 %collective-permute-done.10.refs_1_ = bf16[256,384]{1,0:T(8,128)(2,1)S(1)} collective-permute-done((bf16[256,384]{1,0:T(8,128)(2,1)S(1)}, bf16[256,384]{1,0:T(8,128)(2,1)S(1)}, u32[]{:S(2)}, u32[]{:S(2)}) %collective-permute-start.10) | collective-permute-done | bytes 196640 | tf_op jit(solution)/shard_map/ppermute | solution.py:304
  101.4 2.0 %collective-permute-done.13 = bf16[256,128]{1,0:T(8,128)(2,1)S(1)} collective-permute-done((bf16[256,128]{1,0:T(8,128)(2,1)S(1)}, bf16[256,128]{1,0:T(8,128)(2,1)S(1)}, u32[]{:S(2)}, u32[]{:S(2)}) %collective-permute-start.13) | collective-permute-done | bytes 65568 | tf_op jit(solution)/shard_map/ppermute | solution.py:298
  105.4 5.3 %shard_map.92 = (bf16[144,1536]{1,0:T(8,128)(2,1)S(1)}, bf16[144,1536]{1,0:T(8,128)(2,1)S(1)}) custom-call(bf16[144,3072]{1,0:T(8,128)(2,1)S(1)} %shard_map.89.refs_4_.refs_0_, bf16[144,3072]{1,0:T(8,128)(2,1)S(1)} %collective-permute-done.12.refs_1_, bf16[6144,1536]{1,0:T(8,128)(2,1)} %refs_2_.13, f32[144,1536]{1,0:T(8,128)S(1)} %get-tuple-element.23.refs_4_.refs_3_, ...), custom_call_target="tpu_custom_call" | custom-call | tf_op jit(solution)/shard_map/pallas_call | solution.py:63
  110.8 1.8 %collective-permute-done.15.refs_1_ = bf16[144,1536]{1,0:T(8,128)(2,1)S(1)} collective-permute-done((bf16[144,1536]{1,0:T(8,128)(2,1)S(1)}, bf16[144,1536]{1,0:T(8,128)(2,1)S(1)}, u32[]{:S(2)}, u32[]{:S(2)}) %collective-permute-start.15) | collective-permute-done | bytes 442400 | tf_op jit(solution)/shard_map/ppermute | solution.py:298
  113.8 13.8 %collective-permute-done.16.refs_1_ = bf16[80,6144]{1,0:T(8,128)(2,1)S(1)} collective-permute-done((bf16[80,6144]{1,0:T(8,128)(2,1)S(1)}, bf16[80,6144]{1,0:T(8,128)(2,1)S(1)}, u32[]{:S(2)}, u32[]{:S(2)}) %collective-permute-start.16) | collective-permute-done | bytes 983072 | tf_op jit(solution)/shard_map/ppermute | solution.py:304
  127.6 1.7 shard_map.94.refs_0_
  131.9 7.4 %shard_map.95 = (bf16[80,1536]{1,0:T(8,128)(2,1)S(1)}, bf16[80,1536]{1,0:T(8,128)(2,1)S(1)}) custom-call(bf16[80,6144]{1,0:T(8,128)(2,1)S(1)} %shard_map.94.refs_0_, bf16[80,6144]{1,0:T(8,128)(2,1)S(1)} %collective-permute-done.17.refs_1_, bf16[6144,1536]{1,0:T(8,128)(2,1)} %refs_2_.13, bf16[80,128]{1,0:T(8,128)(2,1)S(1)} %slice.121.refs_3_, ...), custom_call_target="tpu_custom_call" | custom-call | tf_op jit(solution)/shard_map/pallas_call | solution.py:63
  145.8 7.3 %shard_map.98 = (bf16[32,1536]{1,0:T(8,128)(2,1)S(1)}, bf16[32,1536]{1,0:T(8,128)(2,1)S(1)}) custom-call(bf16[32,6144]{1,0:T(8,128)(2,1)S(1)} %shard_map.97.refs_0_, bf16[32,6144]{1,0:T(8,128)(2,1)S(1)} %collective-permute-done.20.refs_1_, bf16[6144,1536]{1,0:T(8,128)(2,1)} %refs_2_.13, bf16[32,128]{1,0:T(8,128)(2,1)S(1)} %slice.123.refs_3_, ...), custom_call_target="tpu_custom_call" | custom-call | tf_op jit(solution)/shard_map/pallas_call | solution.py:63
  154.5 2.6 %collective-permute-start.22 = (bf16[32,768]{1,0:T(8,128)(2,1)S(1)}, bf16[32,768]{1,0:T(8,128)(2,1)S(1)}, u32[]{:S(2)}, u32[]{:S(2)}) collective-permute-start(bf16[32,768]{1,0:T(8,128)(2,1)S(1)} %get-tuple-element.41), channel_id=1, source_target_pairs={{0,12},{4,8},{8,4},{12,0},{1,13},{5,9},{9,5},{13,1},{2,14},{6,10},... | collective-permute-start | bytes 147464 | tf_op jit(solution)/shard_map/ppermute | solution.py:321
  157.1 1.9 %collective-permute-start.24 = (bf16[32,768]{1,0:T(8,128)(2,1)S(1)}, bf16[32,768]{1,0:T(8,128)(2,1)S(1)}, u32[]{:S(2)}, u32[]{:S(2)}) collective-permute-start(bf16[32,768]{1,0:T(8,128)(2,1)S(1)} %get-tuple-element.42), channel_id=1, source_target_pairs={{0,4},{4,0},{8,12},{12,8},{1,5},{5,1},{9,13},{13,9},{2,6},{6,2},{1... | collective-permute-start | bytes 147464 | tf_op jit(solution)/shard_map/ppermute | solution.py:321
  159.0 2.3 %collective-permute-done.22 = bf16[32,768]{1,0:T(8,128)(2,1)S(1)} collective-permute-done((bf16[32,768]{1,0:T(8,128)(2,1)S(1)}, bf16[32,768]{1,0:T(8,128)(2,1)S(1)}, u32[]{:S(2)}, u32[]{:S(2)}) %collective-permute-start.22) | collective-permute-done | bytes 49184 | tf_op jit(solution)/shard_map/ppermute | solution.py:321
  161.3 4.6 %collective-permute-done.23 = bf16[32,768]{1,0:T(8,128)(2,1)S(1)} collective-permute-done((bf16[32,768]{1,0:T(8,128)(2,1)S(1)}, bf16[32,768]{1,0:T(8,128)(2,1)S(1)}, u32[]{:S(2)}, u32[]{:S(2)}) %collective-permute-start.23) | collective-permute-done | bytes 49184 | tf_op jit(solution)/shard_map/ppermute | solution.py:321
  (119 shorter events, 33.2 us)
Async XLA Ops:
  6.5 134.4 %reduce-scatter.3.cloned.1.call-start = ((), (), s32[]{:S(2)}) async-start(), calls=%async_computation.2 | async-start | bytes 1105920 | tf_op jit(solution)/shard_map/reduce_scatter | solution.py:393
  31.5 3.6 %collective-permute-start = (f32[2,144]{1,0:T(2,128)S(1)}, f32[2,144]{1,0:T(2,128)S(1)}, u32[]{:S(2)}, u32[]{:S(2)}) collective-permute-start(f32[2,144]{1,0:T(2,128)S(1)} %pad_maximum_fusion.4), channel_id=1, source_target_pairs={{0,2},{2,0},{1,3},{3,1},{4,6},{6,4},{5,7},{7,5},{8,10},{10,8},{9,1... | collective-permute-start | bytes 3464 | tf_op jit(solution)/shard_map/ppermute | solution.py:304
  35.7 1.9 %collective-permute-start.1 = (bf16[144,1536]{1,0:T(8,128)(2,1)S(1)}, bf16[144,1536]{1,0:T(8,128)(2,1)S(1)}, u32[]{:S(2)}, u32[]{:S(2)}) collective-permute-start(bf16[144,1536]{1,0:T(8,128)(2,1)S(1)} %get-tuple-element.38), channel_id=1, source_target_pairs={{0,1},{1,0},{2,3},{3,2},{4,5},{5,4},{6,7},{7,6},{8,9},{9,8},{10,11... | collective-permute-start | bytes 1327112 | tf_op jit(solution)/shard_map/ppermute | solution.py:298
  43.3 2.5 %collective-permute-start.2 = (bf16[144,3072]{1,0:T(8,128)(2,1)S(1)}, bf16[144,3072]{1,0:T(8,128)(2,1)S(1)}, u32[]{:S(2)}, u32[]{:S(2)}) collective-permute-start(bf16[144,3072]{1,0:T(8,128)(2,1)S(1)} %slice.150), channel_id=1, source_target_pairs={{0,1},{1,0},{2,3},{3,2},{4,5},{5,4},{6,7},{7,6},{8,9},{9,8},{10,11... | collective-permute-start | bytes 2654216 | tf_op jit(solution)/shard_map/ppermute | solution.py:298
  46.5 23.2 %collective-permute-start.6 = (bf16[144,3072]{1,0:T(8,128)(2,1)S(1)}, bf16[144,3072]{1,0:T(8,128)(2,1)S(1)}, u32[]{:S(2)}, u32[]{:S(2)}) collective-permute-start(bf16[144,3072]{1,0:T(8,128)(2,1)S(1)} %fusion.9.refs_0_), channel_id=1, source_target_pairs={{0,2},{2,0},{1,3},{3,1},{4,6},{6,4},{5,7},{7,5},{8,10},{10,8},{9,1... | collective-permute-start | bytes 2654216 | tf_op jit(solution)/shard_map/ppermute | solution.py:304
  65.8 5.8 %collective-permute-start.5 = (f32[2,112]{1,0:T(2,128)S(1)}, f32[2,112]{1,0:T(2,128)S(1)}, u32[]{:S(2)}, u32[]{:S(2)}) collective-permute-start(f32[2,112]{1,0:T(2,128)S(1)} %pad_maximum_fusion.5), channel_id=1, source_target_pairs={{0,2},{2,0},{1,3},{3,1},{4,6},{6,4},{5,7},{7,5},{8,10},{10,8},{9,1... | collective-permute-start | bytes 2696 | tf_op jit(solution)/shard_map/ppermute | solution.py:304
  69.6 3.1 %collective-permute-start.3 = (bf16[144,3072]{1,0:T(8,128)(2,1)S(1)}, bf16[144,3072]{1,0:T(8,128)(2,1)S(1)}, u32[]{:S(2)}, u32[]{:S(2)}) collective-permute-start(bf16[144,3072]{1,0:T(8,128)(2,1)S(1)} %slice.149), channel_id=1, source_target_pairs={{0,1},{1,0},{2,3},{3,2},{4,5},{5,4},{6,7},{7,6},{8,9},{9,8},{10,11... | collective-permute-start | bytes 2654216 | tf_op jit(solution)/shard_map/ppermute | solution.py:298
  71.7 3.1 %collective-permute-start.8 = (bf16[144,3072]{1,0:T(8,128)(2,1)S(1)}, bf16[144,3072]{1,0:T(8,128)(2,1)S(1)}, u32[]{:S(2)}, u32[]{:S(2)}) collective-permute-start(bf16[144,3072]{1,0:T(8,128)(2,1)S(1)} %shard_map.82.refs_0_), channel_id=1, source_target_pairs={{0,1},{1,0},{2,3},{3,2},{4,5},{5,4},{6,7},{7,6},{8,9},{9,8},{10,11... | collective-permute-start | bytes 2654216 | tf_op jit(solution)/shard_map/ppermute | solution.py:298
  72.6 2.2 %collective-permute-start.7 = (bf16[112,1536]{1,0:T(8,128)(2,1)S(1)}, bf16[112,1536]{1,0:T(8,128)(2,1)S(1)}, u32[]{:S(2)}, u32[]{:S(2)}) collective-permute-start(bf16[112,1536]{1,0:T(8,128)(2,1)S(1)} %get-tuple-element.39), channel_id=1, source_target_pairs={{0,1},{1,0},{2,3},{3,2},{4,5},{5,4},{6,7},{7,6},{8,9},{9,8},{10,11... | collective-permute-start | bytes 1032200 | tf_op jit(solution)/shard_map/ppermute | solution.py:298
  72.9 27.1 %collective-permute-start.4 = (bf16[144,3072]{1,0:T(8,128)(2,1)S(1)}, bf16[144,3072]{1,0:T(8,128)(2,1)S(1)}, u32[]{:S(2)}, u32[]{:S(2)}) collective-permute-start(bf16[144,3072]{1,0:T(8,128)(2,1)S(1)} %fusion.8.refs_4_.refs_0_), channel_id=1, source_target_pairs={{0,2},{2,0},{1,3},{3,1},{4,6},{6,4},{5,7},{7,5},{8,10},{10,8},{9,1... | collective-permute-start | bytes 2654216 | tf_op jit(solution)/shard_map/ppermute | solution.py:304
  85.5 13.7 %collective-permute-start.11 = (bf16[112,2048]{1,0:T(8,128)(2,1)S(1)}, bf16[112,2048]{1,0:T(8,128)(2,1)S(1)}, u32[]{:S(2)}, u32[]{:S(2)}) collective-permute-start(bf16[112,2048]{1,0:T(8,128)(2,1)S(1)} %get-tuple-element.24), channel_id=1, source_target_pairs={{0,1},{1,0},{2,3},{3,2},{4,5},{5,4},{6,7},{7,6},{8,9},{9,8},{10,11... | collective-permute-start | bytes 1376264 | tf_op jit(solution)/shard_map/ppermute | solution.py:298
  87.8 11.5 %collective-permute-start.10 = (bf16[256,384]{1,0:T(8,128)(2,1)S(1)}, bf16[256,384]{1,0:T(8,128)(2,1)S(1)}, u32[]{:S(2)}, u32[]{:S(2)}) collective-permute-start(bf16[256,384]{1,0:T(8,128)(2,1)S(1)} %shard_map.84.refs_0_), channel_id=1, source_target_pairs={{0,2},{2,0},{1,3},{3,1},{4,6},{6,4},{5,7},{7,5},{8,10},{10,8},{9,1... | collective-permute-start | bytes 589832 | tf_op jit(solution)/shard_map/ppermute | solution.py:304
  89.3 14.1 %collective-permute-start.14 = (bf16[112,4096]{1,0:T(8,128)(2,1)S(1)}, bf16[112,4096]{1,0:T(8,128)(2,1)S(1)}, u32[]{:S(2)}, u32[]{:S(2)}) collective-permute-start(bf16[112,4096]{1,0:T(8,128)(2,1)S(1)} %get-tuple-element.26), channel_id=1, source_target_pairs={{0,1},{1,0},{2,3},{3,2},{4,5},{5,4},{6,7},{7,6},{8,9},{9,8},{10,11... | collective-permute-start | bytes 2752520 | tf_op jit(solution)/shard_map/ppermute | solution.py:298
  100.9 4.5 %collective-permute-start.12 = (bf16[144,3072]{1,0:T(8,128)(2,1)S(1)}, bf16[144,3072]{1,0:T(8,128)(2,1)S(1)}, u32[]{:S(2)}, u32[]{:S(2)}) collective-permute-start(bf16[144,3072]{1,0:T(8,128)(2,1)S(1)} %shard_map.89.refs_4_.refs_0_), channel_id=1, source_target_pairs={{0,1},{1,0},{2,3},{3,2},{4,5},{5,4},{6,7},{7,6},{8,9},{9,8},{10,11... | collective-permute-start | bytes 2654216 | tf_op jit(solution)/shard_map/ppermute | solution.py:298
  100.9 2.5 %collective-permute-start.13 = (bf16[256,128]{1,0:T(8,128)(2,1)S(1)}, bf16[256,128]{1,0:T(8,128)(2,1)S(1)}, u32[]{:S(2)}, u32[]{:S(2)}) collective-permute-start(bf16[256,128]{1,0:T(8,128)(2,1)S(1)} %shard_map.88.refs_2_), channel_id=1, source_target_pairs={{0,1},{1,0},{2,3},{3,2},{4,5},{5,4},{6,7},{7,6},{8,9},{9,8},{10,11... | collective-permute-start | bytes 196616 | tf_op jit(solution)/shard_map/ppermute | solution.py:298
  103.7 23.9 %collective-permute-start.16 = (bf16[80,6144]{1,0:T(8,128)(2,1)S(1)}, bf16[80,6144]{1,0:T(8,128)(2,1)S(1)}, u32[]{:S(2)}, u32[]{:S(2)}) collective-permute-start(bf16[80,6144]{1,0:T(8,128)(2,1)S(1)} %shard_map.90.refs_4_.refs_0_), channel_id=1, source_target_pairs={{0,2},{2,0},{1,3},{3,1},{4,6},{6,4},{5,7},{7,5},{8,10},{10,8},{9,1... | collective-permute-start | bytes 2949128 | tf_op jit(solution)/shard_map/ppermute | solution.py:304
  110.7 1.9 %collective-permute-start.15 = (bf16[144,1536]{1,0:T(8,128)(2,1)S(1)}, bf16[144,1536]{1,0:T(8,128)(2,1)S(1)}, u32[]{:S(2)}, u32[]{:S(2)}) collective-permute-start(bf16[144,1536]{1,0:T(8,128)(2,1)S(1)} %get-tuple-element.28), channel_id=1, source_target_pairs={{0,1},{1,0},{2,3},{3,2},{4,5},{5,4},{6,7},{7,6},{8,9},{9,8},{10,11... | collective-permute-start | bytes 1327112 | tf_op jit(solution)/shard_map/ppermute | solution.py:298
  113.6 53.6 %reduce-scatter.5.cloned.1.call-start = ((), (), s32[]{:S(2)}) async-start(), calls=%async_computation.3 | async-start | bytes 614400 | tf_op jit(solution)/shard_map/reduce_scatter | solution.py:393
  129.3 2.6 %collective-permute-start.17 = (bf16[80,6144]{1,0:T(8,128)(2,1)S(1)}, bf16[80,6144]{1,0:T(8,128)(2,1)S(1)}, u32[]{:S(2)}, u32[]{:S(2)}) collective-permute-start(bf16[80,6144]{1,0:T(8,128)(2,1)S(1)} %shard_map.94.refs_0_), channel_id=1, source_target_pairs={{0,1},{1,0},{2,3},{3,2},{4,5},{5,4},{6,7},{7,6},{8,9},{9,8},{10,11... | collective-permute-start | bytes 2949128 | tf_op jit(solution)/shard_map/ppermute | solution.py:298
  129.4 13.3 %collective-permute-start.19 = (bf16[32,6144]{1,0:T(8,128)(2,1)S(1)}, bf16[32,6144]{1,0:T(8,128)(2,1)S(1)}, u32[]{:S(2)}, u32[]{:S(2)}) collective-permute-start(bf16[32,6144]{1,0:T(8,128)(2,1)S(1)} %shard_map.91.refs_8_.refs_0_), channel_id=1, source_target_pairs={{0,2},{2,0},{1,3},{3,1},{4,6},{6,4},{5,7},{7,5},{8,10},{10,8},{9,1... | collective-permute-start | bytes 1179656 | tf_op jit(solution)/shard_map/ppermute | solution.py:304
  144.0 1.8 %collective-permute-start.20 = (bf16[32,6144]{1,0:T(8,128)(2,1)S(1)}, bf16[32,6144]{1,0:T(8,128)(2,1)S(1)}, u32[]{:S(2)}, u32[]{:S(2)}) collective-permute-start(bf16[32,6144]{1,0:T(8,128)(2,1)S(1)} %shard_map.97.refs_0_), channel_id=1, source_target_pairs={{0,1},{1,0},{2,3},{3,2},{4,5},{5,4},{6,7},{7,6},{8,9},{9,8},{10,11... | collective-permute-start | bytes 1179656 | tf_op jit(solution)/shard_map/ppermute | solution.py:298
  154.5 6.8 %collective-permute-start.22 = (bf16[32,768]{1,0:T(8,128)(2,1)S(1)}, bf16[32,768]{1,0:T(8,128)(2,1)S(1)}, u32[]{:S(2)}, u32[]{:S(2)}) collective-permute-start(bf16[32,768]{1,0:T(8,128)(2,1)S(1)} %get-tuple-element.41), channel_id=1, source_target_pairs={{0,12},{4,8},{8,4},{12,0},{1,13},{5,9},{9,5},{13,1},{2,14},{6,10},... | collective-permute-start | bytes 147464 | tf_op jit(solution)/shard_map/ppermute | solution.py:321
  157.1 8.8 %collective-permute-start.23 = (bf16[32,768]{1,0:T(8,128)(2,1)S(1)}, bf16[32,768]{1,0:T(8,128)(2,1)S(1)}, u32[]{:S(2)}, u32[]{:S(2)}) collective-permute-start(bf16[32,768]{1,0:T(8,128)(2,1)S(1)} %get-tuple-element.43), channel_id=1, source_target_pairs={{0,8},{4,12},{8,0},{12,4},{1,9},{5,13},{9,1},{13,5},{2,10},{6,14},... | collective-permute-start | bytes 147464 | tf_op jit(solution)/shard_map/ppermute | solution.py:321
  157.1 8.8 %collective-permute-start.24 = (bf16[32,768]{1,0:T(8,128)(2,1)S(1)}, bf16[32,768]{1,0:T(8,128)(2,1)S(1)}, u32[]{:S(2)}, u32[]{:S(2)}) collective-permute-start(bf16[32,768]{1,0:T(8,128)(2,1)S(1)} %get-tuple-element.42), channel_id=1, source_target_pairs={{0,4},{4,0},{8,12},{12,8},{1,5},{5,1},{9,13},{13,9},{2,6},{6,2},{1... | collective-permute-start | bytes 147464 | tf_op jit(solution)/shard_map/ppermute | solution.py:321
  (15 other events, 193.9 us)
Sparse Core Ops, SparseCore 0:
  113.7 24.0 reduce-scatter.2
  144.4 22.7 reduce-scatter.4

commit v17 on v16

--- a/solution.py
+++ b/solution.py
@@ -393,7 +393,7 @@
             return full, lax.psum_scatter(full, "wide", scatter_dimension=1, tiled=True)
 
         terms = output(arrived, arrived_other, pieces[0], (), cuts[0], [halves[-1][0]])
-        earlier = [terms[0], halves[-1][1]]
+        earlier = [terms[0], *(far for _, far in halves)]
         attended = attend(all_red(qkv), q_gain, k_gain, earlier)
         attended_other = swap(attended)
         second = gelu_sum(lead_parts[1], [attended])
@@ -412,9 +412,9 @@
 
         hidden = gelu_sum(coming, [full])
         kept, sent = output(hidden, swap(hidden), slice(0, units), (), cuts[2])
-        outs = [tokens[cut].astype(F32) + got.astype(F32) for cut, got in zip(cuts, scattered)]
-        outs.append(tokens[cuts[2]].astype(F32) + collect(kept, swap(sent), width))
-        return jnp.concatenate(outs, axis=0)
+        outs = [got.astype(F32) for got in scattered]
+        outs.append(collect(kept, swap(sent), width))
+        return tokens.astype(F32) + jnp.concatenate(outs, axis=0)
 
     return body
 

time: 176 us -> 183 us (1.040)
  waiting for transfers between devices: 43.3 us -> 50.7 us
    ppermute x7, waiting for transfers between devices: 20.3 us -> 28.3 us  [all_red(): parts.append(lax.ppermute(x, 'red', pairs))]
  transfers between devices with their start and end apart: 27 -> 27, of which waited for: 16 -> 16; matrix products, arithmetic and copies ran while one was open for 3% -> 3% of each run, Pallas kernels for 24% -> 19%
where the time goes in v17:
time: 183 us
  waiting for transfers between devices  50.7 us (28%)
  Pallas kernels  43.7 us (24%)
  blocking collectives  39.8 us (22%)
  starting transfers between devices  17 us (9%)
  between operations  15.4 us (8%)
  matrix products  8.49 us (5%)
  local copies, waits for them, and re-layouts  4.05 us (2%)
  other arithmetic  3.86 us (2%)
    pallas_call x17, Pallas kernels, call(): pl.pallas_call(body, in_specs=list(specs) + [corner_of(a) for a in earlie...  43.7 us
    ppermute x7, waiting for transfers between devices, all_red(): parts.append(lax.ppermute(x, 'red', pairs))  28.3 us
    all_gather x1, blocking collectives, body(): lead = lax.all_gather(lead, 'wide', axis=1, tiled=True)  23 us
    all_gather x1, blocking collectives, body(): rest = lax.all_gather(rest, 'wide', axis=1, tiled=True)  16.8 us
    ppermute x15, waiting for transfers between devices, swap(): return lax.ppermute(x, 'tok', [(0, 1), (1, 0)])  14.2 us
    ppermute x7, starting transfers between devices, all_red(): parts.append(lax.ppermute(x, 'red', pairs))  8.84 us
    dot_general x2, matrix products, project(): part = jnp.dot(both, weight, preferred_element_type=F32)  8.49 us
    ppermute x3, waiting for transfers between devices, collect(): total = total + lax.ppermute(block(chip ^ k), 'wide', pairs).astype(F32)  6.89 us
  transfers between devices with their start and end apart: 27, of which 16 were waited for; matrix products, arithmetic and copies ran while one was open for 3% of the time, Pallas kernels for 19%

profile of v17, /device:TPU:0, one launch (start us, length us, event | category | flops | bytes accessed | tf_op | source)
XLA Modules:
  0.0 182.9 jit_solution(12614127566895885864)
XLA Ops:
  8.2 23.0 %all_gather.6 = bf16[152,3072]{1,0:T(8,128)(2,1)S(1)} all-gather(bf16[152,768]{1,0:T(8,128)(2,1)S(1)} %pad_maximum_fusion.2), channel_id=1, replica_groups=mesh['grp'=2,'wide'=4,'red'=2,'tok'=2] {'wide'}, dimensions={1}, use_global_device_ids=true | all-gather | bytes 1167360 | tf_op jit(solution)/shard_map/all_gather | solution.py:337
  31.5 1.6 collective-permute-start
  33.1 2.1 %collective-permute-done = f32[2,144]{1,0:T(2,128)S(1)} collective-permute-done((f32[2,144]{1,0:T(2,128)S(1)}, f32[2,144]{1,0:T(2,128)S(1)}, u32[]{:S(2)}, u32[]{:S(2)}) %collective-permute-start) | collective-permute-done | bytes 1184 | tf_op jit(solution)/shard_map/ppermute | solution.py:304
  35.8 1.8 collective-permute-done.1
  37.6 5.6 %fusion.2 = f32[288,3072]{1,0:T(8,128)S(1)} fusion(bf16[1536,6144]{1,0:T(8,128)(2,1)} %refs_2_.8, bf16[144,1536]{1,0:T(8,128)(2,1)S(1)} %collective-permute-done.1, bf16[144,1536]{1,0:T(8,128)(2,1)S(1)} %get-tuple-element.37), kind=kOutput, calls=%fused_computation.2 | convolution fusion | flops 2719678464 | bytes 13860864 | tf_op jit(solution)/shard_map/dot_general | solution.py:354
  43.5 2.3 %collective-permute-done.2 = bf16[144,3072]{1,0:T(8,128)(2,1)S(1)} collective-permute-done((bf16[144,3072]{1,0:T(8,128)(2,1)S(1)}, bf16[144,3072]{1,0:T(8,128)(2,1)S(1)}, u32[]{:S(2)}, u32[]{:S(2)}) %collective-permute-start.2) | collective-permute-done | bytes 884768 | tf_op jit(solution)/shard_map/ppermute | solution.py:298
  48.7 16.8 %all_gather.7 = bf16[112,3072]{1,0:T(8,128)(2,1)S(1)} all-gather(bf16[112,768]{1,0:T(8,128)(2,1)S(1)} %slice_add_fusion.2), channel_id=1, replica_groups=mesh['grp'=2,'wide'=4,'red'=2,'tok'=2] {'wide'}, dimensions={1}, use_global_device_ids=true | all-gather | bytes 860160 | tf_op jit(solution)/shard_map/all_gather | solution.py:365
  66.6 2.9 %fusion = f32[288,3072]{1,0:T(8,128)S(1)} fusion(bf16[1536,6144]{1,0:T(8,128)(2,1)S(1)} %bitcast.29, bf16[144,1536]{1,0:T(8,128)(2,1)S(1)} %get-tuple-element.46, bf16[144,1536]{1,0:T(8,128)(2,1)S(1)} %get-tuple-element.47), kind=kOutput, calls=%fused_computation | convolution fusion | flops 2719678464 | bytes 13860864 | tf_op jit(solution)/shard_map/dot_general | solution.py:354
  73.0 1.8 %collective-permute-done.7.refs_1_ = bf16[112,1536]{1,0:T(8,128)(2,1)S(1)} collective-permute-done((bf16[112,1536]{1,0:T(8,128)(2,1)S(1)}, bf16[112,1536]{1,0:T(8,128)(2,1)S(1)}, u32[]{:S(2)}, u32[]{:S(2)}) %collective-permute-start.7) | collective-permute-done | bytes 344096 | tf_op jit(solution)/shard_map/ppermute | solution.py:298
  76.2 5.7 %shard_map.85 = (bf16[112,4096]{1,0:T(8,128)(2,1)S(1)}, bf16[112,4096]{1,0:T(8,128)(2,1)S(1)}) custom-call(bf16[112,1536]{1,0:T(8,128)(2,1)S(1)} %get-tuple-element.40.refs_0_, bf16[112,1536]{1,0:T(8,128)(2,1)S(1)} %collective-permute-done.7.refs_1_, bf16[1536,6144]{1,0:T(8,128)(2,1)} %refs_2_.8, bf16[256,384]{1,0:T(8,128)(2,1)S(1)} %get-tuple-element.19.refs_0_.refs_3_), custom_call_target="tpu_custom_call" | custom-call | tf_op jit(solution)/shard_map/pallas_call | solution.py:63
  83.9 3.5 %shard_map.86 = (bf16[112,2048]{1,0:T(8,128)(2,1)S(1)}, bf16[112,2048]{1,0:T(8,128)(2,1)S(1)}) custom-call(bf16[112,1536]{1,0:T(8,128)(2,1)S(1)} %get-tuple-element.40.refs_0_, bf16[112,1536]{1,0:T(8,128)(2,1)S(1)} %collective-permute-done.7.refs_1_, bf16[1536,6144]{1,0:T(8,128)(2,1)} %refs_2_.8, bf16[112,4096]{1,0:T(8,128)(2,1)S(1)} %get-tuple-element.21.refs_3_.refs_0_), custom_call_target="tpu_custom_call" | custom-call | tf_op jit(solution)/shard_map/pallas_call | solution.py:63
  88.0 1.6 collective-permute-done.9.refs_1_
  90.3 5.4 %shard_map.87 = (f32[144,1536]{1,0:T(8,128)S(1)}, f32[144,1536]{1,0:T(8,128)S(1)}) custom-call(bf16[144,3072]{1,0:T(8,128)(2,1)S(1)} %shard_map.82.refs_0_, bf16[144,3072]{1,0:T(8,128)(2,1)S(1)} %collective-permute-done.8.refs_3_.refs_1_, bf16[6144,1536]{1,0:T(8,128)(2,1)} %refs_2_.13, bf16[112,2048]{1,0:T(8,128)(2,1)S(1)} %get-tuple-element.22.refs_3_.refs_2_), custom_call_target="tpu_custom_call" | custom-call | tf_op jit(solution)/shard_map/pallas_call | solution.py:63
  95.7 12.6 %collective-permute-done.10.refs_1_ = bf16[256,384]{1,0:T(8,128)(2,1)S(1)} collective-permute-done((bf16[256,384]{1,0:T(8,128)(2,1)S(1)}, bf16[256,384]{1,0:T(8,128)(2,1)S(1)}, u32[]{:S(2)}, u32[]{:S(2)}) %collective-permute-start.10) | collective-permute-done | bytes 196640 | tf_op jit(solution)/shard_map/ppermute | solution.py:304
  112.5 5.3 %shard_map.92 = (bf16[144,1536]{1,0:T(8,128)(2,1)S(1)}, bf16[144,1536]{1,0:T(8,128)(2,1)S(1)}) custom-call(bf16[144,3072]{1,0:T(8,128)(2,1)S(1)} %shard_map.89.refs_4_.refs_0_, bf16[144,3072]{1,0:T(8,128)(2,1)S(1)} %collective-permute-done.13.refs_1_, bf16[6144,1536]{1,0:T(8,128)(2,1)} %refs_2_.13, f32[144,1536]{1,0:T(8,128)S(1)} %get-tuple-element.23.refs_4_.refs_3_, ...), custom_call_target="tpu_custom_call" | custom-call | tf_op jit(solution)/shard_map/pallas_call | solution.py:63
  118.1 1.6 collective-permute-done.15.refs_1_
  121.0 13.6 %collective-permute-done.16.refs_1_ = bf16[80,6144]{1,0:T(8,128)(2,1)S(1)} collective-permute-done((bf16[80,6144]{1,0:T(8,128)(2,1)S(1)}, bf16[80,6144]{1,0:T(8,128)(2,1)S(1)}, u32[]{:S(2)}, u32[]{:S(2)}) %collective-permute-start.16) | collective-permute-done | bytes 983072 | tf_op jit(solution)/shard_map/ppermute | solution.py:304
  134.6 1.7 shard_map.94.refs_0_
  138.9 7.4 %shard_map.95 = (bf16[80,1536]{1,0:T(8,128)(2,1)S(1)}, bf16[80,1536]{1,0:T(8,128)(2,1)S(1)}) custom-call(bf16[80,6144]{1,0:T(8,128)(2,1)S(1)} %shard_map.94.refs_0_, bf16[80,6144]{1,0:T(8,128)(2,1)S(1)} %collective-permute-done.17.refs_1_, bf16[6144,1536]{1,0:T(8,128)(2,1)} %refs_2_.13, bf16[80,128]{1,0:T(8,128)(2,1)S(1)} %slice.112.refs_3_, ...), custom_call_target="tpu_custom_call" | custom-call | tf_op jit(solution)/shard_map/pallas_call | solution.py:63
  152.8 7.3 %shard_map.98 = (bf16[32,1536]{1,0:T(8,128)(2,1)S(1)}, bf16[32,1536]{1,0:T(8,128)(2,1)S(1)}) custom-call(bf16[32,6144]{1,0:T(8,128)(2,1)S(1)} %shard_map.97.refs_0_, bf16[32,6144]{1,0:T(8,128)(2,1)S(1)} %collective-permute-done.20.refs_1_, bf16[6144,1536]{1,0:T(8,128)(2,1)} %refs_2_.13, bf16[32,128]{1,0:T(8,128)(2,1)S(1)} %slice.114.refs_3_, ...), custom_call_target="tpu_custom_call" | custom-call | tf_op jit(solution)/shard_map/pallas_call | solution.py:63
  161.5 2.6 %collective-permute-start.22 = (bf16[32,768]{1,0:T(8,128)(2,1)S(1)}, bf16[32,768]{1,0:T(8,128)(2,1)S(1)}, u32[]{:S(2)}, u32[]{:S(2)}) collective-permute-start(bf16[32,768]{1,0:T(8,128)(2,1)S(1)} %get-tuple-element.41), channel_id=1, source_target_pairs={{0,12},{4,8},{8,4},{12,0},{1,13},{5,9},{9,5},{13,1},{2,14},{6,10},... | collective-permute-start | bytes 147464 | tf_op jit(solution)/shard_map/ppermute | solution.py:321
  164.1 1.9 %collective-permute-start.24 = (bf16[32,768]{1,0:T(8,128)(2,1)S(1)}, bf16[32,768]{1,0:T(8,128)(2,1)S(1)}, u32[]{:S(2)}, u32[]{:S(2)}) collective-permute-start(bf16[32,768]{1,0:T(8,128)(2,1)S(1)} %get-tuple-element.42), channel_id=1, source_target_pairs={{0,4},{4,0},{8,12},{12,8},{1,5},{5,1},{9,13},{13,9},{2,6},{6,2},{1... | collective-permute-start | bytes 147464 | tf_op jit(solution)/shard_map/ppermute | solution.py:321
  166.0 2.3 %collective-permute-done.22 = bf16[32,768]{1,0:T(8,128)(2,1)S(1)} collective-permute-done((bf16[32,768]{1,0:T(8,128)(2,1)S(1)}, bf16[32,768]{1,0:T(8,128)(2,1)S(1)}, u32[]{:S(2)}, u32[]{:S(2)}) %collective-permute-start.22) | collective-permute-done | bytes 49184 | tf_op jit(solution)/shard_map/ppermute | solution.py:321
  168.3 4.6 %collective-permute-done.23 = bf16[32,768]{1,0:T(8,128)(2,1)S(1)} collective-permute-done((bf16[32,768]{1,0:T(8,128)(2,1)S(1)}, bf16[32,768]{1,0:T(8,128)(2,1)S(1)}, u32[]{:S(2)}, u32[]{:S(2)}) %collective-permute-start.23) | collective-permute-done | bytes 49184 | tf_op jit(solution)/shard_map/ppermute | solution.py:321
  (119 shorter events, 32.4 us)
Async XLA Ops:
  6.5 141.4 %reduce-scatter.3.cloned.1.call-start = ((), (), s32[]{:S(2)}) async-start(), calls=%async_computation.2 | async-start | bytes 1105920 | tf_op jit(solution)/shard_map/reduce_scatter | solution.py:393
  31.5 3.6 %collective-permute-start = (f32[2,144]{1,0:T(2,128)S(1)}, f32[2,144]{1,0:T(2,128)S(1)}, u32[]{:S(2)}, u32[]{:S(2)}) collective-permute-start(f32[2,144]{1,0:T(2,128)S(1)} %pad_maximum_fusion.3), channel_id=1, source_target_pairs={{0,2},{2,0},{1,3},{3,1},{4,6},{6,4},{5,7},{7,5},{8,10},{10,8},{9,1... | collective-permute-start | bytes 3464 | tf_op jit(solution)/shard_map/ppermute | solution.py:304
  35.7 1.9 %collective-permute-start.1 = (bf16[144,1536]{1,0:T(8,128)(2,1)S(1)}, bf16[144,1536]{1,0:T(8,128)(2,1)S(1)}, u32[]{:S(2)}, u32[]{:S(2)}) collective-permute-start(bf16[144,1536]{1,0:T(8,128)(2,1)S(1)} %get-tuple-element.38), channel_id=1, source_target_pairs={{0,1},{1,0},{2,3},{3,2},{4,5},{5,4},{6,7},{7,6},{8,9},{9,8},{10,11... | collective-permute-start | bytes 1327112 | tf_op jit(solution)/shard_map/ppermute | solution.py:298
  43.3 2.5 %collective-permute-start.2 = (bf16[144,3072]{1,0:T(8,128)(2,1)S(1)}, bf16[144,3072]{1,0:T(8,128)(2,1)S(1)}, u32[]{:S(2)}, u32[]{:S(2)}) collective-permute-start(bf16[144,3072]{1,0:T(8,128)(2,1)S(1)} %slice.138), channel_id=1, source_target_pairs={{0,1},{1,0},{2,3},{3,2},{4,5},{5,4},{6,7},{7,6},{8,9},{9,8},{10,11... | collective-permute-start | bytes 2654216 | tf_op jit(solution)/shard_map/ppermute | solution.py:298
  46.5 23.2 %collective-permute-start.6 = (bf16[144,3072]{1,0:T(8,128)(2,1)S(1)}, bf16[144,3072]{1,0:T(8,128)(2,1)S(1)}, u32[]{:S(2)}, u32[]{:S(2)}) collective-permute-start(bf16[144,3072]{1,0:T(8,128)(2,1)S(1)} %fusion.9.refs_0_), channel_id=1, source_target_pairs={{0,2},{2,0},{1,3},{3,1},{4,6},{6,4},{5,7},{7,5},{8,10},{10,8},{9,1... | collective-permute-start | bytes 2654216 | tf_op jit(solution)/shard_map/ppermute | solution.py:304
  65.8 5.8 %collective-permute-start.5 = (f32[2,112]{1,0:T(2,128)S(1)}, f32[2,112]{1,0:T(2,128)S(1)}, u32[]{:S(2)}, u32[]{:S(2)}) collective-permute-start(f32[2,112]{1,0:T(2,128)S(1)} %pad_maximum_fusion.4), channel_id=1, source_target_pairs={{0,2},{2,0},{1,3},{3,1},{4,6},{6,4},{5,7},{7,5},{8,10},{10,8},{9,1... | collective-permute-start | bytes 2696 | tf_op jit(solution)/shard_map/ppermute | solution.py:304
  69.6 3.1 %collective-permute-start.3 = (bf16[144,3072]{1,0:T(8,128)(2,1)S(1)}, bf16[144,3072]{1,0:T(8,128)(2,1)S(1)}, u32[]{:S(2)}, u32[]{:S(2)}) collective-permute-start(bf16[144,3072]{1,0:T(8,128)(2,1)S(1)} %slice.137), channel_id=1, source_target_pairs={{0,1},{1,0},{2,3},{3,2},{4,5},{5,4},{6,7},{7,6},{8,9},{9,8},{10,11... | collective-permute-start | bytes 2654216 | tf_op jit(solution)/shard_map/ppermute | solution.py:298
  71.7 3.1 %collective-permute-start.8 = (bf16[144,3072]{1,0:T(8,128)(2,1)S(1)}, bf16[144,3072]{1,0:T(8,128)(2,1)S(1)}, u32[]{:S(2)}, u32[]{:S(2)}) collective-permute-start(bf16[144,3072]{1,0:T(8,128)(2,1)S(1)} %shard_map.82.refs_0_), channel_id=1, source_target_pairs={{0,1},{1,0},{2,3},{3,2},{4,5},{5,4},{6,7},{7,6},{8,9},{9,8},{10,11... | collective-permute-start | bytes 2654216 | tf_op jit(solution)/shard_map/ppermute | solution.py:298
  72.6 2.2 %collective-permute-start.7 = (bf16[112,1536]{1,0:T(8,128)(2,1)S(1)}, bf16[112,1536]{1,0:T(8,128)(2,1)S(1)}, u32[]{:S(2)}, u32[]{:S(2)}) collective-permute-start(bf16[112,1536]{1,0:T(8,128)(2,1)S(1)} %get-tuple-element.39), channel_id=1, source_target_pairs={{0,1},{1,0},{2,3},{3,2},{4,5},{5,4},{6,7},{7,6},{8,9},{9,8},{10,11... | collective-permute-start | bytes 1032200 | tf_op jit(solution)/shard_map/ppermute | solution.py:298
  82.0 26.3 %collective-permute-start.11 = (bf16[112,4096]{1,0:T(8,128)(2,1)S(1)}, bf16[112,4096]{1,0:T(8,128)(2,1)S(1)}, u32[]{:S(2)}, u32[]{:S(2)}) collective-permute-start(bf16[112,4096]{1,0:T(8,128)(2,1)S(1)} %get-tuple-element.24), channel_id=1, source_target_pairs={{0,1},{1,0},{2,3},{3,2},{4,5},{5,4},{6,7},{7,6},{8,9},{9,8},{10,11... | collective-permute-start | bytes 2752520 | tf_op jit(solution)/shard_map/ppermute | solution.py:298
  82.4 26.7 %collective-permute-start.4 = (bf16[144,3072]{1,0:T(8,128)(2,1)S(1)}, bf16[144,3072]{1,0:T(8,128)(2,1)S(1)}, u32[]{:S(2)}, u32[]{:S(2)}) collective-permute-start(bf16[144,3072]{1,0:T(8,128)(2,1)S(1)} %fusion.8.refs_4_.refs_0_), channel_id=1, source_target_pairs={{0,2},{2,0},{1,3},{3,1},{4,6},{6,4},{5,7},{7,5},{8,10},{10,8},{9,1... | collective-permute-start | bytes 2654216 | tf_op jit(solution)/shard_map/ppermute | solution.py:304
  87.4 20.9 %collective-permute-start.12 = (bf16[112,2048]{1,0:T(8,128)(2,1)S(1)}, bf16[112,2048]{1,0:T(8,128)(2,1)S(1)}, u32[]{:S(2)}, u32[]{:S(2)}) collective-permute-start(bf16[112,2048]{1,0:T(8,128)(2,1)S(1)} %get-tuple-element.25), channel_id=1, source_target_pairs={{0,1},{1,0},{2,3},{3,2},{4,5},{5,4},{6,7},{7,6},{8,9},{9,8},{10,11... | collective-permute-start | bytes 1376264 | tf_op jit(solution)/shard_map/ppermute | solution.py:298
  87.5 2.1 %collective-permute-start.9 = (bf16[256,384]{1,0:T(8,128)(2,1)S(1)}, bf16[256,384]{1,0:T(8,128)(2,1)S(1)}, u32[]{:S(2)}, u32[]{:S(2)}) collective-permute-start(bf16[256,384]{1,0:T(8,128)(2,1)S(1)} %get-tuple-element.20), channel_id=1, source_target_pairs={{0,1},{1,0},{2,3},{3,2},{4,5},{5,4},{6,7},{7,6},{8,9},{9,8},{10,11... | collective-permute-start | bytes 589832 | tf_op jit(solution)/shard_map/ppermute | solution.py:298
  89.7 18.7 %collective-permute-start.10 = (bf16[256,384]{1,0:T(8,128)(2,1)S(1)}, bf16[256,384]{1,0:T(8,128)(2,1)S(1)}, u32[]{:S(2)}, u32[]{:S(2)}) collective-permute-start(bf16[256,384]{1,0:T(8,128)(2,1)S(1)} %shard_map.84.refs_0_), channel_id=1, source_target_pairs={{0,2},{2,0},{1,3},{3,1},{4,6},{6,4},{5,7},{7,5},{8,10},{10,8},{9,1... | collective-permute-start | bytes 589832 | tf_op jit(solution)/shard_map/ppermute | solution.py:304
  109.9 2.6 %collective-permute-start.13 = (bf16[144,3072]{1,0:T(8,128)(2,1)S(1)}, bf16[144,3072]{1,0:T(8,128)(2,1)S(1)}, u32[]{:S(2)}, u32[]{:S(2)}) collective-permute-start(bf16[144,3072]{1,0:T(8,128)(2,1)S(1)} %shard_map.89.refs_4_.refs_0_), channel_id=1, source_target_pairs={{0,1},{1,0},{2,3},{3,2},{4,5},{5,4},{6,7},{7,6},{8,9},{9,8},{10,11... | collective-permute-start | bytes 2654216 | tf_op jit(solution)/shard_map/ppermute | solution.py:298
  110.0 2.5 %collective-permute-start.14 = (bf16[256,128]{1,0:T(8,128)(2,1)S(1)}, bf16[256,128]{1,0:T(8,128)(2,1)S(1)}, u32[]{:S(2)}, u32[]{:S(2)}) collective-permute-start(bf16[256,128]{1,0:T(8,128)(2,1)S(1)} %shard_map.88.refs_2_), channel_id=1, source_target_pairs={{0,1},{1,0},{2,3},{3,2},{4,5},{5,4},{6,7},{7,6},{8,9},{9,8},{10,11... | collective-permute-start | bytes 196616 | tf_op jit(solution)/shard_map/ppermute | solution.py:298
  110.8 23.8 %collective-permute-start.16 = (bf16[80,6144]{1,0:T(8,128)(2,1)S(1)}, bf16[80,6144]{1,0:T(8,128)(2,1)S(1)}, u32[]{:S(2)}, u32[]{:S(2)}) collective-permute-start(bf16[80,6144]{1,0:T(8,128)(2,1)S(1)} %shard_map.90.refs_4_.refs_0_), channel_id=1, source_target_pairs={{0,2},{2,0},{1,3},{3,1},{4,6},{6,4},{5,7},{7,5},{8,10},{10,8},{9,1... | collective-permute-start | bytes 2949128 | tf_op jit(solution)/shard_map/ppermute | solution.py:304
  117.9 1.9 %collective-permute-start.15 = (bf16[144,1536]{1,0:T(8,128)(2,1)S(1)}, bf16[144,1536]{1,0:T(8,128)(2,1)S(1)}, u32[]{:S(2)}, u32[]{:S(2)}) collective-permute-start(bf16[144,1536]{1,0:T(8,128)(2,1)S(1)} %get-tuple-element.28), channel_id=1, source_target_pairs={{0,1},{1,0},{2,3},{3,2},{4,5},{5,4},{6,7},{7,6},{8,9},{9,8},{10,11... | collective-permute-start | bytes 1327112 | tf_op jit(solution)/shard_map/ppermute | solution.py:298
  120.7 53.5 %reduce-scatter.5.cloned.1.call-start = ((), (), s32[]{:S(2)}) async-start(), calls=%async_computation.3 | async-start | bytes 614400 | tf_op jit(solution)/shard_map/reduce_scatter | solution.py:393
  136.3 2.6 %collective-permute-start.17 = (bf16[80,6144]{1,0:T(8,128)(2,1)S(1)}, bf16[80,6144]{1,0:T(8,128)(2,1)S(1)}, u32[]{:S(2)}, u32[]{:S(2)}) collective-permute-start(bf16[80,6144]{1,0:T(8,128)(2,1)S(1)} %shard_map.94.refs_0_), channel_id=1, source_target_pairs={{0,1},{1,0},{2,3},{3,2},{4,5},{5,4},{6,7},{7,6},{8,9},{9,8},{10,11... | collective-permute-start | bytes 2949128 | tf_op jit(solution)/shard_map/ppermute | solution.py:298
  136.4 13.3 %collective-permute-start.19 = (bf16[32,6144]{1,0:T(8,128)(2,1)S(1)}, bf16[32,6144]{1,0:T(8,128)(2,1)S(1)}, u32[]{:S(2)}, u32[]{:S(2)}) collective-permute-start(bf16[32,6144]{1,0:T(8,128)(2,1)S(1)} %shard_map.91.refs_8_.refs_0_), channel_id=1, source_target_pairs={{0,2},{2,0},{1,3},{3,1},{4,6},{6,4},{5,7},{7,5},{8,10},{10,8},{9,1... | collective-permute-start | bytes 1179656 | tf_op jit(solution)/shard_map/ppermute | solution.py:304
  161.5 6.8 %collective-permute-start.22 = (bf16[32,768]{1,0:T(8,128)(2,1)S(1)}, bf16[32,768]{1,0:T(8,128)(2,1)S(1)}, u32[]{:S(2)}, u32[]{:S(2)}) collective-permute-start(bf16[32,768]{1,0:T(8,128)(2,1)S(1)} %get-tuple-element.41), channel_id=1, source_target_pairs={{0,12},{4,8},{8,4},{12,0},{1,13},{5,9},{9,5},{13,1},{2,14},{6,10},... | collective-permute-start | bytes 147464 | tf_op jit(solution)/shard_map/ppermute | solution.py:321
  164.1 8.8 %collective-permute-start.23 = (bf16[32,768]{1,0:T(8,128)(2,1)S(1)}, bf16[32,768]{1,0:T(8,128)(2,1)S(1)}, u32[]{:S(2)}, u32[]{:S(2)}) collective-permute-start(bf16[32,768]{1,0:T(8,128)(2,1)S(1)} %get-tuple-element.43), channel_id=1, source_target_pairs={{0,8},{4,12},{8,0},{12,4},{1,9},{5,13},{9,1},{13,5},{2,10},{6,14},... | collective-permute-start | bytes 147464 | tf_op jit(solution)/shard_map/ppermute | solution.py:321
  164.1 8.8 %collective-permute-start.24 = (bf16[32,768]{1,0:T(8,128)(2,1)S(1)}, bf16[32,768]{1,0:T(8,128)(2,1)S(1)}, u32[]{:S(2)}, u32[]{:S(2)}) collective-permute-start(bf16[32,768]{1,0:T(8,128)(2,1)S(1)} %get-tuple-element.42), channel_id=1, source_target_pairs={{0,4},{4,0},{8,12},{12,8},{1,5},{5,1},{9,13},{13,9},{2,6},{6,2},{1... | collective-permute-start | bytes 147464 | tf_op jit(solution)/shard_map/ppermute | solution.py:321
  (15 other events, 210.4 us)
Sparse Core Ops, SparseCore 0:
  120.9 24.7 reduce-scatter.2
  151.3 22.8 reduce-scatter.4

commit v18 on v14

--- a/solution.py
+++ b/solution.py
@@ -14,7 +14,7 @@
 SHARES = (8, 5, 3)
 LEAD_PIECES = (1, 1)
 REST_PIECES = (2, 1)
-AHEAD = 4
+AHEAD = 6
 GAIN_ROWS = 8
 BF16, F32 = jnp.bfloat16, jnp.float32
 PARAMS = pltpu.CompilerParams(vmem_limit_bytes=48 * 2**20)

time: 174 us -> 174 us (level)
  no operation moved by 1% of the time
where the time goes in v18:
time: 174 us
  Pallas kernels  43.7 us (25%)
  waiting for transfers between devices  42.2 us (24%)
  blocking collectives  39.9 us (23%)
  between operations  15.4 us (9%)
  starting transfers between devices  15.2 us (9%)
  matrix products  7.91 us (5%)
  local copies, waits for them, and re-layouts  5.78 us (3%)
  other arithmetic  3.78 us (2%)
    pallas_call x17, Pallas kernels, call(): pl.pallas_call(body, in_specs=list(specs) + [corner_of(a) for a in earlie...  43.7 us
    all_gather x1, blocking collectives, body(): lead = lax.all_gather(lead, 'wide', axis=1, tiled=True)  21.9 us
    ppermute x7, waiting for transfers between devices, all_red(): parts.append(lax.ppermute(x, 'red', pairs))  18.7 us
    all_gather x1, blocking collectives, body(): rest = lax.all_gather(rest, 'wide', axis=1, tiled=True)  18 us
    ppermute x15, waiting for transfers between devices, swap(): return lax.ppermute(x, 'tok', [(0, 1), (1, 0)])  15.6 us
    dot_general x2, matrix products, project(): part = jnp.dot(both, weight, preferred_element_type=F32)  7.91 us
    ppermute x3, waiting for transfers between devices, collect(): total = total + lax.ppermute(block(chip ^ k), 'wide', pairs).astype(F32)  7.75 us
    ppermute x7, starting transfers between devices, all_red(): parts.append(lax.ppermute(x, 'red', pairs))  7.65 us
  transfers between devices with their start and end apart: 27, of which 16 were waited for; matrix products, arithmetic and copies ran while one was open for 3% of the time, Pallas kernels for 24%

profile of v18, /device:TPU:0, one launch (start us, length us, event | category | flops | bytes accessed | tf_op | source)
XLA Modules:
  0.0 173.8 jit_solution(3202930515528654684)
XLA Ops:
  8.2 21.9 %all_gather.6 = bf16[136,3072]{1,0:T(8,128)(2,1)S(1)} all-gather(bf16[136,768]{1,0:T(8,128)(2,1)S(1)} %pad_maximum_fusion.5), channel_id=1, replica_groups=mesh['grp'=2,'wide'=4,'red'=2,'tok'=2] {'wide'}, dimensions={1}, use_global_device_ids=true | all-gather | bytes 1044480 | tf_op jit(solution)/shard_map/all_gather | solution.py:337
  31.9 2.1 %collective-permute-done = f32[2,128]{1,0:T(2,128)S(1)} collective-permute-done((f32[2,128]{1,0:T(2,128)S(1)}, f32[2,128]{1,0:T(2,128)S(1)}, u32[]{:S(2)}, u32[]{:S(2)}) %collective-permute-start) | collective-permute-done | bytes 1056 | tf_op jit(solution)/shard_map/ppermute | solution.py:304
  34.5 1.7 collective-permute-done.1
  36.2 5.3 %fusion.2 = f32[256,3072]{1,0:T(8,128)S(1)} fusion(bf16[1536,6144]{1,0:T(8,128)(2,1)} %refs_2_.8, bf16[128,1536]{1,0:T(8,128)(2,1)S(1)} %get-tuple-element.40, bf16[128,1536]{1,0:T(8,128)(2,1)S(1)} %collective-permute-done.1), kind=kOutput, calls=%fused_computation.2 | convolution fusion | flops 2417491968 | bytes 13369344 | tf_op jit(solution)/shard_map/dot_general | solution.py:354
  41.9 2.1 %collective-permute-done.2 = bf16[128,3072]{1,0:T(8,128)(2,1)S(1)} collective-permute-done((bf16[128,3072]{1,0:T(8,128)(2,1)S(1)}, bf16[128,3072]{1,0:T(8,128)(2,1)S(1)}, u32[]{:S(2)}, u32[]{:S(2)}) %collective-permute-start.2) | collective-permute-done | bytes 786464 | tf_op jit(solution)/shard_map/ppermute | solution.py:298
  46.9 18.0 %all_gather.7 = bf16[128,3072]{1,0:T(8,128)(2,1)S(1)} all-gather(bf16[128,768]{1,0:T(8,128)(2,1)S(1)} %slice_add_fusion.2), channel_id=1, replica_groups=mesh['grp'=2,'wide'=4,'red'=2,'tok'=2] {'wide'}, dimensions={1}, use_global_device_ids=true | all-gather | bytes 983040 | tf_op jit(solution)/shard_map/all_gather | solution.py:365
  65.9 2.6 %fusion = f32[256,3072]{1,0:T(8,128)S(1)} fusion(bf16[1536,6144]{1,0:T(8,128)(2,1)S(1)} %copy-done.6, bf16[128,1536]{1,0:T(8,128)(2,1)S(1)} %get-tuple-element.44, bf16[128,1536]{1,0:T(8,128)(2,1)S(1)} %get-tuple-element.45), kind=kOutput, calls=%fused_computation | convolution fusion | flops 2417491968 | bytes 13369344 | tf_op jit(solution)/shard_map/dot_general | solution.py:354
  71.9 1.6 collective-permute-start.4
  76.1 6.1 %shard_map.85 = (bf16[128,4096]{1,0:T(8,128)(2,1)S(1)}, bf16[128,4096]{1,0:T(8,128)(2,1)S(1)}) custom-call(bf16[128,1536]{1,0:T(8,128)(2,1)S(1)} %get-tuple-element.38.refs_0_, bf16[128,1536]{1,0:T(8,128)(2,1)S(1)} %collective-permute-done.7.refs_1_, bf16[1536,6144]{1,0:T(8,128)(2,1)} %refs_2_.8, bf16[256,384]{1,0:T(8,128)(2,1)S(1)} %get-tuple-element.19.refs_0_.refs_3_), custom_call_target="tpu_custom_call" | custom-call | tf_op jit(solution)/shard_map/pallas_call | solution.py:63
  82.1 3.7 %shard_map.86 = (bf16[128,2048]{1,0:T(8,128)(2,1)S(1)}, bf16[128,2048]{1,0:T(8,128)(2,1)S(1)}) custom-call(bf16[128,1536]{1,0:T(8,128)(2,1)S(1)} %get-tuple-element.38.refs_0_, bf16[128,1536]{1,0:T(8,128)(2,1)S(1)} %collective-permute-done.7.refs_1_, bf16[1536,6144]{1,0:T(8,128)(2,1)} %refs_2_.8, bf16[128,4096]{1,0:T(8,128)(2,1)S(1)} %get-tuple-element.21.refs_3_.refs_0_), custom_call_target="tpu_custom_call" | custom-call | tf_op jit(solution)/shard_map/pallas_call | solution.py:63
  86.7 3.0 %collective-permute-done.9.refs_1_ = bf16[256,384]{1,0:T(8,128)(2,1)S(1)} collective-permute-done((bf16[256,384]{1,0:T(8,128)(2,1)S(1)}, bf16[256,384]{1,0:T(8,128)(2,1)S(1)}, u32[]{:S(2)}, u32[]{:S(2)}) %collective-permute-start.9) | collective-permute-done | bytes 196640 | tf_op jit(solution)/shard_map/ppermute | solution.py:298
  90.3 5.1 %shard_map.87 = (f32[128,1536]{1,0:T(8,128)S(1)}, f32[128,1536]{1,0:T(8,128)S(1)}) custom-call(bf16[128,3072]{1,0:T(8,128)(2,1)S(1)} %shard_map.82.refs_0_, bf16[128,3072]{1,0:T(8,128)(2,1)S(1)} %collective-permute-done.8.refs_3_.refs_1_, bf16[6144,1536]{1,0:T(8,128)(2,1)} %refs_2_.13, bf16[128,2048]{1,0:T(8,128)(2,1)S(1)} %get-tuple-element.22.refs_3_.refs_2_), custom_call_target="tpu_custom_call" | custom-call | tf_op jit(solution)/shard_map/pallas_call | solution.py:63
  101.8 5.3 %shard_map.92 = (bf16[128,1536]{1,0:T(8,128)(2,1)S(1)}, bf16[128,1536]{1,0:T(8,128)(2,1)S(1)}) custom-call(bf16[128,3072]{1,0:T(8,128)(2,1)S(1)} %shard_map.89.refs_4_.refs_0_, bf16[128,3072]{1,0:T(8,128)(2,1)S(1)} %collective-permute-done.12.refs_1_, bf16[6144,1536]{1,0:T(8,128)(2,1)} %refs_2_.13, f32[128,1536]{1,0:T(8,128)S(1)} %get-tuple-element.23.refs_4_.refs_3_, ...), custom_call_target="tpu_custom_call" | custom-call | tf_op jit(solution)/shard_map/pallas_call | solution.py:63
  110.1 12.8 %collective-permute-done.16.refs_1_ = bf16[80,6144]{1,0:T(8,128)(2,1)S(1)} collective-permute-done((bf16[80,6144]{1,0:T(8,128)(2,1)S(1)}, bf16[80,6144]{1,0:T(8,128)(2,1)S(1)}, u32[]{:S(2)}, u32[]{:S(2)}) %collective-permute-start.16) | collective-permute-done | bytes 983072 | tf_op jit(solution)/shard_map/ppermute | solution.py:304
  122.9 1.7 shard_map.94.refs_0_
  125.6 1.6 collective-permute-done.17.refs_1_
  127.2 7.3 %shard_map.95 = (bf16[80,1536]{1,0:T(8,128)(2,1)S(1)}, bf16[80,1536]{1,0:T(8,128)(2,1)S(1)}) custom-call(bf16[80,6144]{1,0:T(8,128)(2,1)S(1)} %shard_map.94.refs_0_, bf16[80,6144]{1,0:T(8,128)(2,1)S(1)} %collective-permute-done.17.refs_1_, bf16[6144,1536]{1,0:T(8,128)(2,1)} %refs_2_.13, bf16[80,128]{1,0:T(8,128)(2,1)S(1)} %slice.119.refs_3_, ...), custom_call_target="tpu_custom_call" | custom-call | tf_op jit(solution)/shard_map/pallas_call | solution.py:63
  137.9 2.5 %collective-permute-done.19.refs_1_ = bf16[48,6144]{1,0:T(8,128)(2,1)S(1)} collective-permute-done((bf16[48,6144]{1,0:T(8,128)(2,1)S(1)}, bf16[48,6144]{1,0:T(8,128)(2,1)S(1)}, u32[]{:S(2)}, u32[]{:S(2)}) %collective-permute-start.19) | collective-permute-done | bytes 589856 | tf_op jit(solution)/shard_map/ppermute | solution.py:304
  142.1 1.8 %collective-permute-done.20.refs_1_ = bf16[48,6144]{1,0:T(8,128)(2,1)S(1)} collective-permute-done((bf16[48,6144]{1,0:T(8,128)(2,1)S(1)}, bf16[48,6144]{1,0:T(8,128)(2,1)S(1)}, u32[]{:S(2)}, u32[]{:S(2)}) %collective-permute-start.20) | collective-permute-done | bytes 589856 | tf_op jit(solution)/shard_map/ppermute | solution.py:298
  143.9 7.3 %shard_map.98 = (bf16[48,1536]{1,0:T(8,128)(2,1)S(1)}, bf16[48,1536]{1,0:T(8,128)(2,1)S(1)}) custom-call(bf16[48,6144]{1,0:T(8,128)(2,1)S(1)} %shard_map.97.refs_0_, bf16[48,6144]{1,0:T(8,128)(2,1)S(1)} %collective-permute-done.20.refs_1_, bf16[6144,1536]{1,0:T(8,128)(2,1)} %refs_2_.13, bf16[48,128]{1,0:T(8,128)(2,1)S(1)} %slice.121.refs_3_, ...), custom_call_target="tpu_custom_call" | custom-call | tf_op jit(solution)/shard_map/pallas_call | solution.py:63
  152.7 1.9 %collective-permute-start.22 = (bf16[48,768]{1,0:T(8,128)(2,1)S(1)}, bf16[48,768]{1,0:T(8,128)(2,1)S(1)}, u32[]{:S(2)}, u32[]{:S(2)}) collective-permute-start(bf16[48,768]{1,0:T(8,128)(2,1)S(1)} %get-tuple-element.41), channel_id=1, source_target_pairs={{0,12},{4,8},{8,4},{12,0},{1,13},{5,9},{9,5},{13,1},{2,14},{6,10},... | collective-permute-start | bytes 221192 | tf_op jit(solution)/shard_map/ppermute | solution.py:321
  154.6 2.6 %collective-permute-start.24 = (bf16[48,768]{1,0:T(8,128)(2,1)S(1)}, bf16[48,768]{1,0:T(8,128)(2,1)S(1)}, u32[]{:S(2)}, u32[]{:S(2)}) collective-permute-start(bf16[48,768]{1,0:T(8,128)(2,1)S(1)} %get-tuple-element.42), channel_id=1, source_target_pairs={{0,4},{4,0},{8,12},{12,8},{1,5},{5,1},{9,13},{13,9},{2,6},{6,2},{1... | collective-permute-start | bytes 221192 | tf_op jit(solution)/shard_map/ppermute | solution.py:321
  157.2 3.2 %collective-permute-done.22 = bf16[48,768]{1,0:T(8,128)(2,1)S(1)} collective-permute-done((bf16[48,768]{1,0:T(8,128)(2,1)S(1)}, bf16[48,768]{1,0:T(8,128)(2,1)S(1)}, u32[]{:S(2)}, u32[]{:S(2)}) %collective-permute-start.22) | collective-permute-done | bytes 73760 | tf_op jit(solution)/shard_map/ppermute | solution.py:321
  160.4 4.5 %collective-permute-done.23 = bf16[48,768]{1,0:T(8,128)(2,1)S(1)} collective-permute-done((bf16[48,768]{1,0:T(8,128)(2,1)S(1)}, bf16[48,768]{1,0:T(8,128)(2,1)S(1)}, u32[]{:S(2)}, u32[]{:S(2)}) %collective-permute-start.23) | collective-permute-done | bytes 73760 | tf_op jit(solution)/shard_map/ppermute | solution.py:321
  (110 shorter events, 32.7 us)
Async XLA Ops:
  6.5 129.6 %reduce-scatter.3.cloned.1.call-start = ((), (), s32[]{:S(2)}) async-start(), calls=%async_computation.2 | async-start | bytes 983040 | tf_op jit(solution)/shard_map/reduce_scatter | solution.py:393
  30.4 3.6 %collective-permute-start = (f32[2,128]{1,0:T(2,128)S(1)}, f32[2,128]{1,0:T(2,128)S(1)}, u32[]{:S(2)}, u32[]{:S(2)}) collective-permute-start(f32[2,128]{1,0:T(2,128)S(1)} %pad_maximum_fusion.6), channel_id=1, source_target_pairs={{0,2},{2,0},{1,3},{3,1},{4,6},{6,4},{5,7},{7,5},{8,10},{10,8},{9,1... | collective-permute-start | bytes 3080 | tf_op jit(solution)/shard_map/ppermute | solution.py:304
  34.4 1.8 %collective-permute-start.1 = (bf16[128,1536]{1,0:T(8,128)(2,1)S(1)}, bf16[128,1536]{1,0:T(8,128)(2,1)S(1)}, u32[]{:S(2)}, u32[]{:S(2)}) collective-permute-start(bf16[128,1536]{1,0:T(8,128)(2,1)S(1)} %get-tuple-element.39), channel_id=1, source_target_pairs={{0,1},{1,0},{2,3},{3,2},{4,5},{5,4},{6,7},{7,6},{8,9},{9,8},{10,11... | collective-permute-start | bytes 1179656 | tf_op jit(solution)/shard_map/ppermute | solution.py:298
  41.7 2.4 %collective-permute-start.2 = (bf16[128,3072]{1,0:T(8,128)(2,1)S(1)}, bf16[128,3072]{1,0:T(8,128)(2,1)S(1)}, u32[]{:S(2)}, u32[]{:S(2)}) collective-permute-start(bf16[128,3072]{1,0:T(8,128)(2,1)S(1)} %slice.152), channel_id=1, source_target_pairs={{0,1},{1,0},{2,3},{3,2},{4,5},{5,4},{6,7},{7,6},{8,9},{9,8},{10,11... | collective-permute-start | bytes 2359304 | tf_op jit(solution)/shard_map/ppermute | solution.py:298
  44.7 24.0 %collective-permute-start.6 = (bf16[128,3072]{1,0:T(8,128)(2,1)S(1)}, bf16[128,3072]{1,0:T(8,128)(2,1)S(1)}, u32[]{:S(2)}, u32[]{:S(2)}) collective-permute-start(bf16[128,3072]{1,0:T(8,128)(2,1)S(1)} %fusion.13.refs_0_), channel_id=1, source_target_pairs={{0,2},{2,0},{1,3},{3,1},{4,6},{6,4},{5,7},{7,5},{8,10},{10,8},{9,1... | collective-permute-start | bytes 2359304 | tf_op jit(solution)/shard_map/ppermute | solution.py:304
  65.3 5.4 %collective-permute-start.5 = (f32[2,128]{1,0:T(2,128)S(1)}, f32[2,128]{1,0:T(2,128)S(1)}, u32[]{:S(2)}, u32[]{:S(2)}) collective-permute-start(f32[2,128]{1,0:T(2,128)S(1)} %pad_maximum_fusion.7), channel_id=1, source_target_pairs={{0,2},{2,0},{1,3},{3,1},{4,6},{6,4},{5,7},{7,5},{8,10},{10,8},{9,1... | collective-permute-start | bytes 3080 | tf_op jit(solution)/shard_map/ppermute | solution.py:304
  68.6 3.1 %collective-permute-start.3 = (bf16[128,3072]{1,0:T(8,128)(2,1)S(1)}, bf16[128,3072]{1,0:T(8,128)(2,1)S(1)}, u32[]{:S(2)}, u32[]{:S(2)}) collective-permute-start(bf16[128,3072]{1,0:T(8,128)(2,1)S(1)} %slice.151), channel_id=1, source_target_pairs={{0,1},{1,0},{2,3},{3,2},{4,5},{5,4},{6,7},{7,6},{8,9},{9,8},{10,11... | collective-permute-start | bytes 2359304 | tf_op jit(solution)/shard_map/ppermute | solution.py:298
  70.7 3.1 %collective-permute-start.8 = (bf16[128,3072]{1,0:T(8,128)(2,1)S(1)}, bf16[128,3072]{1,0:T(8,128)(2,1)S(1)}, u32[]{:S(2)}, u32[]{:S(2)}) collective-permute-start(bf16[128,3072]{1,0:T(8,128)(2,1)S(1)} %shard_map.82.refs_0_), channel_id=1, source_target_pairs={{0,1},{1,0},{2,3},{3,2},{4,5},{5,4},{6,7},{7,6},{8,9},{9,8},{10,11... | collective-permute-start | bytes 2359304 | tf_op jit(solution)/shard_map/ppermute | solution.py:298
  71.6 2.1 %collective-permute-start.7 = (bf16[128,1536]{1,0:T(8,128)(2,1)S(1)}, bf16[128,1536]{1,0:T(8,128)(2,1)S(1)}, u32[]{:S(2)}, u32[]{:S(2)}) collective-permute-start(bf16[128,1536]{1,0:T(8,128)(2,1)S(1)} %get-tuple-element.37), channel_id=1, source_target_pairs={{0,1},{1,0},{2,3},{3,2},{4,5},{5,4},{6,7},{7,6},{8,9},{9,8},{10,11... | collective-permute-start | bytes 1179656 | tf_op jit(solution)/shard_map/ppermute | solution.py:298
  71.9 25.7 %collective-permute-start.4 = (bf16[128,3072]{1,0:T(8,128)(2,1)S(1)}, bf16[128,3072]{1,0:T(8,128)(2,1)S(1)}, u32[]{:S(2)}, u32[]{:S(2)}) collective-permute-start(bf16[128,3072]{1,0:T(8,128)(2,1)S(1)} %fusion.12.refs_4_.refs_0_), channel_id=1, source_target_pairs={{0,2},{2,0},{1,3},{3,1},{4,6},{6,4},{5,7},{7,5},{8,10},{10,8},{9,1... | collective-permute-start | bytes 2359304 | tf_op jit(solution)/shard_map/ppermute | solution.py:304
  85.9 10.9 %collective-permute-start.11 = (bf16[128,2048]{1,0:T(8,128)(2,1)S(1)}, bf16[128,2048]{1,0:T(8,128)(2,1)S(1)}, u32[]{:S(2)}, u32[]{:S(2)}) collective-permute-start(bf16[128,2048]{1,0:T(8,128)(2,1)S(1)} %get-tuple-element.24), channel_id=1, source_target_pairs={{0,1},{1,0},{2,3},{3,2},{4,5},{5,4},{6,7},{7,6},{8,9},{9,8},{10,11... | collective-permute-start | bytes 1572872 | tf_op jit(solution)/shard_map/ppermute | solution.py:298
  86.2 12.2 %collective-permute-start.14 = (bf16[128,4096]{1,0:T(8,128)(2,1)S(1)}, bf16[128,4096]{1,0:T(8,128)(2,1)S(1)}, u32[]{:S(2)}, u32[]{:S(2)}) collective-permute-start(bf16[128,4096]{1,0:T(8,128)(2,1)S(1)} %get-tuple-element.26), channel_id=1, source_target_pairs={{0,1},{1,0},{2,3},{3,2},{4,5},{5,4},{6,7},{7,6},{8,9},{9,8},{10,11... | collective-permute-start | bytes 3145736 | tf_op jit(solution)/shard_map/ppermute | solution.py:298
  86.5 3.2 %collective-permute-start.9 = (bf16[256,384]{1,0:T(8,128)(2,1)S(1)}, bf16[256,384]{1,0:T(8,128)(2,1)S(1)}, u32[]{:S(2)}, u32[]{:S(2)}) collective-permute-start(bf16[256,384]{1,0:T(8,128)(2,1)S(1)} %get-tuple-element.20), channel_id=1, source_target_pairs={{0,1},{1,0},{2,3},{3,2},{4,5},{5,4},{6,7},{7,6},{8,9},{9,8},{10,11... | collective-permute-start | bytes 589832 | tf_op jit(solution)/shard_map/ppermute | solution.py:298
  89.7 7.1 %collective-permute-start.10 = (bf16[256,384]{1,0:T(8,128)(2,1)S(1)}, bf16[256,384]{1,0:T(8,128)(2,1)S(1)}, u32[]{:S(2)}, u32[]{:S(2)}) collective-permute-start(bf16[256,384]{1,0:T(8,128)(2,1)S(1)} %shard_map.84.refs_0_), channel_id=1, source_target_pairs={{0,2},{2,0},{1,3},{3,1},{4,6},{6,4},{5,7},{7,5},{8,10},{10,8},{9,1... | collective-permute-start | bytes 589832 | tf_op jit(solution)/shard_map/ppermute | solution.py:304
  98.3 2.6 %collective-permute-start.12 = (bf16[128,3072]{1,0:T(8,128)(2,1)S(1)}, bf16[128,3072]{1,0:T(8,128)(2,1)S(1)}, u32[]{:S(2)}, u32[]{:S(2)}) collective-permute-start(bf16[128,3072]{1,0:T(8,128)(2,1)S(1)} %shard_map.89.refs_4_.refs_0_), channel_id=1, source_target_pairs={{0,1},{1,0},{2,3},{3,2},{4,5},{5,4},{6,7},{7,6},{8,9},{9,8},{10,11... | collective-permute-start | bytes 2359304 | tf_op jit(solution)/shard_map/ppermute | solution.py:298
  98.6 24.2 %collective-permute-start.16 = (bf16[80,6144]{1,0:T(8,128)(2,1)S(1)}, bf16[80,6144]{1,0:T(8,128)(2,1)S(1)}, u32[]{:S(2)}, u32[]{:S(2)}) collective-permute-start(bf16[80,6144]{1,0:T(8,128)(2,1)S(1)} %shard_map.90.refs_4_.refs_0_), channel_id=1, source_target_pairs={{0,2},{2,0},{1,3},{3,1},{4,6},{6,4},{5,7},{7,5},{8,10},{10,8},{9,1... | collective-permute-start | bytes 2949128 | tf_op jit(solution)/shard_map/ppermute | solution.py:304
  107.1 1.8 %collective-permute-start.15 = (bf16[128,1536]{1,0:T(8,128)(2,1)S(1)}, bf16[128,1536]{1,0:T(8,128)(2,1)S(1)}, u32[]{:S(2)}, u32[]{:S(2)}) collective-permute-start(bf16[128,1536]{1,0:T(8,128)(2,1)S(1)} %get-tuple-element.28), channel_id=1, source_target_pairs={{0,1},{1,0},{2,3},{3,2},{4,5},{5,4},{6,7},{7,6},{8,9},{9,8},{10,11... | collective-permute-start | bytes 1179656 | tf_op jit(solution)/shard_map/ppermute | solution.py:298
  109.9 55.2 %reduce-scatter.5.cloned.1.call-start = ((), (), s32[]{:S(2)}) async-start(), calls=%async_computation.3 | async-start | bytes 614400 | tf_op jit(solution)/shard_map/reduce_scatter | solution.py:393
  124.6 2.6 %collective-permute-start.17 = (bf16[80,6144]{1,0:T(8,128)(2,1)S(1)}, bf16[80,6144]{1,0:T(8,128)(2,1)S(1)}, u32[]{:S(2)}, u32[]{:S(2)}) collective-permute-start(bf16[80,6144]{1,0:T(8,128)(2,1)S(1)} %shard_map.94.refs_0_), channel_id=1, source_target_pairs={{0,1},{1,0},{2,3},{3,2},{4,5},{5,4},{6,7},{7,6},{8,9},{9,8},{10,11... | collective-permute-start | bytes 2949128 | tf_op jit(solution)/shard_map/ppermute | solution.py:298
  124.7 15.7 %collective-permute-start.19 = (bf16[48,6144]{1,0:T(8,128)(2,1)S(1)}, bf16[48,6144]{1,0:T(8,128)(2,1)S(1)}, u32[]{:S(2)}, u32[]{:S(2)}) collective-permute-start(bf16[48,6144]{1,0:T(8,128)(2,1)S(1)} %shard_map.91.refs_8_.refs_0_), channel_id=1, source_target_pairs={{0,2},{2,0},{1,3},{3,1},{4,6},{6,4},{5,7},{7,5},{8,10},{10,8},{9,1... | collective-permute-start | bytes 1769480 | tf_op jit(solution)/shard_map/ppermute | solution.py:304
  141.9 2.1 %collective-permute-start.20 = (bf16[48,6144]{1,0:T(8,128)(2,1)S(1)}, bf16[48,6144]{1,0:T(8,128)(2,1)S(1)}, u32[]{:S(2)}, u32[]{:S(2)}) collective-permute-start(bf16[48,6144]{1,0:T(8,128)(2,1)S(1)} %shard_map.97.refs_0_), channel_id=1, source_target_pairs={{0,1},{1,0},{2,3},{3,2},{4,5},{5,4},{6,7},{7,6},{8,9},{9,8},{10,11... | collective-permute-start | bytes 1769480 | tf_op jit(solution)/shard_map/ppermute | solution.py:298
  152.7 7.7 %collective-permute-start.22 = (bf16[48,768]{1,0:T(8,128)(2,1)S(1)}, bf16[48,768]{1,0:T(8,128)(2,1)S(1)}, u32[]{:S(2)}, u32[]{:S(2)}) collective-permute-start(bf16[48,768]{1,0:T(8,128)(2,1)S(1)} %get-tuple-element.41), channel_id=1, source_target_pairs={{0,12},{4,8},{8,4},{12,0},{1,13},{5,9},{9,5},{13,1},{2,14},{6,10},... | collective-permute-start | bytes 221192 | tf_op jit(solution)/shard_map/ppermute | solution.py:321
  154.6 10.4 %collective-permute-start.23 = (bf16[48,768]{1,0:T(8,128)(2,1)S(1)}, bf16[48,768]{1,0:T(8,128)(2,1)S(1)}, u32[]{:S(2)}, u32[]{:S(2)}) collective-permute-start(bf16[48,768]{1,0:T(8,128)(2,1)S(1)} %get-tuple-element.43), channel_id=1, source_target_pairs={{0,8},{4,12},{8,0},{12,4},{1,9},{5,13},{9,1},{13,5},{2,10},{6,14},... | collective-permute-start | bytes 221192 | tf_op jit(solution)/shard_map/ppermute | solution.py:321
  154.6 10.4 %collective-permute-start.24 = (bf16[48,768]{1,0:T(8,128)(2,1)S(1)}, bf16[48,768]{1,0:T(8,128)(2,1)S(1)}, u32[]{:S(2)}, u32[]{:S(2)}) collective-permute-start(bf16[48,768]{1,0:T(8,128)(2,1)S(1)} %get-tuple-element.42), channel_id=1, source_target_pairs={{0,4},{4,0},{8,12},{12,8},{1,5},{5,1},{9,13},{13,9},{2,6},{6,2},{1... | collective-permute-start | bytes 221192 | tf_op jit(solution)/shard_map/ppermute | solution.py:321
  (11 other events, 70.3 us)
Sparse Core Ops, SparseCore 0:
  110.0 22.4 reduce-scatter.2
  142.2 21.8 reduce-scatter.4

commit v19 on v18

--- a/solution.py
+++ b/solution.py
@@ -44,9 +44,9 @@
     return [slice(a, b) for a, b in zip([0] + ends[:-1], ends)]
 
 
-def steps_of(piece):
+def steps_of(piece, blocks=(512, 384, 256, 128)):
     size = math.gcd(piece.stop - piece.start, piece.start)
-    block = next(b for b in (512, 384, 256, 128) if size % b == 0)
+    block = next(b for b in blocks if size % b == 0)
     return block, (piece.stop - piece.start) // block, piece.start // block
 
 
@@ -71,7 +71,7 @@
 
 def gelu_sum(parts, earlier=()):
     rows, units = parts[0].shape
-    block, steps, _ = steps_of(slice(0, units))
+    block, steps, _ = steps_of(slice(0, units), (1024, 768, 512, 384, 256, 128))
     spec = pl.BlockSpec((rows, block), lambda j: (0, j))
 
     def kernel(ins, outs):

time: 174 us -> 174 us (level)
  no operation moved by 1% of the time
where the time goes in v19:
time: 174 us; the launch traced here: 173 us
  Pallas kernels  43.2 us (25%)
  waiting for transfers between devices  42.2 us (24%)
  blocking collectives  39.9 us (23%)
  between operations  15.4 us (9%)
  starting transfers between devices  15.2 us (9%)
  matrix products  7.91 us (5%)
  local copies, waits for them, and re-layouts  5.78 us (3%)
  other arithmetic  3.78 us (2%)
    pallas_call x17, Pallas kernels, call(): pl.pallas_call(body, in_specs=list(specs) + [corner_of(a) for a in earlie...  43.2 us
    all_gather x1, blocking collectives, body(): lead = lax.all_gather(lead, 'wide', axis=1, tiled=True)  21.9 us
    ppermute x7, waiting for transfers between devices, all_red(): parts.append(lax.ppermute(x, 'red', pairs))  18.7 us
    all_gather x1, blocking collectives, body(): rest = lax.all_gather(rest, 'wide', axis=1, tiled=True)  18 us
    ppermute x15, waiting for transfers between devices, swap(): return lax.ppermute(x, 'tok', [(0, 1), (1, 0)])  15.7 us
    dot_general x2, matrix products, project(): part = jnp.dot(both, weight, preferred_element_type=F32)  7.91 us
    ppermute x3, waiting for transfers between devices, collect(): total = total + lax.ppermute(block(chip ^ k), 'wide', pairs).astype(F32)  7.74 us
    ppermute x7, starting transfers between devices, all_red(): parts.append(lax.ppermute(x, 'red', pairs))  7.63 us
  transfers between devices with their start and end apart: 27, of which 16 were waited for; matrix products, arithmetic and copies ran while one was open for 3% of the time, Pallas kernels for 24%

profile of v19, /device:TPU:0, one launch (start us, length us, event | category | flops | bytes accessed | tf_op | source)
XLA Modules:
  0.0 173.2 jit_solution(7374741020906320494)
XLA Ops:
  8.2 21.9 %all_gather.6 = bf16[136,3072]{1,0:T(8,128)(2,1)S(1)} all-gather(bf16[136,768]{1,0:T(8,128)(2,1)S(1)} %pad_maximum_fusion.5), channel_id=1, replica_groups=mesh['grp'=2,'wide'=4,'red'=2,'tok'=2] {'wide'}, dimensions={1}, use_global_device_ids=true | all-gather | bytes 1044480 | tf_op jit(solution)/shard_map/all_gather | solution.py:337
  30.4 1.6 collective-permute-start
  31.9 2.1 %collective-permute-done = f32[2,128]{1,0:T(2,128)S(1)} collective-permute-done((f32[2,128]{1,0:T(2,128)S(1)}, f32[2,128]{1,0:T(2,128)S(1)}, u32[]{:S(2)}, u32[]{:S(2)}) %collective-permute-start) | collective-permute-done | bytes 1056 | tf_op jit(solution)/shard_map/ppermute | solution.py:304
  34.5 1.7 collective-permute-done.1
  36.2 5.3 %fusion.2 = f32[256,3072]{1,0:T(8,128)S(1)} fusion(bf16[1536,6144]{1,0:T(8,128)(2,1)} %refs_2_.8, bf16[128,1536]{1,0:T(8,128)(2,1)S(1)} %get-tuple-element.40, bf16[128,1536]{1,0:T(8,128)(2,1)S(1)} %collective-permute-done.1), kind=kOutput, calls=%fused_computation.2 | convolution fusion | flops 2417491968 | bytes 13369344 | tf_op jit(solution)/shard_map/dot_general | solution.py:354
  41.9 2.1 %collective-permute-done.2 = bf16[128,3072]{1,0:T(8,128)(2,1)S(1)} collective-permute-done((bf16[128,3072]{1,0:T(8,128)(2,1)S(1)}, bf16[128,3072]{1,0:T(8,128)(2,1)S(1)}, u32[]{:S(2)}, u32[]{:S(2)}) %collective-permute-start.2) | collective-permute-done | bytes 786464 | tf_op jit(solution)/shard_map/ppermute | solution.py:298
  46.9 18.0 %all_gather.7 = bf16[128,3072]{1,0:T(8,128)(2,1)S(1)} all-gather(bf16[128,768]{1,0:T(8,128)(2,1)S(1)} %slice_add_fusion.2), channel_id=1, replica_groups=mesh['grp'=2,'wide'=4,'red'=2,'tok'=2] {'wide'}, dimensions={1}, use_global_device_ids=true | all-gather | bytes 983040 | tf_op jit(solution)/shard_map/all_gather | solution.py:365
  65.9 2.6 %fusion = f32[256,3072]{1,0:T(8,128)S(1)} fusion(bf16[1536,6144]{1,0:T(8,128)(2,1)S(1)} %copy-done.6, bf16[128,1536]{1,0:T(8,128)(2,1)S(1)} %get-tuple-element.44, bf16[128,1536]{1,0:T(8,128)(2,1)S(1)} %get-tuple-element.45), kind=kOutput, calls=%fused_computation | convolution fusion | flops 2417491968 | bytes 13369344 | tf_op jit(solution)/shard_map/dot_general | solution.py:354
  71.8 1.6 collective-permute-start.4
  76.0 6.1 %shard_map.85 = (bf16[128,4096]{1,0:T(8,128)(2,1)S(1)}, bf16[128,4096]{1,0:T(8,128)(2,1)S(1)}) custom-call(bf16[128,1536]{1,0:T(8,128)(2,1)S(1)} %get-tuple-element.38.refs_0_, bf16[128,1536]{1,0:T(8,128)(2,1)S(1)} %collective-permute-done.7.refs_1_, bf16[1536,6144]{1,0:T(8,128)(2,1)} %refs_2_.8, bf16[256,384]{1,0:T(8,128)(2,1)S(1)} %get-tuple-element.19.refs_0_.refs_3_), custom_call_target="tpu_custom_call" | custom-call | tf_op jit(solution)/shard_map/pallas_call | solution.py:63
  82.1 3.7 %shard_map.86 = (bf16[128,2048]{1,0:T(8,128)(2,1)S(1)}, bf16[128,2048]{1,0:T(8,128)(2,1)S(1)}) custom-call(bf16[128,1536]{1,0:T(8,128)(2,1)S(1)} %get-tuple-element.38.refs_0_, bf16[128,1536]{1,0:T(8,128)(2,1)S(1)} %collective-permute-done.7.refs_1_, bf16[1536,6144]{1,0:T(8,128)(2,1)} %refs_2_.8, bf16[128,4096]{1,0:T(8,128)(2,1)S(1)} %get-tuple-element.21.refs_3_.refs_0_), custom_call_target="tpu_custom_call" | custom-call | tf_op jit(solution)/shard_map/pallas_call | solution.py:63
  86.6 3.0 %collective-permute-done.9.refs_1_ = bf16[256,384]{1,0:T(8,128)(2,1)S(1)} collective-permute-done((bf16[256,384]{1,0:T(8,128)(2,1)S(1)}, bf16[256,384]{1,0:T(8,128)(2,1)S(1)}, u32[]{:S(2)}, u32[]{:S(2)}) %collective-permute-start.9) | collective-permute-done | bytes 196640 | tf_op jit(solution)/shard_map/ppermute | solution.py:298
  90.3 5.1 %shard_map.87 = (f32[128,1536]{1,0:T(8,128)S(1)}, f32[128,1536]{1,0:T(8,128)S(1)}) custom-call(bf16[128,3072]{1,0:T(8,128)(2,1)S(1)} %shard_map.82.refs_0_, bf16[128,3072]{1,0:T(8,128)(2,1)S(1)} %collective-permute-done.8.refs_3_.refs_1_, bf16[6144,1536]{1,0:T(8,128)(2,1)} %refs_2_.13, bf16[128,2048]{1,0:T(8,128)(2,1)S(1)} %get-tuple-element.22.refs_3_.refs_2_), custom_call_target="tpu_custom_call" | custom-call | tf_op jit(solution)/shard_map/pallas_call | solution.py:63
  101.6 5.3 %shard_map.92 = (bf16[128,1536]{1,0:T(8,128)(2,1)S(1)}, bf16[128,1536]{1,0:T(8,128)(2,1)S(1)}) custom-call(bf16[128,3072]{1,0:T(8,128)(2,1)S(1)} %shard_map.89.refs_4_.refs_0_, bf16[128,3072]{1,0:T(8,128)(2,1)S(1)} %collective-permute-done.12.refs_1_, bf16[6144,1536]{1,0:T(8,128)(2,1)} %refs_2_.13, f32[128,1536]{1,0:T(8,128)S(1)} %get-tuple-element.23.refs_4_.refs_3_, ...), custom_call_target="tpu_custom_call" | custom-call | tf_op jit(solution)/shard_map/pallas_call | solution.py:63
  109.9 12.8 %collective-permute-done.16.refs_1_ = bf16[80,6144]{1,0:T(8,128)(2,1)S(1)} collective-permute-done((bf16[80,6144]{1,0:T(8,128)(2,1)S(1)}, bf16[80,6144]{1,0:T(8,128)(2,1)S(1)}, u32[]{:S(2)}, u32[]{:S(2)}) %collective-permute-start.16) | collective-permute-done | bytes 983072 | tf_op jit(solution)/shard_map/ppermute | solution.py:304
  125.2 1.7 collective-permute-done.17.refs_1_
  126.9 7.3 %shard_map.95 = (bf16[80,1536]{1,0:T(8,128)(2,1)S(1)}, bf16[80,1536]{1,0:T(8,128)(2,1)S(1)}) custom-call(bf16[80,6144]{1,0:T(8,128)(2,1)S(1)} %shard_map.94.refs_0_, bf16[80,6144]{1,0:T(8,128)(2,1)S(1)} %collective-permute-done.17.refs_1_, bf16[6144,1536]{1,0:T(8,128)(2,1)} %refs_2_.13, bf16[80,128]{1,0:T(8,128)(2,1)S(1)} %slice.119.refs_3_, ...), custom_call_target="tpu_custom_call" | custom-call | tf_op jit(solution)/shard_map/pallas_call | solution.py:63
  137.5 2.5 %collective-permute-done.19.refs_1_ = bf16[48,6144]{1,0:T(8,128)(2,1)S(1)} collective-permute-done((bf16[48,6144]{1,0:T(8,128)(2,1)S(1)}, bf16[48,6144]{1,0:T(8,128)(2,1)S(1)}, u32[]{:S(2)}, u32[]{:S(2)}) %collective-permute-start.19) | collective-permute-done | bytes 589856 | tf_op jit(solution)/shard_map/ppermute | solution.py:304
  141.6 1.8 %collective-permute-done.20.refs_1_ = bf16[48,6144]{1,0:T(8,128)(2,1)S(1)} collective-permute-done((bf16[48,6144]{1,0:T(8,128)(2,1)S(1)}, bf16[48,6144]{1,0:T(8,128)(2,1)S(1)}, u32[]{:S(2)}, u32[]{:S(2)}) %collective-permute-start.20) | collective-permute-done | bytes 589856 | tf_op jit(solution)/shard_map/ppermute | solution.py:298
  143.4 7.3 %shard_map.98 = (bf16[48,1536]{1,0:T(8,128)(2,1)S(1)}, bf16[48,1536]{1,0:T(8,128)(2,1)S(1)}) custom-call(bf16[48,6144]{1,0:T(8,128)(2,1)S(1)} %shard_map.97.refs_0_, bf16[48,6144]{1,0:T(8,128)(2,1)S(1)} %collective-permute-done.20.refs_1_, bf16[6144,1536]{1,0:T(8,128)(2,1)} %refs_2_.13, bf16[48,128]{1,0:T(8,128)(2,1)S(1)} %slice.121.refs_3_, ...), custom_call_target="tpu_custom_call" | custom-call | tf_op jit(solution)/shard_map/pallas_call | solution.py:63
  152.2 1.9 %collective-permute-start.22 = (bf16[48,768]{1,0:T(8,128)(2,1)S(1)}, bf16[48,768]{1,0:T(8,128)(2,1)S(1)}, u32[]{:S(2)}, u32[]{:S(2)}) collective-permute-start(bf16[48,768]{1,0:T(8,128)(2,1)S(1)} %get-tuple-element.41), channel_id=1, source_target_pairs={{0,12},{4,8},{8,4},{12,0},{1,13},{5,9},{9,5},{13,1},{2,14},{6,10},... | collective-permute-start | bytes 221192 | tf_op jit(solution)/shard_map/ppermute | solution.py:321
  154.1 2.6 %collective-permute-start.24 = (bf16[48,768]{1,0:T(8,128)(2,1)S(1)}, bf16[48,768]{1,0:T(8,128)(2,1)S(1)}, u32[]{:S(2)}, u32[]{:S(2)}) collective-permute-start(bf16[48,768]{1,0:T(8,128)(2,1)S(1)} %get-tuple-element.42), channel_id=1, source_target_pairs={{0,4},{4,0},{8,12},{12,8},{1,5},{5,1},{9,13},{13,9},{2,6},{6,2},{1... | collective-permute-start | bytes 221192 | tf_op jit(solution)/shard_map/ppermute | solution.py:321
  156.7 3.2 %collective-permute-done.22 = bf16[48,768]{1,0:T(8,128)(2,1)S(1)} collective-permute-done((bf16[48,768]{1,0:T(8,128)(2,1)S(1)}, bf16[48,768]{1,0:T(8,128)(2,1)S(1)}, u32[]{:S(2)}, u32[]{:S(2)}) %collective-permute-start.22) | collective-permute-done | bytes 73760 | tf_op jit(solution)/shard_map/ppermute | solution.py:321
  159.9 4.5 %collective-permute-done.23 = bf16[48,768]{1,0:T(8,128)(2,1)S(1)} collective-permute-done((bf16[48,768]{1,0:T(8,128)(2,1)S(1)}, bf16[48,768]{1,0:T(8,128)(2,1)S(1)}, u32[]{:S(2)}, u32[]{:S(2)}) %collective-permute-start.23) | collective-permute-done | bytes 73760 | tf_op jit(solution)/shard_map/ppermute | solution.py:321
  (110 shorter events, 32.3 us)
Async XLA Ops:
  6.5 129.3 %reduce-scatter.3.cloned.1.call-start = ((), (), s32[]{:S(2)}) async-start(), calls=%async_computation.2 | async-start | bytes 983040 | tf_op jit(solution)/shard_map/reduce_scatter | solution.py:393
  30.4 3.6 %collective-permute-start = (f32[2,128]{1,0:T(2,128)S(1)}, f32[2,128]{1,0:T(2,128)S(1)}, u32[]{:S(2)}, u32[]{:S(2)}) collective-permute-start(f32[2,128]{1,0:T(2,128)S(1)} %pad_maximum_fusion.6), channel_id=1, source_target_pairs={{0,2},{2,0},{1,3},{3,1},{4,6},{6,4},{5,7},{7,5},{8,10},{10,8},{9,1... | collective-permute-start | bytes 3080 | tf_op jit(solution)/shard_map/ppermute | solution.py:304
  34.4 1.8 %collective-permute-start.1 = (bf16[128,1536]{1,0:T(8,128)(2,1)S(1)}, bf16[128,1536]{1,0:T(8,128)(2,1)S(1)}, u32[]{:S(2)}, u32[]{:S(2)}) collective-permute-start(bf16[128,1536]{1,0:T(8,128)(2,1)S(1)} %get-tuple-element.39), channel_id=1, source_target_pairs={{0,1},{1,0},{2,3},{3,2},{4,5},{5,4},{6,7},{7,6},{8,9},{9,8},{10,11... | collective-permute-start | bytes 1179656 | tf_op jit(solution)/shard_map/ppermute | solution.py:298
  41.7 2.4 %collective-permute-start.2 = (bf16[128,3072]{1,0:T(8,128)(2,1)S(1)}, bf16[128,3072]{1,0:T(8,128)(2,1)S(1)}, u32[]{:S(2)}, u32[]{:S(2)}) collective-permute-start(bf16[128,3072]{1,0:T(8,128)(2,1)S(1)} %slice.152), channel_id=1, source_target_pairs={{0,1},{1,0},{2,3},{3,2},{4,5},{5,4},{6,7},{7,6},{8,9},{9,8},{10,11... | collective-permute-start | bytes 2359304 | tf_op jit(solution)/shard_map/ppermute | solution.py:298
  44.7 24.0 %collective-permute-start.6 = (bf16[128,3072]{1,0:T(8,128)(2,1)S(1)}, bf16[128,3072]{1,0:T(8,128)(2,1)S(1)}, u32[]{:S(2)}, u32[]{:S(2)}) collective-permute-start(bf16[128,3072]{1,0:T(8,128)(2,1)S(1)} %fusion.13.refs_0_), channel_id=1, source_target_pairs={{0,2},{2,0},{1,3},{3,1},{4,6},{6,4},{5,7},{7,5},{8,10},{10,8},{9,1... | collective-permute-start | bytes 2359304 | tf_op jit(solution)/shard_map/ppermute | solution.py:304
  65.3 5.3 %collective-permute-start.5 = (f32[2,128]{1,0:T(2,128)S(1)}, f32[2,128]{1,0:T(2,128)S(1)}, u32[]{:S(2)}, u32[]{:S(2)}) collective-permute-start(f32[2,128]{1,0:T(2,128)S(1)} %pad_maximum_fusion.7), channel_id=1, source_target_pairs={{0,2},{2,0},{1,3},{3,1},{4,6},{6,4},{5,7},{7,5},{8,10},{10,8},{9,1... | collective-permute-start | bytes 3080 | tf_op jit(solution)/shard_map/ppermute | solution.py:304
  68.6 3.0 %collective-permute-start.3 = (bf16[128,3072]{1,0:T(8,128)(2,1)S(1)}, bf16[128,3072]{1,0:T(8,128)(2,1)S(1)}, u32[]{:S(2)}, u32[]{:S(2)}) collective-permute-start(bf16[128,3072]{1,0:T(8,128)(2,1)S(1)} %slice.151), channel_id=1, source_target_pairs={{0,1},{1,0},{2,3},{3,2},{4,5},{5,4},{6,7},{7,6},{8,9},{9,8},{10,11... | collective-permute-start | bytes 2359304 | tf_op jit(solution)/shard_map/ppermute | solution.py:298
  70.6 3.1 %collective-permute-start.8 = (bf16[128,3072]{1,0:T(8,128)(2,1)S(1)}, bf16[128,3072]{1,0:T(8,128)(2,1)S(1)}, u32[]{:S(2)}, u32[]{:S(2)}) collective-permute-start(bf16[128,3072]{1,0:T(8,128)(2,1)S(1)} %shard_map.82.refs_0_), channel_id=1, source_target_pairs={{0,1},{1,0},{2,3},{3,2},{4,5},{5,4},{6,7},{7,6},{8,9},{9,8},{10,11... | collective-permute-start | bytes 2359304 | tf_op jit(solution)/shard_map/ppermute | solution.py:298
  71.6 2.1 %collective-permute-start.7 = (bf16[128,1536]{1,0:T(8,128)(2,1)S(1)}, bf16[128,1536]{1,0:T(8,128)(2,1)S(1)}, u32[]{:S(2)}, u32[]{:S(2)}) collective-permute-start(bf16[128,1536]{1,0:T(8,128)(2,1)S(1)} %get-tuple-element.37), channel_id=1, source_target_pairs={{0,1},{1,0},{2,3},{3,2},{4,5},{5,4},{6,7},{7,6},{8,9},{9,8},{10,11... | collective-permute-start | bytes 1179656 | tf_op jit(solution)/shard_map/ppermute | solution.py:298
  71.8 25.7 %collective-permute-start.4 = (bf16[128,3072]{1,0:T(8,128)(2,1)S(1)}, bf16[128,3072]{1,0:T(8,128)(2,1)S(1)}, u32[]{:S(2)}, u32[]{:S(2)}) collective-permute-start(bf16[128,3072]{1,0:T(8,128)(2,1)S(1)} %fusion.12.refs_4_.refs_0_), channel_id=1, source_target_pairs={{0,2},{2,0},{1,3},{3,1},{4,6},{6,4},{5,7},{7,5},{8,10},{10,8},{9,1... | collective-permute-start | bytes 2359304 | tf_op jit(solution)/shard_map/ppermute | solution.py:304
  85.8 10.9 %collective-permute-start.11 = (bf16[128,2048]{1,0:T(8,128)(2,1)S(1)}, bf16[128,2048]{1,0:T(8,128)(2,1)S(1)}, u32[]{:S(2)}, u32[]{:S(2)}) collective-permute-start(bf16[128,2048]{1,0:T(8,128)(2,1)S(1)} %get-tuple-element.24), channel_id=1, source_target_pairs={{0,1},{1,0},{2,3},{3,2},{4,5},{5,4},{6,7},{7,6},{8,9},{9,8},{10,11... | collective-permute-start | bytes 1572872 | tf_op jit(solution)/shard_map/ppermute | solution.py:298
  86.1 12.2 %collective-permute-start.14 = (bf16[128,4096]{1,0:T(8,128)(2,1)S(1)}, bf16[128,4096]{1,0:T(8,128)(2,1)S(1)}, u32[]{:S(2)}, u32[]{:S(2)}) collective-permute-start(bf16[128,4096]{1,0:T(8,128)(2,1)S(1)} %get-tuple-element.26), channel_id=1, source_target_pairs={{0,1},{1,0},{2,3},{3,2},{4,5},{5,4},{6,7},{7,6},{8,9},{9,8},{10,11... | collective-permute-start | bytes 3145736 | tf_op jit(solution)/shard_map/ppermute | solution.py:298
  86.4 3.2 %collective-permute-start.9 = (bf16[256,384]{1,0:T(8,128)(2,1)S(1)}, bf16[256,384]{1,0:T(8,128)(2,1)S(1)}, u32[]{:S(2)}, u32[]{:S(2)}) collective-permute-start(bf16[256,384]{1,0:T(8,128)(2,1)S(1)} %get-tuple-element.20), channel_id=1, source_target_pairs={{0,1},{1,0},{2,3},{3,2},{4,5},{5,4},{6,7},{7,6},{8,9},{9,8},{10,11... | collective-permute-start | bytes 589832 | tf_op jit(solution)/shard_map/ppermute | solution.py:298
  89.6 7.1 %collective-permute-start.10 = (bf16[256,384]{1,0:T(8,128)(2,1)S(1)}, bf16[256,384]{1,0:T(8,128)(2,1)S(1)}, u32[]{:S(2)}, u32[]{:S(2)}) collective-permute-start(bf16[256,384]{1,0:T(8,128)(2,1)S(1)} %shard_map.84.refs_0_), channel_id=1, source_target_pairs={{0,2},{2,0},{1,3},{3,1},{4,6},{6,4},{5,7},{7,5},{8,10},{10,8},{9,1... | collective-permute-start | bytes 589832 | tf_op jit(solution)/shard_map/ppermute | solution.py:304
  98.2 2.6 %collective-permute-start.12 = (bf16[128,3072]{1,0:T(8,128)(2,1)S(1)}, bf16[128,3072]{1,0:T(8,128)(2,1)S(1)}, u32[]{:S(2)}, u32[]{:S(2)}) collective-permute-start(bf16[128,3072]{1,0:T(8,128)(2,1)S(1)} %shard_map.89.refs_4_.refs_0_), channel_id=1, source_target_pairs={{0,1},{1,0},{2,3},{3,2},{4,5},{5,4},{6,7},{7,6},{8,9},{9,8},{10,11... | collective-permute-start | bytes 2359304 | tf_op jit(solution)/shard_map/ppermute | solution.py:298
  98.5 24.2 %collective-permute-start.16 = (bf16[80,6144]{1,0:T(8,128)(2,1)S(1)}, bf16[80,6144]{1,0:T(8,128)(2,1)S(1)}, u32[]{:S(2)}, u32[]{:S(2)}) collective-permute-start(bf16[80,6144]{1,0:T(8,128)(2,1)S(1)} %shard_map.90.refs_4_.refs_0_), channel_id=1, source_target_pairs={{0,2},{2,0},{1,3},{3,1},{4,6},{6,4},{5,7},{7,5},{8,10},{10,8},{9,1... | collective-permute-start | bytes 2949128 | tf_op jit(solution)/shard_map/ppermute | solution.py:304
  107.0 1.8 %collective-permute-start.15 = (bf16[128,1536]{1,0:T(8,128)(2,1)S(1)}, bf16[128,1536]{1,0:T(8,128)(2,1)S(1)}, u32[]{:S(2)}, u32[]{:S(2)}) collective-permute-start(bf16[128,1536]{1,0:T(8,128)(2,1)S(1)} %get-tuple-element.28), channel_id=1, source_target_pairs={{0,1},{1,0},{2,3},{3,2},{4,5},{5,4},{6,7},{7,6},{8,9},{9,8},{10,11... | collective-permute-start | bytes 1179656 | tf_op jit(solution)/shard_map/ppermute | solution.py:298
  109.7 54.8 %reduce-scatter.5.cloned.1.call-start = ((), (), s32[]{:S(2)}) async-start(), calls=%async_computation.3 | async-start | bytes 614400 | tf_op jit(solution)/shard_map/reduce_scatter | solution.py:393
  124.2 2.6 %collective-permute-start.17 = (bf16[80,6144]{1,0:T(8,128)(2,1)S(1)}, bf16[80,6144]{1,0:T(8,128)(2,1)S(1)}, u32[]{:S(2)}, u32[]{:S(2)}) collective-permute-start(bf16[80,6144]{1,0:T(8,128)(2,1)S(1)} %shard_map.94.refs_0_), channel_id=1, source_target_pairs={{0,1},{1,0},{2,3},{3,2},{4,5},{5,4},{6,7},{7,6},{8,9},{9,8},{10,11... | collective-permute-start | bytes 2949128 | tf_op jit(solution)/shard_map/ppermute | solution.py:298
  124.3 15.7 %collective-permute-start.19 = (bf16[48,6144]{1,0:T(8,128)(2,1)S(1)}, bf16[48,6144]{1,0:T(8,128)(2,1)S(1)}, u32[]{:S(2)}, u32[]{:S(2)}) collective-permute-start(bf16[48,6144]{1,0:T(8,128)(2,1)S(1)} %shard_map.91.refs_8_.refs_0_), channel_id=1, source_target_pairs={{0,2},{2,0},{1,3},{3,1},{4,6},{6,4},{5,7},{7,5},{8,10},{10,8},{9,1... | collective-permute-start | bytes 1769480 | tf_op jit(solution)/shard_map/ppermute | solution.py:304
  141.4 2.1 %collective-permute-start.20 = (bf16[48,6144]{1,0:T(8,128)(2,1)S(1)}, bf16[48,6144]{1,0:T(8,128)(2,1)S(1)}, u32[]{:S(2)}, u32[]{:S(2)}) collective-permute-start(bf16[48,6144]{1,0:T(8,128)(2,1)S(1)} %shard_map.97.refs_0_), channel_id=1, source_target_pairs={{0,1},{1,0},{2,3},{3,2},{4,5},{5,4},{6,7},{7,6},{8,9},{9,8},{10,11... | collective-permute-start | bytes 1769480 | tf_op jit(solution)/shard_map/ppermute | solution.py:298
  152.2 7.7 %collective-permute-start.22 = (bf16[48,768]{1,0:T(8,128)(2,1)S(1)}, bf16[48,768]{1,0:T(8,128)(2,1)S(1)}, u32[]{:S(2)}, u32[]{:S(2)}) collective-permute-start(bf16[48,768]{1,0:T(8,128)(2,1)S(1)} %get-tuple-element.41), channel_id=1, source_target_pairs={{0,12},{4,8},{8,4},{12,0},{1,13},{5,9},{9,5},{13,1},{2,14},{6,10},... | collective-permute-start | bytes 221192 | tf_op jit(solution)/shard_map/ppermute | solution.py:321
  154.1 10.4 %collective-permute-start.23 = (bf16[48,768]{1,0:T(8,128)(2,1)S(1)}, bf16[48,768]{1,0:T(8,128)(2,1)S(1)}, u32[]{:S(2)}, u32[]{:S(2)}) collective-permute-start(bf16[48,768]{1,0:T(8,128)(2,1)S(1)} %get-tuple-element.43), channel_id=1, source_target_pairs={{0,8},{4,12},{8,0},{12,4},{1,9},{5,13},{9,1},{13,5},{2,10},{6,14},... | collective-permute-start | bytes 221192 | tf_op jit(solution)/shard_map/ppermute | solution.py:321
  154.1 10.4 %collective-permute-start.24 = (bf16[48,768]{1,0:T(8,128)(2,1)S(1)}, bf16[48,768]{1,0:T(8,128)(2,1)S(1)}, u32[]{:S(2)}, u32[]{:S(2)}) collective-permute-start(bf16[48,768]{1,0:T(8,128)(2,1)S(1)} %get-tuple-element.42), channel_id=1, source_target_pairs={{0,4},{4,0},{8,12},{12,8},{1,5},{5,1},{9,13},{13,9},{2,6},{6,2},{1... | collective-permute-start | bytes 221192 | tf_op jit(solution)/shard_map/ppermute | solution.py:321
  (11 other events, 70.4 us)
Sparse Core Ops, SparseCore 0:
  109.8 22.5 reduce-scatter.2
  141.7 21.9 reduce-scatter.4

commit v20 on v18

--- a/solution.py
+++ b/solution.py
@@ -407,10 +407,10 @@
 
         hidden = gelu_sum(parts, [full])
         terms = output(hidden, swap(hidden), slice(0, units), (), cuts[1])
-        full, got = scatter(terms[0], swap(terms[1]), [scattered[0]])
+        full, got = scatter(terms[0], swap(terms[1]), [])
         scattered.append(got)
 
-        hidden = gelu_sum(coming, [full])
+        hidden = gelu_sum(coming, [full, scattered[0]])
         kept, sent = output(hidden, swap(hidden), slice(0, units), (), cuts[2])
         outs = [tokens[cut].astype(F32) + got.astype(F32) for cut, got in zip(cuts, scattered)]
         outs.append(tokens[cuts[2]].astype(F32) + collect(kept, swap(sent), width))

time: 174 us -> 175 us (level)
  no operation moved by 1% of the time
where the time goes in v20:
time: 175 us
  Pallas kernels  43.7 us (25%)
  waiting for transfers between devices  43.1 us (25%)
  blocking collectives  39.9 us (23%)
  between operations  15.4 us (9%)
  starting transfers between devices  15.2 us (9%)
  matrix products  7.91 us (5%)
  local copies, waits for them, and re-layouts  5.78 us (3%)
  other arithmetic  3.78 us (2%)
    pallas_call x17, Pallas kernels, call(): pl.pallas_call(body, in_specs=list(specs) + [corner_of(a) for a in earlie...  43.7 us
    all_gather x1, blocking collectives, body(): lead = lax.all_gather(lead, 'wide', axis=1, tiled=True)  21.9 us
    ppermute x7, waiting for transfers between devices, all_red(): parts.append(lax.ppermute(x, 'red', pairs))  19.6 us
    all_gather x1, blocking collectives, body(): rest = lax.all_gather(rest, 'wide', axis=1, tiled=True)  18 us
    ppermute x15, waiting for transfers between devices, swap(): return lax.ppermute(x, 'tok', [(0, 1), (1, 0)])  15.7 us
    dot_general x2, matrix products, project(): part = jnp.dot(both, weight, preferred_element_type=F32)  7.91 us
    ppermute x3, waiting for transfers between devices, collect(): total = total + lax.ppermute(block(chip ^ k), 'wide', pairs).astype(F32)  7.75 us
    ppermute x7, starting transfers between devices, all_red(): parts.append(lax.ppermute(x, 'red', pairs))  7.65 us
  transfers between devices with their start and end apart: 27, of which 16 were waited for; matrix products, arithmetic and copies ran while one was open for 3% of the time, Pallas kernels for 24%

profile of v20, /device:TPU:0, one launch (start us, length us, event | category | flops | bytes accessed | tf_op | source)
XLA Modules:
  0.0 174.7 jit_solution(4091799767194598091)
XLA Ops:
  8.2 21.9 %all_gather.6 = bf16[136,3072]{1,0:T(8,128)(2,1)S(1)} all-gather(bf16[136,768]{1,0:T(8,128)(2,1)S(1)} %pad_maximum_fusion.5), channel_id=1, replica_groups=mesh['grp'=2,'wide'=4,'red'=2,'tok'=2] {'wide'}, dimensions={1}, use_global_device_ids=true | all-gather | bytes 1044480 | tf_op jit(solution)/shard_map/all_gather | solution.py:337
  31.9 2.1 %collective-permute-done = f32[2,128]{1,0:T(2,128)S(1)} collective-permute-done((f32[2,128]{1,0:T(2,128)S(1)}, f32[2,128]{1,0:T(2,128)S(1)}, u32[]{:S(2)}, u32[]{:S(2)}) %collective-permute-start) | collective-permute-done | bytes 1056 | tf_op jit(solution)/shard_map/ppermute | solution.py:304
  34.5 1.7 collective-permute-done.1
  36.2 5.3 %fusion.2 = f32[256,3072]{1,0:T(8,128)S(1)} fusion(bf16[1536,6144]{1,0:T(8,128)(2,1)} %refs_2_.8, bf16[128,1536]{1,0:T(8,128)(2,1)S(1)} %get-tuple-element.40, bf16[128,1536]{1,0:T(8,128)(2,1)S(1)} %collective-permute-done.1), kind=kOutput, calls=%fused_computation.2 | convolution fusion | flops 2417491968 | bytes 13369344 | tf_op jit(solution)/shard_map/dot_general | solution.py:354
  41.9 2.1 %collective-permute-done.2 = bf16[128,3072]{1,0:T(8,128)(2,1)S(1)} collective-permute-done((bf16[128,3072]{1,0:T(8,128)(2,1)S(1)}, bf16[128,3072]{1,0:T(8,128)(2,1)S(1)}, u32[]{:S(2)}, u32[]{:S(2)}) %collective-permute-start.2) | collective-permute-done | bytes 786464 | tf_op jit(solution)/shard_map/ppermute | solution.py:298
  46.9 18.0 %all_gather.7 = bf16[128,3072]{1,0:T(8,128)(2,1)S(1)} all-gather(bf16[128,768]{1,0:T(8,128)(2,1)S(1)} %slice_add_fusion.2), channel_id=1, replica_groups=mesh['grp'=2,'wide'=4,'red'=2,'tok'=2] {'wide'}, dimensions={1}, use_global_device_ids=true | all-gather | bytes 983040 | tf_op jit(solution)/shard_map/all_gather | solution.py:365
  65.9 2.6 %fusion = f32[256,3072]{1,0:T(8,128)S(1)} fusion(bf16[1536,6144]{1,0:T(8,128)(2,1)S(1)} %copy-done.5, bf16[128,1536]{1,0:T(8,128)(2,1)S(1)} %get-tuple-element.44, bf16[128,1536]{1,0:T(8,128)(2,1)S(1)} %get-tuple-element.45), kind=kOutput, calls=%fused_computation | convolution fusion | flops 2417491968 | bytes 13369344 | tf_op jit(solution)/shard_map/dot_general | solution.py:354
  71.9 1.6 collective-permute-start.4
  76.1 6.1 %shard_map.85 = (bf16[128,4096]{1,0:T(8,128)(2,1)S(1)}, bf16[128,4096]{1,0:T(8,128)(2,1)S(1)}) custom-call(bf16[128,1536]{1,0:T(8,128)(2,1)S(1)} %get-tuple-element.38.refs_0_, bf16[128,1536]{1,0:T(8,128)(2,1)S(1)} %collective-permute-done.7.refs_1_, bf16[1536,6144]{1,0:T(8,128)(2,1)} %refs_2_.8, bf16[256,384]{1,0:T(8,128)(2,1)S(1)} %get-tuple-element.19.refs_0_.refs_3_), custom_call_target="tpu_custom_call" | custom-call | tf_op jit(solution)/shard_map/pallas_call | solution.py:63
  82.1 3.7 %shard_map.86 = (bf16[128,2048]{1,0:T(8,128)(2,1)S(1)}, bf16[128,2048]{1,0:T(8,128)(2,1)S(1)}) custom-call(bf16[128,1536]{1,0:T(8,128)(2,1)S(1)} %get-tuple-element.38.refs_0_, bf16[128,1536]{1,0:T(8,128)(2,1)S(1)} %collective-permute-done.7.refs_1_, bf16[1536,6144]{1,0:T(8,128)(2,1)} %refs_2_.8, bf16[128,4096]{1,0:T(8,128)(2,1)S(1)} %get-tuple-element.21.refs_3_.refs_0_), custom_call_target="tpu_custom_call" | custom-call | tf_op jit(solution)/shard_map/pallas_call | solution.py:63
  86.7 3.0 %collective-permute-done.9.refs_1_ = bf16[256,384]{1,0:T(8,128)(2,1)S(1)} collective-permute-done((bf16[256,384]{1,0:T(8,128)(2,1)S(1)}, bf16[256,384]{1,0:T(8,128)(2,1)S(1)}, u32[]{:S(2)}, u32[]{:S(2)}) %collective-permute-start.9) | collective-permute-done | bytes 196640 | tf_op jit(solution)/shard_map/ppermute | solution.py:298
  90.3 5.1 %shard_map.87 = (f32[128,1536]{1,0:T(8,128)S(1)}, f32[128,1536]{1,0:T(8,128)S(1)}) custom-call(bf16[128,3072]{1,0:T(8,128)(2,1)S(1)} %shard_map.82.refs_0_, bf16[128,3072]{1,0:T(8,128)(2,1)S(1)} %collective-permute-done.8.refs_3_.refs_1_, bf16[6144,1536]{1,0:T(8,128)(2,1)} %refs_2_.13, bf16[128,2048]{1,0:T(8,128)(2,1)S(1)} %get-tuple-element.22.refs_3_.refs_2_), custom_call_target="tpu_custom_call" | custom-call | tf_op jit(solution)/shard_map/pallas_call | solution.py:63
  101.8 5.3 %shard_map.92 = (bf16[128,1536]{1,0:T(8,128)(2,1)S(1)}, bf16[128,1536]{1,0:T(8,128)(2,1)S(1)}) custom-call(bf16[128,3072]{1,0:T(8,128)(2,1)S(1)} %shard_map.89.refs_4_.refs_0_, bf16[128,3072]{1,0:T(8,128)(2,1)S(1)} %collective-permute-done.12.refs_1_, bf16[6144,1536]{1,0:T(8,128)(2,1)} %refs_2_.13, f32[128,1536]{1,0:T(8,128)S(1)} %get-tuple-element.23.refs_4_.refs_3_, ...), custom_call_target="tpu_custom_call" | custom-call | tf_op jit(solution)/shard_map/pallas_call | solution.py:63
  110.1 12.8 %collective-permute-done.16.refs_1_ = bf16[80,6144]{1,0:T(8,128)(2,1)S(1)} collective-permute-done((bf16[80,6144]{1,0:T(8,128)(2,1)S(1)}, bf16[80,6144]{1,0:T(8,128)(2,1)S(1)}, u32[]{:S(2)}, u32[]{:S(2)}) %collective-permute-start.16) | collective-permute-done | bytes 983072 | tf_op jit(solution)/shard_map/ppermute | solution.py:304
  122.9 1.7 shard_map.94.refs_0_
  125.6 1.6 collective-permute-done.17.refs_1_
  127.2 7.3 %shard_map.95 = (bf16[80,1536]{1,0:T(8,128)(2,1)S(1)}, bf16[80,1536]{1,0:T(8,128)(2,1)S(1)}) custom-call(bf16[80,6144]{1,0:T(8,128)(2,1)S(1)} %shard_map.94.refs_0_, bf16[80,6144]{1,0:T(8,128)(2,1)S(1)} %collective-permute-done.17.refs_1_, bf16[6144,1536]{1,0:T(8,128)(2,1)} %refs_2_.13, bf16[80,128]{1,0:T(8,128)(2,1)S(1)} %slice.119.refs_3_, ...), custom_call_target="tpu_custom_call" | custom-call | tf_op jit(solution)/shard_map/pallas_call | solution.py:63
  136.9 3.4 %collective-permute-done.19.refs_1_ = bf16[48,6144]{1,0:T(8,128)(2,1)S(1)} collective-permute-done((bf16[48,6144]{1,0:T(8,128)(2,1)S(1)}, bf16[48,6144]{1,0:T(8,128)(2,1)S(1)}, u32[]{:S(2)}, u32[]{:S(2)}) %collective-permute-start.19) | collective-permute-done | bytes 589856 | tf_op jit(solution)/shard_map/ppermute | solution.py:304
  143.1 1.8 %collective-permute-done.20.refs_1_ = bf16[48,6144]{1,0:T(8,128)(2,1)S(1)} collective-permute-done((bf16[48,6144]{1,0:T(8,128)(2,1)S(1)}, bf16[48,6144]{1,0:T(8,128)(2,1)S(1)}, u32[]{:S(2)}, u32[]{:S(2)}) %collective-permute-start.20) | collective-permute-done | bytes 589856 | tf_op jit(solution)/shard_map/ppermute | solution.py:298
  144.9 7.3 %shard_map.98 = (bf16[48,1536]{1,0:T(8,128)(2,1)S(1)}, bf16[48,1536]{1,0:T(8,128)(2,1)S(1)}) custom-call(bf16[48,6144]{1,0:T(8,128)(2,1)S(1)} %shard_map.97.refs_0_, bf16[48,6144]{1,0:T(8,128)(2,1)S(1)} %collective-permute-done.20.refs_1_, bf16[6144,1536]{1,0:T(8,128)(2,1)} %refs_2_.13, bf16[48,128]{1,0:T(8,128)(2,1)S(1)} %slice.121.refs_3_, ...), custom_call_target="tpu_custom_call" | custom-call | tf_op jit(solution)/shard_map/pallas_call | solution.py:63
  153.7 1.9 %collective-permute-start.22 = (bf16[48,768]{1,0:T(8,128)(2,1)S(1)}, bf16[48,768]{1,0:T(8,128)(2,1)S(1)}, u32[]{:S(2)}, u32[]{:S(2)}) collective-permute-start(bf16[48,768]{1,0:T(8,128)(2,1)S(1)} %get-tuple-element.41), channel_id=1, source_target_pairs={{0,12},{4,8},{8,4},{12,0},{1,13},{5,9},{9,5},{13,1},{2,14},{6,10},... | collective-permute-start | bytes 221192 | tf_op jit(solution)/shard_map/ppermute | solution.py:321
  155.6 2.6 %collective-permute-start.24 = (bf16[48,768]{1,0:T(8,128)(2,1)S(1)}, bf16[48,768]{1,0:T(8,128)(2,1)S(1)}, u32[]{:S(2)}, u32[]{:S(2)}) collective-permute-start(bf16[48,768]{1,0:T(8,128)(2,1)S(1)} %get-tuple-element.42), channel_id=1, source_target_pairs={{0,4},{4,0},{8,12},{12,8},{1,5},{5,1},{9,13},{13,9},{2,6},{6,2},{1... | collective-permute-start | bytes 221192 | tf_op jit(solution)/shard_map/ppermute | solution.py:321
  158.2 3.2 %collective-permute-done.22 = bf16[48,768]{1,0:T(8,128)(2,1)S(1)} collective-permute-done((bf16[48,768]{1,0:T(8,128)(2,1)S(1)}, bf16[48,768]{1,0:T(8,128)(2,1)S(1)}, u32[]{:S(2)}, u32[]{:S(2)}) %collective-permute-start.22) | collective-permute-done | bytes 73760 | tf_op jit(solution)/shard_map/ppermute | solution.py:321
  161.4 4.5 %collective-permute-done.23 = bf16[48,768]{1,0:T(8,128)(2,1)S(1)} collective-permute-done((bf16[48,768]{1,0:T(8,128)(2,1)S(1)}, bf16[48,768]{1,0:T(8,128)(2,1)S(1)}, u32[]{:S(2)}, u32[]{:S(2)}) %collective-permute-start.23) | collective-permute-done | bytes 73760 | tf_op jit(solution)/shard_map/ppermute | solution.py:321
  (108 shorter events, 32.7 us)
Async XLA Ops:
  6.5 133.9 %reduce-scatter.3.cloned.1.call-start = ((), (), s32[]{:S(2)}) async-start(), calls=%async_computation.2 | async-start | bytes 983040 | tf_op jit(solution)/shard_map/reduce_scatter | solution.py:393
  30.4 3.6 %collective-permute-start = (f32[2,128]{1,0:T(2,128)S(1)}, f32[2,128]{1,0:T(2,128)S(1)}, u32[]{:S(2)}, u32[]{:S(2)}) collective-permute-start(f32[2,128]{1,0:T(2,128)S(1)} %pad_maximum_fusion.6), channel_id=1, source_target_pairs={{0,2},{2,0},{1,3},{3,1},{4,6},{6,4},{5,7},{7,5},{8,10},{10,8},{9,1... | collective-permute-start | bytes 3080 | tf_op jit(solution)/shard_map/ppermute | solution.py:304
  34.4 1.8 %collective-permute-start.1 = (bf16[128,1536]{1,0:T(8,128)(2,1)S(1)}, bf16[128,1536]{1,0:T(8,128)(2,1)S(1)}, u32[]{:S(2)}, u32[]{:S(2)}) collective-permute-start(bf16[128,1536]{1,0:T(8,128)(2,1)S(1)} %get-tuple-element.39), channel_id=1, source_target_pairs={{0,1},{1,0},{2,3},{3,2},{4,5},{5,4},{6,7},{7,6},{8,9},{9,8},{10,11... | collective-permute-start | bytes 1179656 | tf_op jit(solution)/shard_map/ppermute | solution.py:298
  41.7 2.4 %collective-permute-start.2 = (bf16[128,3072]{1,0:T(8,128)(2,1)S(1)}, bf16[128,3072]{1,0:T(8,128)(2,1)S(1)}, u32[]{:S(2)}, u32[]{:S(2)}) collective-permute-start(bf16[128,3072]{1,0:T(8,128)(2,1)S(1)} %slice.152), channel_id=1, source_target_pairs={{0,1},{1,0},{2,3},{3,2},{4,5},{5,4},{6,7},{7,6},{8,9},{9,8},{10,11... | collective-permute-start | bytes 2359304 | tf_op jit(solution)/shard_map/ppermute | solution.py:298
  44.7 24.0 %collective-permute-start.6 = (bf16[128,3072]{1,0:T(8,128)(2,1)S(1)}, bf16[128,3072]{1,0:T(8,128)(2,1)S(1)}, u32[]{:S(2)}, u32[]{:S(2)}) collective-permute-start(bf16[128,3072]{1,0:T(8,128)(2,1)S(1)} %fusion.13.refs_0_), channel_id=1, source_target_pairs={{0,2},{2,0},{1,3},{3,1},{4,6},{6,4},{5,7},{7,5},{8,10},{10,8},{9,1... | collective-permute-start | bytes 2359304 | tf_op jit(solution)/shard_map/ppermute | solution.py:304
  65.3 5.4 %collective-permute-start.5 = (f32[2,128]{1,0:T(2,128)S(1)}, f32[2,128]{1,0:T(2,128)S(1)}, u32[]{:S(2)}, u32[]{:S(2)}) collective-permute-start(f32[2,128]{1,0:T(2,128)S(1)} %pad_maximum_fusion.7), channel_id=1, source_target_pairs={{0,2},{2,0},{1,3},{3,1},{4,6},{6,4},{5,7},{7,5},{8,10},{10,8},{9,1... | collective-permute-start | bytes 3080 | tf_op jit(solution)/shard_map/ppermute | solution.py:304
  68.6 3.1 %collective-permute-start.3 = (bf16[128,3072]{1,0:T(8,128)(2,1)S(1)}, bf16[128,3072]{1,0:T(8,128)(2,1)S(1)}, u32[]{:S(2)}, u32[]{:S(2)}) collective-permute-start(bf16[128,3072]{1,0:T(8,128)(2,1)S(1)} %slice.151), channel_id=1, source_target_pairs={{0,1},{1,0},{2,3},{3,2},{4,5},{5,4},{6,7},{7,6},{8,9},{9,8},{10,11... | collective-permute-start | bytes 2359304 | tf_op jit(solution)/shard_map/ppermute | solution.py:298
  70.7 3.1 %collective-permute-start.8 = (bf16[128,3072]{1,0:T(8,128)(2,1)S(1)}, bf16[128,3072]{1,0:T(8,128)(2,1)S(1)}, u32[]{:S(2)}, u32[]{:S(2)}) collective-permute-start(bf16[128,3072]{1,0:T(8,128)(2,1)S(1)} %shard_map.82.refs_0_), channel_id=1, source_target_pairs={{0,1},{1,0},{2,3},{3,2},{4,5},{5,4},{6,7},{7,6},{8,9},{9,8},{10,11... | collective-permute-start | bytes 2359304 | tf_op jit(solution)/shard_map/ppermute | solution.py:298
  71.6 2.1 %collective-permute-start.7 = (bf16[128,1536]{1,0:T(8,128)(2,1)S(1)}, bf16[128,1536]{1,0:T(8,128)(2,1)S(1)}, u32[]{:S(2)}, u32[]{:S(2)}) collective-permute-start(bf16[128,1536]{1,0:T(8,128)(2,1)S(1)} %get-tuple-element.37), channel_id=1, source_target_pairs={{0,1},{1,0},{2,3},{3,2},{4,5},{5,4},{6,7},{7,6},{8,9},{9,8},{10,11... | collective-permute-start | bytes 1179656 | tf_op jit(solution)/shard_map/ppermute | solution.py:298
  71.9 25.7 %collective-permute-start.4 = (bf16[128,3072]{1,0:T(8,128)(2,1)S(1)}, bf16[128,3072]{1,0:T(8,128)(2,1)S(1)}, u32[]{:S(2)}, u32[]{:S(2)}) collective-permute-start(bf16[128,3072]{1,0:T(8,128)(2,1)S(1)} %fusion.12.refs_4_.refs_0_), channel_id=1, source_target_pairs={{0,2},{2,0},{1,3},{3,1},{4,6},{6,4},{5,7},{7,5},{8,10},{10,8},{9,1... | collective-permute-start | bytes 2359304 | tf_op jit(solution)/shard_map/ppermute | solution.py:304
  85.9 10.9 %collective-permute-start.11 = (bf16[128,2048]{1,0:T(8,128)(2,1)S(1)}, bf16[128,2048]{1,0:T(8,128)(2,1)S(1)}, u32[]{:S(2)}, u32[]{:S(2)}) collective-permute-start(bf16[128,2048]{1,0:T(8,128)(2,1)S(1)} %get-tuple-element.24), channel_id=1, source_target_pairs={{0,1},{1,0},{2,3},{3,2},{4,5},{5,4},{6,7},{7,6},{8,9},{9,8},{10,11... | collective-permute-start | bytes 1572872 | tf_op jit(solution)/shard_map/ppermute | solution.py:298
  86.2 12.2 %collective-permute-start.14 = (bf16[128,4096]{1,0:T(8,128)(2,1)S(1)}, bf16[128,4096]{1,0:T(8,128)(2,1)S(1)}, u32[]{:S(2)}, u32[]{:S(2)}) collective-permute-start(bf16[128,4096]{1,0:T(8,128)(2,1)S(1)} %get-tuple-element.26), channel_id=1, source_target_pairs={{0,1},{1,0},{2,3},{3,2},{4,5},{5,4},{6,7},{7,6},{8,9},{9,8},{10,11... | collective-permute-start | bytes 3145736 | tf_op jit(solution)/shard_map/ppermute | solution.py:298
  86.5 3.2 %collective-permute-start.9 = (bf16[256,384]{1,0:T(8,128)(2,1)S(1)}, bf16[256,384]{1,0:T(8,128)(2,1)S(1)}, u32[]{:S(2)}, u32[]{:S(2)}) collective-permute-start(bf16[256,384]{1,0:T(8,128)(2,1)S(1)} %get-tuple-element.20), channel_id=1, source_target_pairs={{0,1},{1,0},{2,3},{3,2},{4,5},{5,4},{6,7},{7,6},{8,9},{9,8},{10,11... | collective-permute-start | bytes 589832 | tf_op jit(solution)/shard_map/ppermute | solution.py:298
  89.7 7.1 %collective-permute-start.10 = (bf16[256,384]{1,0:T(8,128)(2,1)S(1)}, bf16[256,384]{1,0:T(8,128)(2,1)S(1)}, u32[]{:S(2)}, u32[]{:S(2)}) collective-permute-start(bf16[256,384]{1,0:T(8,128)(2,1)S(1)} %shard_map.84.refs_0_), channel_id=1, source_target_pairs={{0,2},{2,0},{1,3},{3,1},{4,6},{6,4},{5,7},{7,5},{8,10},{10,8},{9,1... | collective-permute-start | bytes 589832 | tf_op jit(solution)/shard_map/ppermute | solution.py:304
  98.3 2.6 %collective-permute-start.12 = (bf16[128,3072]{1,0:T(8,128)(2,1)S(1)}, bf16[128,3072]{1,0:T(8,128)(2,1)S(1)}, u32[]{:S(2)}, u32[]{:S(2)}) collective-permute-start(bf16[128,3072]{1,0:T(8,128)(2,1)S(1)} %shard_map.89.refs_4_.refs_0_), channel_id=1, source_target_pairs={{0,1},{1,0},{2,3},{3,2},{4,5},{5,4},{6,7},{7,6},{8,9},{9,8},{10,11... | collective-permute-start | bytes 2359304 | tf_op jit(solution)/shard_map/ppermute | solution.py:298
  98.6 24.2 %collective-permute-start.16 = (bf16[80,6144]{1,0:T(8,128)(2,1)S(1)}, bf16[80,6144]{1,0:T(8,128)(2,1)S(1)}, u32[]{:S(2)}, u32[]{:S(2)}) collective-permute-start(bf16[80,6144]{1,0:T(8,128)(2,1)S(1)} %shard_map.90.refs_4_.refs_0_), channel_id=1, source_target_pairs={{0,2},{2,0},{1,3},{3,1},{4,6},{6,4},{5,7},{7,5},{8,10},{10,8},{9,1... | collective-permute-start | bytes 2949128 | tf_op jit(solution)/shard_map/ppermute | solution.py:304
  107.1 1.8 %collective-permute-start.15 = (bf16[128,1536]{1,0:T(8,128)(2,1)S(1)}, bf16[128,1536]{1,0:T(8,128)(2,1)S(1)}, u32[]{:S(2)}, u32[]{:S(2)}) collective-permute-start(bf16[128,1536]{1,0:T(8,128)(2,1)S(1)} %get-tuple-element.28), channel_id=1, source_target_pairs={{0,1},{1,0},{2,3},{3,2},{4,5},{5,4},{6,7},{7,6},{8,9},{9,8},{10,11... | collective-permute-start | bytes 1179656 | tf_op jit(solution)/shard_map/ppermute | solution.py:298
  109.9 56.1 %reduce-scatter.5.cloned.1.call-start = ((), (), s32[]{:S(2)}) async-start(), calls=%async_computation.3 | async-start | bytes 614400 | tf_op jit(solution)/shard_map/reduce_scatter | solution.py:393
  124.6 2.6 %collective-permute-start.17 = (bf16[80,6144]{1,0:T(8,128)(2,1)S(1)}, bf16[80,6144]{1,0:T(8,128)(2,1)S(1)}, u32[]{:S(2)}, u32[]{:S(2)}) collective-permute-start(bf16[80,6144]{1,0:T(8,128)(2,1)S(1)} %shard_map.94.refs_0_), channel_id=1, source_target_pairs={{0,1},{1,0},{2,3},{3,2},{4,5},{5,4},{6,7},{7,6},{8,9},{9,8},{10,11... | collective-permute-start | bytes 2949128 | tf_op jit(solution)/shard_map/ppermute | solution.py:298
  124.7 15.7 %collective-permute-start.19 = (bf16[48,6144]{1,0:T(8,128)(2,1)S(1)}, bf16[48,6144]{1,0:T(8,128)(2,1)S(1)}, u32[]{:S(2)}, u32[]{:S(2)}) collective-permute-start(bf16[48,6144]{1,0:T(8,128)(2,1)S(1)} %shard_map.91.refs_8_.refs_0_), channel_id=1, source_target_pairs={{0,2},{2,0},{1,3},{3,1},{4,6},{6,4},{5,7},{7,5},{8,10},{10,8},{9,1... | collective-permute-start | bytes 1769480 | tf_op jit(solution)/shard_map/ppermute | solution.py:304
  142.8 2.1 %collective-permute-start.20 = (bf16[48,6144]{1,0:T(8,128)(2,1)S(1)}, bf16[48,6144]{1,0:T(8,128)(2,1)S(1)}, u32[]{:S(2)}, u32[]{:S(2)}) collective-permute-start(bf16[48,6144]{1,0:T(8,128)(2,1)S(1)} %shard_map.97.refs_0_), channel_id=1, source_target_pairs={{0,1},{1,0},{2,3},{3,2},{4,5},{5,4},{6,7},{7,6},{8,9},{9,8},{10,11... | collective-permute-start | bytes 1769480 | tf_op jit(solution)/shard_map/ppermute | solution.py:298
  153.7 7.7 %collective-permute-start.22 = (bf16[48,768]{1,0:T(8,128)(2,1)S(1)}, bf16[48,768]{1,0:T(8,128)(2,1)S(1)}, u32[]{:S(2)}, u32[]{:S(2)}) collective-permute-start(bf16[48,768]{1,0:T(8,128)(2,1)S(1)} %get-tuple-element.41), channel_id=1, source_target_pairs={{0,12},{4,8},{8,4},{12,0},{1,13},{5,9},{9,5},{13,1},{2,14},{6,10},... | collective-permute-start | bytes 221192 | tf_op jit(solution)/shard_map/ppermute | solution.py:321
  155.6 10.4 %collective-permute-start.23 = (bf16[48,768]{1,0:T(8,128)(2,1)S(1)}, bf16[48,768]{1,0:T(8,128)(2,1)S(1)}, u32[]{:S(2)}, u32[]{:S(2)}) collective-permute-start(bf16[48,768]{1,0:T(8,128)(2,1)S(1)} %get-tuple-element.43), channel_id=1, source_target_pairs={{0,8},{4,12},{8,0},{12,4},{1,9},{5,13},{9,1},{13,5},{2,10},{6,14},... | collective-permute-start | bytes 221192 | tf_op jit(solution)/shard_map/ppermute | solution.py:321
  155.6 10.4 %collective-permute-start.24 = (bf16[48,768]{1,0:T(8,128)(2,1)S(1)}, bf16[48,768]{1,0:T(8,128)(2,1)S(1)}, u32[]{:S(2)}, u32[]{:S(2)}) collective-permute-start(bf16[48,768]{1,0:T(8,128)(2,1)S(1)} %get-tuple-element.42), channel_id=1, source_target_pairs={{0,4},{4,0},{8,12},{12,8},{1,5},{5,1},{9,13},{13,9},{2,6},{6,2},{1... | collective-permute-start | bytes 221192 | tf_op jit(solution)/shard_map/ppermute | solution.py:321
  (10 other events, 55.3 us)
Sparse Core Ops, SparseCore 0:
  110.0 22.4 reduce-scatter.2
  143.2 21.8 reduce-scatter.4
